TPU v7x, 512 devices: a whole 4x4x16 slice. The times are simulated.
512 devices in a mesh: edge: 128 (over z, x, core), rep: 4 (over y).
Axes of the slice: x: 4, y: 4, z: 16, core: 2. Of those that a mesh axis runs over, the one named last changes fastest.
Arguments:
- node_feat: bfloat16 [4, 512, 3200], P('rep', 'edge'), may hold values from -6 to 6
- rotation: bfloat16 [4, 20480, 475], P('rep', 'edge'), may hold values from -4 to 4, as said below
- source_owner: int32 [4, 20480, 1], P('rep', 'edge'), may hold values from 0 to 127; in each aligned block of 160 rows (0 to 159, 160 to 319, ..., all dimensions but the last counted through in order) at most 2 rows name the same one
- source_row: int32 [4, 20480], P('rep', 'edge'), may hold values from 0 to 3
- target_row: int32 [4, 20480], P('rep', 'edge'), may hold values from 0 to 3
- live_count: int32 [4, 128], P('rep', 'edge'), may hold values from 1 to 160, 17920 in all within a row
- edge_bias: float32 [4, 20480, 8], P('rep', 'edge'), may hold values from -3 to 303
- w_m0: bfloat16 [1280, 640], P('edge'), may hold values from -0.15625 to 0.15625
- w_m1: bfloat16 [2, 1024, 512], P(None, 'edge'), may hold values from -0.125 to 0.125
- w_m2: bfloat16 [2, 768, 384], P(None, 'edge'), may hold values from -0.15625 to 0.15625
- w_alpha: bfloat16 [128, 8], replicated, may hold values from -1.5 to 1.5
- out_grad: float32 [4, 512, 3200], P('rep', 'edge'), may hold values from -6 to 6
Outputs:
- node_out: bfloat16 [4, 512, 3200], P('rep', 'edge')
- grad_nodes: float32 [4, 512, 3200], P('rep', 'edge')
- grad_w0: float32 [1280, 640], P('edge')
Inputs may be any that keep to these rules, and one draw needn't show every extreme that they name: `source_owner`: within the edge rows of one device at most 2 have sources on one owner, and in some device exactly 2 do. `rotation`: an entry is zero unless its row and column belong to the same degree l.
All inputs are finite; a program needn't handle non-finite values. No bound on the sum of `live_count` on one device may be relied on, other than what follows from the above.
Results may differ from a plain program's by a relative error of at most 0.02.
Values may be sent and summed in bfloat16 or wider, within the bound.
No kernel may reach another device: no remote copies, remote signals or barrier semaphores. Data moves between devices by JAX's collectives and lax.ppermute only.
A program may use at most 128 MiB of HBM per device.

v0:
```python
import jax
import jax.numpy as jnp
from jax import lax
from jax.sharding import PartitionSpec as P

LCOEF = 25
MCOEF = 19


row_degrees = (0, 1, 2, 3, 4, 1, 2, 3, 4, 1, 2, 3, 4, 2, 3, 4, 2, 3, 4)


def rotate_into(rotor_rows, feature_blocks):
    coeffs = feature_blocks.shape[1]
    turned = []
    for row in range(len(row_degrees)):
        degree = row_degrees[row]
        total = None
        for column in range(degree * degree, (degree + 1) * (degree + 1)):
            term = rotor_rows[:, row * coeffs + column, None].astype(jnp.float32) * feature_blocks[
                :, column, :
            ].astype(jnp.float32)
            total = term if total is None else total + term
        turned.append(total)
    return jnp.stack(turned, axis=1)


def rotate_back(rotor_rows, frame_blocks, coeffs):
    restored = []
    for column in range(coeffs):
        degree = 0
        while (degree + 1) * (degree + 1) <= column:
            degree = degree + 1
        total = None
        for row in range(len(row_degrees)):
            if row_degrees[row] == degree:
                term = rotor_rows[:, row * coeffs + column, None].astype(
                    jnp.float32
                ) * frame_blocks[:, row, :].astype(jnp.float32)
                total = term if total is None else total + term
        restored.append(total)
    return jnp.stack(restored, axis=1)


def layer_sums(
    message_in, w_zero, w_one, w_two, w_alpha, edge_bias, rotor_rows, targets, is_live, row_count
):
    edge_count = message_in.shape[0]
    full_width = message_in.shape[2]
    channels = full_width // 2
    heads = w_alpha.shape[1]

    def flat(first, last):
        return message_in[:, first:last, :].reshape(edge_count, (last - first) * full_width)

    def pair(plus, minus, weights):
        real_part = jnp.dot(plus, weights[0], preferred_element_type=jnp.float32) - jnp.dot(
            minus, weights[1], preferred_element_type=jnp.float32
        )
        imag_part = jnp.dot(minus, weights[0], preferred_element_type=jnp.float32) + jnp.dot(
            plus, weights[1], preferred_element_type=jnp.float32
        )
        return (real_part, imag_part)

    z_zero = jnp.dot(flat(0, 5), w_zero, preferred_element_type=jnp.float32)
    z_plus1, z_minus1 = pair(flat(5, 9), flat(9, 13), w_one)
    z_plus2, z_minus2 = pair(flat(13, 16), flat(16, 19), w_two)
    z_all = jnp.concatenate([z_zero, z_plus1, z_minus1, z_plus2, z_minus2], axis=1).reshape(
        edge_count, MCOEF, channels
    )
    values = z_all.astype(jnp.bfloat16)
    scalars = jax.nn.silu(z_all[:, 0, :]).astype(jnp.bfloat16)
    logits = edge_bias + jnp.dot(scalars, w_alpha, preferred_element_type=jnp.float32)
    member = (jnp.arange(row_count, dtype=jnp.int32)[:, None] == targets[None, :]) & is_live[
        None, :
    ]
    highest = jnp.max(jnp.where(member[:, :, None], logits[None, :, :], jnp.float32(-1e30)), axis=1)
    highest = lax.stop_gradient(highest)
    shifted = jnp.where(is_live[:, None], logits - highest[targets], jnp.float32(0.0))
    expo = jnp.where(is_live[:, None], jnp.exp(shifted), jnp.float32(0.0))
    member_f = member.astype(jnp.float32)
    totals = jnp.dot(member_f, expo, precision=lax.Precision.HIGHEST)
    denom = jnp.where(is_live[:, None], totals[targets], jnp.float32(1.0))
    attn = expo / denom
    back = rotate_back(rotor_rows, values, LCOEF)
    scale = jnp.repeat(attn, channels // heads, axis=1)
    weighted = (back * scale[:, None, :]).reshape(edge_count, LCOEF * channels)
    return jnp.dot(member_f, weighted, precision=lax.Precision.HIGHEST)


def local(
    node_feat,
    rotation,
    source_owner,
    source_row,
    target_row,
    live_count,
    edge_bias,
    w_m0,
    w_m1,
    w_m2,
    w_alpha,
    out_grad,
):
    features = node_feat[0]
    row_count = features.shape[0]
    full_width = features.shape[1]
    channels = full_width // LCOEF
    edge_count = rotation.shape[1]
    peer_count = lax.axis_size("edge")
    capacity = max(2, edge_count // peer_count + 1)
    rotor_rows = rotation[0]
    owners = source_owner[0, :, 0]
    wanted = source_row[0]
    targets = target_row[0]
    is_live = jnp.arange(edge_count, dtype=jnp.int32) < live_count[0, 0]
    biases = edge_bias[0]
    whole_zero, whole_one, whole_two = (
        lax.all_gather(w_m0, "edge", axis=0, tiled=True),
        lax.all_gather(w_m1, "edge", axis=1, tiled=True),
        lax.all_gather(w_m2, "edge", axis=1, tiled=True),
    )
    owner_hot = (owners[:, None] == jnp.arange(peer_count, dtype=jnp.int32)[None, :]).astype(
        jnp.int32
    )
    earlier = jnp.cumsum(owner_hot, axis=0) - owner_hot
    slots = jnp.sum(earlier * owner_hot, axis=1)
    requests = jnp.zeros((peer_count, capacity), jnp.int32).at[owners, slots].set(wanted)
    target_feat = features[targets].reshape(edge_count, LCOEF, channels)
    rotated_dst = rotate_into(rotor_rows, target_feat).astype(jnp.bfloat16)
    received = lax.all_to_all(requests, "edge", split_axis=0, concat_axis=0, tiled=True)
    returned = lax.all_to_all(features[received], "edge", split_axis=0, concat_axis=0, tiled=True)
    source_feat = returned[owners, slots].reshape(edge_count, LCOEF, channels)
    rotated_src = rotate_into(rotor_rows, source_feat).astype(jnp.bfloat16)
    message_in = jnp.concatenate([rotated_src, rotated_dst], axis=2)

    def local_sums(message, weight):
        return layer_sums(
            message,
            weight,
            whole_one,
            whole_two,
            w_alpha,
            biases,
            rotor_rows,
            targets,
            is_live,
            row_count,
        )

    node_sums, pullback = jax.vjp(local_sums, message_in, whole_zero)
    grad_msg, grad_weight = pullback(out_grad[0])
    target_hot = (jnp.arange(row_count, dtype=jnp.int32)[:, None] == targets[None, :]).astype(
        jnp.float32
    )
    dst_terms = rotate_back(rotor_rows, grad_msg[:, :, channels:], LCOEF).reshape(
        edge_count, full_width
    )
    grad_local = jnp.dot(target_hot, dst_terms, precision=lax.Precision.HIGHEST)
    src_terms = rotate_back(rotor_rows, grad_msg[:, :, :channels], LCOEF).astype(jnp.bfloat16)
    grad_slots = (
        jnp.zeros((peer_count, capacity, full_width), jnp.bfloat16)
        .at[owners, slots]
        .set(src_terms.reshape(edge_count, full_width))
    )
    remote_terms = lax.all_to_all(
        grad_slots, "edge", split_axis=0, concat_axis=0, tiled=True
    ).reshape(peer_count * capacity, full_width)
    asked_hot = (
        jnp.arange(row_count, dtype=jnp.int32)[:, None] == received.reshape(-1)[None, :]
    ).astype(jnp.bfloat16)
    grad_remote = jnp.dot(asked_hot, remote_terms, preferred_element_type=jnp.float32)
    grad_nodes = (grad_local + grad_remote)[None]
    weight_shard = lax.psum_scatter(
        grad_weight.astype(jnp.float32), "edge", scatter_dimension=0, tiled=True
    )
    grad_w0 = lax.psum(weight_shard, "rep")
    return (node_sums.astype(jnp.bfloat16)[None], grad_nodes, grad_w0)


def solution(mesh):
    placed = (
        P("rep", "edge", None),
        P("rep", "edge", None),
        P("rep", "edge", None),
        P("rep", "edge"),
        P("rep", "edge"),
        P("rep", "edge"),
        P("rep", "edge", None),
        P("edge", None),
        P(None, "edge", None),
        P(None, "edge", None),
        P(),
        P("rep", "edge", None),
    )
    return jax.shard_map(
        local,
        mesh=mesh,
        in_specs=placed,
        out_specs=(P("rep", "edge", None), P("rep", "edge", None), P("edge", None)),
        check_vma=False,
    )
```

profile of v0, /device:TPU:6, one launch (start us, length us, event | category | flops | bytes accessed | tf_op | source)
XLA Modules:
  0.0 979.2 jit_solution(5049266614281041108)
XLA Ops:
  10.5 13.8 %scatter_fusion = s32[128,2]{0,1:T(2,128)S(1)} fusion(s32[128,2]{0,1:T(2,128)S(1)} %broadcast.3114, s32[160]{0:T(256)S(1)} %bitcast.187, s32[160]{0:T(256)} %bitcast.225), kind=kCustom, calls=%fused_computation.5 | custom fusion | bytes 3200 | tf_op jit(solution)/shard_map/scatter | solution.py:128
  25.1 19.4 %all-to-all-start = ((s32[128,1,2]{2,1,0:T(1,128)}), s32[128,1,2]{2,1,0:T(1,128)S(1)}, u32[]{:S(2)}, u32[]{:S(2)}) async-start(s32[128,1,2]{2,1,0:T(1,128)} %copy.179), calls=%async_computation | async-start | bytes 131072 | tf_op jit(solution)/shard_map/all_to_all | solution.py:131
  44.5 13.7 %all-to-all-done = s32[128,1,2]{2,1,0:T(1,128)S(1)} async-done(((s32[128,1,2]{2,1,0:T(1,128)}), s32[128,1,2]{2,1,0:T(1,128)S(1)}, u32[]{:S(2)}, u32[]{:S(2)}) %all-to-all-start) | async-done | bytes 1056 | tf_op jit(solution)/shard_map/all_to_all | solution.py:131
  58.4 1.7 gather_fusion
  60.1 1.6 reshape.4618
  61.7 7.1 all-to-all-start.1
  70.9 1.3 dynamic-slice
  73.5 1.2 convert_reduce_fusion.98
  74.7 1.3 convert_reduce_fusion.81
  76.0 1.3 convert_reduce_fusion.57
  77.3 1.3 convert_reduce_fusion.41
  78.6 1.3 convert_reduce_fusion.20
  79.9 1.3 convert_reduce_fusion.8
  81.7 2.2 gather_fusion.2
  83.9 2.4 reshape.4485
  88.4 1.1 fusion.591
  89.5 2.4 fusion.590
  92.0 72.6 %all-gather.7.cloned.1.call-done = bf16[2,768,384]{2,0,1:T(2,128)(2,1)} async-done(((bf16[2,6,384]{2,0,1:T(2,128)(2,1)}), bf16[2,768,384]{2,0,1:T(2,128)(2,1)}) %all-gather.7.cloned.1.call-update) | async-done | bytes 1179664 | tf_op jit(solution)/shard_map/all_gather | solution.py:121
  164.6 3.6 fusion.594
  168.3 1.3 copy_bitcast_fusion.3
  169.6 133.3 %all-gather.9.cloned.1.call-done = bf16[128,10,640]{2,1,0:T(8,128)(2,1)} async-done(((bf16[1,10,640]{2,1,0:T(8,128)(2,1)}), bf16[128,10,640]{2,1,0:T(8,128)(2,1)}) %all-gather.9.cloned.1.call-update) | async-done | bytes 1638416 | tf_op jit(solution)/shard_map/all_gather | solution.py:119
  302.8 2.7 reshape.4677
  305.6 5.5 gather_fusion.1
  311.1 2.6 reshape.4484
  314.3 1.7 fusion.592
  325.4 0.9 constant_dynamic-update-slice_fusion.24
  329.5 0.9 copy-done.4
  330.4 1.0 fusion.599
  331.4 1.0 fusion.600
  332.4 1.3 convolution_dynamic-update-slice_fusion
  333.7 102.5 %all-gather.5.cloned.1.call-done = bf16[2,1024,512]{2,1,0:T(8,128)(2,1)} async-done(((bf16[2,8,512]{2,1,0:T(8,128)(2,1)}), bf16[2,1024,512]{2,1,0:T(8,128)(2,1)}) %all-gather.5.cloned.1.call-update) | async-done | bytes 2097168 | tf_op jit(solution)/shard_map/all_gather | solution.py:120
  436.2 1.7 fusion.21
  437.9 1.6 fusion.20
  439.5 1.1 fusion.11
  440.6 1.1 fusion.10
  441.7 1.1 fusion.15
  442.7 1.0 fusion.14
  443.8 1.7 copy_bitcast_fusion.1
  445.8 1.0 copy-done.12
  449.8 1.0 constant_dynamic-update-slice_fusion.58
  465.8 2.7 broadcast_multiply_fusion
  469.4 1.5 multiply_convert_fusion.69
  471.0 1.6 multiply_convert_fusion.54
  472.6 1.7 multiply_convert_fusion.74
  474.4 1.7 multiply_convert_fusion.79
  476.1 1.7 multiply_convert_fusion.84
  477.9 1.7 multiply_convert_fusion.89
  479.6 1.7 multiply_convert_fusion.94
  481.3 1.0 multiply_convert_fusion.99
  482.3 1.0 multiply_convert_fusion.104
  483.3 1.0 multiply_convert_fusion.109
  484.4 1.0 multiply_convert_fusion.114
  486.2 1.5 scatter_custom_fusion.1
  488.6 1.1 fusion.71
  489.8 6.9 copy_bitcast_fusion
  520.3 2.0 broadcast_in_dim.67
  522.4 33.1 %scatter_fusion.1 = bf16[128,2,3200]{2,1,0:T(2,128)(2,1)} fusion(bf16[128,2,3200]{2,1,0:T(2,128)(2,1)} %broadcast_in_dim.67, s32[160]{0:T(256)S(1)} %bitcast.188, bf16[160,3200]{1,0:T(8,128)(2,1)S(1)} %copy_bitcast_fusion.2), kind=kCustom, calls=%fused_computation.7 | custom fusion | bytes 3073280 | tf_op jit(solution)/shard_map/scatter | solution.py:164
  555.5 11.0 %all-to-all-start.2 = ((bf16[128,2,3200]{2,1,0:T(2,128)(2,1)}), bf16[128,2,3200]{2,1,0:T(2,128)(2,1)S(1)}, u32[]{:S(2)}, u32[]{:S(2)}) async-start(bf16[128,2,3200]{2,1,0:T(2,128)(2,1)} %scatter_fusion.1), calls=%async_computation.2 | async-start | bytes 3276800 | tf_op jit(solution)/shard_map/all_to_all | solution.py:166
  566.8 3.5 fusion.2
  571.1 3.0 fusion.1
  583.0 366.3 %all-reduce.125.cloned.1.call-done = f32[1280,640]{1,0:T(8,128)} async-done(((f32[1280,640]{1,0:T(8,128)}), f32[1280,640]{1,0:T(8,128)}) %all-reduce.125.cloned.1.call-update) | async-done | bytes 3276816
  950.2 18.1 %psum.7 = f32[10,640]{1,0:T(8,128)} all-reduce(f32[10,640]{1,0:T(8,128)S(1)} %constant_dynamic-slice_fusion), channel_id=1, replica_groups=mesh['edge'=128,'rep'=4] {'rep'}, use_global_device_ids=true, to_apply=%region_10.11 | all-reduce | flops 6400 | bytes 51200 | tf_op jit(solution)/shard_map/psum | solution.py:177
  968.3 1.6 reshape.4500
  969.8 2.4 fusion
  (883 shorter events, 72.4 us)
Async XLA Ops:
  7.2 458.5 %copy-start = (f32[1,4,3200]{2,1,0:T(4,128)S(1)}, f32[1,4,3200]{2,1,0:T(4,128)}, u32[]{:S(2)}) copy-start(f32[1,4,3200]{2,1,0:T(4,128)} %param.23) | copy-start | bytes 153604
  7.2 37.3 %copy-start.346 = (s32[1,160]{1,0:T(1,128)S(1)}, s32[1,160]{1,0:T(1,128)}, u32[]{:S(2)}) copy-start(s32[1,160]{1,0:T(1,128)} %param.16) | copy-start | bytes 1924
  7.2 51.2 %copy-start.2 = (bf16[1,4,3200]{2,1,0:T(4,128)(2,1)S(1)}, bf16[1,4,3200]{2,1,0:T(4,128)(2,1)}, u32[]{:S(2)}) copy-start(bf16[1,4,3200]{2,1,0:T(4,128)(2,1)} %param.12) | copy-start | bytes 76804
  7.2 157.4 %all-gather.7.cloned.1.call-start = ((), (), s32[]{:S(2)}) async-start(), calls=%async_computation.4 | async-start | bytes 1188864 | tf_op jit(solution)/shard_map/all_gather | solution.py:121
  25.1 33.1 %all-to-all-start = ((s32[128,1,2]{2,1,0:T(1,128)}), s32[128,1,2]{2,1,0:T(1,128)S(1)}, u32[]{:S(2)}, u32[]{:S(2)}) async-start(s32[128,1,2]{2,1,0:T(1,128)} %copy.179), calls=%async_computation | async-start | bytes 131072 | tf_op jit(solution)/shard_map/all_to_all | solution.py:131
  44.5 15.6 %copy-start.349 = (s32[160,1]{0,1:T(1,128)}, s32[160,1]{0,1:T(1,128)S(1)}, u32[]{:S(2)}) copy-start(s32[160,1]{0,1:T(1,128)S(1)} %compare_select_fusion.1) | copy-start | bytes 1924
  58.3 23.3 %copy-start.344 = (s32[1024]{0:T(1024)}, s32[1024]{0:T(1024)S(1)}, u32[]{:S(2)}) copy-start(s32[1024]{0:T(1024)S(1)} %get-tuple-element.363) | copy-start | bytes 12292
  61.7 243.9 %all-to-all-start.1 = ((bf16[128,2,3200]{2,1,0:T(2,128)(2,1)}), bf16[128,2,3200]{2,1,0:T(2,128)(2,1)S(1)}, u32[]{:S(2)}, u32[]{:S(2)}) async-start(bf16[128,2,3200]{2,1,0:T(2,128)(2,1)} %reshape.4618), calls=%async_computation.1 | async-start | bytes 3276800 | tf_op jit(solution)/shard_map/all_to_all | solution.py:132
  68.8 234.1 %all-gather.9.cloned.1.call-start = ((), (), s32[]{:S(2)}) async-start(), calls=%async_computation.5 | async-start | bytes 2641920 | tf_op jit(solution)/shard_map/all_gather | solution.py:119
  69.5 366.7 %all-gather.5.cloned.1.call-start = ((), (), s32[]{:S(2)}) async-start(), calls=%async_computation.3 | async-start | bytes 2113536 | tf_op jit(solution)/shard_map/all_gather | solution.py:120
  77.3 244.5 %copy-start.50 = (f32[160]{0:T(256)}, f32[160]{0:T(256)S(1)}, u32[]{:S(2)}) copy-start(f32[160]{0:T(256)S(1)} %get-tuple-element.75) | copy-start | bytes 1924
  77.3 244.6 %copy-start.59 = (f32[160]{0:T(256)}, f32[160]{0:T(256)S(1)}, u32[]{:S(2)}) copy-start(f32[160]{0:T(256)S(1)} %get-tuple-element.76) | copy-start | bytes 1924
  77.3 385.8 %copy-start.44 = (f32[160]{0:T(256)}, f32[160]{0:T(256)S(1)}, u32[]{:S(2)}) copy-start(f32[160]{0:T(256)S(1)} %get-tuple-element.74) | copy-start | bytes 1924
  77.3 386.7 %copy-start.40 = (f32[160]{0:T(256)}, f32[160]{0:T(256)S(1)}, u32[]{:S(2)}) copy-start(f32[160]{0:T(256)S(1)} %get-tuple-element.73) | copy-start | bytes 1924
  78.6 246.5 %copy-start.53 = (f32[160]{0:T(256)}, f32[160]{0:T(256)S(1)}, u32[]{:S(2)}) copy-start(f32[160]{0:T(256)S(1)} %get-tuple-element.48) | copy-start | bytes 1924
  78.6 386.5 %copy-start.47 = (f32[160]{0:T(256)}, f32[160]{0:T(256)S(1)}, u32[]{:S(2)}) copy-start(f32[160]{0:T(256)S(1)} %get-tuple-element.47) | copy-start | bytes 1924
  78.6 386.7 %copy-start.42 = (f32[160]{0:T(256)}, f32[160]{0:T(256)S(1)}, u32[]{:S(2)}) copy-start(f32[160]{0:T(256)S(1)} %get-tuple-element.46) | copy-start | bytes 1924
  78.6 386.9 %copy-start.38 = (f32[160]{0:T(256)}, f32[160]{0:T(256)S(1)}, u32[]{:S(2)}) copy-start(f32[160]{0:T(256)S(1)} %get-tuple-element.45) | copy-start | bytes 1924
  79.9 247.4 %copy-start.56 = (f32[160]{0:T(256)}, f32[160]{0:T(256)S(1)}, u32[]{:S(2)}) copy-start(f32[160]{0:T(256)S(1)} %get-tuple-element.24) | copy-start | bytes 1924
  449.6 11.9 %copy-start.60 = (f32[160]{0:T(256)S(1)}, f32[160]{0:T(256)}, u32[]{:S(2)}) copy-start(f32[160]{0:T(256)} %copy-done.59) | copy-start | bytes 1924
  449.6 11.9 %copy-start.103 = (f32[160]{0:T(256)S(1)}, f32[160]{0:T(256)}, u32[]{:S(2)}) copy-start(f32[160]{0:T(256)} %get-tuple-element.52) | copy-start | bytes 1924
  449.6 11.9 %copy-start.147 = (f32[160]{0:T(256)S(1)}, f32[160]{0:T(256)}, u32[]{:S(2)}) copy-start(f32[160]{0:T(256)} %get-tuple-element.31) | copy-start | bytes 1924
  449.6 11.9 %copy-start.186 = (f32[160]{0:T(256)S(1)}, f32[160]{0:T(256)}, u32[]{:S(2)}) copy-start(f32[160]{0:T(256)} %get-tuple-element.11) | copy-start | bytes 1924
  449.8 12.5 %copy-start.51 = (f32[160]{0:T(256)S(1)}, f32[160]{0:T(256)}, u32[]{:S(2)}) copy-start(f32[160]{0:T(256)} %copy-done.50) | copy-start | bytes 1924
  449.8 12.5 %copy-start.90 = (f32[160]{0:T(256)S(1)}, f32[160]{0:T(256)}, u32[]{:S(2)}) copy-start(f32[160]{0:T(256)} %get-tuple-element.51) | copy-start | bytes 1924
  449.8 12.5 %copy-start.133 = (f32[160]{0:T(256)S(1)}, f32[160]{0:T(256)}, u32[]{:S(2)}) copy-start(f32[160]{0:T(256)} %get-tuple-element.30) | copy-start | bytes 1924
  450.8 12.3 %copy-start.76 = (f32[160]{0:T(256)S(1)}, f32[160]{0:T(256)}, u32[]{:S(2)}) copy-start(f32[160]{0:T(256)} %get-tuple-element.50) | copy-start | bytes 1924
  450.8 12.3 %copy-start.119 = (f32[160]{0:T(256)S(1)}, f32[160]{0:T(256)}, u32[]{:S(2)}) copy-start(f32[160]{0:T(256)} %get-tuple-element.29) | copy-start | bytes 1924
  451.7 12.2 %copy-start.63 = (f32[160]{0:T(256)S(1)}, f32[160]{0:T(256)}, u32[]{:S(2)}) copy-start(f32[160]{0:T(256)} %get-tuple-element.49) | copy-start | bytes 1924
  451.7 12.2 %copy-start.106 = (f32[160]{0:T(256)S(1)}, f32[160]{0:T(256)}, u32[]{:S(2)}) copy-start(f32[160]{0:T(256)} %get-tuple-element.28) | copy-start | bytes 1924
  452.6 12.2 %copy-start.54 = (f32[160]{0:T(256)S(1)}, f32[160]{0:T(256)}, u32[]{:S(2)}) copy-start(f32[160]{0:T(256)} %copy-done.53) | copy-start | bytes 1924
  452.6 12.2 %copy-start.93 = (f32[160]{0:T(256)S(1)}, f32[160]{0:T(256)}, u32[]{:S(2)}) copy-start(f32[160]{0:T(256)} %get-tuple-element.27) | copy-start | bytes 1924
  453.5 11.5 %copy-start.79 = (f32[160]{0:T(256)S(1)}, f32[160]{0:T(256)}, u32[]{:S(2)}) copy-start(f32[160]{0:T(256)} %get-tuple-element.26) | copy-start | bytes 1924
  502.5 11.7 %copy-start.74 = (f32[160]{0:T(256)S(1)}, f32[160]{0:T(256)}, u32[]{:S(2)}) copy-start(f32[160]{0:T(256)} %get-tuple-element.77) | copy-start | bytes 1924
  502.5 11.7 %copy-start.117 = (f32[160]{0:T(256)S(1)}, f32[160]{0:T(256)}, u32[]{:S(2)}) copy-start(f32[160]{0:T(256)} %get-tuple-element.53) | copy-start | bytes 1924
  502.5 11.7 %copy-start.158 = (f32[160]{0:T(256)S(1)}, f32[160]{0:T(256)}, u32[]{:S(2)}) copy-start(f32[160]{0:T(256)} %get-tuple-element.32) | copy-start | bytes 1924
  502.6 12.6 %copy-start.61 = (f32[160]{0:T(256)S(1)}, f32[160]{0:T(256)}, u32[]{:S(2)}) copy-start(f32[160]{0:T(256)} %copy-done.59) | copy-start | bytes 1924
  502.6 12.6 %copy-start.104 = (f32[160]{0:T(256)S(1)}, f32[160]{0:T(256)}, u32[]{:S(2)}) copy-start(f32[160]{0:T(256)} %get-tuple-element.52) | copy-start | bytes 1924
  502.6 12.6 %copy-start.148 = (f32[160]{0:T(256)S(1)}, f32[160]{0:T(256)}, u32[]{:S(2)}) copy-start(f32[160]{0:T(256)} %get-tuple-element.31) | copy-start | bytes 1924
  502.6 13.4 %copy-start.52 = (f32[160]{0:T(256)S(1)}, f32[160]{0:T(256)}, u32[]{:S(2)}) copy-start(f32[160]{0:T(256)} %copy-done.50) | copy-start | bytes 1924
  502.6 13.4 %copy-start.91 = (f32[160]{0:T(256)S(1)}, f32[160]{0:T(256)}, u32[]{:S(2)}) copy-start(f32[160]{0:T(256)} %get-tuple-element.51) | copy-start | bytes 1924
  502.6 13.4 %copy-start.134 = (f32[160]{0:T(256)S(1)}, f32[160]{0:T(256)}, u32[]{:S(2)}) copy-start(f32[160]{0:T(256)} %get-tuple-element.30) | copy-start | bytes 1924
  502.6 13.4 %copy-start.172 = (f32[160]{0:T(256)S(1)}, f32[160]{0:T(256)}, u32[]{:S(2)}) copy-start(f32[160]{0:T(256)} %get-tuple-element.10) | copy-start | bytes 1924
  502.9 14.0 %copy-start.46 = (f32[160]{0:T(256)S(1)}, f32[160]{0:T(256)}, u32[]{:S(2)}) copy-start(f32[160]{0:T(256)} %copy-done.44) | copy-start | bytes 1924
  502.9 14.0 %copy-start.77 = (f32[160]{0:T(256)S(1)}, f32[160]{0:T(256)}, u32[]{:S(2)}) copy-start(f32[160]{0:T(256)} %get-tuple-element.50) | copy-start | bytes 1924
  502.9 14.0 %copy-start.120 = (f32[160]{0:T(256)S(1)}, f32[160]{0:T(256)}, u32[]{:S(2)}) copy-start(f32[160]{0:T(256)} %get-tuple-element.29) | copy-start | bytes 1924
  503.0 14.0 %copy-start.161 = (f32[160]{0:T(256)S(1)}, f32[160]{0:T(256)}, u32[]{:S(2)}) copy-start(f32[160]{0:T(256)} %get-tuple-element.9) | copy-start | bytes 1924
  503.3 14.5 %copy-start.64 = (f32[160]{0:T(256)S(1)}, f32[160]{0:T(256)}, u32[]{:S(2)}) copy-start(f32[160]{0:T(256)} %get-tuple-element.49) | copy-start | bytes 1924
  503.3 14.5 %copy-start.107 = (f32[160]{0:T(256)S(1)}, f32[160]{0:T(256)}, u32[]{:S(2)}) copy-start(f32[160]{0:T(256)} %get-tuple-element.28) | copy-start | bytes 1924
  503.3 14.5 %copy-start.151 = (f32[160]{0:T(256)S(1)}, f32[160]{0:T(256)}, u32[]{:S(2)}) copy-start(f32[160]{0:T(256)} %get-tuple-element.8) | copy-start | bytes 1924
  504.2 14.4 %copy-start.55 = (f32[160]{0:T(256)S(1)}, f32[160]{0:T(256)}, u32[]{:S(2)}) copy-start(f32[160]{0:T(256)} %copy-done.53) | copy-start | bytes 1924
  504.2 14.4 %copy-start.94 = (f32[160]{0:T(256)S(1)}, f32[160]{0:T(256)}, u32[]{:S(2)}) copy-start(f32[160]{0:T(256)} %get-tuple-element.27) | copy-start | bytes 1924
  504.2 14.4 %copy-start.141 = (f32[160]{0:T(256)S(1)}, f32[160]{0:T(256)}, u32[]{:S(2)}) copy-start(f32[160]{0:T(256)} %get-tuple-element.7) | copy-start | bytes 1924
  505.2 14.4 %copy-start.49 = (f32[160]{0:T(256)S(1)}, f32[160]{0:T(256)}, u32[]{:S(2)}) copy-start(f32[160]{0:T(256)} %copy-done.47) | copy-start | bytes 1924
  505.2 14.4 %copy-start.80 = (f32[160]{0:T(256)S(1)}, f32[160]{0:T(256)}, u32[]{:S(2)}) copy-start(f32[160]{0:T(256)} %get-tuple-element.26) | copy-start | bytes 1924
  505.2 14.4 %copy-start.127 = (f32[160]{0:T(256)S(1)}, f32[160]{0:T(256)}, u32[]{:S(2)}) copy-start(f32[160]{0:T(256)} %get-tuple-element.6) | copy-start | bytes 1924
  506.1 13.7 %copy-start.67 = (f32[160]{0:T(256)S(1)}, f32[160]{0:T(256)}, u32[]{:S(2)}) copy-start(f32[160]{0:T(256)} %get-tuple-element.25) | copy-start | bytes 1924
  506.1 13.7 %copy-start.114 = (f32[160]{0:T(256)S(1)}, f32[160]{0:T(256)}, u32[]{:S(2)}) copy-start(f32[160]{0:T(256)} %get-tuple-element.5) | copy-start | bytes 1924
  507.0 13.0 %copy-start.58 = (f32[160]{0:T(256)S(1)}, f32[160]{0:T(256)}, u32[]{:S(2)}) copy-start(f32[160]{0:T(256)} %copy-done.56) | copy-start | bytes 1924
  507.0 13.0 %copy-start.101 = (f32[160]{0:T(256)S(1)}, f32[160]{0:T(256)}, u32[]{:S(2)}) copy-start(f32[160]{0:T(256)} %get-tuple-element.4) | copy-start | bytes 1924
  555.5 412.8 %all-to-all-start.2 = ((bf16[128,2,3200]{2,1,0:T(2,128)(2,1)}), bf16[128,2,3200]{2,1,0:T(2,128)(2,1)S(1)}, u32[]{:S(2)}, u32[]{:S(2)}) async-start(bf16[128,2,3200]{2,1,0:T(2,128)(2,1)} %scatter_fusion.1), calls=%async_computation.2 | async-start | bytes 3276800 | tf_op jit(solution)/shard_map/all_to_all | solution.py:166
  566.5 382.8 %all-reduce.125.cloned.1.call-start = ((), (), s32[]{:S(2)}) async-start(), calls=%async_computation.6 | async-start | bytes 6553600
  583.0 386.8 %copy-start.348 = (s32[256]{0:T(256)S(1)}, s32[256]{0:T(256)}, u32[]{:S(2)}) copy-start(s32[256]{0:T(256)} %eq.75) | copy-start | bytes 3076
  950.2 22.0 %copy-start.1 = (f32[1,4,3200]{2,1,0:T(4,128)S(1)}, f32[1,4,3200]{2,1,0:T(4,128)}, u32[]{:S(2)}) copy-start(f32[1,4,3200]{2,1,0:T(4,128)} %param.23) | copy-start | bytes 153604
  (295 other events, 1566.6 us)
Sparse Core Ops, SparseCore 0:
  11.2 153.3 all-gather.6
  167.7 135.1 all-gather.8
  305.8 130.2 all-gather.4
  570.5 378.7 all-reduce.124
where the time goes:
time: 991 us; the launch traced here: 979 us
  waiting for transfers between devices  690 us (70%)
  local copies, waits for them, and re-layouts  93.3 us (9%)
  other arithmetic  88.7 us (9%)
  starting transfers between devices  37.9 us (4%)
  matrix products  29.4 us (3%)
  between operations  21.5 us (2%)
  blocking collectives  18.1 us (2%)
    unnamed x5, waiting for transfers between devices  368 us
    all_gather x1, waiting for transfers between devices, local(): lax.all_gather(w_m0, 'edge', axis=0, tiled=True)  133 us
    all_gather x1, waiting for transfers between devices, local(): lax.all_gather(w_m1, 'edge', axis=1, tiled=True)  102 us
    all_gather x1, waiting for transfers between devices, local(): lax.all_gather(w_m2, 'edge', axis=1, tiled=True)  72.6 us
    unnamed x102, other arithmetic  49.9 us
    scatter x1, local copies, waits for them, and re-layouts, local(): grad_slots = jnp.zeros((peer_count, capacity, full_width), jnp.bfloat16)....  33.1 us
  transfers between devices with their start and end apart: 7, of which 5 were waited for; matrix products, arithmetic and copies ran while one was open for 9% of the time, Pallas kernels for 0%

commit v1 on v0

v1 whole, which is shorter than its diff:
```python
import jax
import jax.numpy as jnp
from jax import lax
from jax.experimental import pallas as pl
from jax.experimental.pallas import tpu as pltpu
from jax.sharding import PartitionSpec as P

LCOEF = 25
MCOEF = 19
CH = 128
HEADS = 8
EDGES = 160
BLOCK = 16
NZ, NX = 16, 4
FULL = LCOEF * CH
ROWS_OF = {0: (0,), 1: (1, 5, 9), 2: (2, 6, 10, 13, 16), 3: (3, 7, 11, 14, 17), 4: (4, 8, 12, 15, 18)}
NEAR = (0, 1, 2, -1)
W_SPLIT = 800 + 3 * 128
VMEM_LIMIT = 56 * 2**20
F32, BF16 = jnp.float32, jnp.bfloat16


def where_to(i, dz, dx, dc):
    z, x, c = i // 8, (i // 2) % 4, i % 2
    sign = 1 - 2 * c
    return ((z + sign * dz) % NZ) * 8 + ((x + dx) % NX) * 2 + (c + dc) % 2


def pull(a, dz=0, dx=0, dc=0):
    return lax.ppermute(a, "edge", [(where_to(i, dz, dx, dc), i) for i in range(128)])


def push(a, dz=0, dx=0, dc=0):
    return lax.ppermute(a, "edge", [(i, where_to(i, dz, dx, dc)) for i in range(128)])


def block_place(owner, me):
    sign = 1 - 2 * (owner % 2)
    jz = (sign * (owner // 8 - me // 8) + 1) % NZ
    xr = ((owner // 2) % 4 - (me // 2) % 4) % NX
    cr = (owner % 2 + me % 2) % 2
    near = (jz % 4 + 3) % 4
    return cr * 64 + xr * 16 + near * 4 + jz // 4


def block_owner(place, me):
    cr, xr, near, far = place // 64, (place // 16) % 4, (place // 4) % 4, place % 4
    sign = 1 - 2 * ((me + cr) % 2)
    offset = (near + 1) % 4 - 1
    z = (me // 8 + sign * (4 * far + offset)) % NZ
    x = ((me // 2) % 4 + xr) % NX
    return z * 8 + x * 2 + (me % 2 + cr) % 2


def x_and_core(block, split):
    right, left = pull(block, dx=1), pull(block, dx=3)
    upper, lower = pull(right[:split], dx=1), pull(left[split:], dx=3)
    mine = (block, right, upper, lower, left)
    return mine + tuple(pull(a, dc=1) for a in mine)


def scatter_sum(pieces, split, near_rows, far_rows):
    def add(a, *more):
        total = a.astype(F32)
        for m in more:
            total = total + m.astype(F32)
        return total

    a = [add(pieces[x], push(pieces[4 + x], dc=1)).astype(BF16) for x in range(4)]
    up, down = push(a[2][:split], dx=1), push(a[2][split:], dx=3)
    right = jnp.concatenate([add(a[1][:split], up).astype(BF16), a[1][split:]], axis=0)
    left = jnp.concatenate([a[3][:split], add(a[3][split:], down).astype(BF16)], axis=0)
    total = add(a[0], push(right, dx=1), push(left, dx=3)).astype(BF16)
    parts = [total[n * near_rows : (n + 1) * near_rows] for n in range(4)]
    total = add(parts[0], *(push(parts[n], dz=NEAR[n]) for n in (1, 2, 3))).astype(BF16)
    parts = [total[n * far_rows : (n + 1) * far_rows] for n in range(4)]
    return add(parts[0], *(push(parts[n], dz=4 * n) for n in (1, 2, 3)))


def hot(index, shape, axis):
    return jnp.where(index == lax.broadcasted_iota(jnp.int32, shape, axis), F32(1), F32(0)).astype(BF16)


def mm(a, b):
    return jnp.dot(a, b, preferred_element_type=F32)


def mm_nt(a, b):
    return lax.dot_general(a, b, (((1,), (1,)), ((), ())), preferred_element_type=F32)


def frame_slot(row):
    if row < 5:
        return 0, 0, row
    if row < 13:
        return 1, ((row - 5) // 4) * EDGES, (row - 5) % 4
    return 2, ((row - 13) // 3) * EDGES, (row - 13) % 3


def rotate_kernel(*refs):
    pieces = refs[:10]
    rot, place, target, local, inv0, inv1, inv2 = refs[10:17]
    m0, m1, m2, turned_grad = refs[17:21]
    feats, srcf, dstf, gradf, n0, n1, n2 = refs[21:]
    for core in range(2):
        row = core * 256
        for piece in pieces[core * 5 : core * 5 + 5]:
            feats[row : row + piece.shape[0], :] = piece[...]
            row += piece.shape[0]
    source_hot = hot(place[...], (EDGES, 512), 1)
    t = target[...]
    lanes = lax.broadcasted_iota(jnp.int32, (EDGES, 16), 1)
    feat_hot = jnp.where(lanes == t, F32(1), F32(0)).astype(BF16)
    grad_hot = jnp.where((lanes == t + 4) | (lanes == t + 8), F32(1), F32(0)).astype(BF16)
    for first in range(0, FULL, 640):
        cut = slice(first, first + 640)
        srcf[:, cut] = mm(source_hot, feats[:, cut]).astype(BF16)
        dstf[:, cut] = mm(feat_hot, local[:, cut]).astype(BF16)
        gradf[:, cut] = mm(grad_hot, local[:, cut])

    stacked = (n0, n1, n2)

    def turn(step, carry):
        e0 = pl.multiple_of(step * BLOCK, BLOCK)
        rows_here = pl.ds(e0, BLOCK)
        rotors = rot[rows_here, :].astype(F32)
        for degree, rows in ROWS_OF.items():
            sums = [None] * len(rows)
            for col in range(degree * degree, (degree + 1) ** 2):
                cut = slice(col * CH, (col + 1) * CH)
                s, d, g = srcf[rows_here, cut].astype(F32), dstf[rows_here, cut].astype(F32), gradf[rows_here, cut]
                for n, row in enumerate(rows):
                    r = jnp.broadcast_to(rotors[:, row * LCOEF + col : row * LCOEF + col + 1], (BLOCK, CH))
                    terms = (r * s, r * d, r * g)
                    sums[n] = terms if sums[n] is None else tuple(a + b for a, b in zip(sums[n], terms))
            for n, row in enumerate(rows):
                array, base, column = frame_slot(row)
                out = stacked[array]
                out_rows = pl.ds(pl.multiple_of(base + e0, BLOCK), BLOCK)
                out[out_rows, column * 256 : column * 256 + CH] = sums[n][0].astype(BF16)
                out[out_rows, column * 256 + CH : column * 256 + 256] = sums[n][1].astype(BF16)
                turned_grad[rows_here, row * CH : (row + 1) * CH] = sums[n][2]
        return carry

    lax.fori_loop(0, EDGES // BLOCK, turn, 0)
    for natural, ordered, inverse in ((n0, m0, inv0), (n1, m1, inv1), (n2, m2, inv2)):
        depth = natural.shape[1]
        for first in range(0, depth, 256):
            cut = slice(first, first + 256)
            ordered[:, cut] = mm(natural[...], hot(inverse[:, cut], (depth, 256), 0)).astype(BF16)


def layer_kernel(*refs):
    pieces = refs[:10]
    m0, m1, m2, turned_grad, rot, bias, target, live_ref, alpha_ref, place, pos0, pos1, pos2 = refs[10:23]
    terms_out = refs[23:31]
    w0_out = refs[31:39]
    scaled_out, grad_dst = refs[39:41]
    w0, w1, w2, values, d0, d1, d2, p0, p1, p2, g0, g1, g2, src_terms = refs[41:]

    def place_rows(piece, core, x, begin, end):
        k = core * 4 + x
        at = 0
        for out, units, rows in ((w0, 5, 160), (w1, 8, 128), (w2, 6, 96)):
            for u in range(units):
                if begin <= at < end:
                    out[k * rows : (k + 1) * rows, u * CH : (u + 1) * CH] = piece[at - begin : at - begin + rows, :]
                at += rows

    for core in range(2):
        own, right, upper, lower, left = pieces[core * 5 : core * 5 + 5]
        place_rows(own, core, 0, 0, 2400)
        place_rows(right, core, 1, 0, 2400)
        place_rows(upper, core, 2, 0, W_SPLIT)
        place_rows(lower, core, 2, W_SPLIT, 2400)
        place_rows(left, core, 3, 0, 2400)

    z0 = mm(m0[...], w0[...])
    for row in range(5):
        values[:, row * CH : (row + 1) * CH] = z0[:, row * CH : (row + 1) * CH].astype(BF16)
    z1 = mm(m1[...], w1[...])
    values[:, 5 * CH : 9 * CH] = (z1[:EDGES, :512] - z1[EDGES:, 512:]).astype(BF16)
    values[:, 9 * CH : 13 * CH] = (z1[EDGES:, :512] + z1[:EDGES, 512:]).astype(BF16)
    z2 = mm(m2[...], w2[...])
    values[:, 13 * CH : 16 * CH] = (z2[:EDGES, :384] - z2[EDGES:, 384:]).astype(BF16)
    values[:, 16 * CH : 19 * CH] = (z2[EDGES:, :384] + z2[:EDGES, 384:]).astype(BF16)

    v = z0[:, :CH]
    sigma = 1.0 / (1.0 + jnp.exp(-v))
    alpha = alpha_ref[...]
    logits = bias[...] + mm((v * sigma).astype(BF16), alpha)
    live = live_ref[...] > 0
    t = target[...]
    members = [live & (t == n) for n in range(4)]

    def over_targets(array, empty, reduce):
        result = jnp.zeros((EDGES, HEADS), F32)
        for member in members:
            one = reduce(jnp.where(member, array, F32(empty)), axis=0, keepdims=True)
            result = jnp.where(member, one, result)
        return result

    top = over_targets(logits, -1e30, jnp.max)
    expo = jnp.where(live, jnp.exp(jnp.where(live, logits - top, F32(0))), F32(0))
    denom = jnp.where(live, over_targets(expo, 0.0, jnp.sum), F32(1))
    attn = expo / denom
    head_of = (
        lax.broadcasted_iota(jnp.int32, (HEADS, CH), 1) // (CH // HEADS)
        == lax.broadcasted_iota(jnp.int32, (HEADS, CH), 0)
    )
    spread = jnp.where(head_of, F32(1), F32(0))
    scale = jnp.dot(attn, spread, precision=lax.Precision.HIGHEST, preferred_element_type=F32)
    dscale = jnp.zeros((EDGES, CH), F32)
    for row in range(MCOEF):
        cut = slice(row * CH, (row + 1) * CH)
        value = values[:, cut].astype(F32)
        dscale = dscale + turned_grad[:, cut] * value
        scaled_out[:, cut] = (scale * value).astype(BF16)
    dattn = lax.dot_general(
        dscale, spread, (((1,), (1,)), ((), ())), precision=lax.Precision.HIGHEST, preferred_element_type=F32
    )
    dlogits = attn * (dattn - over_targets(attn * dattn, 0.0, jnp.sum))
    dscalars = lax.dot_general(
        dlogits, alpha.astype(F32), (((1,), (1,)), ((), ())), precision=lax.Precision.HIGHEST,
        preferred_element_type=F32,
    ).astype(BF16).astype(F32)
    dv = dscalars * (sigma * (1.0 + v * (1.0 - sigma)))
    for row in range(MCOEF):
        cut = slice(row * CH, (row + 1) * CH)
        dvalue = (scale * turned_grad[:, cut]).astype(BF16)
        if row == 0:
            dvalue = (dvalue.astype(F32) + dv).astype(BF16)
        if row < 5:
            d0[:, cut] = dvalue
            continue
        out, width, column, plus = (d1, 512, (row - 5) % 4, row < 9) if row < 13 else (d2, 384, (row - 13) % 3, row < 16)
        a, b = column * CH, width + column * CH
        if plus:
            out[:EDGES, a : a + CH] = dvalue
            out[EDGES:, b : b + CH] = -dvalue
        else:
            out[EDGES:, a : a + CH] = dvalue
            out[:EDGES, b : b + CH] = dvalue
    dw = lax.dot_general(m0[...], d0[...], (((0,), (0,)), ((), ())), preferred_element_type=F32)
    for k in range(8):
        w0_out[k][...] = dw[k * 160 : (k + 1) * 160].astype(BF16)
    for d, w, p, g, pos in ((d0, w0, p0, g0, pos0), (d1, w1, p1, g1, pos1), (d2, w2, p2, g2, pos2)):
        depth = w.shape[0]
        p[...] = mm_nt(d[...], w[...]).astype(BF16)
        for first in range(0, depth, 256):
            cut = slice(first, first + 256)
            g[:, cut] = mm(p[...], hot(pos[:, cut], (depth, 256), 0)).astype(BF16)
    stacked = (g0, g1, g2)
    for row in range(MCOEF):
        array, base, column = frame_slot(row)
        grad_dst[:, row * CH : (row + 1) * CH] = stacked[array][base : base + EDGES, column * 256 + CH : column * 256 + 256]

    def turn(step, carry):
        e0 = pl.multiple_of(step * BLOCK, BLOCK)
        rows_here = pl.ds(e0, BLOCK)
        rotors = rot[rows_here, :].astype(F32)
        for degree, rows in ROWS_OF.items():
            first = degree * degree
            sums = [None] * (2 * degree + 1)
            for row in rows:
                array, base, column = frame_slot(row)
                s = stacked[array][pl.ds(pl.multiple_of(base + e0, BLOCK), BLOCK), column * 256 : column * 256 + CH]
                s = s.astype(F32)
                for n in range(2 * degree + 1):
                    at = row * LCOEF + first + n
                    term = jnp.broadcast_to(rotors[:, at : at + 1], (BLOCK, CH)) * s
                    sums[n] = term if sums[n] is None else sums[n] + term
            for n in range(2 * degree + 1):
                src_terms[rows_here, (first + n) * CH : (first + n + 1) * CH] = sums[n].astype(BF16)
        return carry

    lax.fori_loop(0, EDGES // BLOCK, turn, 0)
    for k in range(8):
        chosen = hot(place[...] - k * 64, (64, EDGES), 0)
        for first in range(0, FULL, 640):
            cut = slice(first, first + 640)
            terms_out[k][:, cut] = mm(chosen, src_terms[:, cut]).astype(BF16)


def nodes_kernel(rot, scaled, grad_dst, target, node_out, grad_local, back, terms):
    def turn(step, carry):
        e0 = pl.multiple_of(step * BLOCK, BLOCK)
        rows_here = pl.ds(e0, BLOCK)
        rotors = rot[rows_here, :].astype(F32)
        for degree, rows in ROWS_OF.items():
            first = degree * degree
            sums = [None] * (2 * degree + 1)
            for row in rows:
                a = scaled[rows_here, row * CH : (row + 1) * CH].astype(F32)
                b = grad_dst[rows_here, row * CH : (row + 1) * CH].astype(F32)
                for n in range(2 * degree + 1):
                    at = row * LCOEF + first + n
                    r = jnp.broadcast_to(rotors[:, at : at + 1], (BLOCK, CH))
                    sums[n] = (r * a, r * b) if sums[n] is None else (sums[n][0] + r * a, sums[n][1] + r * b)
            for n in range(2 * degree + 1):
                cut = slice((first + n) * CH, (first + n + 1) * CH)
                back[rows_here, cut] = sums[n][0].astype(BF16)
                terms[rows_here, cut] = sums[n][1].astype(BF16)
        return carry

    lax.fori_loop(0, EDGES // BLOCK, turn, 0)
    chosen = hot(target[...], (16, EDGES), 0)
    for first in range(0, FULL, 640):
        cut = slice(first, first + 640)
        node_out[:, cut] = mm(chosen, back[:, cut])[:4].astype(BF16)
        grad_local[:, cut] = mm(chosen, terms[:, cut])[:4]


def call(kernel, name, args, outs, scratch, flops, transcendentals=0):
    moved = sum(a.size * a.dtype.itemsize for a in args)
    return pl.pallas_call(
        kernel,
        out_shape=tuple(jax.ShapeDtypeStruct(s, t) for s, t in outs),
        in_specs=[pl.BlockSpec(memory_space=pltpu.VMEM)] * len(args),
        out_specs=tuple(pl.BlockSpec(memory_space=pltpu.VMEM) for _ in outs),
        scratch_shapes=[pltpu.VMEM(s, t) for s, t in scratch],
        compiler_params=pltpu.CompilerParams(vmem_limit_bytes=VMEM_LIMIT),
        cost_estimate=pl.CostEstimate(flops=flops, bytes_accessed=moved, transcendentals=transcendentals),
        name=name,
    )(*args)


def pack_units(array, rows):
    n, _, width = array.shape
    return array.reshape(n, rows, width // CH, CH).transpose(2, 0, 1, 3).reshape(width // CH, n * rows, CH)


def local(
    node_feat, rotation, source_owner, source_row, target_row, live_count, edge_bias,
    w_m0, w_m1, w_m2, w_alpha, out_grad,
):
    me = lax.axis_index("edge")
    features = node_feat[0]
    rotor_rows = rotation[0]
    targets = target_row[0]
    live = (jnp.arange(EDGES, dtype=jnp.int32) < live_count[0, 0]).astype(jnp.int32)
    place = block_place(source_owner[0, :, 0], me) * 4 + source_row[0]

    far = jnp.concatenate([features] + [pull(features, dz=4 * a) for a in (1, 2, 3)], axis=0)
    near = jnp.concatenate([far] + [pull(far, dz=NEAR[n]) for n in (1, 2, 3)], axis=0)
    feature_pieces = x_and_core(near, 32)

    w1 = jnp.concatenate([w_m1[0], w_m1[1]], axis=1)
    w2 = jnp.concatenate([w_m2[0], w_m2[1]], axis=1)

    def packed(parts):
        return jnp.concatenate([a.reshape(-1, CH) for a in parts], axis=0)

    block = packed([pack_units(w_m0[None], 10), pack_units(w1[None], 8), pack_units(w2[None], 6)])

    def merged(blocks, rows):
        cuts, at = [], 0
        for units, depth in ((5, rows[0]), (8, rows[1]), (6, rows[2])):
            parts = [b[at : at + units * depth].reshape(units, depth, CH) for b in blocks]
            cuts.append(jnp.concatenate(parts, axis=1))
            at += units * depth
        return packed(cuts)

    far_w = merged([block] + [pull(block, dz=4 * a) for a in (1, 2, 3)], (10, 8, 6))
    near_w = merged([far_w] + [pull(far_w, dz=NEAR[n]) for n in (1, 2, 3)], (40, 32, 24))
    weight_pieces = x_and_core(near_w, W_SPLIT)

    def inverse_of(depth, rows):
        p = jnp.arange(depth, dtype=jnp.int32)
        return (block_owner(p // rows, me) * rows + p % rows)[None]

    def position_of(depth, rows):
        k = jnp.arange(depth, dtype=jnp.int32)
        return (block_place(k // rows, me) * rows + k % rows)[None]

    sizes = ((1280, 10), (1024, 8), (768, 6))
    inverses = [inverse_of(*s) for s in sizes]
    positions = [position_of(*s) for s in sizes]

    cotangent = out_grad[0]
    high = lax.reduce_precision(cotangent, 8, 7)
    own_rows = jnp.concatenate(
        [features, high.astype(BF16), (cotangent - high).astype(BF16), jnp.zeros((4, FULL), BF16)], axis=0
    )

    m0, m1, m2, turned_grad = call(
        rotate_kernel, "rotate",
        (*feature_pieces, rotor_rows, place[:, None], targets[:, None], own_rows, *inverses),
        [((160, 1280), BF16), ((320, 1024), BF16), ((320, 768), BF16), ((160, MCOEF * CH), F32)],
        [((512, FULL), BF16), ((160, FULL), BF16), ((160, FULL), BF16), ((160, FULL), F32),
         ((160, 1280), BF16), ((320, 1024), BF16), ((320, 768), BF16)],
        3_000_000_000,
    )
    outs = call(
        layer_kernel, "layer",
        (*weight_pieces, m0, m1, m2, turned_grad, rotor_rows, edge_bias[0], targets[:, None], live[:, None],
         w_alpha, place[None], *positions),
        [((64, FULL), BF16)] * 8 + [((160, 640), BF16)] * 8
        + [((160, MCOEF * CH), BF16), ((160, MCOEF * CH), BF16)],
        [((1280, 640), BF16), ((1024, 1024), BF16), ((768, 768), BF16), ((160, MCOEF * CH), BF16),
         ((160, 640), BF16), ((320, 1024), BF16), ((320, 768), BF16),
         ((160, 1280), BF16), ((320, 1024), BF16), ((320, 768), BF16),
         ((160, 1280), BF16), ((320, 1024), BF16), ((320, 768), BF16), ((160, FULL), BF16)],
        5_000_000_000, 160 * 136,
    )
    term_pieces, w0_pieces, (scaled, grad_dst) = outs[:8], outs[8:16], outs[16:]
    node_out, grad_local = call(
        nodes_kernel, "nodes", (rotor_rows, scaled, grad_dst, targets[None]),
        [((4, FULL), BF16), ((4, FULL), F32)], [((160, FULL), BF16), ((160, FULL), BF16)],
        600_000_000,
    )
    grad_remote = scatter_sum(term_pieces, 32, 16, 4)
    shard = scatter_sum(w0_pieces, 80, 40, 10)
    n_rep = lax.axis_size("rep")
    grad_w0 = shard
    for r in range(1, n_rep):
        grad_w0 = grad_w0 + lax.ppermute(shard, "rep", [(i, (i + r) % n_rep) for i in range(n_rep)])
    return node_out[None], (grad_local + grad_remote)[None], grad_w0


def solution(mesh):
    placed = (
        P("rep", "edge", None), P("rep", "edge", None), P("rep", "edge", None), P("rep", "edge"),
        P("rep", "edge"), P("rep", "edge"), P("rep", "edge", None), P("edge", None),
        P(None, "edge", None), P(None, "edge", None), P(), P("rep", "edge", None),
    )
    return jax.shard_map(
        local, mesh=mesh, in_specs=placed,
        out_specs=(P("rep", "edge", None), P("rep", "edge", None), P("edge", None)),
        check_vma=False,
    )
```

time: 991 us -> 297 us (0.30)
  waiting for transfers between devices: 690 us -> 24.9 us
  starting transfers between devices: 37.9 us -> 211 us
  local copies, waits for them, and re-layouts: 93.3 us -> 9.58 us
  other arithmetic: 88.7 us -> 11.7 us
  Pallas kernels: 0 us -> 30.8 us
  matrix products: 29.4 us -> 0 us
  between operations: 21.5 us -> 3.16 us
  blocking collectives: 18.1 us -> 0 us
    unnamed x5 -> x0, waiting for transfers between devices: 368 us -> none
    all_gather x3 -> x0, waiting for transfers between devices: 308 us -> none  [the longest x1 133 us: local(): lax.all_gather(w_m0, 'edge', axis=0, tiled=True)]
    ppermute x0 -> x61, starting transfers between devices: none -> 211 us  [the longest x30 107 us: pull(): lax.ppermute(a, 'edge', [(where_to(i, dz, dx, dc), i) for i in range(128)])]
    unnamed x102 -> x1, other arithmetic: 49.9 us -> 0.01 us
    scatter x2 -> x0, local copies, waits for them, and re-layouts: 47 us -> none  [the longest x1 33.1 us: local(): grad_slots = jnp.zeros((peer_count, capacity, full_width), jnp.bfloat16)....]
    all_to_all x3 -> x0, starting transfers between devices: 37.5 us -> none  [the longest x1 19.4 us: local(): lax.all_to_all(requests, 'edge', split_axis=0, concat_axis=0, tiled=True)]
    pallas_call x0 -> x3, Pallas kernels: none -> 30.8 us  [call(): pl.pallas_call(kernel, out_shape=tuple((jax.ShapeDtypeStruct(s, t) for s,...]
    dot_general x27 -> x0, matrix products: 29.4 us -> none  [the longest x2 5.63 us: layer_sums(): return jnp.dot(member_f, weighted, precision=lax.Precision.HIGHEST)]
  transfers between devices with their start and end apart: 7 -> 61, of which waited for: 5 -> 7; matrix products, arithmetic and copies ran while one was open for 9% -> 7% of each run, Pallas kernels for 0% -> 5%
where the time goes in v1:
time: 297 us; the launch traced here: 291 us
  starting transfers between devices  211 us (71%)
  Pallas kernels  30.8 us (10%)
  waiting for transfers between devices  24.9 us (8%)
  other arithmetic  11.7 us (4%)
  local copies, waits for them, and re-layouts  9.58 us (3%)
  between operations  3.16 us (1%)
    ppermute x30, starting transfers between devices, pull(): lax.ppermute(a, 'edge', [(where_to(i, dz, dx, dc), i) for i in range(128)])  107 us
    ppermute x28, starting transfers between devices, push(): lax.ppermute(a, 'edge', [(i, where_to(i, dz, dx, dc)) for i in range(128)])  93.7 us
    pallas_call x3, Pallas kernels, call(): pl.pallas_call(kernel, out_shape=tuple((jax.ShapeDtypeStruct(s, t) for s,...  30.8 us
    ppermute x28, waiting for transfers between devices, push(): lax.ppermute(a, 'edge', [(i, where_to(i, dz, dx, dc)) for i in range(128)])  18.7 us
    ppermute x3, starting transfers between devices, local(): lax.ppermute(shard, 'rep', [(i, (i + r) % n_rep) for i in range(n_rep)])  10.3 us
    ppermute x30, waiting for transfers between devices, pull(): lax.ppermute(a, 'edge', [(where_to(i, dz, dx, dc), i) for i in range(128)])  6.24 us
  transfers between devices with their start and end apart: 61, of which 7 were waited for; matrix products, arithmetic and copies ran while one was open for 7% of the time, Pallas kernels for 5%

profile of v1, /device:TPU:6, one launch (start us, length us, event | category | flops | bytes accessed | tf_op | source)
XLA Modules:
  0.0 291.5 jit_solution(3999732599594816663)
XLA Ops:
  0.6 9.1 %collective-permute-start.17 = (bf16[4,3200]{1,0:T(4,128)(2,1)}, bf16[4,3200]{1,0:T(4,128)(2,1)S(1)}, u32[]{:S(2)}, u32[]{:S(2)}) collective-permute-start(bf16[4,3200]{1,0:T(4,128)(2,1)} %bitcast.111), channel_id=1, source_target_pairs={{384,0},{132,4},{392,8},{140,12},{400,16},{148,20},{408,24},{156,2... | collective-permute-start | bytes 76808 | tf_op jit(solution)/shard_map/ppermute | solution.py:30
  9.7 10.9 %collective-permute-start.16 = (bf16[4,3200]{1,0:T(4,128)(2,1)}, bf16[4,3200]{1,0:T(4,128)(2,1)S(1)}, u32[]{:S(2)}, u32[]{:S(2)}) collective-permute-start(bf16[4,3200]{1,0:T(4,128)(2,1)} %bitcast.112), channel_id=1, source_target_pairs={{256,0},{260,4},{264,8},{268,12},{272,16},{276,20},{280,24},{284,2... | collective-permute-start | bytes 76808 | tf_op jit(solution)/shard_map/ppermute | solution.py:30
  20.7 5.5 %collective-permute-start.15 = (bf16[4,3200]{1,0:T(4,128)(2,1)}, bf16[4,3200]{1,0:T(4,128)(2,1)S(1)}, u32[]{:S(2)}, u32[]{:S(2)}) collective-permute-start(bf16[4,3200]{1,0:T(4,128)(2,1)} %bitcast.113), channel_id=1, source_target_pairs={{128,0},{388,4},{136,8},{396,12},{144,16},{404,20},{152,24},{412,2... | collective-permute-start | bytes 76808 | tf_op jit(solution)/shard_map/ppermute | solution.py:30
  28.5 4.3 %collective-permute-start.2 = (bf16[150,128]{1,0:T(8,128)(2,1)S(1)}, bf16[150,128]{1,0:T(8,128)(2,1)S(1)}, u32[]{:S(2)}, u32[]{:S(2)}) collective-permute-start(bf16[150,128]{1,0:T(8,128)(2,1)S(1)} %pad_maximum_fusion.10), channel_id=1, source_target_pairs={{384,0},{132,4},{392,8},{140,12},{400,16},{148,20},{408,24},{156,2... | collective-permute-start | bytes 115208 | tf_op jit(solution)/shard_map/ppermute | solution.py:30
  32.8 4.9 %collective-permute-start.1 = (bf16[150,128]{1,0:T(8,128)(2,1)S(1)}, bf16[150,128]{1,0:T(8,128)(2,1)S(1)}, u32[]{:S(2)}, u32[]{:S(2)}) collective-permute-start(bf16[150,128]{1,0:T(8,128)(2,1)S(1)} %pad_maximum_fusion.10), channel_id=1, source_target_pairs={{256,0},{260,4},{264,8},{268,12},{272,16},{276,20},{280,24},{284,2... | collective-permute-start | bytes 115208 | tf_op jit(solution)/shard_map/ppermute | solution.py:30
  40.3 4.3 %collective-permute-start = (bf16[150,128]{1,0:T(8,128)(2,1)S(1)}, bf16[150,128]{1,0:T(8,128)(2,1)S(1)}, u32[]{:S(2)}, u32[]{:S(2)}) collective-permute-start(bf16[150,128]{1,0:T(8,128)(2,1)S(1)} %pad_maximum_fusion.10), channel_id=1, source_target_pairs={{128,0},{388,4},{136,8},{396,12},{144,16},{404,20},{152,24},{412,2... | collective-permute-start | bytes 115208 | tf_op jit(solution)/shard_map/ppermute | solution.py:30
  46.1 2.9 collective-permute-start.20
  49.1 6.9 %collective-permute-start.19 = (bf16[16,3200]{1,0:T(8,128)(2,1)S(1)}, bf16[16,3200]{1,0:T(8,128)(2,1)S(1)}, u32[]{:S(2)}, u32[]{:S(2)}) collective-permute-start(bf16[16,3200]{1,0:T(8,128)(2,1)S(1)} %get-tuple-element.70), channel_id=1, source_target_pairs={{64,0},{452,4},{72,8},{460,12},{80,16},{468,20},{88,24},{476,28},{... | collective-permute-start | bytes 307208 | tf_op jit(solution)/shard_map/ppermute | solution.py:30
  56.0 2.9 %collective-permute-start.18 = (bf16[16,3200]{1,0:T(8,128)(2,1)S(1)}, bf16[16,3200]{1,0:T(8,128)(2,1)S(1)}, u32[]{:S(2)}, u32[]{:S(2)}) collective-permute-start(bf16[16,3200]{1,0:T(8,128)(2,1)S(1)} %get-tuple-element.70), channel_id=1, source_target_pairs={{32,0},{484,4},{40,8},{492,12},{48,16},{500,20},{56,24},{508,28},{... | collective-permute-start | bytes 307208 | tf_op jit(solution)/shard_map/ppermute | solution.py:30
  59.3 4.6 %collective-permute-start.4 = (bf16[600,128]{1,0:T(8,128)(2,1)S(1)}, bf16[600,128]{1,0:T(8,128)(2,1)S(1)}, u32[]{:S(2)}, u32[]{:S(2)}) collective-permute-start(bf16[600,128]{1,0:T(8,128)(2,1)S(1)} %pad_maximum_fusion.5), channel_id=1, source_target_pairs={{64,0},{452,4},{72,8},{460,12},{80,16},{468,20},{88,24},{476,28},{... | collective-permute-start | bytes 460808 | tf_op jit(solution)/shard_map/ppermute | solution.py:30
  63.9 2.9 %collective-permute-start.3 = (bf16[600,128]{1,0:T(8,128)(2,1)S(1)}, bf16[600,128]{1,0:T(8,128)(2,1)S(1)}, u32[]{:S(2)}, u32[]{:S(2)}) collective-permute-start(bf16[600,128]{1,0:T(8,128)(2,1)S(1)} %pad_maximum_fusion.5), channel_id=1, source_target_pairs={{32,0},{484,4},{40,8},{492,12},{48,16},{500,20},{56,24},{508,28},{... | collective-permute-start | bytes 460808 | tf_op jit(solution)/shard_map/ppermute | solution.py:30
  66.9 2.9 %collective-permute-start.5 = (bf16[600,128]{1,0:T(8,128)(2,1)S(1)}, bf16[600,128]{1,0:T(8,128)(2,1)S(1)}, u32[]{:S(2)}, u32[]{:S(2)}) collective-permute-start(bf16[600,128]{1,0:T(8,128)(2,1)S(1)} %pad_maximum_fusion.5), channel_id=1, source_target_pairs={{480,0},{36,4},{488,8},{44,12},{496,16},{52,20},{504,24},{60,28},{... | collective-permute-start | bytes 460808 | tf_op jit(solution)/shard_map/ppermute | solution.py:30
  70.0 2.4 collective-permute-start.23
  72.4 3.5 %collective-permute-start.21 = (bf16[64,3200]{1,0:T(8,128)(2,1)S(1)}, bf16[64,3200]{1,0:T(8,128)(2,1)}, u32[]{:S(2)}, u32[]{:S(2)}) collective-permute-start(bf16[64,3200]{1,0:T(8,128)(2,1)S(1)} %concatenate.70.refs_0_), channel_id=1, source_target_pairs={{8,0},{12,4},{16,8},{20,12},{24,16},{28,20},{0,24},{4,28},{40,32},... | collective-permute-start | bytes 1228808 | tf_op jit(solution)/shard_map/ppermute | solution.py:30
  77.0 3.7 %collective-permute-start.8 = (bf16[2400,128]{1,0:T(8,128)(2,1)S(1)}, bf16[2400,128]{1,0:T(8,128)(2,1)S(1)}, u32[]{:S(2)}, u32[]{:S(2)}) collective-permute-start(bf16[2400,128]{1,0:T(8,128)(2,1)S(1)} %pad_maximum_fusion.refs_0_), channel_id=1, source_target_pairs={{24,0},{28,4},{0,8},{4,12},{8,16},{12,20},{16,24},{20,28},{56,32},... | collective-permute-start | bytes 1843208 | tf_op jit(solution)/shard_map/ppermute | solution.py:30
  81.8 2.2 collective-permute-start.6
  86.8 4.8 %collective-permute-start.24 = (bf16[32,3200]{1,0:T(8,128)(2,1)S(1)}, bf16[32,3200]{1,0:T(8,128)(2,1)S(1)}, u32[]{:S(2)}, u32[]{:S(2)}) collective-permute-start(bf16[32,3200]{1,0:T(8,128)(2,1)S(1)} %slice.237), channel_id=1, source_target_pairs={{24,0},{28,4},{0,8},{4,12},{8,16},{12,20},{16,24},{20,28},{56,32},... | collective-permute-start | bytes 614408 | tf_op jit(solution)/shard_map/ppermute | solution.py:30
  92.6 1.9 collective-permute-start.22
  99.3 3.5 %collective-permute-done.22.refs_2_ = bf16[32,3200]{1,0:T(8,128)(2,1)S(1)} collective-permute-done((bf16[32,3200]{1,0:T(8,128)(2,1)S(1)}, bf16[32,3200]{1,0:T(8,128)(2,1)S(1)}, u32[]{:S(2)}, u32[]{:S(2)}) %collective-permute-start.22) | collective-permute-done | bytes 204832 | tf_op jit(solution)/shard_map/ppermute | solution.py:30
  105.4 2.4 collective-permute-start.28
  108.6 1.9 collective-permute-start.27
  111.3 1.9 collective-permute-start.9
  113.2 3.9 %collective-permute-start.7 = (bf16[1184,128]{1,0:T(8,128)(2,1)S(1)}, bf16[1184,128]{1,0:T(8,128)(2,1)}, u32[]{:S(2)}, u32[]{:S(2)}) collective-permute-start(bf16[1184,128]{1,0:T(8,128)(2,1)S(1)} %slice.234), channel_id=1, source_target_pairs={{8,0},{12,4},{16,8},{20,12},{24,16},{28,20},{0,24},{4,28},{40,32},... | collective-permute-start | bytes 909320 | tf_op jit(solution)/shard_map/ppermute | solution.py:30
  117.9 1.9 collective-permute-start.10
  119.8 2.4 collective-permute-start.14
  122.2 1.9 collective-permute-start.11
  126.0 1.9 collective-permute-start.12
  127.9 2.6 collective-permute-start.13
  133.5 9.5 %rotate.1 = (bf16[160,1280]{1,0:T(8,128)(2,1)}, bf16[320,1024]{1,0:T(8,128)(2,1)}, bf16[320,768]{1,0:T(8,128)(2,1)}, f32[160,2432]{1,0:T(8,128)}) custom-call(bf16[64,3200]{1,0:T(8,128)(2,1)} %copy-done.1, bf16[64,3200]{1,0:T(8,128)(2,1)} %collective-permute-done.21.refs_1_, bf16[32,3200]{1,0:T(8,128)(2,1)} %copy-done.29, bf16[32,3200]{1,0:T(8,128)(2,1)} %copy-done.28, ...), custom_call_target="tpu_custom_call" | custom-call | flops 3000000000 | bytes 3544768 | tf_op jit(solution)/shard_map/rotate/pallas_call | solution.py:316
  144.0 15.9 %layer.1 = (bf16[64,3200]{1,0:T(8,128)(2,1)}, bf16[64,3200]{1,0:T(8,128)(2,1)}, bf16[64,3200]{1,0:T(8,128)(2,1)}, bf16[64,3200]{1,0:T(8,128)(2,1)}, bf16[64,3200...) custom-call(bf16[2400,128]{1,0:T(8,128)(2,1)} %copy-done, ...), custom_call_target="tpu_custom_call" | custom-call | flops 5000000000 | bytes 8201536 | tf_op jit(solution)/shard_map/layer/pallas_call | solution.py:316
  159.9 2.1 collective-permute-start.45
  162.0 2.6 collective-permute-start.44
  164.6 1.9 collective-permute-start.46
  166.6 2.4 collective-permute-start.49
  169.0 1.9 collective-permute-start.30
  170.9 5.3 %nodes.1 = (bf16[4,3200]{1,0:T(4,128)(2,1)}, f32[4,3200]{1,0:T(4,128)}) custom-call(bf16[160,475]{1,0:T(8,128)(2,1)} %bitcast.122, bf16[160,2432]{1,0:T(8,128)(2,1)} %get-tuple-element.31.scaled, bf16[160,2432]{1,0:T(8,128)(2,1)} %get-tuple-element.32.grad_dst, s32[1,160]{1,0:T(1,128)} %target.1), custom_call_target="tpu_custom_call" | custom-call | flops 600000000 | bytes 1709120 | tf_op jit(solution)/shard_map/nodes/pallas_call | solution.py:316
  176.3 2.5 collective-permute-start.31
  178.9 1.9 collective-permute-start.32
  180.9 2.6 collective-permute-start.47
  183.6 4.6 %collective-permute-done.47 = bf16[80,640]{1,0:T(8,128)(2,1)S(1)} collective-permute-done((bf16[80,640]{1,0:T(8,128)(2,1)S(1)}, bf16[80,640]{1,0:T(8,128)(2,1)S(1)}, u32[]{:S(2)}, u32[]{:S(2)}) %collective-permute-start.47) | collective-permute-done | bytes 102432 | tf_op jit(solution)/shard_map/ppermute | solution.py:34
  188.3 2.4 collective-permute-start.50
  190.8 5.3 %collective-permute-done.50 = bf16[80,640]{1,0:T(8,128)(2,1)S(1)} collective-permute-done((bf16[80,640]{1,0:T(8,128)(2,1)S(1)}, bf16[80,640]{1,0:T(8,128)(2,1)S(1)}, u32[]{:S(2)}, u32[]{:S(2)}) %collective-permute-start.50) | collective-permute-done | bytes 102432 | tf_op jit(solution)/shard_map/ppermute | solution.py:34
  198.0 2.2 collective-permute-start.48
  200.3 3.6 %collective-permute-start.51 = (bf16[160,640]{1,0:T(8,128)(2,1)S(1)}, bf16[160,640]{1,0:T(8,128)(2,1)S(1)}, u32[]{:S(2)}, u32[]{:S(2)}) collective-permute-start(bf16[160,640]{1,0:T(8,128)(2,1)S(1)} %pad_maximum_fusion.4), channel_id=1, source_target_pairs={{0,24},{4,28},{8,0},{12,4},{16,8},{20,12},{24,16},{28,20},{32,56},... | collective-permute-start | bytes 614408 | tf_op jit(solution)/shard_map/ppermute | solution.py:34
  204.2 3.5 %collective-permute-start.33 = (bf16[32,3200]{1,0:T(8,128)(2,1)S(1)}, bf16[32,3200]{1,0:T(8,128)(2,1)S(1)}, u32[]{:S(2)}, u32[]{:S(2)}) collective-permute-start(bf16[32,3200]{1,0:T(8,128)(2,1)S(1)} %get-tuple-element.54), channel_id=1, source_target_pairs={{0,8},{4,12},{8,16},{12,20},{16,24},{20,28},{24,0},{28,4},{32,40},... | collective-permute-start | bytes 614408 | tf_op jit(solution)/shard_map/ppermute | solution.py:34
  207.9 2.4 collective-permute-start.36
  210.8 1.9 collective-permute-start.52
  212.7 5.1 %collective-permute-start.54 = (bf16[40,640]{1,0:T(8,128)(2,1)S(1)}, bf16[40,640]{1,0:T(8,128)(2,1)S(1)}, u32[]{:S(2)}, u32[]{:S(2)}) collective-permute-start(bf16[40,640]{1,0:T(8,128)(2,1)S(1)} %get-tuple-element.57), channel_id=1, source_target_pairs={{0,480},{4,36},{8,488},{12,44},{16,496},{20,52},{24,504},{28,60},{... | collective-permute-start | bytes 153608 | tf_op jit(solution)/shard_map/ppermute | solution.py:34
  217.9 1.9 collective-permute-start.53
  219.9 4.5 %collective-permute-start.34 = (bf16[64,3200]{1,0:T(8,128)(2,1)S(1)}, bf16[64,3200]{1,0:T(8,128)(2,1)S(1)}, u32[]{:S(2)}, u32[]{:S(2)}) collective-permute-start(bf16[64,3200]{1,0:T(8,128)(2,1)S(1)} %pad_maximum_fusion.1), channel_id=1, source_target_pairs={{0,8},{4,12},{8,16},{12,20},{16,24},{20,28},{24,0},{28,4},{32,40},... | collective-permute-start | bytes 1228808 | tf_op jit(solution)/shard_map/ppermute | solution.py:34
  224.5 1.9 collective-permute-start.37
  226.5 3.8 %collective-permute-start.55 = (bf16[10,640]{1,0:T(8,128)(2,1)S(1)}, bf16[10,640]{1,0:T(8,128)(2,1)S(1)}, u32[]{:S(2)}, u32[]{:S(2)}) collective-permute-start(bf16[10,640]{1,0:T(8,128)(2,1)S(1)} %get-tuple-element.64), channel_id=1, source_target_pairs={{0,128},{4,388},{8,136},{12,396},{16,144},{20,404},{24,152},{28,41... | collective-permute-start | bytes 38408 | tf_op jit(solution)/shard_map/ppermute | solution.py:34
  230.3 6.0 %collective-permute-start.57 = (bf16[10,640]{1,0:T(8,128)(2,1)S(1)}, bf16[10,640]{1,0:T(8,128)(2,1)S(1)}, u32[]{:S(2)}, u32[]{:S(2)}) collective-permute-start(bf16[10,640]{1,0:T(8,128)(2,1)S(1)} %get-tuple-element.65), channel_id=1, source_target_pairs={{0,384},{4,132},{8,392},{12,140},{16,400},{20,148},{24,408},{28,15... | collective-permute-start | bytes 38408 | tf_op jit(solution)/shard_map/ppermute | solution.py:34
  236.3 6.7 %collective-permute-start.56 = (bf16[10,640]{1,0:T(8,128)(2,1)S(1)}, bf16[10,640]{1,0:T(8,128)(2,1)S(1)}, u32[]{:S(2)}, u32[]{:S(2)}) collective-permute-start(bf16[10,640]{1,0:T(8,128)(2,1)S(1)} %get-tuple-element.66), channel_id=1, source_target_pairs={{0,256},{4,260},{8,264},{12,268},{16,272},{20,276},{24,280},{28,28... | collective-permute-start | bytes 38408 | tf_op jit(solution)/shard_map/ppermute | solution.py:34
  243.3 3.9 %collective-permute-start.38 = (bf16[16,3200]{1,0:T(8,128)(2,1)S(1)}, bf16[16,3200]{1,0:T(8,128)(2,1)S(1)}, u32[]{:S(2)}, u32[]{:S(2)}) collective-permute-start(bf16[16,3200]{1,0:T(8,128)(2,1)S(1)} %get-tuple-element.51), channel_id=1, source_target_pairs={{0,32},{4,484},{8,40},{12,492},{16,48},{20,500},{24,56},{28,508},{... | collective-permute-start | bytes 307208 | tf_op jit(solution)/shard_map/ppermute | solution.py:34
  247.2 3.1 %collective-permute-start.40 = (bf16[16,3200]{1,0:T(8,128)(2,1)S(1)}, bf16[16,3200]{1,0:T(8,128)(2,1)S(1)}, u32[]{:S(2)}, u32[]{:S(2)}) collective-permute-start(bf16[16,3200]{1,0:T(8,128)(2,1)S(1)} %get-tuple-element.52), channel_id=1, source_target_pairs={{0,480},{4,36},{8,488},{12,44},{16,496},{20,52},{24,504},{28,60},{... | collective-permute-start | bytes 307208 | tf_op jit(solution)/shard_map/ppermute | solution.py:34
  250.4 5.4 %collective-permute-start.39 = (bf16[16,3200]{1,0:T(8,128)(2,1)S(1)}, bf16[16,3200]{1,0:T(8,128)(2,1)S(1)}, u32[]{:S(2)}, u32[]{:S(2)}) collective-permute-start(bf16[16,3200]{1,0:T(8,128)(2,1)S(1)} %get-tuple-element.53), channel_id=1, source_target_pairs={{0,64},{4,452},{8,72},{12,460},{16,80},{20,468},{24,88},{28,476},{... | collective-permute-start | bytes 307208 | tf_op jit(solution)/shard_map/ppermute | solution.py:34
  255.8 4.9 %collective-permute-start.60 = (f32[10,640]{1,0:T(8,128)S(1)}, f32[10,640]{1,0:T(8,128)S(1)}, u32[]{:S(2)}, u32[]{:S(2)}) collective-permute-start(f32[10,640]{1,0:T(8,128)S(1)} %convert_add_fusion), channel_id=1, source_target_pairs={{0,3},{1,0},{2,1},{3,2},{4,7},{5,4},{6,5},{7,6},{8,11},{9,8},{10,9... | collective-permute-start | bytes 76808 | tf_op jit(solution)/shard_map/ppermute | solution.py:417
  260.8 2.5 collective-permute-start.59
  263.3 2.9 collective-permute-start.58
  266.3 4.3 %collective-permute-start.41 = (bf16[4,3200]{1,0:T(4,128)(2,1)S(1)}, bf16[4,3200]{1,0:T(4,128)(2,1)S(1)}, u32[]{:S(2)}, u32[]{:S(2)}) collective-permute-start(bf16[4,3200]{1,0:T(4,128)(2,1)S(1)} %get-tuple-element.61), channel_id=1, source_target_pairs={{0,128},{4,388},{8,136},{12,396},{16,144},{20,404},{24,152},{28,41... | collective-permute-start | bytes 76808 | tf_op jit(solution)/shard_map/ppermute | solution.py:34
  270.6 5.5 %collective-permute-start.43 = (bf16[4,3200]{1,0:T(4,128)(2,1)S(1)}, bf16[4,3200]{1,0:T(4,128)(2,1)S(1)}, u32[]{:S(2)}, u32[]{:S(2)}) collective-permute-start(bf16[4,3200]{1,0:T(4,128)(2,1)S(1)} %get-tuple-element.62), channel_id=1, source_target_pairs={{0,384},{4,132},{8,392},{12,140},{16,400},{20,148},{24,408},{28,15... | collective-permute-start | bytes 76808 | tf_op jit(solution)/shard_map/ppermute | solution.py:34
  276.1 5.6 %collective-permute-start.42 = (bf16[4,3200]{1,0:T(4,128)(2,1)S(1)}, bf16[4,3200]{1,0:T(4,128)(2,1)S(1)}, u32[]{:S(2)}, u32[]{:S(2)}) collective-permute-start(bf16[4,3200]{1,0:T(4,128)(2,1)S(1)} %get-tuple-element.63), channel_id=1, source_target_pairs={{0,256},{4,260},{8,264},{12,268},{16,272},{20,276},{24,280},{28,28... | collective-permute-start | bytes 76808 | tf_op jit(solution)/shard_map/ppermute | solution.py:34
  282.4 8.5 %collective-permute-done.42 = bf16[4,3200]{1,0:T(4,128)(2,1)S(1)} collective-permute-done((bf16[4,3200]{1,0:T(4,128)(2,1)S(1)}, bf16[4,3200]{1,0:T(4,128)(2,1)S(1)}, u32[]{:S(2)}, u32[]{:S(2)}) %collective-permute-start.42) | collective-permute-done | bytes 25632 | tf_op jit(solution)/shard_map/ppermute | solution.py:34
  (227 shorter events, 32.0 us)
Async XLA Ops:
  0.6 69.2 %copy-start.13 = (bf16[1,4,3200]{2,1,0:T(4,128)(2,1)S(1)}, bf16[1,4,3200]{2,1,0:T(4,128)(2,1)}, u32[]{:S(2)}) copy-start(bf16[1,4,3200]{2,1,0:T(4,128)(2,1)} %param.12) | copy-start | bytes 76804
  0.6 39.7 %collective-permute-start.17 = (bf16[4,3200]{1,0:T(4,128)(2,1)}, bf16[4,3200]{1,0:T(4,128)(2,1)S(1)}, u32[]{:S(2)}, u32[]{:S(2)}) collective-permute-start(bf16[4,3200]{1,0:T(4,128)(2,1)} %bitcast.111), channel_id=1, source_target_pairs={{384,0},{132,4},{392,8},{140,12},{400,16},{148,20},{408,24},{156,2... | collective-permute-start | bytes 76808 | tf_op jit(solution)/shard_map/ppermute | solution.py:30
  9.7 34.9 %collective-permute-start.16 = (bf16[4,3200]{1,0:T(4,128)(2,1)}, bf16[4,3200]{1,0:T(4,128)(2,1)S(1)}, u32[]{:S(2)}, u32[]{:S(2)}) collective-permute-start(bf16[4,3200]{1,0:T(4,128)(2,1)} %bitcast.112), channel_id=1, source_target_pairs={{256,0},{260,4},{264,8},{268,12},{272,16},{276,20},{280,24},{284,2... | collective-permute-start | bytes 76808 | tf_op jit(solution)/shard_map/ppermute | solution.py:30
  20.7 24.0 %collective-permute-start.15 = (bf16[4,3200]{1,0:T(4,128)(2,1)}, bf16[4,3200]{1,0:T(4,128)(2,1)S(1)}, u32[]{:S(2)}, u32[]{:S(2)}) collective-permute-start(bf16[4,3200]{1,0:T(4,128)(2,1)} %bitcast.113), channel_id=1, source_target_pairs={{128,0},{388,4},{136,8},{396,12},{144,16},{404,20},{152,24},{412,2... | collective-permute-start | bytes 76808 | tf_op jit(solution)/shard_map/ppermute | solution.py:30
  28.5 27.5 %collective-permute-start.2 = (bf16[150,128]{1,0:T(8,128)(2,1)S(1)}, bf16[150,128]{1,0:T(8,128)(2,1)S(1)}, u32[]{:S(2)}, u32[]{:S(2)}) collective-permute-start(bf16[150,128]{1,0:T(8,128)(2,1)S(1)} %pad_maximum_fusion.10), channel_id=1, source_target_pairs={{384,0},{132,4},{392,8},{140,12},{400,16},{148,20},{408,24},{156,2... | collective-permute-start | bytes 115208 | tf_op jit(solution)/shard_map/ppermute | solution.py:30
  32.8 26.2 %collective-permute-start.1 = (bf16[150,128]{1,0:T(8,128)(2,1)S(1)}, bf16[150,128]{1,0:T(8,128)(2,1)S(1)}, u32[]{:S(2)}, u32[]{:S(2)}) collective-permute-start(bf16[150,128]{1,0:T(8,128)(2,1)S(1)} %pad_maximum_fusion.10), channel_id=1, source_target_pairs={{256,0},{260,4},{264,8},{268,12},{272,16},{276,20},{280,24},{284,2... | collective-permute-start | bytes 115208 | tf_op jit(solution)/shard_map/ppermute | solution.py:30
  40.3 18.7 %collective-permute-start = (bf16[150,128]{1,0:T(8,128)(2,1)S(1)}, bf16[150,128]{1,0:T(8,128)(2,1)S(1)}, u32[]{:S(2)}, u32[]{:S(2)}) collective-permute-start(bf16[150,128]{1,0:T(8,128)(2,1)S(1)} %pad_maximum_fusion.10), channel_id=1, source_target_pairs={{128,0},{388,4},{136,8},{396,12},{144,16},{404,20},{152,24},{412,2... | collective-permute-start | bytes 115208 | tf_op jit(solution)/shard_map/ppermute | solution.py:30
  46.1 20.8 %collective-permute-start.20 = (bf16[16,3200]{1,0:T(8,128)(2,1)S(1)}, bf16[16,3200]{1,0:T(8,128)(2,1)S(1)}, u32[]{:S(2)}, u32[]{:S(2)}) collective-permute-start(bf16[16,3200]{1,0:T(8,128)(2,1)S(1)} %get-tuple-element.70), channel_id=1, source_target_pairs={{480,0},{36,4},{488,8},{44,12},{496,16},{52,20},{504,24},{60,28},{... | collective-permute-start | bytes 307208 | tf_op jit(solution)/shard_map/ppermute | solution.py:30
  49.1 20.8 %collective-permute-start.19 = (bf16[16,3200]{1,0:T(8,128)(2,1)S(1)}, bf16[16,3200]{1,0:T(8,128)(2,1)S(1)}, u32[]{:S(2)}, u32[]{:S(2)}) collective-permute-start(bf16[16,3200]{1,0:T(8,128)(2,1)S(1)} %get-tuple-element.70), channel_id=1, source_target_pairs={{64,0},{452,4},{72,8},{460,12},{80,16},{468,20},{88,24},{476,28},{... | collective-permute-start | bytes 307208 | tf_op jit(solution)/shard_map/ppermute | solution.py:30
  56.0 13.8 %collective-permute-start.18 = (bf16[16,3200]{1,0:T(8,128)(2,1)S(1)}, bf16[16,3200]{1,0:T(8,128)(2,1)S(1)}, u32[]{:S(2)}, u32[]{:S(2)}) collective-permute-start(bf16[16,3200]{1,0:T(8,128)(2,1)S(1)} %get-tuple-element.70), channel_id=1, source_target_pairs={{32,0},{484,4},{40,8},{492,12},{48,16},{500,20},{56,24},{508,28},{... | collective-permute-start | bytes 307208 | tf_op jit(solution)/shard_map/ppermute | solution.py:30
  59.3 16.6 %collective-permute-start.4 = (bf16[600,128]{1,0:T(8,128)(2,1)S(1)}, bf16[600,128]{1,0:T(8,128)(2,1)S(1)}, u32[]{:S(2)}, u32[]{:S(2)}) collective-permute-start(bf16[600,128]{1,0:T(8,128)(2,1)S(1)} %pad_maximum_fusion.5), channel_id=1, source_target_pairs={{64,0},{452,4},{72,8},{460,12},{80,16},{468,20},{88,24},{476,28},{... | collective-permute-start | bytes 460808 | tf_op jit(solution)/shard_map/ppermute | solution.py:30
  63.9 12.0 %collective-permute-start.3 = (bf16[600,128]{1,0:T(8,128)(2,1)S(1)}, bf16[600,128]{1,0:T(8,128)(2,1)S(1)}, u32[]{:S(2)}, u32[]{:S(2)}) collective-permute-start(bf16[600,128]{1,0:T(8,128)(2,1)S(1)} %pad_maximum_fusion.5), channel_id=1, source_target_pairs={{32,0},{484,4},{40,8},{492,12},{48,16},{500,20},{56,24},{508,28},{... | collective-permute-start | bytes 460808 | tf_op jit(solution)/shard_map/ppermute | solution.py:30
  66.9 9.1 %collective-permute-start.5 = (bf16[600,128]{1,0:T(8,128)(2,1)S(1)}, bf16[600,128]{1,0:T(8,128)(2,1)S(1)}, u32[]{:S(2)}, u32[]{:S(2)}) collective-permute-start(bf16[600,128]{1,0:T(8,128)(2,1)S(1)} %pad_maximum_fusion.5), channel_id=1, source_target_pairs={{480,0},{36,4},{488,8},{44,12},{496,16},{52,20},{504,24},{60,28},{... | collective-permute-start | bytes 460808 | tf_op jit(solution)/shard_map/ppermute | solution.py:30
  70.0 16.7 %collective-permute-start.23 = (bf16[64,3200]{1,0:T(8,128)(2,1)S(1)}, bf16[64,3200]{1,0:T(8,128)(2,1)S(1)}, u32[]{:S(2)}, u32[]{:S(2)}) collective-permute-start(bf16[64,3200]{1,0:T(8,128)(2,1)S(1)} %concatenate.70.refs_0_), channel_id=1, source_target_pairs={{24,0},{28,4},{0,8},{4,12},{8,16},{12,20},{16,24},{20,28},{56,32},... | collective-permute-start | bytes 1228808 | tf_op jit(solution)/shard_map/ppermute | solution.py:30
  72.4 19.2 %collective-permute-start.21 = (bf16[64,3200]{1,0:T(8,128)(2,1)S(1)}, bf16[64,3200]{1,0:T(8,128)(2,1)}, u32[]{:S(2)}, u32[]{:S(2)}) collective-permute-start(bf16[64,3200]{1,0:T(8,128)(2,1)S(1)} %concatenate.70.refs_0_), channel_id=1, source_target_pairs={{8,0},{12,4},{16,8},{20,12},{24,16},{28,20},{0,24},{4,28},{40,32},... | collective-permute-start | bytes 1228808 | tf_op jit(solution)/shard_map/ppermute | solution.py:30
  77.0 55.1 %copy-start = (bf16[2400,128]{1,0:T(8,128)(2,1)}, bf16[2400,128]{1,0:T(8,128)(2,1)S(1)}, u32[]{:S(2)}) copy-start(bf16[2400,128]{1,0:T(8,128)(2,1)S(1)} %pad_maximum_fusion.refs_0_) | copy-start | bytes 1843204
  77.0 55.8 %copy-start.15 = (f32[1,160,8]{1,2,0:T(8,128)S(1)}, f32[1,160,8]{1,2,0:T(8,128)}, u32[]{:S(2)}) copy-start(f32[1,160,8]{1,2,0:T(8,128)} %param.18) | copy-start | bytes 15364
  77.0 28.4 %collective-permute-start.8 = (bf16[2400,128]{1,0:T(8,128)(2,1)S(1)}, bf16[2400,128]{1,0:T(8,128)(2,1)S(1)}, u32[]{:S(2)}, u32[]{:S(2)}) collective-permute-start(bf16[2400,128]{1,0:T(8,128)(2,1)S(1)} %pad_maximum_fusion.refs_0_), channel_id=1, source_target_pairs={{24,0},{28,4},{0,8},{4,12},{8,16},{12,20},{16,24},{20,28},{56,32},... | collective-permute-start | bytes 1843208 | tf_op jit(solution)/shard_map/ppermute | solution.py:30
  81.8 26.8 %collective-permute-start.6 = (bf16[2400,128]{1,0:T(8,128)(2,1)S(1)}, bf16[2400,128]{1,0:T(8,128)(2,1)S(1)}, u32[]{:S(2)}, u32[]{:S(2)}) collective-permute-start(bf16[2400,128]{1,0:T(8,128)(2,1)S(1)} %pad_maximum_fusion.refs_0_), channel_id=1, source_target_pairs={{8,0},{12,4},{16,8},{20,12},{24,16},{28,20},{0,24},{4,28},{40,32},... | collective-permute-start | bytes 1843208 | tf_op jit(solution)/shard_map/ppermute | solution.py:30
  84.8 26.4 %collective-permute-start.25 = (bf16[64,3200]{1,0:T(8,128)(2,1)S(1)}, bf16[64,3200]{1,0:T(8,128)(2,1)S(1)}, u32[]{:S(2)}, u32[]{:S(2)}) collective-permute-start(bf16[64,3200]{1,0:T(8,128)(2,1)S(1)} %concatenate.70.refs_0_), channel_id=1, source_target_pairs={{4,0},{0,4},{12,8},{8,12},{20,16},{16,20},{28,24},{24,28},{36,32},... | collective-permute-start | bytes 1228808 | tf_op jit(solution)/shard_map/ppermute | solution.py:30
  86.8 10.6 %collective-permute-start.24 = (bf16[32,3200]{1,0:T(8,128)(2,1)S(1)}, bf16[32,3200]{1,0:T(8,128)(2,1)S(1)}, u32[]{:S(2)}, u32[]{:S(2)}) collective-permute-start(bf16[32,3200]{1,0:T(8,128)(2,1)S(1)} %slice.237), channel_id=1, source_target_pairs={{24,0},{28,4},{0,8},{4,12},{8,16},{12,20},{16,24},{20,28},{56,32},... | collective-permute-start | bytes 614408 | tf_op jit(solution)/shard_map/ppermute | solution.py:30
  92.6 10.3 %collective-permute-start.22 = (bf16[32,3200]{1,0:T(8,128)(2,1)S(1)}, bf16[32,3200]{1,0:T(8,128)(2,1)S(1)}, u32[]{:S(2)}, u32[]{:S(2)}) collective-permute-start(bf16[32,3200]{1,0:T(8,128)(2,1)S(1)} %slice.236), channel_id=1, source_target_pairs={{8,0},{12,4},{16,8},{20,12},{24,16},{28,20},{0,24},{4,28},{40,32},... | collective-permute-start | bytes 614408 | tf_op jit(solution)/shard_map/ppermute | solution.py:30
  97.4 20.4 %collective-permute-start.29 = (bf16[64,3200]{1,0:T(8,128)(2,1)S(1)}, bf16[64,3200]{1,0:T(8,128)(2,1)S(1)}, u32[]{:S(2)}, u32[]{:S(2)}) collective-permute-start(bf16[64,3200]{1,0:T(8,128)(2,1)S(1)} %collective-permute-done.23.refs_4_), channel_id=1, source_target_pairs={{4,0},{0,4},{12,8},{8,12},{20,16},{16,20},{28,24},{24,28},{36,32},... | collective-permute-start | bytes 1228808 | tf_op jit(solution)/shard_map/ppermute | solution.py:30
  102.9 19.4 %collective-permute-start.26 = (bf16[64,3200]{1,0:T(8,128)(2,1)}, bf16[64,3200]{1,0:T(8,128)(2,1)S(1)}, u32[]{:S(2)}, u32[]{:S(2)}) collective-permute-start(bf16[64,3200]{1,0:T(8,128)(2,1)} %collective-permute-done.21.refs_1_), channel_id=1, source_target_pairs={{4,0},{0,4},{12,8},{8,12},{20,16},{16,20},{28,24},{24,28},{36,32},... | collective-permute-start | bytes 1228808 | tf_op jit(solution)/shard_map/ppermute | solution.py:30
  105.4 7.8 %collective-permute-start.28 = (bf16[32,3200]{1,0:T(8,128)(2,1)S(1)}, bf16[32,3200]{1,0:T(8,128)(2,1)S(1)}, u32[]{:S(2)}, u32[]{:S(2)}) collective-permute-start(bf16[32,3200]{1,0:T(8,128)(2,1)S(1)} %collective-permute-done.24.refs_3_), channel_id=1, source_target_pairs={{4,0},{0,4},{12,8},{8,12},{20,16},{16,20},{28,24},{24,28},{36,32},... | collective-permute-start | bytes 614408 | tf_op jit(solution)/shard_map/ppermute | solution.py:30
  108.6 11.2 %collective-permute-start.27 = (bf16[32,3200]{1,0:T(8,128)(2,1)S(1)}, bf16[32,3200]{1,0:T(8,128)(2,1)S(1)}, u32[]{:S(2)}, u32[]{:S(2)}) collective-permute-start(bf16[32,3200]{1,0:T(8,128)(2,1)S(1)} %collective-permute-done.22.refs_2_), channel_id=1, source_target_pairs={{4,0},{0,4},{12,8},{8,12},{20,16},{16,20},{28,24},{24,28},{36,32},... | collective-permute-start | bytes 614408 | tf_op jit(solution)/shard_map/ppermute | solution.py:30
  111.3 16.7 %collective-permute-start.9 = (bf16[1216,128]{1,0:T(8,128)(2,1)S(1)}, bf16[1216,128]{1,0:T(8,128)(2,1)S(1)}, u32[]{:S(2)}, u32[]{:S(2)}) collective-permute-start(bf16[1216,128]{1,0:T(8,128)(2,1)S(1)} %slice.235), channel_id=1, source_target_pairs={{24,0},{28,4},{0,8},{4,12},{8,16},{12,20},{16,24},{20,28},{56,32},... | collective-permute-start | bytes 933896 | tf_op jit(solution)/shard_map/ppermute | solution.py:30
  113.2 12.8 %collective-permute-start.7 = (bf16[1184,128]{1,0:T(8,128)(2,1)S(1)}, bf16[1184,128]{1,0:T(8,128)(2,1)}, u32[]{:S(2)}, u32[]{:S(2)}) collective-permute-start(bf16[1184,128]{1,0:T(8,128)(2,1)S(1)} %slice.234), channel_id=1, source_target_pairs={{8,0},{12,4},{16,8},{20,12},{24,16},{28,20},{0,24},{4,28},{40,32},... | collective-permute-start | bytes 909320 | tf_op jit(solution)/shard_map/ppermute | solution.py:30
  117.9 25.3 %collective-permute-start.10 = (bf16[2400,128]{1,0:T(8,128)(2,1)S(1)}, bf16[2400,128]{1,0:T(8,128)(2,1)S(1)}, u32[]{:S(2)}, u32[]{:S(2)}) collective-permute-start(bf16[2400,128]{1,0:T(8,128)(2,1)S(1)} %pad_maximum_fusion.refs_0_), channel_id=1, source_target_pairs={{4,0},{0,4},{12,8},{8,12},{20,16},{16,20},{28,24},{24,28},{36,32},... | collective-permute-start | bytes 1843208 | tf_op jit(solution)/shard_map/ppermute | solution.py:30
  119.8 23.3 %collective-permute-start.14 = (bf16[2400,128]{1,0:T(8,128)(2,1)S(1)}, bf16[2400,128]{1,0:T(8,128)(2,1)}, u32[]{:S(2)}, u32[]{:S(2)}) collective-permute-start(bf16[2400,128]{1,0:T(8,128)(2,1)S(1)} %collective-permute-done.8.refs_4_), channel_id=1, source_target_pairs={{4,0},{0,4},{12,8},{8,12},{20,16},{16,20},{28,24},{24,28},{36,32},... | collective-permute-start | bytes 1843208 | tf_op jit(solution)/shard_map/ppermute | solution.py:30
  122.2 20.9 %collective-permute-start.11 = (bf16[2400,128]{1,0:T(8,128)(2,1)S(1)}, bf16[2400,128]{1,0:T(8,128)(2,1)}, u32[]{:S(2)}, u32[]{:S(2)}) collective-permute-start(bf16[2400,128]{1,0:T(8,128)(2,1)S(1)} %collective-permute-done.6.refs_1_), channel_id=1, source_target_pairs={{4,0},{0,4},{12,8},{8,12},{20,16},{16,20},{28,24},{24,28},{36,32},... | collective-permute-start | bytes 1843208 | tf_op jit(solution)/shard_map/ppermute | solution.py:30
  126.0 17.1 %collective-permute-start.12 = (bf16[1184,128]{1,0:T(8,128)(2,1)}, bf16[1184,128]{1,0:T(8,128)(2,1)}, u32[]{:S(2)}, u32[]{:S(2)}) collective-permute-start(bf16[1184,128]{1,0:T(8,128)(2,1)} %collective-permute-done.7.refs_2_), channel_id=1, source_target_pairs={{4,0},{0,4},{12,8},{8,12},{20,16},{16,20},{28,24},{24,28},{36,32},... | collective-permute-start | bytes 909320 | tf_op jit(solution)/shard_map/ppermute | solution.py:30
  127.9 15.2 %collective-permute-start.13 = (bf16[1216,128]{1,0:T(8,128)(2,1)S(1)}, bf16[1216,128]{1,0:T(8,128)(2,1)}, u32[]{:S(2)}, u32[]{:S(2)}) collective-permute-start(bf16[1216,128]{1,0:T(8,128)(2,1)S(1)} %collective-permute-done.9.refs_3_), channel_id=1, source_target_pairs={{4,0},{0,4},{12,8},{8,12},{20,16},{16,20},{28,24},{24,28},{36,32},... | collective-permute-start | bytes 933896 | tf_op jit(solution)/shard_map/ppermute | solution.py:30
  159.9 16.3 %collective-permute-start.45 = (bf16[160,640]{1,0:T(8,128)(2,1)}, bf16[160,640]{1,0:T(8,128)(2,1)S(1)}, u32[]{:S(2)}, u32[]{:S(2)}) collective-permute-start(bf16[160,640]{1,0:T(8,128)(2,1)} %get-tuple-element.46), channel_id=1, source_target_pairs={{0,4},{4,0},{8,12},{12,8},{16,20},{20,16},{24,28},{28,24},{32,36},... | collective-permute-start | bytes 614408 | tf_op jit(solution)/shard_map/ppermute | solution.py:34
  162.0 45.9 %collective-permute-start.44 = (bf16[160,640]{1,0:T(8,128)(2,1)}, bf16[160,640]{1,0:T(8,128)(2,1)S(1)}, u32[]{:S(2)}, u32[]{:S(2)}) collective-permute-start(bf16[160,640]{1,0:T(8,128)(2,1)} %get-tuple-element.44), channel_id=1, source_target_pairs={{0,4},{4,0},{8,12},{12,8},{16,20},{20,16},{24,28},{28,24},{32,36},... | collective-permute-start | bytes 614408 | tf_op jit(solution)/shard_map/ppermute | solution.py:34
  164.6 14.2 %collective-permute-start.46 = (bf16[160,640]{1,0:T(8,128)(2,1)}, bf16[160,640]{1,0:T(8,128)(2,1)S(1)}, u32[]{:S(2)}, u32[]{:S(2)}) collective-permute-start(bf16[160,640]{1,0:T(8,128)(2,1)} %get-tuple-element.48), channel_id=1, source_target_pairs={{0,4},{4,0},{8,12},{12,8},{16,20},{20,16},{24,28},{28,24},{32,36},... | collective-permute-start | bytes 614408 | tf_op jit(solution)/shard_map/ppermute | solution.py:34
  166.6 14.4 %collective-permute-start.49 = (bf16[160,640]{1,0:T(8,128)(2,1)}, bf16[160,640]{1,0:T(8,128)(2,1)S(1)}, u32[]{:S(2)}, u32[]{:S(2)}) collective-permute-start(bf16[160,640]{1,0:T(8,128)(2,1)} %get-tuple-element.50), channel_id=1, source_target_pairs={{0,4},{4,0},{8,12},{12,8},{16,20},{20,16},{24,28},{28,24},{32,36},... | collective-permute-start | bytes 614408 | tf_op jit(solution)/shard_map/ppermute | solution.py:34
  169.0 67.3 %collective-permute-start.30 = (bf16[64,3200]{1,0:T(8,128)(2,1)}, bf16[64,3200]{1,0:T(8,128)(2,1)S(1)}, u32[]{:S(2)}, u32[]{:S(2)}) collective-permute-start(bf16[64,3200]{1,0:T(8,128)(2,1)} %get-tuple-element.36), channel_id=1, source_target_pairs={{0,4},{4,0},{8,12},{12,8},{16,20},{20,16},{24,28},{28,24},{32,36},... | collective-permute-start | bytes 1228808 | tf_op jit(solution)/shard_map/ppermute | solution.py:34
  176.3 21.7 %collective-permute-start.31 = (bf16[64,3200]{1,0:T(8,128)(2,1)S(1)}, bf16[64,3200]{1,0:T(8,128)(2,1)S(1)}, u32[]{:S(2)}, u32[]{:S(2)}) collective-permute-start(bf16[64,3200]{1,0:T(8,128)(2,1)S(1)} %copy-done.24), channel_id=1, source_target_pairs={{0,4},{4,0},{8,12},{12,8},{16,20},{20,16},{24,28},{28,24},{32,36},... | collective-permute-start | bytes 1228808 | tf_op jit(solution)/shard_map/ppermute | solution.py:34
  178.9 21.4 %collective-permute-start.32 = (bf16[64,3200]{1,0:T(8,128)(2,1)S(1)}, bf16[64,3200]{1,0:T(8,128)(2,1)S(1)}, u32[]{:S(2)}, u32[]{:S(2)}) collective-permute-start(bf16[64,3200]{1,0:T(8,128)(2,1)S(1)} %copy-done.22), channel_id=1, source_target_pairs={{0,4},{4,0},{8,12},{12,8},{16,20},{20,16},{24,28},{28,24},{32,36},... | collective-permute-start | bytes 1228808 | tf_op jit(solution)/shard_map/ppermute | solution.py:34
  180.9 7.3 %collective-permute-start.47 = (bf16[80,640]{1,0:T(8,128)(2,1)S(1)}, bf16[80,640]{1,0:T(8,128)(2,1)S(1)}, u32[]{:S(2)}, u32[]{:S(2)}) collective-permute-start(bf16[80,640]{1,0:T(8,128)(2,1)S(1)} %get-tuple-element.59), channel_id=1, source_target_pairs={{0,8},{4,12},{8,16},{12,20},{16,24},{20,28},{24,0},{28,4},{32,40},... | collective-permute-start | bytes 307208 | tf_op jit(solution)/shard_map/ppermute | solution.py:34
  188.3 7.8 %collective-permute-start.50 = (bf16[80,640]{1,0:T(8,128)(2,1)S(1)}, bf16[80,640]{1,0:T(8,128)(2,1)S(1)}, u32[]{:S(2)}, u32[]{:S(2)}) collective-permute-start(bf16[80,640]{1,0:T(8,128)(2,1)S(1)} %get-tuple-element.60), channel_id=1, source_target_pairs={{0,24},{4,28},{8,0},{12,4},{16,8},{20,12},{24,16},{28,20},{32,56},... | collective-permute-start | bytes 307208 | tf_op jit(solution)/shard_map/ppermute | solution.py:34
  196.0 8.2 %collective-permute-start.35 = (bf16[64,3200]{1,0:T(8,128)(2,1)S(1)}, bf16[64,3200]{1,0:T(8,128)(2,1)S(1)}, u32[]{:S(2)}, u32[]{:S(2)}) collective-permute-start(bf16[64,3200]{1,0:T(8,128)(2,1)S(1)} %copy-done.21), channel_id=1, source_target_pairs={{0,4},{4,0},{8,12},{12,8},{16,20},{20,16},{24,28},{28,24},{32,36},... | collective-permute-start | bytes 1228808 | tf_op jit(solution)/shard_map/ppermute | solution.py:34
  198.0 12.3 %collective-permute-start.48 = (bf16[160,640]{1,0:T(8,128)(2,1)S(1)}, bf16[160,640]{1,0:T(8,128)(2,1)S(1)}, u32[]{:S(2)}, u32[]{:S(2)}) collective-permute-start(bf16[160,640]{1,0:T(8,128)(2,1)S(1)} %pad_maximum_fusion.3), channel_id=1, source_target_pairs={{0,8},{4,12},{8,16},{12,20},{16,24},{20,28},{24,0},{28,4},{32,40},... | collective-permute-start | bytes 614408 | tf_op jit(solution)/shard_map/ppermute | solution.py:34
  200.3 10.3 %collective-permute-start.51 = (bf16[160,640]{1,0:T(8,128)(2,1)S(1)}, bf16[160,640]{1,0:T(8,128)(2,1)S(1)}, u32[]{:S(2)}, u32[]{:S(2)}) collective-permute-start(bf16[160,640]{1,0:T(8,128)(2,1)S(1)} %pad_maximum_fusion.4), channel_id=1, source_target_pairs={{0,24},{4,28},{8,0},{12,4},{16,8},{20,12},{24,16},{28,20},{32,56},... | collective-permute-start | bytes 614408 | tf_op jit(solution)/shard_map/ppermute | solution.py:34
  204.2 13.7 %collective-permute-start.33 = (bf16[32,3200]{1,0:T(8,128)(2,1)S(1)}, bf16[32,3200]{1,0:T(8,128)(2,1)S(1)}, u32[]{:S(2)}, u32[]{:S(2)}) collective-permute-start(bf16[32,3200]{1,0:T(8,128)(2,1)S(1)} %get-tuple-element.54), channel_id=1, source_target_pairs={{0,8},{4,12},{8,16},{12,20},{16,24},{20,28},{24,0},{28,4},{32,40},... | collective-permute-start | bytes 614408 | tf_op jit(solution)/shard_map/ppermute | solution.py:34
  207.9 12.0 %collective-permute-start.36 = (bf16[32,3200]{1,0:T(8,128)(2,1)S(1)}, bf16[32,3200]{1,0:T(8,128)(2,1)S(1)}, u32[]{:S(2)}, u32[]{:S(2)}) collective-permute-start(bf16[32,3200]{1,0:T(8,128)(2,1)S(1)} %get-tuple-element.55), channel_id=1, source_target_pairs={{0,24},{4,28},{8,0},{12,4},{16,8},{20,12},{24,16},{28,20},{32,56},... | collective-permute-start | bytes 614408 | tf_op jit(solution)/shard_map/ppermute | solution.py:34
  210.8 13.7 %collective-permute-start.52 = (bf16[40,640]{1,0:T(8,128)(2,1)S(1)}, bf16[40,640]{1,0:T(8,128)(2,1)S(1)}, u32[]{:S(2)}, u32[]{:S(2)}) collective-permute-start(bf16[40,640]{1,0:T(8,128)(2,1)S(1)} %get-tuple-element.56), channel_id=1, source_target_pairs={{0,32},{4,484},{8,40},{12,492},{16,48},{20,500},{24,56},{28,508},{... | collective-permute-start | bytes 153608 | tf_op jit(solution)/shard_map/ppermute | solution.py:34
  212.7 13.7 %collective-permute-start.54 = (bf16[40,640]{1,0:T(8,128)(2,1)S(1)}, bf16[40,640]{1,0:T(8,128)(2,1)S(1)}, u32[]{:S(2)}, u32[]{:S(2)}) collective-permute-start(bf16[40,640]{1,0:T(8,128)(2,1)S(1)} %get-tuple-element.57), channel_id=1, source_target_pairs={{0,480},{4,36},{8,488},{12,44},{16,496},{20,52},{24,504},{28,60},{... | collective-permute-start | bytes 153608 | tf_op jit(solution)/shard_map/ppermute | solution.py:34
  217.9 8.6 %collective-permute-start.53 = (bf16[40,640]{1,0:T(8,128)(2,1)S(1)}, bf16[40,640]{1,0:T(8,128)(2,1)S(1)}, u32[]{:S(2)}, u32[]{:S(2)}) collective-permute-start(bf16[40,640]{1,0:T(8,128)(2,1)S(1)} %get-tuple-element.58), channel_id=1, source_target_pairs={{0,64},{4,452},{8,72},{12,460},{16,80},{20,468},{24,88},{28,476},{... | collective-permute-start | bytes 153608 | tf_op jit(solution)/shard_map/ppermute | solution.py:34
  219.9 23.1 %collective-permute-start.34 = (bf16[64,3200]{1,0:T(8,128)(2,1)S(1)}, bf16[64,3200]{1,0:T(8,128)(2,1)S(1)}, u32[]{:S(2)}, u32[]{:S(2)}) collective-permute-start(bf16[64,3200]{1,0:T(8,128)(2,1)S(1)} %pad_maximum_fusion.1), channel_id=1, source_target_pairs={{0,8},{4,12},{8,16},{12,20},{16,24},{20,28},{24,0},{28,4},{32,40},... | collective-permute-start | bytes 1228808 | tf_op jit(solution)/shard_map/ppermute | solution.py:34
  224.5 18.5 %collective-permute-start.37 = (bf16[64,3200]{1,0:T(8,128)(2,1)S(1)}, bf16[64,3200]{1,0:T(8,128)(2,1)S(1)}, u32[]{:S(2)}, u32[]{:S(2)}) collective-permute-start(bf16[64,3200]{1,0:T(8,128)(2,1)S(1)} %pad_maximum_fusion.2), channel_id=1, source_target_pairs={{0,24},{4,28},{8,0},{12,4},{16,8},{20,12},{24,16},{28,20},{32,56},... | collective-permute-start | bytes 1228808 | tf_op jit(solution)/shard_map/ppermute | solution.py:34
  226.5 23.8 %collective-permute-start.55 = (bf16[10,640]{1,0:T(8,128)(2,1)S(1)}, bf16[10,640]{1,0:T(8,128)(2,1)S(1)}, u32[]{:S(2)}, u32[]{:S(2)}) collective-permute-start(bf16[10,640]{1,0:T(8,128)(2,1)S(1)} %get-tuple-element.64), channel_id=1, source_target_pairs={{0,128},{4,388},{8,136},{12,396},{16,144},{20,404},{24,152},{28,41... | collective-permute-start | bytes 38408 | tf_op jit(solution)/shard_map/ppermute | solution.py:34
  230.3 25.5 %collective-permute-start.57 = (bf16[10,640]{1,0:T(8,128)(2,1)S(1)}, bf16[10,640]{1,0:T(8,128)(2,1)S(1)}, u32[]{:S(2)}, u32[]{:S(2)}) collective-permute-start(bf16[10,640]{1,0:T(8,128)(2,1)S(1)} %get-tuple-element.65), channel_id=1, source_target_pairs={{0,384},{4,132},{8,392},{12,140},{16,400},{20,148},{24,408},{28,15... | collective-permute-start | bytes 38408 | tf_op jit(solution)/shard_map/ppermute | solution.py:34
  236.3 19.5 %collective-permute-start.56 = (bf16[10,640]{1,0:T(8,128)(2,1)S(1)}, bf16[10,640]{1,0:T(8,128)(2,1)S(1)}, u32[]{:S(2)}, u32[]{:S(2)}) collective-permute-start(bf16[10,640]{1,0:T(8,128)(2,1)S(1)} %get-tuple-element.66), channel_id=1, source_target_pairs={{0,256},{4,260},{8,264},{12,268},{16,272},{20,276},{24,280},{28,28... | collective-permute-start | bytes 38408 | tf_op jit(solution)/shard_map/ppermute | solution.py:34
  243.3 20.0 %collective-permute-start.38 = (bf16[16,3200]{1,0:T(8,128)(2,1)S(1)}, bf16[16,3200]{1,0:T(8,128)(2,1)S(1)}, u32[]{:S(2)}, u32[]{:S(2)}) collective-permute-start(bf16[16,3200]{1,0:T(8,128)(2,1)S(1)} %get-tuple-element.51), channel_id=1, source_target_pairs={{0,32},{4,484},{8,40},{12,492},{16,48},{20,500},{24,56},{28,508},{... | collective-permute-start | bytes 307208 | tf_op jit(solution)/shard_map/ppermute | solution.py:34
  247.2 19.0 %collective-permute-start.40 = (bf16[16,3200]{1,0:T(8,128)(2,1)S(1)}, bf16[16,3200]{1,0:T(8,128)(2,1)S(1)}, u32[]{:S(2)}, u32[]{:S(2)}) collective-permute-start(bf16[16,3200]{1,0:T(8,128)(2,1)S(1)} %get-tuple-element.52), channel_id=1, source_target_pairs={{0,480},{4,36},{8,488},{12,44},{16,496},{20,52},{24,504},{28,60},{... | collective-permute-start | bytes 307208 | tf_op jit(solution)/shard_map/ppermute | solution.py:34
  250.4 15.8 %collective-permute-start.39 = (bf16[16,3200]{1,0:T(8,128)(2,1)S(1)}, bf16[16,3200]{1,0:T(8,128)(2,1)S(1)}, u32[]{:S(2)}, u32[]{:S(2)}) collective-permute-start(bf16[16,3200]{1,0:T(8,128)(2,1)S(1)} %get-tuple-element.53), channel_id=1, source_target_pairs={{0,64},{4,452},{8,72},{12,460},{16,80},{20,468},{24,88},{28,476},{... | collective-permute-start | bytes 307208 | tf_op jit(solution)/shard_map/ppermute | solution.py:34
  255.8 20.3 %collective-permute-start.60 = (f32[10,640]{1,0:T(8,128)S(1)}, f32[10,640]{1,0:T(8,128)S(1)}, u32[]{:S(2)}, u32[]{:S(2)}) collective-permute-start(f32[10,640]{1,0:T(8,128)S(1)} %convert_add_fusion), channel_id=1, source_target_pairs={{0,3},{1,0},{2,1},{3,2},{4,7},{5,4},{6,5},{7,6},{8,11},{9,8},{10,9... | collective-permute-start | bytes 76808 | tf_op jit(solution)/shard_map/ppermute | solution.py:417
  260.8 21.0 %collective-permute-start.59 = (f32[10,640]{1,0:T(8,128)S(1)}, f32[10,640]{1,0:T(8,128)S(1)}, u32[]{:S(2)}, u32[]{:S(2)}) collective-permute-start(f32[10,640]{1,0:T(8,128)S(1)} %convert_add_fusion), channel_id=1, source_target_pairs={{0,2},{1,3},{2,0},{3,1},{4,6},{5,7},{6,4},{7,5},{8,10},{9,11},{10,... | collective-permute-start | bytes 76808 | tf_op jit(solution)/shard_map/ppermute | solution.py:417
  263.3 18.4 %collective-permute-start.58 = (f32[10,640]{1,0:T(8,128)S(1)}, f32[10,640]{1,0:T(8,128)S(1)}, u32[]{:S(2)}, u32[]{:S(2)}) collective-permute-start(f32[10,640]{1,0:T(8,128)S(1)} %convert_add_fusion), channel_id=1, source_target_pairs={{0,1},{1,2},{2,3},{3,0},{4,5},{5,6},{6,7},{7,4},{8,9},{9,10},{10,1... | collective-permute-start | bytes 76808 | tf_op jit(solution)/shard_map/ppermute | solution.py:417
  266.3 16.0 %collective-permute-start.41 = (bf16[4,3200]{1,0:T(4,128)(2,1)S(1)}, bf16[4,3200]{1,0:T(4,128)(2,1)S(1)}, u32[]{:S(2)}, u32[]{:S(2)}) collective-permute-start(bf16[4,3200]{1,0:T(4,128)(2,1)S(1)} %get-tuple-element.61), channel_id=1, source_target_pairs={{0,128},{4,388},{8,136},{12,396},{16,144},{20,404},{24,152},{28,41... | collective-permute-start | bytes 76808 | tf_op jit(solution)/shard_map/ppermute | solution.py:34
  270.6 11.8 %collective-permute-start.43 = (bf16[4,3200]{1,0:T(4,128)(2,1)S(1)}, bf16[4,3200]{1,0:T(4,128)(2,1)S(1)}, u32[]{:S(2)}, u32[]{:S(2)}) collective-permute-start(bf16[4,3200]{1,0:T(4,128)(2,1)S(1)} %get-tuple-element.62), channel_id=1, source_target_pairs={{0,384},{4,132},{8,392},{12,140},{16,400},{20,148},{24,408},{28,15... | collective-permute-start | bytes 76808 | tf_op jit(solution)/shard_map/ppermute | solution.py:34
  276.1 14.7 %collective-permute-start.42 = (bf16[4,3200]{1,0:T(4,128)(2,1)S(1)}, bf16[4,3200]{1,0:T(4,128)(2,1)S(1)}, u32[]{:S(2)}, u32[]{:S(2)}) collective-permute-start(bf16[4,3200]{1,0:T(4,128)(2,1)S(1)} %get-tuple-element.63), channel_id=1, source_target_pairs={{0,256},{4,260},{8,264},{12,268},{16,272},{20,276},{24,280},{28,28... | collective-permute-start | bytes 76808 | tf_op jit(solution)/shard_map/ppermute | solution.py:34
  (29 other events, 669.7 us)

commit v2 on v1

--- a/solution.py
+++ b/solution.py
@@ -15,7 +15,11 @@
 FULL = LCOEF * CH
 ROWS_OF = {0: (0,), 1: (1, 5, 9), 2: (2, 6, 10, 13, 16), 3: (3, 7, 11, 14, 17), 4: (4, 8, 12, 15, 18)}
 NEAR = (0, 1, 2, -1)
-W_SPLIT = 800 + 3 * 128
+FAR_ROWS = 400
+DEPTHS = (48, 32, 32)
+UNITS = (5, 8, 6)
+WEIGHT_ROWS = 240 + 256 + 192
+TERM_ROWS = 400 + 240
 VMEM_LIMIT = 56 * 2**20
 F32, BF16 = jnp.float32, jnp.bfloat16
 
@@ -40,11 +44,11 @@
     xr = ((owner // 2) % 4 - (me // 2) % 4) % NX
     cr = (owner % 2 + me % 2) % 2
     near = (jz % 4 + 3) % 4
-    return cr * 64 + xr * 16 + near * 4 + jz // 4
-
-
-def block_owner(place, me):
-    cr, xr, near, far = place // 64, (place // 16) % 4, (place // 4) % 4, place % 4
+    return cr * 16 + xr * 4 + near, jz // 4
+
+
+def block_owner(place, far, me):
+    cr, xr, near = place // 16, (place // 4) % 4, place % 4
     sign = 1 - 2 * ((me + cr) % 2)
     offset = (near + 1) % 4 - 1
     z = (me // 8 + sign * (4 * far + offset)) % NZ
@@ -52,14 +56,12 @@
     return z * 8 + x * 2 + (me % 2 + cr) % 2
 
 
-def x_and_core(block, split):
-    right, left = pull(block, dx=1), pull(block, dx=3)
-    upper, lower = pull(right[:split], dx=1), pull(left[split:], dx=3)
-    mine = (block, right, upper, lower, left)
+def x_and_core(block):
+    mine = (block,) + tuple(pull(block, dx=x) for x in (1, 2, 3))
     return mine + tuple(pull(a, dc=1) for a in mine)
 
 
-def scatter_sum(pieces, split, near_rows, far_rows):
+def scatter_sum(pieces):
     def add(a, *more):
         total = a.astype(F32)
         for m in more:
@@ -67,14 +69,18 @@
         return total
 
     a = [add(pieces[x], push(pieces[4 + x], dc=1)).astype(BF16) for x in range(4)]
-    up, down = push(a[2][:split], dx=1), push(a[2][split:], dx=3)
-    right = jnp.concatenate([add(a[1][:split], up).astype(BF16), a[1][split:]], axis=0)
-    left = jnp.concatenate([a[3][:split], add(a[3][split:], down).astype(BF16)], axis=0)
-    total = add(a[0], push(right, dx=1), push(left, dx=3)).astype(BF16)
-    parts = [total[n * near_rows : (n + 1) * near_rows] for n in range(4)]
+    total = add(a[0], *(push(a[x], dx=x) for x in (1, 2, 3))).astype(BF16)
+    parts = [total[n * TERM_ROWS : (n + 1) * TERM_ROWS] for n in range(4)]
     total = add(parts[0], *(push(parts[n], dz=NEAR[n]) for n in (1, 2, 3))).astype(BF16)
-    parts = [total[n * far_rows : (n + 1) * far_rows] for n in range(4)]
-    return add(parts[0], *(push(parts[n], dz=4 * n) for n in (1, 2, 3)))
+    terms, shard = total[:400].reshape(25, 16, CH), total[400:].reshape(5, 48, CH)
+
+    def part(n):
+        return jnp.concatenate(
+            [terms[:, 4 * n : 4 * n + 4].reshape(100, CH), shard[:, 10 * n : 10 * n + 10].reshape(50, CH)], axis=0
+        )
+
+    total = add(part(0), *(push(part(n), dz=4 * n) for n in (1, 2, 3)))
+    return total[:100].reshape(25, 4, CH), total[100:].reshape(5, 10, CH)
 
 
 def hot(index, shape, axis):
@@ -98,15 +104,16 @@
 
 
 def rotate_kernel(*refs):
-    pieces = refs[:10]
-    rot, place, target, local, inv0, inv1, inv2 = refs[10:17]
-    m0, m1, m2, turned_grad = refs[17:21]
-    feats, srcf, dstf, gradf, n0, n1, n2 = refs[21:]
-    for core in range(2):
-        row = core * 256
-        for piece in pieces[core * 5 : core * 5 + 5]:
-            feats[row : row + piece.shape[0], :] = piece[...]
-            row += piece.shape[0]
+    pieces = refs[:8]
+    rot, place, target, local, inv0, inv1, inv2 = refs[8:15]
+    m0, m1, m2, turned_grad = refs[15:19]
+    feats, srcf, dstf, gradf, n0, n1, n2 = refs[19:]
+    for k, piece in enumerate(pieces):
+        for near in range(4):
+            row = k * 64 + near * 16
+            for u in range(LCOEF):
+                at = near * FAR_ROWS + u * 16
+                feats[row : row + 16, u * CH : (u + 1) * CH] = piece[at : at + 16, :]
     source_hot = hot(place[...], (EDGES, 512), 1)
     t = target[...]
     lanes = lax.broadcasted_iota(jnp.int32, (EDGES, 16), 1)
@@ -145,36 +152,25 @@
     lax.fori_loop(0, EDGES // BLOCK, turn, 0)
     for natural, ordered, inverse in ((n0, m0, inv0), (n1, m1, inv1), (n2, m2, inv2)):
         depth = natural.shape[1]
-        for first in range(0, depth, 256):
+        for first in range(0, ordered.shape[1], 256):
             cut = slice(first, first + 256)
             ordered[:, cut] = mm(natural[...], hot(inverse[:, cut], (depth, 256), 0)).astype(BF16)
 
 
 def layer_kernel(*refs):
-    pieces = refs[:10]
-    m0, m1, m2, turned_grad, rot, bias, target, live_ref, alpha_ref, place, pos0, pos1, pos2 = refs[10:23]
-    terms_out = refs[23:31]
-    w0_out = refs[31:39]
-    scaled_out, grad_dst = refs[39:41]
-    w0, w1, w2, values, d0, d1, d2, p0, p1, p2, g0, g1, g2, src_terms = refs[41:]
-
-    def place_rows(piece, core, x, begin, end):
-        k = core * 4 + x
-        at = 0
-        for out, units, rows in ((w0, 5, 160), (w1, 8, 128), (w2, 6, 96)):
-            for u in range(units):
-                if begin <= at < end:
-                    out[k * rows : (k + 1) * rows, u * CH : (u + 1) * CH] = piece[at - begin : at - begin + rows, :]
-                at += rows
-
-    for core in range(2):
-        own, right, upper, lower, left = pieces[core * 5 : core * 5 + 5]
-        place_rows(own, core, 0, 0, 2400)
-        place_rows(right, core, 1, 0, 2400)
-        place_rows(upper, core, 2, 0, W_SPLIT)
-        place_rows(lower, core, 2, W_SPLIT, 2400)
-        place_rows(left, core, 3, 0, 2400)
-
+    pieces = refs[:8]
+    m0, m1, m2, turned_grad, rot, bias, target, live_ref, alpha_ref, place, pos0, pos1, pos2 = refs[8:21]
+    terms_out = refs[21:29]
+    scaled_out, grad_dst = refs[29:31]
+    w0, w1, w2, values, d0, d1, d2, p0, p1, p2, g0, g1, g2, src_terms = refs[31:]
+    for k, piece in enumerate(pieces):
+        for near in range(4):
+            at = near * WEIGHT_ROWS
+            for out, units, rows in zip((w0, w1, w2), UNITS, DEPTHS):
+                to = (k * 4 + near) * rows
+                for u in range(units):
+                    out[to : to + rows, u * CH : (u + 1) * CH] = piece[at : at + rows, :]
+                    at += rows
     z0 = mm(m0[...], w0[...])
     for row in range(5):
         values[:, row * CH : (row + 1) * CH] = z0[:, row * CH : (row + 1) * CH].astype(BF16)
@@ -243,13 +239,16 @@
             out[:EDGES, b : b + CH] = dvalue
     dw = lax.dot_general(m0[...], d0[...], (((0,), (0,)), ((), ())), preferred_element_type=F32)
     for k in range(8):
-        w0_out[k][...] = dw[k * 160 : (k + 1) * 160].astype(BF16)
+        for near in range(4):
+            row = (k * 4 + near) * 48
+            for u in range(5):
+                at = near * TERM_ROWS + 400 + u * 48
+                terms_out[k][at : at + 48, :] = dw[row : row + 48, u * CH : (u + 1) * CH].astype(BF16)
     for d, w, p, g, pos in ((d0, w0, p0, g0, pos0), (d1, w1, p1, g1, pos1), (d2, w2, p2, g2, pos2)):
-        depth = w.shape[0]
         p[...] = mm_nt(d[...], w[...]).astype(BF16)
-        for first in range(0, depth, 256):
+        for first in range(0, g.shape[1], 256):
             cut = slice(first, first + 256)
-            g[:, cut] = mm(p[...], hot(pos[:, cut], (depth, 256), 0)).astype(BF16)
+            g[:, cut] = mm(p[...], hot(pos[:, cut], (w.shape[0], 256), 0)).astype(BF16)
     stacked = (g0, g1, g2)
     for row in range(MCOEF):
         array, base, column = frame_slot(row)
@@ -278,8 +277,11 @@
     for k in range(8):
         chosen = hot(place[...] - k * 64, (64, EDGES), 0)
         for first in range(0, FULL, 640):
-            cut = slice(first, first + 640)
-            terms_out[k][:, cut] = mm(chosen, src_terms[:, cut]).astype(BF16)
+            block = mm(chosen, src_terms[:, first : first + 640]).astype(BF16)
+            for near in range(4):
+                for n in range(5):
+                    at = near * TERM_ROWS + (first // CH + n) * 16
+                    terms_out[k][at : at + 16, :] = block[near * 16 : near * 16 + 16, n * CH : (n + 1) * CH]
 
 
 def nodes_kernel(rot, scaled, grad_dst, target, node_out, grad_local, back, terms):
@@ -325,9 +327,9 @@
     )(*args)
 
 
-def pack_units(array, rows):
-    n, _, width = array.shape
-    return array.reshape(n, rows, width // CH, CH).transpose(2, 0, 1, 3).reshape(width // CH, n * rows, CH)
+def units_of(array):
+    rows, width = array.shape
+    return array.reshape(rows, width // CH, CH).transpose(1, 0, 2).reshape(-1, CH)
 
 
 def local(
@@ -339,41 +341,39 @@
     rotor_rows = rotation[0]
     targets = target_row[0]
     live = (jnp.arange(EDGES, dtype=jnp.int32) < live_count[0, 0]).astype(jnp.int32)
-    place = block_place(source_owner[0, :, 0], me) * 4 + source_row[0]
-
-    far = jnp.concatenate([features] + [pull(features, dz=4 * a) for a in (1, 2, 3)], axis=0)
-    near = jnp.concatenate([far] + [pull(far, dz=NEAR[n]) for n in (1, 2, 3)], axis=0)
-    feature_pieces = x_and_core(near, 32)
+    block, far = block_place(source_owner[0, :, 0], me)
+    place = block * 16 + far * 4 + source_row[0]
 
     w1 = jnp.concatenate([w_m1[0], w_m1[1]], axis=1)
     w2 = jnp.concatenate([w_m2[0], w_m2[1]], axis=1)
-
-    def packed(parts):
-        return jnp.concatenate([a.reshape(-1, CH) for a in parts], axis=0)
-
-    block = packed([pack_units(w_m0[None], 10), pack_units(w1[None], 8), pack_units(w2[None], 6)])
-
-    def merged(blocks, rows):
-        cuts, at = [], 0
-        for units, depth in ((5, rows[0]), (8, rows[1]), (6, rows[2])):
-            parts = [b[at : at + units * depth].reshape(units, depth, CH) for b in blocks]
-            cuts.append(jnp.concatenate(parts, axis=1))
-            at += units * depth
-        return packed(cuts)
-
-    far_w = merged([block] + [pull(block, dz=4 * a) for a in (1, 2, 3)], (10, 8, 6))
-    near_w = merged([far_w] + [pull(far_w, dz=NEAR[n]) for n in (1, 2, 3)], (40, 32, 24))
-    weight_pieces = x_and_core(near_w, W_SPLIT)
-
-    def inverse_of(depth, rows):
-        p = jnp.arange(depth, dtype=jnp.int32)
-        return (block_owner(p // rows, me) * rows + p % rows)[None]
-
-    def position_of(depth, rows):
-        k = jnp.arange(depth, dtype=jnp.int32)
-        return (block_place(k // rows, me) * rows + k % rows)[None]
-
-    sizes = ((1280, 10), (1024, 8), (768, 6))
+    shards = (features, w_m0, w1, w2)
+    own = jnp.concatenate([units_of(a) for a in shards], axis=0)
+    blocks = [own] + [pull(own, dz=4 * a) for a in (1, 2, 3)]
+    merged, at = [], 0
+    for shard, depth in zip(shards, (16,) + DEPTHS):
+        rows, units = shard.shape[0], shard.shape[1] // CH
+        parts = [b[at : at + units * rows].reshape(units, rows, CH) for b in blocks]
+        if depth > 4 * rows:
+            parts.append(jnp.zeros((units, depth - 4 * rows, CH), BF16))
+        merged.append(jnp.concatenate(parts, axis=1).reshape(units * depth, CH))
+        at += units * rows
+    far_block = jnp.concatenate(merged, axis=0)
+    blocks = [far_block] + [pull(far_block, dz=NEAR[n]) for n in (1, 2, 3)]
+    feature_pieces = x_and_core(jnp.concatenate([b[:FAR_ROWS] for b in blocks], axis=0))
+    weight_pieces = x_and_core(jnp.concatenate([b[FAR_ROWS:] for b in blocks], axis=0))
+
+    def inverse_of(rows, depth):
+        p = jnp.arange(32 * depth, dtype=jnp.int32)
+        inside = p % depth
+        owner = block_owner(p // depth, inside // rows, me)
+        return jnp.where(inside < 4 * rows, owner * rows + inside % rows, -1)[None]
+
+    def position_of(rows, depth):
+        k = jnp.arange(128 * rows, dtype=jnp.int32)
+        block, far = block_place(k // rows, me)
+        return (block * depth + far * rows + k % rows)[None]
+
+    sizes = tuple(zip((10, 8, 6), DEPTHS))
     inverses = [inverse_of(*s) for s in sizes]
     positions = [position_of(*s) for s in sizes]
 
@@ -386,7 +386,7 @@
     m0, m1, m2, turned_grad = call(
         rotate_kernel, "rotate",
         (*feature_pieces, rotor_rows, place[:, None], targets[:, None], own_rows, *inverses),
-        [((160, 1280), BF16), ((320, 1024), BF16), ((320, 768), BF16), ((160, MCOEF * CH), F32)],
+        [((160, 1536), BF16), ((320, 1024), BF16), ((320, 1024), BF16), ((160, MCOEF * CH), F32)],
         [((512, FULL), BF16), ((160, FULL), BF16), ((160, FULL), BF16), ((160, FULL), F32),
          ((160, 1280), BF16), ((320, 1024), BF16), ((320, 768), BF16)],
         3_000_000_000,
@@ -395,22 +395,22 @@
         layer_kernel, "layer",
         (*weight_pieces, m0, m1, m2, turned_grad, rotor_rows, edge_bias[0], targets[:, None], live[:, None],
          w_alpha, place[None], *positions),
-        [((64, FULL), BF16)] * 8 + [((160, 640), BF16)] * 8
-        + [((160, MCOEF * CH), BF16), ((160, MCOEF * CH), BF16)],
-        [((1280, 640), BF16), ((1024, 1024), BF16), ((768, 768), BF16), ((160, MCOEF * CH), BF16),
+        [((4 * TERM_ROWS, CH), BF16)] * 8 + [((160, MCOEF * CH), BF16), ((160, MCOEF * CH), BF16)],
+        [((1536, 640), BF16), ((1024, 1024), BF16), ((1024, 768), BF16), ((160, MCOEF * CH), BF16),
          ((160, 640), BF16), ((320, 1024), BF16), ((320, 768), BF16),
-         ((160, 1280), BF16), ((320, 1024), BF16), ((320, 768), BF16),
+         ((160, 1536), BF16), ((320, 1024), BF16), ((320, 1024), BF16),
          ((160, 1280), BF16), ((320, 1024), BF16), ((320, 768), BF16), ((160, FULL), BF16)],
         5_000_000_000, 160 * 136,
     )
-    term_pieces, w0_pieces, (scaled, grad_dst) = outs[:8], outs[8:16], outs[16:]
+    term_pieces, (scaled, grad_dst) = outs[:8], outs[8:]
     node_out, grad_local = call(
         nodes_kernel, "nodes", (rotor_rows, scaled, grad_dst, targets[None]),
         [((4, FULL), BF16), ((4, FULL), F32)], [((160, FULL), BF16), ((160, FULL), BF16)],
         600_000_000,
     )
-    grad_remote = scatter_sum(term_pieces, 32, 16, 4)
-    shard = scatter_sum(w0_pieces, 80, 40, 10)
+    terms, shard = scatter_sum(term_pieces)
+    grad_remote = terms.transpose(1, 0, 2).reshape(4, FULL)
+    shard = shard.transpose(1, 0, 2).reshape(10, 640)
     n_rep = lax.axis_size("rep")
     grad_w0 = shard
     for r in range(1, n_rep):

time: 297 us -> 257 us (0.87); the launches traced: 291 us -> 255 us
  starting transfers between devices: 211 us -> 134 us
  waiting for transfers between devices: 24.9 us -> 63.9 us
    ppermute x28 -> x13, starting transfers between devices: 93.7 us -> 44.8 us  [push(): lax.ppermute(a, 'edge', [(i, where_to(i, dz, dx, dc)) for i in range(128)])]
    ppermute x30 -> x20, starting transfers between devices: 107 us -> 78.5 us  [pull(): lax.ppermute(a, 'edge', [(where_to(i, dz, dx, dc), i) for i in range(128)])]
    ppermute x30 -> x20, waiting for transfers between devices: 6.24 us -> 24.8 us  [pull(): lax.ppermute(a, 'edge', [(where_to(i, dz, dx, dc), i) for i in range(128)])]
    ppermute x28 -> x13, waiting for transfers between devices: 18.7 us -> 36.4 us  [push(): lax.ppermute(a, 'edge', [(i, where_to(i, dz, dx, dc)) for i in range(128)])]
    add x8 -> x5, other arithmetic: 6.13 us -> 3.9 us  [the longest x3 2.25 us: position_of(): return (block * depth + far * rows + k % rows)[None]]
  transfers between devices with their start and end apart: 61 -> 36, of which waited for: 7 -> 14; matrix products, arithmetic and copies ran while one was open for 7% -> 6% of each run, Pallas kernels for 5% -> 6%
where the time goes in v2:
time: 257 us; the launch traced here: 255 us
  starting transfers between devices  134 us (52%)
  waiting for transfers between devices  63.9 us (25%)
  Pallas kernels  32.4 us (13%)
  other arithmetic  12.8 us (5%)
  local copies, waits for them, and re-layouts  9.54 us (4%)
    ppermute x20, starting transfers between devices, pull(): lax.ppermute(a, 'edge', [(where_to(i, dz, dx, dc), i) for i in range(128)])  78.5 us
    ppermute x13, starting transfers between devices, push(): lax.ppermute(a, 'edge', [(i, where_to(i, dz, dx, dc)) for i in range(128)])  44.8 us
    ppermute x13, waiting for transfers between devices, push(): lax.ppermute(a, 'edge', [(i, where_to(i, dz, dx, dc)) for i in range(128)])  36.4 us
    pallas_call x3, Pallas kernels, call(): pl.pallas_call(kernel, out_shape=tuple((jax.ShapeDtypeStruct(s, t) for s,...  32.4 us
    ppermute x20, waiting for transfers between devices, pull(): lax.ppermute(a, 'edge', [(where_to(i, dz, dx, dc), i) for i in range(128)])  24.8 us
    ppermute x3, starting transfers between devices, local(): lax.ppermute(shard, 'rep', [(i, (i + r) % n_rep) for i in range(n_rep)])  10.3 us
  transfers between devices with their start and end apart: 36, of which 14 were waited for; matrix products, arithmetic and copies ran while one was open for 6% of the time, Pallas kernels for 6%

profile of v2, /device:TPU:6, one launch (start us, length us, event | category | flops | bytes accessed | tf_op | source)
XLA Modules:
  0.0 254.9 jit_solution(15294989750079339592)
XLA Ops:
  1.3 0.8 fusion.118
  2.2 0.8 reshape.3175
  3.0 0.8 reshape_squeeze.3
  3.9 9.1 %collective-permute-start.2 = (bf16[250,128]{1,0:T(8,128)(2,1)S(1)}, bf16[250,128]{1,0:T(8,128)(2,1)S(1)}, u32[]{:S(2)}, u32[]{:S(2)}) collective-permute-start(bf16[250,128]{1,0:T(8,128)(2,1)S(1)} %pad_maximum_fusion.3), channel_id=1, source_target_pairs={{384,0},{132,4},{392,8},{140,12},{400,16},{148,20},{408,24},{156,2... | collective-permute-start | bytes 192008 | tf_op jit(solution)/shard_map/ppermute | solution.py:34
  13.0 10.9 %collective-permute-start.1 = (bf16[250,128]{1,0:T(8,128)(2,1)S(1)}, bf16[250,128]{1,0:T(8,128)(2,1)S(1)}, u32[]{:S(2)}, u32[]{:S(2)}) collective-permute-start(bf16[250,128]{1,0:T(8,128)(2,1)S(1)} %pad_maximum_fusion.3), channel_id=1, source_target_pairs={{256,0},{260,4},{264,8},{268,12},{272,16},{276,20},{280,24},{284,2... | collective-permute-start | bytes 192008 | tf_op jit(solution)/shard_map/ppermute | solution.py:34
  23.9 5.5 %collective-permute-start = (bf16[250,128]{1,0:T(8,128)(2,1)S(1)}, bf16[250,128]{1,0:T(8,128)(2,1)S(1)}, u32[]{:S(2)}, u32[]{:S(2)}) collective-permute-start(bf16[250,128]{1,0:T(8,128)(2,1)S(1)} %pad_maximum_fusion.3), channel_id=1, source_target_pairs={{128,0},{388,4},{136,8},{396,12},{144,16},{404,20},{152,24},{412,2... | collective-permute-start | bytes 192008 | tf_op jit(solution)/shard_map/ppermute | solution.py:34
  29.4 0.8 reduce-precision_convert_fusion
  30.3 1.5 maximum_maximum_fusion.refs_11_
  32.8 2.5 collective-permute-done
  36.3 2.3 collective-permute-start.5
  38.6 5.8 %collective-permute-start.4 = (bf16[1088,128]{1,0:T(8,128)(2,1)S(1)}, bf16[1088,128]{1,0:T(8,128)(2,1)S(1)}, u32[]{:S(2)}, u32[]{:S(2)}) collective-permute-start(bf16[1088,128]{1,0:T(8,128)(2,1)S(1)} %pad_maximum_fusion.1), channel_id=1, source_target_pairs={{64,0},{452,4},{72,8},{460,12},{80,16},{468,20},{88,24},{476,28},{... | collective-permute-start | bytes 835592 | tf_op jit(solution)/shard_map/ppermute | solution.py:34
  44.4 3.4 %collective-permute-start.3 = (bf16[1088,128]{1,0:T(8,128)(2,1)S(1)}, bf16[1088,128]{1,0:T(8,128)(2,1)S(1)}, u32[]{:S(2)}, u32[]{:S(2)}) collective-permute-start(bf16[1088,128]{1,0:T(8,128)(2,1)S(1)} %pad_maximum_fusion.1), channel_id=1, source_target_pairs={{32,0},{484,4},{40,8},{492,12},{48,16},{500,20},{56,24},{508,28},{... | collective-permute-start | bytes 835592 | tf_op jit(solution)/shard_map/ppermute | solution.py:34
  47.9 1.4 collective-permute-done.5
  49.3 2.1 collective-permute-done.4
  51.4 3.0 %collective-permute-done.3 = bf16[1088,128]{1,0:T(8,128)(2,1)S(1)} collective-permute-done((bf16[1088,128]{1,0:T(8,128)(2,1)S(1)}, bf16[1088,128]{1,0:T(8,128)(2,1)S(1)}, u32[]{:S(2)}, u32[]{:S(2)}) %collective-permute-start.3) | collective-permute-done | bytes 278560 | tf_op jit(solution)/shard_map/ppermute | solution.py:34
  54.5 2.2 collective-permute-start.16
  56.7 2.4 collective-permute-start.15
  59.1 4.3 %collective-permute-start.14 = (bf16[1600,128]{1,0:T(8,128)(2,1)S(1)}, bf16[1600,128]{1,0:T(8,128)(2,1)}, u32[]{:S(2)}, u32[]{:S(2)}) collective-permute-start(bf16[1600,128]{1,0:T(8,128)(2,1)S(1)} %pad_maximum_fusion.refs_0_), channel_id=1, source_target_pairs={{16,0},{20,4},{24,8},{28,12},{0,16},{4,20},{8,24},{12,28},{48,32},... | collective-permute-start | bytes 1228808 | tf_op jit(solution)/shard_map/ppermute | solution.py:34
  63.4 1.9 collective-permute-start.13
  65.5 5.1 %collective-permute-start.8 = (bf16[2752,128]{1,0:T(8,128)(2,1)S(1)}, bf16[2752,128]{1,0:T(8,128)(2,1)S(1)}, u32[]{:S(2)}, u32[]{:S(2)}) collective-permute-start(bf16[2752,128]{1,0:T(8,128)(2,1)S(1)} %slice_dynamic-update-slice_fusion.refs_0_), channel_id=1, source_target_pairs={{24,0},{28,4},{0,8},{4,12},{8,16},{12,20},{16,24},{20,28},{56,32},... | collective-permute-start | bytes 2113544 | tf_op jit(solution)/shard_map/ppermute | solution.py:34
  70.6 1.9 collective-permute-start.7
  72.6 9.2 %collective-permute-start.6 = (bf16[2752,128]{1,0:T(8,128)(2,1)S(1)}, bf16[2752,128]{1,0:T(8,128)(2,1)S(1)}, u32[]{:S(2)}, u32[]{:S(2)}) collective-permute-start(bf16[2752,128]{1,0:T(8,128)(2,1)S(1)} %slice_dynamic-update-slice_fusion.refs_0_), channel_id=1, source_target_pairs={{8,0},{12,4},{16,8},{20,12},{24,16},{28,20},{0,24},{4,28},{40,32},... | collective-permute-start | bytes 2113544 | tf_op jit(solution)/shard_map/ppermute | solution.py:34
  87.1 1.9 collective-permute-start.19
  89.0 2.4 collective-permute-start.18
  91.4 0.8 fusion.47.refs_18_
  92.2 0.9 compare_select_fusion.12.refs_12_
  93.1 1.7 collective-permute-done.8.refs_3_
  94.8 1.9 collective-permute-start.9
  96.8 2.1 collective-permute-done.7.refs_2_
  98.8 1.9 collective-permute-start.17
  100.7 12.0 %collective-permute-done.6.refs_1_ = bf16[2752,128]{1,0:T(8,128)(2,1)S(1)} collective-permute-done((bf16[2752,128]{1,0:T(8,128)(2,1)S(1)}, bf16[2752,128]{1,0:T(8,128)(2,1)S(1)}, u32[]{:S(2)}, u32[]{:S(2)}) %collective-permute-start.6) | collective-permute-done | bytes 704544 | tf_op jit(solution)/shard_map/ppermute | solution.py:34
  112.8 1.9 collective-permute-start.12
  114.7 2.4 collective-permute-start.11
  117.1 1.9 collective-permute-start.10
  119.7 1.0 fusion.6.refs_9_
  120.7 0.8 copy-done.20
  121.5 9.9 %rotate.1 = (bf16[160,1536]{1,0:T(8,128)(2,1)}, bf16[320,1024]{1,0:T(8,128)(2,1)}, bf16[320,1024]{1,0:T(8,128)(2,1)}, f32[160,2432]{1,0:T(8,128)}) custom-call(bf16[1600,128]{1,0:T(8,128)(2,1)} %copy-done.3, bf16[1600,128]{1,0:T(8,128)(2,1)} %collective-permute-done.13.refs_1_, bf16[1600,128]{1,0:T(8,128)(2,1)} %collective-permute-done.14.refs_2_, ...), custom_call_target="tpu_custom_call" | custom-call | flops 3000000000 | bytes 3546816 | tf_op jit(solution)/shard_map/rotate/pallas_call | solution.py:318
  131.5 0.8 copy-done.13
  133.0 17.3 %layer.1 = (bf16[2560,128]{1,0:T(8,128)(2,1)}, bf16[2560,128]{1,0:T(8,128)(2,1)}, bf16[2560,128]{1,0:T(8,128)(2,1)}, bf16[2560,128]{1,0:T(8,128)(2,1)}, bf16[256...) custom-call(bf16[2752,128]{1,0:T(8,128)(2,1)} %copy-done.5, ...), custom_call_target="tpu_custom_call" | custom-call | flops 5000000000 | bytes 9168192 | tf_op jit(solution)/shard_map/layer/pallas_call | solution.py:318
  150.4 2.5 collective-permute-start.21
  152.9 1.9 collective-permute-start.20
  154.8 2.4 collective-permute-start.23
  157.2 1.9 collective-permute-start.25
  159.2 1.3 add_convert_fusion.3
  160.5 3.6 %collective-permute-start.22 = (bf16[2560,128]{1,0:T(8,128)(2,1)S(1)}, bf16[2560,128]{1,0:T(8,128)(2,1)S(1)}, u32[]{:S(2)}, u32[]{:S(2)}) collective-permute-start(bf16[2560,128]{1,0:T(8,128)(2,1)S(1)} %add_convert_fusion.3), channel_id=1, source_target_pairs={{0,8},{4,12},{8,16},{12,20},{16,24},{20,28},{24,0},{28,4},{32,40},... | collective-permute-start | bytes 1966088 | tf_op jit(solution)/shard_map/ppermute | solution.py:38
  164.3 3.8 %collective-permute-start.24 = (bf16[2560,128]{1,0:T(8,128)(2,1)S(1)}, bf16[2560,128]{1,0:T(8,128)(2,1)S(1)}, u32[]{:S(2)}, u32[]{:S(2)}) collective-permute-start(bf16[2560,128]{1,0:T(8,128)(2,1)S(1)} %add_convert_fusion.2), channel_id=1, source_target_pairs={{0,16},{4,20},{8,24},{12,28},{16,0},{20,4},{24,8},{28,12},{32,48},... | collective-permute-start | bytes 1966088 | tf_op jit(solution)/shard_map/ppermute | solution.py:38
  168.3 2.7 %collective-permute-start.26 = (bf16[2560,128]{1,0:T(8,128)(2,1)S(1)}, bf16[2560,128]{1,0:T(8,128)(2,1)S(1)}, u32[]{:S(2)}, u32[]{:S(2)}) collective-permute-start(bf16[2560,128]{1,0:T(8,128)(2,1)S(1)} %add_convert_fusion.1), channel_id=1, source_target_pairs={{0,24},{4,28},{8,0},{12,4},{16,8},{20,12},{24,16},{28,20},{32,56},... | collective-permute-start | bytes 1966088 | tf_op jit(solution)/shard_map/ppermute | solution.py:38
  171.0 9.0 %collective-permute-done.22 = bf16[2560,128]{1,0:T(8,128)(2,1)S(1)} collective-permute-done((bf16[2560,128]{1,0:T(8,128)(2,1)S(1)}, bf16[2560,128]{1,0:T(8,128)(2,1)S(1)}, u32[]{:S(2)}, u32[]{:S(2)}) %collective-permute-start.22) | collective-permute-done | bytes 655392 | tf_op jit(solution)/shard_map/ppermute | solution.py:38
  180.0 5.5 %collective-permute-done.24 = bf16[2560,128]{1,0:T(8,128)(2,1)S(1)} collective-permute-done((bf16[2560,128]{1,0:T(8,128)(2,1)S(1)}, bf16[2560,128]{1,0:T(8,128)(2,1)S(1)}, u32[]{:S(2)}, u32[]{:S(2)}) %collective-permute-start.24) | collective-permute-done | bytes 655392 | tf_op jit(solution)/shard_map/ppermute | solution.py:38
  185.5 12.7 %collective-permute-done.26 = bf16[2560,128]{1,0:T(8,128)(2,1)S(1)} collective-permute-done((bf16[2560,128]{1,0:T(8,128)(2,1)S(1)}, bf16[2560,128]{1,0:T(8,128)(2,1)S(1)}, u32[]{:S(2)}, u32[]{:S(2)}) %collective-permute-start.26) | collective-permute-done | bytes 655392 | tf_op jit(solution)/shard_map/ppermute | solution.py:38
  198.7 2.8 %collective-permute-start.27 = (bf16[640,128]{1,0:T(8,128)(2,1)S(1)}, bf16[640,128]{1,0:T(8,128)(2,1)S(1)}, u32[]{:S(2)}, u32[]{:S(2)}) collective-permute-start(bf16[640,128]{1,0:T(8,128)(2,1)S(1)} %get-tuple-element.35), channel_id=1, source_target_pairs={{0,32},{4,484},{8,40},{12,492},{16,48},{20,500},{24,56},{28,508},{... | collective-permute-start | bytes 491528 | tf_op jit(solution)/shard_map/ppermute | solution.py:38
  201.4 4.8 %collective-permute-start.29 = (bf16[640,128]{1,0:T(8,128)(2,1)S(1)}, bf16[640,128]{1,0:T(8,128)(2,1)S(1)}, u32[]{:S(2)}, u32[]{:S(2)}) collective-permute-start(bf16[640,128]{1,0:T(8,128)(2,1)S(1)} %get-tuple-element.36), channel_id=1, source_target_pairs={{0,480},{4,36},{8,488},{12,44},{16,496},{20,52},{24,504},{28,60},{... | collective-permute-start | bytes 491528 | tf_op jit(solution)/shard_map/ppermute | solution.py:38
  206.2 1.9 collective-permute-start.28
  208.2 0.9 collective-permute-done.29
  209.0 8.2 %collective-permute-done.28 = bf16[640,128]{1,0:T(8,128)(2,1)S(1)} collective-permute-done((bf16[640,128]{1,0:T(8,128)(2,1)S(1)}, bf16[640,128]{1,0:T(8,128)(2,1)S(1)}, u32[]{:S(2)}, u32[]{:S(2)}) %collective-permute-start.28) | collective-permute-done | bytes 163872 | tf_op jit(solution)/shard_map/ppermute | solution.py:38
  217.6 4.4 %collective-permute-start.30 = (bf16[150,128]{1,0:T(8,128)(2,1)S(1)}, bf16[150,128]{1,0:T(8,128)(2,1)S(1)}, u32[]{:S(2)}, u32[]{:S(2)}) collective-permute-start(bf16[150,128]{1,0:T(8,128)(2,1)S(1)} %pad_maximum_fusion.5), channel_id=1, source_target_pairs={{0,128},{4,388},{8,136},{12,396},{16,144},{20,404},{24,152},{28,41... | collective-permute-start | bytes 115208 | tf_op jit(solution)/shard_map/ppermute | solution.py:38
  222.1 7.3 %collective-permute-start.31 = (bf16[150,128]{1,0:T(8,128)(2,1)S(1)}, bf16[150,128]{1,0:T(8,128)(2,1)S(1)}, u32[]{:S(2)}, u32[]{:S(2)}) collective-permute-start(bf16[150,128]{1,0:T(8,128)(2,1)S(1)} %pad_maximum_fusion.6), channel_id=1, source_target_pairs={{0,256},{4,260},{8,264},{12,268},{16,272},{20,276},{24,280},{28,28... | collective-permute-start | bytes 115208 | tf_op jit(solution)/shard_map/ppermute | solution.py:38
  229.4 4.8 %collective-permute-start.32 = (bf16[150,128]{1,0:T(8,128)(2,1)S(1)}, bf16[150,128]{1,0:T(8,128)(2,1)S(1)}, u32[]{:S(2)}, u32[]{:S(2)}) collective-permute-start(bf16[150,128]{1,0:T(8,128)(2,1)S(1)} %pad_maximum_fusion.7), channel_id=1, source_target_pairs={{0,384},{4,132},{8,392},{12,140},{16,400},{20,148},{24,408},{28,15... | collective-permute-start | bytes 115208 | tf_op jit(solution)/shard_map/ppermute | solution.py:38
  234.2 5.3 %nodes.1 = (bf16[4,3200]{1,0:T(4,128)(2,1)}, f32[4,3200]{1,0:T(4,128)}) custom-call(bf16[160,475]{1,0:T(8,128)(2,1)} %bitcast.98, bf16[160,2432]{1,0:T(8,128)(2,1)} %get-tuple-element.23.scaled, bf16[160,2432]{1,0:T(8,128)(2,1)} %get-tuple-element.24.grad_dst, s32[1,160]{1,0:T(1,128)} %target.1), custom_call_target="tpu_custom_call" | custom-call | flops 600000000 | bytes 1709120 | tf_op jit(solution)/shard_map/nodes/pallas_call | solution.py:318
  239.6 4.9 %collective-permute-start.35 = (f32[10,640]{1,0:T(8,128)S(1)}, f32[10,640]{1,0:T(8,128)S(1)}, u32[]{:S(2)}, u32[]{:S(2)}) collective-permute-start(f32[10,640]{1,0:T(8,128)S(1)} %bitcast.87), channel_id=1, source_target_pairs={{0,3},{1,0},{2,1},{3,2},{4,7},{5,4},{6,5},{7,6},{8,11},{9,8},{10,9... | collective-permute-start | bytes 76808 | tf_op jit(solution)/shard_map/ppermute | solution.py:417
  244.6 2.5 collective-permute-start.34
  247.1 2.9 %collective-permute-start.33 = (f32[10,640]{1,0:T(8,128)S(1)}, f32[10,640]{1,0:T(8,128)S(1)}, u32[]{:S(2)}, u32[]{:S(2)}) collective-permute-start(f32[10,640]{1,0:T(8,128)S(1)} %bitcast.89), channel_id=1, source_target_pairs={{0,1},{1,2},{2,3},{3,0},{4,5},{5,6},{6,7},{7,4},{8,9},{9,10},{10,1... | collective-permute-start | bytes 76808 | tf_op jit(solution)/shard_map/ppermute | solution.py:417
  250.0 1.4 fusion.26
  252.0 2.3 collective-permute-done.33
  (156 shorter events, 11.4 us)
Async XLA Ops:
  3.9 28.7 %collective-permute-start.2 = (bf16[250,128]{1,0:T(8,128)(2,1)S(1)}, bf16[250,128]{1,0:T(8,128)(2,1)S(1)}, u32[]{:S(2)}, u32[]{:S(2)}) collective-permute-start(bf16[250,128]{1,0:T(8,128)(2,1)S(1)} %pad_maximum_fusion.3), channel_id=1, source_target_pairs={{384,0},{132,4},{392,8},{140,12},{400,16},{148,20},{408,24},{156,2... | collective-permute-start | bytes 192008 | tf_op jit(solution)/shard_map/ppermute | solution.py:34
  13.0 19.7 %collective-permute-start.1 = (bf16[250,128]{1,0:T(8,128)(2,1)S(1)}, bf16[250,128]{1,0:T(8,128)(2,1)S(1)}, u32[]{:S(2)}, u32[]{:S(2)}) collective-permute-start(bf16[250,128]{1,0:T(8,128)(2,1)S(1)} %pad_maximum_fusion.3), channel_id=1, source_target_pairs={{256,0},{260,4},{264,8},{268,12},{272,16},{276,20},{280,24},{284,2... | collective-permute-start | bytes 192008 | tf_op jit(solution)/shard_map/ppermute | solution.py:34
  23.9 11.3 %collective-permute-start = (bf16[250,128]{1,0:T(8,128)(2,1)S(1)}, bf16[250,128]{1,0:T(8,128)(2,1)S(1)}, u32[]{:S(2)}, u32[]{:S(2)}) collective-permute-start(bf16[250,128]{1,0:T(8,128)(2,1)S(1)} %pad_maximum_fusion.3), channel_id=1, source_target_pairs={{128,0},{388,4},{136,8},{396,12},{144,16},{404,20},{152,24},{412,2... | collective-permute-start | bytes 192008 | tf_op jit(solution)/shard_map/ppermute | solution.py:34
  36.3 13.0 %collective-permute-start.5 = (bf16[1088,128]{1,0:T(8,128)(2,1)S(1)}, bf16[1088,128]{1,0:T(8,128)(2,1)S(1)}, u32[]{:S(2)}, u32[]{:S(2)}) collective-permute-start(bf16[1088,128]{1,0:T(8,128)(2,1)S(1)} %pad_maximum_fusion.1), channel_id=1, source_target_pairs={{480,0},{36,4},{488,8},{44,12},{496,16},{52,20},{504,24},{60,28},{... | collective-permute-start | bytes 835592 | tf_op jit(solution)/shard_map/ppermute | solution.py:34
  38.6 12.8 %collective-permute-start.4 = (bf16[1088,128]{1,0:T(8,128)(2,1)S(1)}, bf16[1088,128]{1,0:T(8,128)(2,1)S(1)}, u32[]{:S(2)}, u32[]{:S(2)}) collective-permute-start(bf16[1088,128]{1,0:T(8,128)(2,1)S(1)} %pad_maximum_fusion.1), channel_id=1, source_target_pairs={{64,0},{452,4},{72,8},{460,12},{80,16},{468,20},{88,24},{476,28},{... | collective-permute-start | bytes 835592 | tf_op jit(solution)/shard_map/ppermute | solution.py:34
  44.4 10.0 %collective-permute-start.3 = (bf16[1088,128]{1,0:T(8,128)(2,1)S(1)}, bf16[1088,128]{1,0:T(8,128)(2,1)S(1)}, u32[]{:S(2)}, u32[]{:S(2)}) collective-permute-start(bf16[1088,128]{1,0:T(8,128)(2,1)S(1)} %pad_maximum_fusion.1), channel_id=1, source_target_pairs={{32,0},{484,4},{40,8},{492,12},{48,16},{500,20},{56,24},{508,28},{... | collective-permute-start | bytes 835592 | tf_op jit(solution)/shard_map/ppermute | solution.py:34
  47.9 35.4 %copy-start.8 = (bf16[128,8]{0,1:T(8,128)(2,1)S(1)}, bf16[128,8]{0,1:T(8,128)(2,1)}, u32[]{:S(2)}) copy-start(bf16[128,8]{0,1:T(8,128)(2,1)} %param.22) | copy-start | bytes 6148
  47.9 36.1 %copy-start.9 = (s32[1,160]{1,0:T(1,128)S(1)}, s32[1,160]{1,0:T(1,128)}, u32[]{:S(2)}) copy-start(s32[1,160]{1,0:T(1,128)} %target.1) | copy-start | bytes 1924
  47.9 36.8 %copy-start.4 = (f32[1,160,8]{1,2,0:T(8,128)S(1)}, f32[1,160,8]{1,2,0:T(8,128)}, u32[]{:S(2)}) copy-start(f32[1,160,8]{1,2,0:T(8,128)} %param.18) | copy-start | bytes 15364
  47.9 37.5 %copy-start.6 = (s32[1,160]{1,0:T(1,128)S(1)}, s32[1,160]{1,0:T(1,128)}, u32[]{:S(2)}) copy-start(s32[1,160]{1,0:T(1,128)} %param.15) | copy-start | bytes 1924
  49.3 36.3 %copy-start.7 = (s32[1,160,1]{1,2,0:T(1,128)S(1)}, s32[1,160,1]{1,2,0:T(1,128)}, u32[]{:S(2)}) copy-start(s32[1,160,1]{1,2,0:T(1,128)} %param.14) | copy-start | bytes 1924
  54.5 66.3 %copy-start.3 = (bf16[1600,128]{1,0:T(8,128)(2,1)}, bf16[1600,128]{1,0:T(8,128)(2,1)S(1)}, u32[]{:S(2)}) copy-start(bf16[1600,128]{1,0:T(8,128)(2,1)S(1)} %pad_maximum_fusion.refs_0_) | copy-start | bytes 1228804
  54.5 16.2 %collective-permute-start.16 = (bf16[1600,128]{1,0:T(8,128)(2,1)S(1)}, bf16[1600,128]{1,0:T(8,128)(2,1)S(1)}, u32[]{:S(2)}, u32[]{:S(2)}) collective-permute-start(bf16[1600,128]{1,0:T(8,128)(2,1)S(1)} %pad_maximum_fusion.refs_0_), channel_id=1, source_target_pairs={{4,0},{0,4},{12,8},{8,12},{20,16},{16,20},{28,24},{24,28},{36,32},... | collective-permute-start | bytes 1228808 | tf_op jit(solution)/shard_map/ppermute | solution.py:34
  56.7 15.9 %collective-permute-start.15 = (bf16[1600,128]{1,0:T(8,128)(2,1)S(1)}, bf16[1600,128]{1,0:T(8,128)(2,1)}, u32[]{:S(2)}, u32[]{:S(2)}) collective-permute-start(bf16[1600,128]{1,0:T(8,128)(2,1)S(1)} %pad_maximum_fusion.refs_0_), channel_id=1, source_target_pairs={{24,0},{28,4},{0,8},{4,12},{8,16},{12,20},{16,24},{20,28},{56,32},... | collective-permute-start | bytes 1228808 | tf_op jit(solution)/shard_map/ppermute | solution.py:34
  59.1 28.0 %collective-permute-start.14 = (bf16[1600,128]{1,0:T(8,128)(2,1)S(1)}, bf16[1600,128]{1,0:T(8,128)(2,1)}, u32[]{:S(2)}, u32[]{:S(2)}) collective-permute-start(bf16[1600,128]{1,0:T(8,128)(2,1)S(1)} %pad_maximum_fusion.refs_0_), channel_id=1, source_target_pairs={{16,0},{20,4},{24,8},{28,12},{0,16},{4,20},{8,24},{12,28},{48,32},... | collective-permute-start | bytes 1228808 | tf_op jit(solution)/shard_map/ppermute | solution.py:34
  63.4 25.6 %collective-permute-start.13 = (bf16[1600,128]{1,0:T(8,128)(2,1)S(1)}, bf16[1600,128]{1,0:T(8,128)(2,1)}, u32[]{:S(2)}, u32[]{:S(2)}) collective-permute-start(bf16[1600,128]{1,0:T(8,128)(2,1)S(1)} %pad_maximum_fusion.refs_0_), channel_id=1, source_target_pairs={{8,0},{12,4},{16,8},{20,12},{24,16},{28,20},{0,24},{4,28},{40,32},... | collective-permute-start | bytes 1228808 | tf_op jit(solution)/shard_map/ppermute | solution.py:34
  65.5 65.9 %copy-start.5 = (bf16[2752,128]{1,0:T(8,128)(2,1)}, bf16[2752,128]{1,0:T(8,128)(2,1)S(1)}, u32[]{:S(2)}) copy-start(bf16[2752,128]{1,0:T(8,128)(2,1)S(1)} %slice_dynamic-update-slice_fusion.refs_0_) | copy-start | bytes 2113540
  65.5 29.4 %collective-permute-start.8 = (bf16[2752,128]{1,0:T(8,128)(2,1)S(1)}, bf16[2752,128]{1,0:T(8,128)(2,1)S(1)}, u32[]{:S(2)}, u32[]{:S(2)}) collective-permute-start(bf16[2752,128]{1,0:T(8,128)(2,1)S(1)} %slice_dynamic-update-slice_fusion.refs_0_), channel_id=1, source_target_pairs={{24,0},{28,4},{0,8},{4,12},{8,16},{12,20},{16,24},{20,28},{56,32},... | collective-permute-start | bytes 2113544 | tf_op jit(solution)/shard_map/ppermute | solution.py:34
  70.6 2.0 copy-start.17
  70.6 28.2 %collective-permute-start.7 = (bf16[2752,128]{1,0:T(8,128)(2,1)S(1)}, bf16[2752,128]{1,0:T(8,128)(2,1)S(1)}, u32[]{:S(2)}, u32[]{:S(2)}) collective-permute-start(bf16[2752,128]{1,0:T(8,128)(2,1)S(1)} %slice_dynamic-update-slice_fusion.refs_0_), channel_id=1, source_target_pairs={{16,0},{20,4},{24,8},{28,12},{0,16},{4,20},{8,24},{12,28},{48,32},... | collective-permute-start | bytes 2113544 | tf_op jit(solution)/shard_map/ppermute | solution.py:34
  72.6 40.1 %collective-permute-start.6 = (bf16[2752,128]{1,0:T(8,128)(2,1)S(1)}, bf16[2752,128]{1,0:T(8,128)(2,1)S(1)}, u32[]{:S(2)}, u32[]{:S(2)}) collective-permute-start(bf16[2752,128]{1,0:T(8,128)(2,1)S(1)} %slice_dynamic-update-slice_fusion.refs_0_), channel_id=1, source_target_pairs={{8,0},{12,4},{16,8},{20,12},{24,16},{28,20},{0,24},{4,28},{40,32},... | collective-permute-start | bytes 2113544 | tf_op jit(solution)/shard_map/ppermute | solution.py:34
  87.1 27.6 %collective-permute-start.19 = (bf16[1600,128]{1,0:T(8,128)(2,1)}, bf16[1600,128]{1,0:T(8,128)(2,1)S(1)}, u32[]{:S(2)}, u32[]{:S(2)}) collective-permute-start(bf16[1600,128]{1,0:T(8,128)(2,1)} %collective-permute-done.15.refs_3_), channel_id=1, source_target_pairs={{4,0},{0,4},{12,8},{8,12},{20,16},{16,20},{28,24},{24,28},{36,32},... | collective-permute-start | bytes 1228808 | tf_op jit(solution)/shard_map/ppermute | solution.py:34
  89.0 28.1 %collective-permute-start.18 = (bf16[1600,128]{1,0:T(8,128)(2,1)}, bf16[1600,128]{1,0:T(8,128)(2,1)S(1)}, u32[]{:S(2)}, u32[]{:S(2)}) collective-permute-start(bf16[1600,128]{1,0:T(8,128)(2,1)} %collective-permute-done.14.refs_2_), channel_id=1, source_target_pairs={{4,0},{0,4},{12,8},{8,12},{20,16},{16,20},{28,24},{24,28},{36,32},... | collective-permute-start | bytes 1228808 | tf_op jit(solution)/shard_map/ppermute | solution.py:34
  94.8 36.6 %copy-start.10 = (bf16[2752,128]{1,0:T(8,128)(2,1)}, bf16[2752,128]{1,0:T(8,128)(2,1)S(1)}, u32[]{:S(2)}) copy-start(bf16[2752,128]{1,0:T(8,128)(2,1)S(1)} %collective-permute-done.8.refs_3_) | copy-start | bytes 2113540
  94.8 36.6 %collective-permute-start.9 = (bf16[2752,128]{1,0:T(8,128)(2,1)S(1)}, bf16[2752,128]{1,0:T(8,128)(2,1)S(1)}, u32[]{:S(2)}, u32[]{:S(2)}) collective-permute-start(bf16[2752,128]{1,0:T(8,128)(2,1)S(1)} %slice_dynamic-update-slice_fusion.refs_0_), channel_id=1, source_target_pairs={{4,0},{0,4},{12,8},{8,12},{20,16},{16,20},{28,24},{24,28},{36,32},... | collective-permute-start | bytes 2113544 | tf_op jit(solution)/shard_map/ppermute | solution.py:34
  98.8 32.6 %copy-start.11 = (bf16[2752,128]{1,0:T(8,128)(2,1)}, bf16[2752,128]{1,0:T(8,128)(2,1)S(1)}, u32[]{:S(2)}) copy-start(bf16[2752,128]{1,0:T(8,128)(2,1)S(1)} %collective-permute-done.7.refs_2_) | copy-start | bytes 2113540
  98.8 21.9 %collective-permute-start.17 = (bf16[1600,128]{1,0:T(8,128)(2,1)}, bf16[1600,128]{1,0:T(8,128)(2,1)S(1)}, u32[]{:S(2)}, u32[]{:S(2)}) collective-permute-start(bf16[1600,128]{1,0:T(8,128)(2,1)} %collective-permute-done.13.refs_1_), channel_id=1, source_target_pairs={{4,0},{0,4},{12,8},{8,12},{20,16},{16,20},{28,24},{24,28},{36,32},... | collective-permute-start | bytes 1228808 | tf_op jit(solution)/shard_map/ppermute | solution.py:34
  112.8 18.7 %copy-start.12 = (bf16[2752,128]{1,0:T(8,128)(2,1)}, bf16[2752,128]{1,0:T(8,128)(2,1)S(1)}, u32[]{:S(2)}) copy-start(bf16[2752,128]{1,0:T(8,128)(2,1)S(1)} %collective-permute-done.6.refs_1_) | copy-start | bytes 2113540
  112.8 18.7 %collective-permute-start.12 = (bf16[2752,128]{1,0:T(8,128)(2,1)S(1)}, bf16[2752,128]{1,0:T(8,128)(2,1)S(1)}, u32[]{:S(2)}, u32[]{:S(2)}) collective-permute-start(bf16[2752,128]{1,0:T(8,128)(2,1)S(1)} %collective-permute-done.8.refs_3_), channel_id=1, source_target_pairs={{4,0},{0,4},{12,8},{8,12},{20,16},{16,20},{28,24},{24,28},{36,32},... | collective-permute-start | bytes 2113544 | tf_op jit(solution)/shard_map/ppermute | solution.py:34
  114.7 6.0 %copy-start.18 = (bf16[1600,128]{1,0:T(8,128)(2,1)}, bf16[1600,128]{1,0:T(8,128)(2,1)S(1)}, u32[]{:S(2)}) copy-start(bf16[1600,128]{1,0:T(8,128)(2,1)S(1)} %collective-permute-done.19.refs_7_) | copy-start | bytes 1228804
  114.7 16.8 %collective-permute-start.11 = (bf16[2752,128]{1,0:T(8,128)(2,1)S(1)}, bf16[2752,128]{1,0:T(8,128)(2,1)S(1)}, u32[]{:S(2)}, u32[]{:S(2)}) collective-permute-start(bf16[2752,128]{1,0:T(8,128)(2,1)S(1)} %collective-permute-done.7.refs_2_), channel_id=1, source_target_pairs={{4,0},{0,4},{12,8},{8,12},{20,16},{16,20},{28,24},{24,28},{36,32},... | collective-permute-start | bytes 2113544 | tf_op jit(solution)/shard_map/ppermute | solution.py:34
  117.1 3.6 %copy-start.19 = (bf16[1600,128]{1,0:T(8,128)(2,1)}, bf16[1600,128]{1,0:T(8,128)(2,1)S(1)}, u32[]{:S(2)}) copy-start(bf16[1600,128]{1,0:T(8,128)(2,1)S(1)} %collective-permute-done.18.refs_6_) | copy-start | bytes 1228804
  117.1 14.4 %collective-permute-start.10 = (bf16[2752,128]{1,0:T(8,128)(2,1)S(1)}, bf16[2752,128]{1,0:T(8,128)(2,1)S(1)}, u32[]{:S(2)}, u32[]{:S(2)}) collective-permute-start(bf16[2752,128]{1,0:T(8,128)(2,1)S(1)} %collective-permute-done.6.refs_1_), channel_id=1, source_target_pairs={{4,0},{0,4},{12,8},{8,12},{20,16},{16,20},{28,24},{24,28},{36,32},... | collective-permute-start | bytes 2113544 | tf_op jit(solution)/shard_map/ppermute | solution.py:34
  120.7 0.8 copy-start.20
  131.4 0.8 copy-start.13
  131.4 1.1 copy-start.14
  131.5 1.3 copy-start.15
  131.5 1.6 copy-start.16
  150.3 13.7 %copy-start.1 = (bf16[2560,128]{1,0:T(8,128)(2,1)S(1)}, bf16[2560,128]{1,0:T(8,128)(2,1)}, u32[]{:S(2)}) copy-start(bf16[2560,128]{1,0:T(8,128)(2,1)} %get-tuple-element.31) | copy-start | bytes 1966084
  150.4 8.8 %collective-permute-start.21 = (bf16[2560,128]{1,0:T(8,128)(2,1)}, bf16[2560,128]{1,0:T(8,128)(2,1)S(1)}, u32[]{:S(2)}, u32[]{:S(2)}) collective-permute-start(bf16[2560,128]{1,0:T(8,128)(2,1)} %get-tuple-element.30), channel_id=1, source_target_pairs={{0,4},{4,0},{8,12},{12,8},{16,20},{20,16},{24,28},{28,24},{32,36},... | collective-permute-start | bytes 1966088 | tf_op jit(solution)/shard_map/ppermute | solution.py:38
  152.9 18.1 %collective-permute-start.20 = (bf16[2560,128]{1,0:T(8,128)(2,1)}, bf16[2560,128]{1,0:T(8,128)(2,1)S(1)}, u32[]{:S(2)}, u32[]{:S(2)}) collective-permute-start(bf16[2560,128]{1,0:T(8,128)(2,1)} %get-tuple-element.28), channel_id=1, source_target_pairs={{0,4},{4,0},{8,12},{12,8},{16,20},{20,16},{24,28},{28,24},{32,36},... | collective-permute-start | bytes 1966088 | tf_op jit(solution)/shard_map/ppermute | solution.py:38
  154.8 9.2 %collective-permute-start.23 = (bf16[2560,128]{1,0:T(8,128)(2,1)}, bf16[2560,128]{1,0:T(8,128)(2,1)S(1)}, u32[]{:S(2)}, u32[]{:S(2)}) collective-permute-start(bf16[2560,128]{1,0:T(8,128)(2,1)} %get-tuple-element.32), channel_id=1, source_target_pairs={{0,4},{4,0},{8,12},{12,8},{16,20},{20,16},{24,28},{28,24},{32,36},... | collective-permute-start | bytes 1966088 | tf_op jit(solution)/shard_map/ppermute | solution.py:38
  157.2 10.8 %collective-permute-start.25 = (bf16[2560,128]{1,0:T(8,128)(2,1)}, bf16[2560,128]{1,0:T(8,128)(2,1)S(1)}, u32[]{:S(2)}, u32[]{:S(2)}) collective-permute-start(bf16[2560,128]{1,0:T(8,128)(2,1)} %get-tuple-element.34), channel_id=1, source_target_pairs={{0,4},{4,0},{8,12},{12,8},{16,20},{20,16},{24,28},{28,24},{32,36},... | collective-permute-start | bytes 1966088 | tf_op jit(solution)/shard_map/ppermute | solution.py:38
  160.4 7.6 %copy-start = (bf16[2560,128]{1,0:T(8,128)(2,1)S(1)}, bf16[2560,128]{1,0:T(8,128)(2,1)}, u32[]{:S(2)}) copy-start(bf16[2560,128]{1,0:T(8,128)(2,1)} %get-tuple-element.33) | copy-start | bytes 1966084
  160.5 19.6 %collective-permute-start.22 = (bf16[2560,128]{1,0:T(8,128)(2,1)S(1)}, bf16[2560,128]{1,0:T(8,128)(2,1)S(1)}, u32[]{:S(2)}, u32[]{:S(2)}) collective-permute-start(bf16[2560,128]{1,0:T(8,128)(2,1)S(1)} %add_convert_fusion.3), channel_id=1, source_target_pairs={{0,8},{4,12},{8,16},{12,20},{16,24},{20,28},{24,0},{28,4},{32,40},... | collective-permute-start | bytes 1966088 | tf_op jit(solution)/shard_map/ppermute | solution.py:38
  164.2 34.0 %copy-start.2 = (bf16[2560,128]{1,0:T(8,128)(2,1)S(1)}, bf16[2560,128]{1,0:T(8,128)(2,1)}, u32[]{:S(2)}) copy-start(bf16[2560,128]{1,0:T(8,128)(2,1)} %get-tuple-element.27) | copy-start | bytes 1966084
  164.3 21.2 %collective-permute-start.24 = (bf16[2560,128]{1,0:T(8,128)(2,1)S(1)}, bf16[2560,128]{1,0:T(8,128)(2,1)S(1)}, u32[]{:S(2)}, u32[]{:S(2)}) collective-permute-start(bf16[2560,128]{1,0:T(8,128)(2,1)S(1)} %add_convert_fusion.2), channel_id=1, source_target_pairs={{0,16},{4,20},{8,24},{12,28},{16,0},{20,4},{24,8},{28,12},{32,48},... | collective-permute-start | bytes 1966088 | tf_op jit(solution)/shard_map/ppermute | solution.py:38
  168.3 29.9 %collective-permute-start.26 = (bf16[2560,128]{1,0:T(8,128)(2,1)S(1)}, bf16[2560,128]{1,0:T(8,128)(2,1)S(1)}, u32[]{:S(2)}, u32[]{:S(2)}) collective-permute-start(bf16[2560,128]{1,0:T(8,128)(2,1)S(1)} %add_convert_fusion.1), channel_id=1, source_target_pairs={{0,24},{4,28},{8,0},{12,4},{16,8},{20,12},{24,16},{28,20},{32,56},... | collective-permute-start | bytes 1966088 | tf_op jit(solution)/shard_map/ppermute | solution.py:38
  198.7 9.5 %collective-permute-start.27 = (bf16[640,128]{1,0:T(8,128)(2,1)S(1)}, bf16[640,128]{1,0:T(8,128)(2,1)S(1)}, u32[]{:S(2)}, u32[]{:S(2)}) collective-permute-start(bf16[640,128]{1,0:T(8,128)(2,1)S(1)} %get-tuple-element.35), channel_id=1, source_target_pairs={{0,32},{4,484},{8,40},{12,492},{16,48},{20,500},{24,56},{28,508},{... | collective-permute-start | bytes 491528 | tf_op jit(solution)/shard_map/ppermute | solution.py:38
  201.4 7.6 %collective-permute-start.29 = (bf16[640,128]{1,0:T(8,128)(2,1)S(1)}, bf16[640,128]{1,0:T(8,128)(2,1)S(1)}, u32[]{:S(2)}, u32[]{:S(2)}) collective-permute-start(bf16[640,128]{1,0:T(8,128)(2,1)S(1)} %get-tuple-element.36), channel_id=1, source_target_pairs={{0,480},{4,36},{8,488},{12,44},{16,496},{20,52},{24,504},{28,60},{... | collective-permute-start | bytes 491528 | tf_op jit(solution)/shard_map/ppermute | solution.py:38
  206.2 11.0 %collective-permute-start.28 = (bf16[640,128]{1,0:T(8,128)(2,1)S(1)}, bf16[640,128]{1,0:T(8,128)(2,1)S(1)}, u32[]{:S(2)}, u32[]{:S(2)}) collective-permute-start(bf16[640,128]{1,0:T(8,128)(2,1)S(1)} %get-tuple-element.37), channel_id=1, source_target_pairs={{0,64},{4,452},{8,72},{12,460},{16,80},{20,468},{24,88},{28,476},{... | collective-permute-start | bytes 491528 | tf_op jit(solution)/shard_map/ppermute | solution.py:38
  217.6 21.9 %collective-permute-start.30 = (bf16[150,128]{1,0:T(8,128)(2,1)S(1)}, bf16[150,128]{1,0:T(8,128)(2,1)S(1)}, u32[]{:S(2)}, u32[]{:S(2)}) collective-permute-start(bf16[150,128]{1,0:T(8,128)(2,1)S(1)} %pad_maximum_fusion.5), channel_id=1, source_target_pairs={{0,128},{4,388},{8,136},{12,396},{16,144},{20,404},{24,152},{28,41... | collective-permute-start | bytes 115208 | tf_op jit(solution)/shard_map/ppermute | solution.py:38
  222.1 17.4 %collective-permute-start.31 = (bf16[150,128]{1,0:T(8,128)(2,1)S(1)}, bf16[150,128]{1,0:T(8,128)(2,1)S(1)}, u32[]{:S(2)}, u32[]{:S(2)}) collective-permute-start(bf16[150,128]{1,0:T(8,128)(2,1)S(1)} %pad_maximum_fusion.6), channel_id=1, source_target_pairs={{0,256},{4,260},{8,264},{12,268},{16,272},{20,276},{24,280},{28,28... | collective-permute-start | bytes 115208 | tf_op jit(solution)/shard_map/ppermute | solution.py:38
  229.4 10.1 %collective-permute-start.32 = (bf16[150,128]{1,0:T(8,128)(2,1)S(1)}, bf16[150,128]{1,0:T(8,128)(2,1)S(1)}, u32[]{:S(2)}, u32[]{:S(2)}) collective-permute-start(bf16[150,128]{1,0:T(8,128)(2,1)S(1)} %pad_maximum_fusion.7), channel_id=1, source_target_pairs={{0,384},{4,132},{8,392},{12,140},{16,400},{20,148},{24,408},{28,15... | collective-permute-start | bytes 115208 | tf_op jit(solution)/shard_map/ppermute | solution.py:38
  239.6 11.8 %collective-permute-start.35 = (f32[10,640]{1,0:T(8,128)S(1)}, f32[10,640]{1,0:T(8,128)S(1)}, u32[]{:S(2)}, u32[]{:S(2)}) collective-permute-start(f32[10,640]{1,0:T(8,128)S(1)} %bitcast.87), channel_id=1, source_target_pairs={{0,3},{1,0},{2,1},{3,2},{4,7},{5,4},{6,5},{7,6},{8,11},{9,8},{10,9... | collective-permute-start | bytes 76808 | tf_op jit(solution)/shard_map/ppermute | solution.py:417
  244.6 7.4 %collective-permute-start.34 = (f32[10,640]{1,0:T(8,128)S(1)}, f32[10,640]{1,0:T(8,128)S(1)}, u32[]{:S(2)}, u32[]{:S(2)}) collective-permute-start(f32[10,640]{1,0:T(8,128)S(1)} %bitcast.88), channel_id=1, source_target_pairs={{0,2},{1,3},{2,0},{3,1},{4,6},{5,7},{6,4},{7,5},{8,10},{9,11},{10,... | collective-permute-start | bytes 76808 | tf_op jit(solution)/shard_map/ppermute | solution.py:417
  247.1 7.1 %collective-permute-start.33 = (f32[10,640]{1,0:T(8,128)S(1)}, f32[10,640]{1,0:T(8,128)S(1)}, u32[]{:S(2)}, u32[]{:S(2)}) collective-permute-start(f32[10,640]{1,0:T(8,128)S(1)} %bitcast.89), channel_id=1, source_target_pairs={{0,1},{1,2},{2,3},{3,0},{4,5},{5,6},{6,7},{7,4},{8,9},{9,10},{10,1... | collective-permute-start | bytes 76808 | tf_op jit(solution)/shard_map/ppermute | solution.py:417

commit v3 on v2

--- a/solution.py
+++ b/solution.py
@@ -56,12 +56,11 @@
     return z * 8 + x * 2 + (me % 2 + cr) % 2
 
 
-def x_and_core(block):
-    mine = (block,) + tuple(pull(block, dx=x) for x in (1, 2, 3))
-    return mine + tuple(pull(a, dc=1) for a in mine)
-
-
-def scatter_sum(pieces):
+def x_pieces(block):
+    return (block,) + tuple(pull(block, dx=x) for x in (1, 2, 3))
+
+
+def scatter_sum(pieces, beside):
     def add(a, *more):
         total = a.astype(F32)
         for m in more:
@@ -69,7 +68,8 @@
         return total
 
     a = [add(pieces[x], push(pieces[4 + x], dc=1)).astype(BF16) for x in range(4)]
-    total = add(a[0], *(push(a[x], dx=x) for x in (1, 2, 3))).astype(BF16)
+    arrived, beside = lax.optimization_barrier(([push(a[x], dx=x) for x in (1, 2, 3)], beside))
+    total = add(a[0], *arrived).astype(BF16)
     parts = [total[n * TERM_ROWS : (n + 1) * TERM_ROWS] for n in range(4)]
     total = add(parts[0], *(push(parts[n], dz=NEAR[n]) for n in (1, 2, 3))).astype(BF16)
     terms, shard = total[:400].reshape(25, 16, CH), total[400:].reshape(5, 48, CH)
@@ -80,7 +80,7 @@
         )
 
     total = add(part(0), *(push(part(n), dz=4 * n) for n in (1, 2, 3)))
-    return total[:100].reshape(25, 4, CH), total[100:].reshape(5, 10, CH)
+    return total[:100].reshape(25, 4, CH), total[100:].reshape(5, 10, CH), beside
 
 
 def hot(index, shape, axis):
@@ -274,14 +274,15 @@
         return carry
 
     lax.fori_loop(0, EDGES // BLOCK, turn, 0)
-    for k in range(8):
-        chosen = hot(place[...] - k * 64, (64, EDGES), 0)
-        for first in range(0, FULL, 640):
-            block = mm(chosen, src_terms[:, first : first + 640]).astype(BF16)
+    chosen = hot(place[...], (512, EDGES), 0)
+    for first in range(0, FULL, 640):
+        block = mm(chosen, src_terms[:, first : first + 640]).astype(BF16)
+        for k in range(8):
             for near in range(4):
+                row = k * 64 + near * 16
                 for n in range(5):
                     at = near * TERM_ROWS + (first // CH + n) * 16
-                    terms_out[k][at : at + 16, :] = block[near * 16 : near * 16 + 16, n * CH : (n + 1) * CH]
+                    terms_out[k][at : at + 16, :] = block[row : row + 16, n * CH : (n + 1) * CH]
 
 
 def nodes_kernel(rot, scaled, grad_dst, target, node_out, grad_local, back, terms):
@@ -359,8 +360,9 @@
         at += units * rows
     far_block = jnp.concatenate(merged, axis=0)
     blocks = [far_block] + [pull(far_block, dz=NEAR[n]) for n in (1, 2, 3)]
-    feature_pieces = x_and_core(jnp.concatenate([b[:FAR_ROWS] for b in blocks], axis=0))
-    weight_pieces = x_and_core(jnp.concatenate([b[FAR_ROWS:] for b in blocks], axis=0))
+    feature_x = x_pieces(jnp.concatenate([b[:FAR_ROWS] for b in blocks], axis=0))
+    weight_x = x_pieces(jnp.concatenate([b[FAR_ROWS:] for b in blocks], axis=0))
+    feature_pieces = feature_x + tuple(pull(a, dc=1) for a in feature_x)
 
     def inverse_of(rows, depth):
         p = jnp.arange(32 * depth, dtype=jnp.int32)
@@ -391,6 +393,10 @@
          ((160, 1280), BF16), ((320, 1024), BF16), ((320, 768), BF16)],
         3_000_000_000,
     )
+    turned, others = lax.optimization_barrier(((m0, m1, m2, turned_grad), weight_x[1:]))
+    m0, m1, m2, turned_grad = turned
+    weight_x = weight_x[:1] + tuple(others)
+    weight_pieces = weight_x + tuple(pull(a, dc=1) for a in weight_x)
     outs = call(
         layer_kernel, "layer",
         (*weight_pieces, m0, m1, m2, turned_grad, rotor_rows, edge_bias[0], targets[:, None], live[:, None],
@@ -408,13 +414,12 @@
         [((4, FULL), BF16), ((4, FULL), F32)], [((160, FULL), BF16), ((160, FULL), BF16)],
         600_000_000,
     )
-    terms, shard = scatter_sum(term_pieces)
+    terms, shard, (node_out, grad_local) = scatter_sum(term_pieces, (node_out, grad_local))
     grad_remote = terms.transpose(1, 0, 2).reshape(4, FULL)
     shard = shard.transpose(1, 0, 2).reshape(10, 640)
     n_rep = lax.axis_size("rep")
-    grad_w0 = shard
-    for r in range(1, n_rep):
-        grad_w0 = grad_w0 + lax.ppermute(shard, "rep", [(i, (i + r) % n_rep) for i in range(n_rep)])
+    copies = lax.all_to_all(jnp.broadcast_to(shard, (n_rep, 10, 640)), "rep", split_axis=0, concat_axis=0, tiled=True)
+    grad_w0 = jnp.sum(copies, axis=0)
     return node_out[None], (grad_local + grad_remote)[None], grad_w0
 
 

time: 257 us -> 244 us (0.949)
  starting transfers between devices: 134 us -> 121 us
    ppermute x3 -> x0, starting transfers between devices: 10.3 us -> none  [local(): lax.ppermute(shard, 'rep', [(i, (i + r) % n_rep) for i in range(n_rep)])]
    ppermute x20, starting transfers between devices: 78.5 us -> 71.5 us  [pull(): lax.ppermute(a, 'edge', [(where_to(i, dz, dx, dc), i) for i in range(128)])]
    all_to_all x0 -> x1, waiting for transfers between devices: none -> 5.51 us  [local(): lax.all_to_all(jnp.broadcast_to(shard, (n_rep, 10, 640)), 'rep', split_ax...]
    all_to_all x0 -> x1, starting transfers between devices: none -> 4.62 us  [local(): lax.all_to_all(jnp.broadcast_to(shard, (n_rep, 10, 640)), 'rep', split_ax...]
    ppermute x13, waiting for transfers between devices: 36.4 us -> 32.6 us  [push(): lax.ppermute(a, 'edge', [(i, where_to(i, dz, dx, dc)) for i in range(128)])]
    ppermute x3 -> x0, waiting for transfers between devices: 2.75 us -> none  [local(): lax.ppermute(shard, 'rep', [(i, (i + r) % n_rep) for i in range(n_rep)])]
  transfers between devices with their start and end apart: 36 -> 34, of which waited for: 14 -> 14; matrix products, arithmetic and copies ran while one was open for 6% -> 5% of each run, Pallas kernels for 6% -> 6%
where the time goes in v3:
time: 244 us; the launch traced here: 242 us
  starting transfers between devices  121 us (50%)
  waiting for transfers between devices  64.7 us (27%)
  Pallas kernels  33.1 us (14%)
  other arithmetic  11.2 us (5%)
  local copies, waits for them, and re-layouts  8.63 us (4%)
  between operations  2.49 us (1%)
    ppermute x20, starting transfers between devices, pull(): lax.ppermute(a, 'edge', [(where_to(i, dz, dx, dc), i) for i in range(128)])  71.5 us
    ppermute x13, starting transfers between devices, push(): lax.ppermute(a, 'edge', [(i, where_to(i, dz, dx, dc)) for i in range(128)])  45.3 us
    pallas_call x3, Pallas kernels, call(): pl.pallas_call(kernel, out_shape=tuple((jax.ShapeDtypeStruct(s, t) for s,...  33.1 us
    ppermute x13, waiting for transfers between devices, push(): lax.ppermute(a, 'edge', [(i, where_to(i, dz, dx, dc)) for i in range(128)])  32.6 us
    ppermute x20, waiting for transfers between devices, pull(): lax.ppermute(a, 'edge', [(where_to(i, dz, dx, dc), i) for i in range(128)])  26.6 us
    all_to_all x1, waiting for transfers between devices, local(): lax.all_to_all(jnp.broadcast_to(shard, (n_rep, 10, 640)), 'rep', split_ax...  5.51 us
  transfers between devices with their start and end apart: 34, of which 14 were waited for; matrix products, arithmetic and copies ran while one was open for 5% of the time, Pallas kernels for 6%

profile of v3, /device:TPU:6, one launch (start us, length us, event | category | flops | bytes accessed | tf_op | source)
XLA Modules:
  0.0 241.6 jit_solution(12194802130834487430)
XLA Ops:
  1.3 0.8 fusion.118
  2.2 0.8 reshape.3175
  3.0 0.8 reshape_squeeze.3
  3.9 9.1 %collective-permute-start.2 = (bf16[250,128]{1,0:T(8,128)(2,1)S(1)}, bf16[250,128]{1,0:T(8,128)(2,1)S(1)}, u32[]{:S(2)}, u32[]{:S(2)}) collective-permute-start(bf16[250,128]{1,0:T(8,128)(2,1)S(1)} %pad_maximum_fusion.3), channel_id=1, source_target_pairs={{384,0},{132,4},{392,8},{140,12},{400,16},{148,20},{408,24},{156,2... | collective-permute-start | bytes 192008 | tf_op jit(solution)/shard_map/ppermute | solution.py:34
  13.0 10.9 %collective-permute-start.1 = (bf16[250,128]{1,0:T(8,128)(2,1)S(1)}, bf16[250,128]{1,0:T(8,128)(2,1)S(1)}, u32[]{:S(2)}, u32[]{:S(2)}) collective-permute-start(bf16[250,128]{1,0:T(8,128)(2,1)S(1)} %pad_maximum_fusion.3), channel_id=1, source_target_pairs={{256,0},{260,4},{264,8},{268,12},{272,16},{276,20},{280,24},{284,2... | collective-permute-start | bytes 192008 | tf_op jit(solution)/shard_map/ppermute | solution.py:34
  23.9 5.5 %collective-permute-start = (bf16[250,128]{1,0:T(8,128)(2,1)S(1)}, bf16[250,128]{1,0:T(8,128)(2,1)S(1)}, u32[]{:S(2)}, u32[]{:S(2)}) collective-permute-start(bf16[250,128]{1,0:T(8,128)(2,1)S(1)} %pad_maximum_fusion.3), channel_id=1, source_target_pairs={{128,0},{388,4},{136,8},{396,12},{144,16},{404,20},{152,24},{412,2... | collective-permute-start | bytes 192008 | tf_op jit(solution)/shard_map/ppermute | solution.py:34
  29.4 0.8 reduce-precision_convert_fusion
  30.6 4.7 %collective-permute-done = bf16[250,128]{1,0:T(8,128)(2,1)S(1)} collective-permute-done((bf16[250,128]{1,0:T(8,128)(2,1)S(1)}, bf16[250,128]{1,0:T(8,128)(2,1)S(1)}, u32[]{:S(2)}, u32[]{:S(2)}) %collective-permute-start) | collective-permute-done | bytes 64032 | tf_op jit(solution)/shard_map/ppermute | solution.py:34
  36.3 2.3 collective-permute-start.5
  38.7 5.8 %collective-permute-start.4 = (bf16[1088,128]{1,0:T(8,128)(2,1)S(1)}, bf16[1088,128]{1,0:T(8,128)(2,1)S(1)}, u32[]{:S(2)}, u32[]{:S(2)}) collective-permute-start(bf16[1088,128]{1,0:T(8,128)(2,1)S(1)} %pad_maximum_fusion.1), channel_id=1, source_target_pairs={{64,0},{452,4},{72,8},{460,12},{80,16},{468,20},{88,24},{476,28},{... | collective-permute-start | bytes 835592 | tf_op jit(solution)/shard_map/ppermute | solution.py:34
  44.4 3.4 %collective-permute-start.3 = (bf16[1088,128]{1,0:T(8,128)(2,1)S(1)}, bf16[1088,128]{1,0:T(8,128)(2,1)S(1)}, u32[]{:S(2)}, u32[]{:S(2)}) collective-permute-start(bf16[1088,128]{1,0:T(8,128)(2,1)S(1)} %pad_maximum_fusion.1), channel_id=1, source_target_pairs={{32,0},{484,4},{40,8},{492,12},{48,16},{500,20},{56,24},{508,28},{... | collective-permute-start | bytes 835592 | tf_op jit(solution)/shard_map/ppermute | solution.py:34
  47.8 0.7 maximum_maximum_fusion.refs_11_
  48.6 0.8 copy.83.refs_10_.refs_14_
  49.6 0.8 compare_select_fusion.47
  50.4 1.1 collective-permute-done.4
  51.5 3.0 %collective-permute-done.3 = bf16[1088,128]{1,0:T(8,128)(2,1)S(1)} collective-permute-done((bf16[1088,128]{1,0:T(8,128)(2,1)S(1)}, bf16[1088,128]{1,0:T(8,128)(2,1)S(1)}, u32[]{:S(2)}, u32[]{:S(2)}) %collective-permute-start.3) | collective-permute-done | bytes 278560 | tf_op jit(solution)/shard_map/ppermute | solution.py:34
  54.5 2.4 collective-permute-start.8
  56.9 2.0 collective-permute-start.9
  58.9 4.3 %collective-permute-start.7 = (bf16[1600,128]{1,0:T(8,128)(2,1)S(1)}, bf16[1600,128]{1,0:T(8,128)(2,1)S(1)}, u32[]{:S(2)}, u32[]{:S(2)}) collective-permute-start(bf16[1600,128]{1,0:T(8,128)(2,1)S(1)} %pad_maximum_fusion.refs_0_), channel_id=1, source_target_pairs={{16,0},{20,4},{24,8},{28,12},{0,16},{4,20},{8,24},{12,28},{48,32},... | collective-permute-start | bytes 1228808 | tf_op jit(solution)/shard_map/ppermute | solution.py:34
  63.2 1.9 collective-permute-start.6
  65.2 3.5 %collective-permute-done.8.refs_3_ = bf16[1600,128]{1,0:T(8,128)(2,1)S(1)} collective-permute-done((bf16[1600,128]{1,0:T(8,128)(2,1)S(1)}, bf16[1600,128]{1,0:T(8,128)(2,1)S(1)}, u32[]{:S(2)}, u32[]{:S(2)}) %collective-permute-start.8) | collective-permute-done | bytes 409632 | tf_op jit(solution)/shard_map/ppermute | solution.py:34
  68.7 1.9 collective-permute-start.12
  70.7 3.0 %collective-permute-start.15 = (bf16[2752,128]{1,0:T(8,128)(2,1)S(1)}, bf16[2752,128]{1,0:T(8,128)(2,1)S(1)}, u32[]{:S(2)}, u32[]{:S(2)}) collective-permute-start(bf16[2752,128]{1,0:T(8,128)(2,1)S(1)} %slice_dynamic-update-slice_fusion.refs_0_), channel_id=1, source_target_pairs={{24,0},{28,4},{0,8},{4,12},{8,16},{12,20},{16,24},{20,28},{56,32},... | collective-permute-start | bytes 2113544 | tf_op jit(solution)/shard_map/ppermute | solution.py:34
  73.7 3.7 %collective-permute-start.14 = (bf16[2752,128]{1,0:T(8,128)(2,1)S(1)}, bf16[2752,128]{1,0:T(8,128)(2,1)S(1)}, u32[]{:S(2)}, u32[]{:S(2)}) collective-permute-start(bf16[2752,128]{1,0:T(8,128)(2,1)S(1)} %slice_dynamic-update-slice_fusion.refs_0_), channel_id=1, source_target_pairs={{16,0},{20,4},{24,8},{28,12},{0,16},{4,20},{8,24},{12,28},{48,32},... | collective-permute-start | bytes 2113544 | tf_op jit(solution)/shard_map/ppermute | solution.py:34
  77.4 2.7 %collective-permute-start.13 = (bf16[2752,128]{1,0:T(8,128)(2,1)S(1)}, bf16[2752,128]{1,0:T(8,128)(2,1)}, u32[]{:S(2)}, u32[]{:S(2)}) collective-permute-start(bf16[2752,128]{1,0:T(8,128)(2,1)S(1)} %slice_dynamic-update-slice_fusion.refs_0_), channel_id=1, source_target_pairs={{8,0},{12,4},{16,8},{20,12},{24,16},{28,20},{0,24},{4,28},{40,32},... | collective-permute-start | bytes 2113544 | tf_op jit(solution)/shard_map/ppermute | solution.py:34
  80.2 3.2 %collective-permute-done.6.refs_1_ = bf16[1600,128]{1,0:T(8,128)(2,1)S(1)} collective-permute-done((bf16[1600,128]{1,0:T(8,128)(2,1)S(1)}, bf16[1600,128]{1,0:T(8,128)(2,1)S(1)}, u32[]{:S(2)}, u32[]{:S(2)}) %collective-permute-start.6) | collective-permute-done | bytes 409632 | tf_op jit(solution)/shard_map/ppermute | solution.py:34
  83.4 1.9 collective-permute-start.11
  85.3 2.4 collective-permute-start.10
  87.8 0.9 compare_select_fusion.12.refs_12_
  88.6 1.0 fusion.6.refs_9_
  89.6 1.9 collective-permute-start.16
  92.3 9.7 %rotate.1 = (bf16[160,1536]{1,0:T(8,128)(2,1)}, bf16[320,1024]{1,0:T(8,128)(2,1)}, bf16[320,1024]{1,0:T(8,128)(2,1)}, f32[160,2432]{1,0:T(8,128)}) custom-call(bf16[1600,128]{1,0:T(8,128)(2,1)} %copy-done.3, bf16[1600,128]{1,0:T(8,128)(2,1)} %copy-done.18, bf16[1600,128]{1,0:T(8,128)(2,1)} %copy-done.17, bf16[1600,128]{1,0:T(8,128)(2,1)} %copy-done.15, ...), custom_call_target="tpu_custom_call" | custom-call | flops 3000000000 | bytes 3546816 | tf_op jit(solution)/shard_map/rotate/pallas_call | solution.py:319
  102.1 11.1 %collective-permute-done.13.refs_1_ = bf16[2752,128]{1,0:T(8,128)(2,1)} collective-permute-done((bf16[2752,128]{1,0:T(8,128)(2,1)S(1)}, bf16[2752,128]{1,0:T(8,128)(2,1)}, u32[]{:S(2)}, u32[]{:S(2)}) %collective-permute-start.13) | collective-permute-done | bytes 704544 | tf_op jit(solution)/shard_map/ppermute | solution.py:34
  113.2 1.9 collective-permute-start.17
  115.1 2.4 collective-permute-start.18
  117.5 2.1 collective-permute-start.19
  121.0 0.7 copy.86.refs_16_
  121.7 0.7 copy.84
  122.5 0.7 fusion.59.refs_19_
  124.4 0.8 fusion.47.refs_18_
  125.3 18.1 %layer.1 = (bf16[2560,128]{1,0:T(8,128)(2,1)}, bf16[2560,128]{1,0:T(8,128)(2,1)}, bf16[2560,128]{1,0:T(8,128)(2,1)}, bf16[2560,128]{1,0:T(8,128)(2,1)}, bf16[256...) custom-call(bf16[2752,128]{1,0:T(8,128)(2,1)} %copy-done.7, ...), custom_call_target="tpu_custom_call" | custom-call | flops 5000000000 | bytes 9168192 | tf_op jit(solution)/shard_map/layer/pallas_call | solution.py:319
  143.4 2.5 %collective-permute-start.20 = (bf16[2560,128]{1,0:T(8,128)(2,1)}, bf16[2560,128]{1,0:T(8,128)(2,1)S(1)}, u32[]{:S(2)}, u32[]{:S(2)}) collective-permute-start(bf16[2560,128]{1,0:T(8,128)(2,1)} %get-tuple-element.43), channel_id=1, source_target_pairs={{0,4},{4,0},{8,12},{12,8},{16,20},{20,16},{24,28},{28,24},{32,36},... | collective-permute-start | bytes 1966088 | tf_op jit(solution)/shard_map/ppermute | solution.py:38
  145.9 1.9 collective-permute-start.22
  147.9 2.4 collective-permute-start.24
  150.3 1.3 add_convert_fusion.4
  151.6 2.7 %collective-permute-start.21 = (bf16[2560,128]{1,0:T(8,128)(2,1)S(1)}, bf16[2560,128]{1,0:T(8,128)(2,1)S(1)}, u32[]{:S(2)}, u32[]{:S(2)}) collective-permute-start(bf16[2560,128]{1,0:T(8,128)(2,1)S(1)} %add_convert_fusion.4), channel_id=1, source_target_pairs={{0,8},{4,12},{8,16},{12,20},{16,24},{20,28},{24,0},{28,4},{32,40},... | collective-permute-start | bytes 1966088 | tf_op jit(solution)/shard_map/ppermute | solution.py:38
  154.5 4.5 %collective-permute-start.23 = (bf16[2560,128]{1,0:T(8,128)(2,1)S(1)}, bf16[2560,128]{1,0:T(8,128)(2,1)S(1)}, u32[]{:S(2)}, u32[]{:S(2)}) collective-permute-start(bf16[2560,128]{1,0:T(8,128)(2,1)S(1)} %add_convert_fusion.3), channel_id=1, source_target_pairs={{0,16},{4,20},{8,24},{12,28},{16,0},{20,4},{24,8},{28,12},{32,48},... | collective-permute-start | bytes 1966088 | tf_op jit(solution)/shard_map/ppermute | solution.py:38
  159.2 2.8 %collective-permute-start.25 = (bf16[2560,128]{1,0:T(8,128)(2,1)S(1)}, bf16[2560,128]{1,0:T(8,128)(2,1)S(1)}, u32[]{:S(2)}, u32[]{:S(2)}) collective-permute-start(bf16[2560,128]{1,0:T(8,128)(2,1)S(1)} %add_convert_fusion.2), channel_id=1, source_target_pairs={{0,24},{4,28},{8,0},{12,4},{16,8},{20,12},{24,16},{28,20},{32,56},... | collective-permute-start | bytes 1966088 | tf_op jit(solution)/shard_map/ppermute | solution.py:38
  162.0 1.9 collective-permute-start.26
  163.9 5.3 %nodes.1 = (bf16[4,3200]{1,0:T(4,128)(2,1)}, f32[4,3200]{1,0:T(4,128)}) custom-call(bf16[160,475]{1,0:T(8,128)(2,1)} %bitcast.95, bf16[160,2432]{1,0:T(8,128)(2,1)} %get-tuple-element.48.scaled, bf16[160,2432]{1,0:T(8,128)(2,1)} %get-tuple-element.49.grad_dst, s32[1,160]{1,0:T(1,128)} %target.1), custom_call_target="tpu_custom_call" | custom-call | flops 600000000 | bytes 1709120 | tf_op jit(solution)/shard_map/nodes/pallas_call | solution.py:319
  169.2 2.0 collective-permute-done.21
  171.2 4.5 %collective-permute-done.23 = bf16[2560,128]{1,0:T(8,128)(2,1)S(1)} collective-permute-done((bf16[2560,128]{1,0:T(8,128)(2,1)S(1)}, bf16[2560,128]{1,0:T(8,128)(2,1)S(1)}, u32[]{:S(2)}, u32[]{:S(2)}) %collective-permute-start.23) | collective-permute-done | bytes 655392 | tf_op jit(solution)/shard_map/ppermute | solution.py:38
  175.7 12.7 %collective-permute-done.25 = bf16[2560,128]{1,0:T(8,128)(2,1)S(1)} collective-permute-done((bf16[2560,128]{1,0:T(8,128)(2,1)S(1)}, bf16[2560,128]{1,0:T(8,128)(2,1)S(1)}, u32[]{:S(2)}, u32[]{:S(2)}) %collective-permute-start.25) | collective-permute-done | bytes 655392 | tf_op jit(solution)/shard_map/ppermute | solution.py:38
  188.9 2.4 collective-permute-start.27
  191.3 5.1 %collective-permute-start.29 = (bf16[640,128]{1,0:T(8,128)(2,1)S(1)}, bf16[640,128]{1,0:T(8,128)(2,1)S(1)}, u32[]{:S(2)}, u32[]{:S(2)}) collective-permute-start(bf16[640,128]{1,0:T(8,128)(2,1)S(1)} %get-tuple-element.60), channel_id=1, source_target_pairs={{0,480},{4,36},{8,488},{12,44},{16,496},{20,52},{24,504},{28,60},{... | collective-permute-start | bytes 491528 | tf_op jit(solution)/shard_map/ppermute | solution.py:38
  196.4 2.2 collective-permute-start.28
  199.3 7.9 %collective-permute-done.28 = bf16[640,128]{1,0:T(8,128)(2,1)S(1)} collective-permute-done((bf16[640,128]{1,0:T(8,128)(2,1)S(1)}, bf16[640,128]{1,0:T(8,128)(2,1)S(1)}, u32[]{:S(2)}, u32[]{:S(2)}) %collective-permute-start.28) | collective-permute-done | bytes 163872 | tf_op jit(solution)/shard_map/ppermute | solution.py:38
  207.6 4.7 %collective-permute-start.30 = (bf16[150,128]{1,0:T(8,128)(2,1)S(1)}, bf16[150,128]{1,0:T(8,128)(2,1)S(1)}, u32[]{:S(2)}, u32[]{:S(2)}) collective-permute-start(bf16[150,128]{1,0:T(8,128)(2,1)S(1)} %pad_maximum_fusion.5), channel_id=1, source_target_pairs={{0,128},{4,388},{8,136},{12,396},{16,144},{20,404},{24,152},{28,41... | collective-permute-start | bytes 115208 | tf_op jit(solution)/shard_map/ppermute | solution.py:38
  212.3 7.2 %collective-permute-start.31 = (bf16[150,128]{1,0:T(8,128)(2,1)S(1)}, bf16[150,128]{1,0:T(8,128)(2,1)S(1)}, u32[]{:S(2)}, u32[]{:S(2)}) collective-permute-start(bf16[150,128]{1,0:T(8,128)(2,1)S(1)} %pad_maximum_fusion.6), channel_id=1, source_target_pairs={{0,256},{4,260},{8,264},{12,268},{16,272},{20,276},{24,280},{28,28... | collective-permute-start | bytes 115208 | tf_op jit(solution)/shard_map/ppermute | solution.py:38
  219.6 5.0 %collective-permute-start.32 = (bf16[150,128]{1,0:T(8,128)(2,1)S(1)}, bf16[150,128]{1,0:T(8,128)(2,1)S(1)}, u32[]{:S(2)}, u32[]{:S(2)}) collective-permute-start(bf16[150,128]{1,0:T(8,128)(2,1)S(1)} %pad_maximum_fusion.7), channel_id=1, source_target_pairs={{0,384},{4,132},{8,392},{12,140},{16,400},{20,148},{24,408},{28,15... | collective-permute-start | bytes 115208 | tf_op jit(solution)/shard_map/ppermute | solution.py:38
  224.6 2.6 %collective-permute-done.31 = bf16[150,128]{1,0:T(8,128)(2,1)S(1)} collective-permute-done((bf16[150,128]{1,0:T(8,128)(2,1)S(1)}, bf16[150,128]{1,0:T(8,128)(2,1)S(1)}, u32[]{:S(2)}, u32[]{:S(2)}) %collective-permute-start.31) | collective-permute-done | bytes 38432 | tf_op jit(solution)/shard_map/ppermute | solution.py:38
  227.2 2.2 collective-permute-done.32
  230.2 4.6 %all-to-all-start = ((f32[4,10,640]{2,1,0:T(8,128)}), f32[4,10,640]{2,1,0:T(8,128)S(1)}, u32[]{:S(2)}, u32[]{:S(2)}) async-start(f32[4,10,640]{2,1,0:T(8,128)} %broadcast_in_dim.37), calls=%async_computation | async-start | bytes 327680 | tf_op jit(solution)/shard_map/all_to_all | solution.py:421
  235.5 5.5 %all-to-all-done = f32[4,10,640]{2,1,0:T(8,128)S(1)} async-done(((f32[4,10,640]{2,1,0:T(8,128)}), f32[4,10,640]{2,1,0:T(8,128)S(1)}, u32[]{:S(2)}, u32[]{:S(2)}) %all-to-all-start) | async-done | bytes 102432 | tf_op jit(solution)/shard_map/all_to_all | solution.py:421
  (155 shorter events, 9.1 us)
Async XLA Ops:
  3.8 44.0 %copy-start.4 = (bf16[1,4,3200]{2,1,0:T(4,128)(2,1)S(1)}, bf16[1,4,3200]{2,1,0:T(4,128)(2,1)}, u32[]{:S(2)}) copy-start(bf16[1,4,3200]{2,1,0:T(4,128)(2,1)} %param.12) | copy-start | bytes 76804
  3.9 26.4 %collective-permute-start.2 = (bf16[250,128]{1,0:T(8,128)(2,1)S(1)}, bf16[250,128]{1,0:T(8,128)(2,1)S(1)}, u32[]{:S(2)}, u32[]{:S(2)}) collective-permute-start(bf16[250,128]{1,0:T(8,128)(2,1)S(1)} %pad_maximum_fusion.3), channel_id=1, source_target_pairs={{384,0},{132,4},{392,8},{140,12},{400,16},{148,20},{408,24},{156,2... | collective-permute-start | bytes 192008 | tf_op jit(solution)/shard_map/ppermute | solution.py:34
  13.0 17.5 %collective-permute-start.1 = (bf16[250,128]{1,0:T(8,128)(2,1)S(1)}, bf16[250,128]{1,0:T(8,128)(2,1)S(1)}, u32[]{:S(2)}, u32[]{:S(2)}) collective-permute-start(bf16[250,128]{1,0:T(8,128)(2,1)S(1)} %pad_maximum_fusion.3), channel_id=1, source_target_pairs={{256,0},{260,4},{264,8},{268,12},{272,16},{276,20},{280,24},{284,2... | collective-permute-start | bytes 192008 | tf_op jit(solution)/shard_map/ppermute | solution.py:34
  23.9 11.3 %collective-permute-start = (bf16[250,128]{1,0:T(8,128)(2,1)S(1)}, bf16[250,128]{1,0:T(8,128)(2,1)S(1)}, u32[]{:S(2)}, u32[]{:S(2)}) collective-permute-start(bf16[250,128]{1,0:T(8,128)(2,1)S(1)} %pad_maximum_fusion.3), channel_id=1, source_target_pairs={{128,0},{388,4},{136,8},{396,12},{144,16},{404,20},{152,24},{412,2... | collective-permute-start | bytes 192008 | tf_op jit(solution)/shard_map/ppermute | solution.py:34
  30.3 18.2 %copy-start.11 = (s32[1,160]{1,0:T(1,128)S(1)}, s32[1,160]{1,0:T(1,128)}, u32[]{:S(2)}) copy-start(s32[1,160]{1,0:T(1,128)} %target.1) | copy-start | bytes 1924
  30.4 19.0 %copy-start.8 = (s32[1,160]{1,0:T(1,128)S(1)}, s32[1,160]{1,0:T(1,128)}, u32[]{:S(2)}) copy-start(s32[1,160]{1,0:T(1,128)} %param.15) | copy-start | bytes 1924
  30.4 19.0 %copy-start.9 = (s32[1,160,1]{1,2,0:T(1,128)S(1)}, s32[1,160,1]{1,2,0:T(1,128)}, u32[]{:S(2)}) copy-start(s32[1,160,1]{1,2,0:T(1,128)} %param.14) | copy-start | bytes 1924
  36.3 14.0 %collective-permute-start.5 = (bf16[1088,128]{1,0:T(8,128)(2,1)S(1)}, bf16[1088,128]{1,0:T(8,128)(2,1)S(1)}, u32[]{:S(2)}, u32[]{:S(2)}) collective-permute-start(bf16[1088,128]{1,0:T(8,128)(2,1)S(1)} %pad_maximum_fusion.1), channel_id=1, source_target_pairs={{480,0},{36,4},{488,8},{44,12},{496,16},{52,20},{504,24},{60,28},{... | collective-permute-start | bytes 835592 | tf_op jit(solution)/shard_map/ppermute | solution.py:34
  38.7 12.8 %collective-permute-start.4 = (bf16[1088,128]{1,0:T(8,128)(2,1)S(1)}, bf16[1088,128]{1,0:T(8,128)(2,1)S(1)}, u32[]{:S(2)}, u32[]{:S(2)}) collective-permute-start(bf16[1088,128]{1,0:T(8,128)(2,1)S(1)} %pad_maximum_fusion.1), channel_id=1, source_target_pairs={{64,0},{452,4},{72,8},{460,12},{80,16},{468,20},{88,24},{476,28},{... | collective-permute-start | bytes 835592 | tf_op jit(solution)/shard_map/ppermute | solution.py:34
  44.4 10.0 %collective-permute-start.3 = (bf16[1088,128]{1,0:T(8,128)(2,1)S(1)}, bf16[1088,128]{1,0:T(8,128)(2,1)S(1)}, u32[]{:S(2)}, u32[]{:S(2)}) collective-permute-start(bf16[1088,128]{1,0:T(8,128)(2,1)S(1)} %pad_maximum_fusion.1), channel_id=1, source_target_pairs={{32,0},{484,4},{40,8},{492,12},{48,16},{500,20},{56,24},{508,28},{... | collective-permute-start | bytes 835592 | tf_op jit(solution)/shard_map/ppermute | solution.py:34
  54.5 37.1 %copy-start.3 = (bf16[1600,128]{1,0:T(8,128)(2,1)}, bf16[1600,128]{1,0:T(8,128)(2,1)S(1)}, u32[]{:S(2)}) copy-start(bf16[1600,128]{1,0:T(8,128)(2,1)S(1)} %pad_maximum_fusion.refs_0_) | copy-start | bytes 1228804
  54.5 14.2 %collective-permute-start.8 = (bf16[1600,128]{1,0:T(8,128)(2,1)S(1)}, bf16[1600,128]{1,0:T(8,128)(2,1)S(1)}, u32[]{:S(2)}, u32[]{:S(2)}) collective-permute-start(bf16[1600,128]{1,0:T(8,128)(2,1)S(1)} %pad_maximum_fusion.refs_0_), channel_id=1, source_target_pairs={{24,0},{28,4},{0,8},{4,12},{8,16},{12,20},{16,24},{20,28},{56,32},... | collective-permute-start | bytes 1228808 | tf_op jit(solution)/shard_map/ppermute | solution.py:34
  56.9 16.8 %collective-permute-start.9 = (bf16[1600,128]{1,0:T(8,128)(2,1)S(1)}, bf16[1600,128]{1,0:T(8,128)(2,1)S(1)}, u32[]{:S(2)}, u32[]{:S(2)}) collective-permute-start(bf16[1600,128]{1,0:T(8,128)(2,1)S(1)} %pad_maximum_fusion.refs_0_), channel_id=1, source_target_pairs={{4,0},{0,4},{12,8},{8,12},{20,16},{16,20},{28,24},{24,28},{36,32},... | collective-permute-start | bytes 1228808 | tf_op jit(solution)/shard_map/ppermute | solution.py:34
  58.9 18.6 %collective-permute-start.7 = (bf16[1600,128]{1,0:T(8,128)(2,1)S(1)}, bf16[1600,128]{1,0:T(8,128)(2,1)S(1)}, u32[]{:S(2)}, u32[]{:S(2)}) collective-permute-start(bf16[1600,128]{1,0:T(8,128)(2,1)S(1)} %pad_maximum_fusion.refs_0_), channel_id=1, source_target_pairs={{16,0},{20,4},{24,8},{28,12},{0,16},{4,20},{8,24},{12,28},{48,32},... | collective-permute-start | bytes 1228808 | tf_op jit(solution)/shard_map/ppermute | solution.py:34
  63.2 20.2 %collective-permute-start.6 = (bf16[1600,128]{1,0:T(8,128)(2,1)S(1)}, bf16[1600,128]{1,0:T(8,128)(2,1)S(1)}, u32[]{:S(2)}, u32[]{:S(2)}) collective-permute-start(bf16[1600,128]{1,0:T(8,128)(2,1)S(1)} %pad_maximum_fusion.refs_0_), channel_id=1, source_target_pairs={{8,0},{12,4},{16,8},{20,12},{24,16},{28,20},{0,24},{4,28},{40,32},... | collective-permute-start | bytes 1228808 | tf_op jit(solution)/shard_map/ppermute | solution.py:34
  68.7 22.9 %copy-start.15 = (bf16[1600,128]{1,0:T(8,128)(2,1)}, bf16[1600,128]{1,0:T(8,128)(2,1)S(1)}, u32[]{:S(2)}) copy-start(bf16[1600,128]{1,0:T(8,128)(2,1)S(1)} %collective-permute-done.8.refs_3_) | copy-start | bytes 1228804
  68.7 16.6 %collective-permute-start.12 = (bf16[1600,128]{1,0:T(8,128)(2,1)S(1)}, bf16[1600,128]{1,0:T(8,128)(2,1)S(1)}, u32[]{:S(2)}, u32[]{:S(2)}) collective-permute-start(bf16[1600,128]{1,0:T(8,128)(2,1)S(1)} %collective-permute-done.8.refs_3_), channel_id=1, source_target_pairs={{4,0},{0,4},{12,8},{8,12},{20,16},{16,20},{28,24},{24,28},{36,32},... | collective-permute-start | bytes 1228808 | tf_op jit(solution)/shard_map/ppermute | solution.py:34
  70.7 31.4 %copy-start.7 = (bf16[2752,128]{1,0:T(8,128)(2,1)}, bf16[2752,128]{1,0:T(8,128)(2,1)S(1)}, u32[]{:S(2)}) copy-start(bf16[2752,128]{1,0:T(8,128)(2,1)S(1)} %slice_dynamic-update-slice_fusion.refs_0_) | copy-start | bytes 2113540
  70.7 31.4 %collective-permute-start.15 = (bf16[2752,128]{1,0:T(8,128)(2,1)S(1)}, bf16[2752,128]{1,0:T(8,128)(2,1)S(1)}, u32[]{:S(2)}, u32[]{:S(2)}) collective-permute-start(bf16[2752,128]{1,0:T(8,128)(2,1)S(1)} %slice_dynamic-update-slice_fusion.refs_0_), channel_id=1, source_target_pairs={{24,0},{28,4},{0,8},{4,12},{8,16},{12,20},{16,24},{20,28},{56,32},... | collective-permute-start | bytes 2113544 | tf_op jit(solution)/shard_map/ppermute | solution.py:34
  73.7 17.9 %copy-start.16 = (bf16[1600,128]{1,0:T(8,128)(2,1)}, bf16[1600,128]{1,0:T(8,128)(2,1)S(1)}, u32[]{:S(2)}) copy-start(bf16[1600,128]{1,0:T(8,128)(2,1)S(1)} %collective-permute-done.9.refs_4_) | copy-start | bytes 1228804
  73.7 28.4 %collective-permute-start.14 = (bf16[2752,128]{1,0:T(8,128)(2,1)S(1)}, bf16[2752,128]{1,0:T(8,128)(2,1)S(1)}, u32[]{:S(2)}, u32[]{:S(2)}) collective-permute-start(bf16[2752,128]{1,0:T(8,128)(2,1)S(1)} %slice_dynamic-update-slice_fusion.refs_0_), channel_id=1, source_target_pairs={{16,0},{20,4},{24,8},{28,12},{0,16},{4,20},{8,24},{12,28},{48,32},... | collective-permute-start | bytes 2113544 | tf_op jit(solution)/shard_map/ppermute | solution.py:34
  77.4 14.2 %copy-start.17 = (bf16[1600,128]{1,0:T(8,128)(2,1)}, bf16[1600,128]{1,0:T(8,128)(2,1)S(1)}, u32[]{:S(2)}) copy-start(bf16[1600,128]{1,0:T(8,128)(2,1)S(1)} %collective-permute-done.7.refs_2_) | copy-start | bytes 1228804
  77.4 35.7 %collective-permute-start.13 = (bf16[2752,128]{1,0:T(8,128)(2,1)S(1)}, bf16[2752,128]{1,0:T(8,128)(2,1)}, u32[]{:S(2)}, u32[]{:S(2)}) collective-permute-start(bf16[2752,128]{1,0:T(8,128)(2,1)S(1)} %slice_dynamic-update-slice_fusion.refs_0_), channel_id=1, source_target_pairs={{8,0},{12,4},{16,8},{20,12},{24,16},{28,20},{0,24},{4,28},{40,32},... | collective-permute-start | bytes 2113544 | tf_op jit(solution)/shard_map/ppermute | solution.py:34
  83.4 8.2 %copy-start.18 = (bf16[1600,128]{1,0:T(8,128)(2,1)}, bf16[1600,128]{1,0:T(8,128)(2,1)S(1)}, u32[]{:S(2)}) copy-start(bf16[1600,128]{1,0:T(8,128)(2,1)S(1)} %collective-permute-done.6.refs_1_) | copy-start | bytes 1228804
  83.4 6.2 %collective-permute-start.11 = (bf16[1600,128]{1,0:T(8,128)(2,1)S(1)}, bf16[1600,128]{1,0:T(8,128)(2,1)S(1)}, u32[]{:S(2)}, u32[]{:S(2)}) collective-permute-start(bf16[1600,128]{1,0:T(8,128)(2,1)S(1)} %collective-permute-done.7.refs_2_), channel_id=1, source_target_pairs={{4,0},{0,4},{12,8},{8,12},{20,16},{16,20},{28,24},{24,28},{36,32},... | collective-permute-start | bytes 1228808 | tf_op jit(solution)/shard_map/ppermute | solution.py:34
  85.3 6.3 %copy-start.19 = (bf16[1600,128]{1,0:T(8,128)(2,1)}, bf16[1600,128]{1,0:T(8,128)(2,1)S(1)}, u32[]{:S(2)}) copy-start(bf16[1600,128]{1,0:T(8,128)(2,1)S(1)} %collective-permute-done.12.refs_7_) | copy-start | bytes 1228804
  85.3 6.2 %collective-permute-start.10 = (bf16[1600,128]{1,0:T(8,128)(2,1)S(1)}, bf16[1600,128]{1,0:T(8,128)(2,1)S(1)}, u32[]{:S(2)}, u32[]{:S(2)}) collective-permute-start(bf16[1600,128]{1,0:T(8,128)(2,1)S(1)} %collective-permute-done.6.refs_1_), channel_id=1, source_target_pairs={{4,0},{0,4},{12,8},{8,12},{20,16},{16,20},{28,24},{24,28},{36,32},... | collective-permute-start | bytes 1228808 | tf_op jit(solution)/shard_map/ppermute | solution.py:34
  89.6 2.0 copy-start.20
  89.6 35.6 %collective-permute-start.16 = (bf16[2752,128]{1,0:T(8,128)(2,1)S(1)}, bf16[2752,128]{1,0:T(8,128)(2,1)}, u32[]{:S(2)}, u32[]{:S(2)}) collective-permute-start(bf16[2752,128]{1,0:T(8,128)(2,1)S(1)} %slice_dynamic-update-slice_fusion.refs_0_), channel_id=1, source_target_pairs={{4,0},{0,4},{12,8},{8,12},{20,16},{16,20},{28,24},{24,28},{36,32},... | collective-permute-start | bytes 2113544 | tf_op jit(solution)/shard_map/ppermute | solution.py:34
  91.6 0.8 copy-start.21
  92.3 28.7 %copy-start.10 = (bf16[128,8]{0,1:T(8,128)(2,1)S(1)}, bf16[128,8]{0,1:T(8,128)(2,1)}, u32[]{:S(2)}) copy-start(bf16[128,8]{0,1:T(8,128)(2,1)} %param.22) | copy-start | bytes 6148
  92.3 29.4 %copy-start.6 = (f32[1,160,8]{1,2,0:T(8,128)S(1)}, f32[1,160,8]{1,2,0:T(8,128)}, u32[]{:S(2)}) copy-start(f32[1,160,8]{1,2,0:T(8,128)} %param.18) | copy-start | bytes 15364
  102.1 23.2 %copy-start.12 = (bf16[2752,128]{1,0:T(8,128)(2,1)}, bf16[2752,128]{1,0:T(8,128)(2,1)S(1)}, u32[]{:S(2)}) copy-start(bf16[2752,128]{1,0:T(8,128)(2,1)S(1)} %collective-permute-done.15.refs_3_) | copy-start | bytes 2113540
  102.1 23.2 %copy-start.13 = (bf16[2752,128]{1,0:T(8,128)(2,1)}, bf16[2752,128]{1,0:T(8,128)(2,1)S(1)}, u32[]{:S(2)}) copy-start(bf16[2752,128]{1,0:T(8,128)(2,1)S(1)} %collective-permute-done.14.refs_2_) | copy-start | bytes 2113540
  113.2 12.1 %collective-permute-start.17 = (bf16[2752,128]{1,0:T(8,128)(2,1)}, bf16[2752,128]{1,0:T(8,128)(2,1)}, u32[]{:S(2)}, u32[]{:S(2)}) collective-permute-start(bf16[2752,128]{1,0:T(8,128)(2,1)} %collective-permute-done.13.refs_1_), channel_id=1, source_target_pairs={{4,0},{0,4},{12,8},{8,12},{20,16},{16,20},{28,24},{24,28},{36,32},... | collective-permute-start | bytes 2113544 | tf_op jit(solution)/shard_map/ppermute | solution.py:34
  115.1 10.2 %collective-permute-start.18 = (bf16[2752,128]{1,0:T(8,128)(2,1)S(1)}, bf16[2752,128]{1,0:T(8,128)(2,1)}, u32[]{:S(2)}, u32[]{:S(2)}) collective-permute-start(bf16[2752,128]{1,0:T(8,128)(2,1)S(1)} %collective-permute-done.14.refs_2_), channel_id=1, source_target_pairs={{4,0},{0,4},{12,8},{8,12},{20,16},{16,20},{28,24},{24,28},{36,32},... | collective-permute-start | bytes 2113544 | tf_op jit(solution)/shard_map/ppermute | solution.py:34
  117.5 7.7 %collective-permute-start.19 = (bf16[2752,128]{1,0:T(8,128)(2,1)S(1)}, bf16[2752,128]{1,0:T(8,128)(2,1)}, u32[]{:S(2)}, u32[]{:S(2)}) collective-permute-start(bf16[2752,128]{1,0:T(8,128)(2,1)S(1)} %collective-permute-done.15.refs_3_), channel_id=1, source_target_pairs={{4,0},{0,4},{12,8},{8,12},{20,16},{16,20},{28,24},{24,28},{36,32},... | collective-permute-start | bytes 2113544 | tf_op jit(solution)/shard_map/ppermute | solution.py:34
  143.4 10.9 %copy-start.1 = (bf16[2560,128]{1,0:T(8,128)(2,1)S(1)}, bf16[2560,128]{1,0:T(8,128)(2,1)}, u32[]{:S(2)}) copy-start(bf16[2560,128]{1,0:T(8,128)(2,1)} %get-tuple-element.44) | copy-start | bytes 1966084
  143.4 6.9 %collective-permute-start.20 = (bf16[2560,128]{1,0:T(8,128)(2,1)}, bf16[2560,128]{1,0:T(8,128)(2,1)S(1)}, u32[]{:S(2)}, u32[]{:S(2)}) collective-permute-start(bf16[2560,128]{1,0:T(8,128)(2,1)} %get-tuple-element.43), channel_id=1, source_target_pairs={{0,4},{4,0},{8,12},{12,8},{16,20},{20,16},{24,28},{28,24},{32,36},... | collective-permute-start | bytes 1966088 | tf_op jit(solution)/shard_map/ppermute | solution.py:38
  145.9 8.3 %collective-permute-start.22 = (bf16[2560,128]{1,0:T(8,128)(2,1)}, bf16[2560,128]{1,0:T(8,128)(2,1)S(1)}, u32[]{:S(2)}, u32[]{:S(2)}) collective-permute-start(bf16[2560,128]{1,0:T(8,128)(2,1)} %get-tuple-element.45), channel_id=1, source_target_pairs={{0,4},{4,0},{8,12},{12,8},{16,20},{20,16},{24,28},{28,24},{32,36},... | collective-permute-start | bytes 1966088 | tf_op jit(solution)/shard_map/ppermute | solution.py:38
  147.9 11.1 %collective-permute-start.24 = (bf16[2560,128]{1,0:T(8,128)(2,1)}, bf16[2560,128]{1,0:T(8,128)(2,1)S(1)}, u32[]{:S(2)}, u32[]{:S(2)}) collective-permute-start(bf16[2560,128]{1,0:T(8,128)(2,1)} %get-tuple-element.47), channel_id=1, source_target_pairs={{0,4},{4,0},{8,12},{12,8},{16,20},{20,16},{24,28},{28,24},{32,36},... | collective-permute-start | bytes 1966088 | tf_op jit(solution)/shard_map/ppermute | solution.py:38
  151.6 7.4 %copy-start = (bf16[2560,128]{1,0:T(8,128)(2,1)S(1)}, bf16[2560,128]{1,0:T(8,128)(2,1)}, u32[]{:S(2)}) copy-start(bf16[2560,128]{1,0:T(8,128)(2,1)} %get-tuple-element.46) | copy-start | bytes 1966084
  151.6 19.6 %collective-permute-start.21 = (bf16[2560,128]{1,0:T(8,128)(2,1)S(1)}, bf16[2560,128]{1,0:T(8,128)(2,1)S(1)}, u32[]{:S(2)}, u32[]{:S(2)}) collective-permute-start(bf16[2560,128]{1,0:T(8,128)(2,1)S(1)} %add_convert_fusion.4), channel_id=1, source_target_pairs={{0,8},{4,12},{8,16},{12,20},{16,24},{20,28},{24,0},{28,4},{32,40},... | collective-permute-start | bytes 1966088 | tf_op jit(solution)/shard_map/ppermute | solution.py:38
  154.5 7.5 %copy-start.14 = (bf16[2560,128]{1,0:T(8,128)(2,1)S(1)}, bf16[2560,128]{1,0:T(8,128)(2,1)}, u32[]{:S(2)}) copy-start(bf16[2560,128]{1,0:T(8,128)(2,1)} %get-tuple-element.55) | copy-start | bytes 1966084
  154.5 21.2 %collective-permute-start.23 = (bf16[2560,128]{1,0:T(8,128)(2,1)S(1)}, bf16[2560,128]{1,0:T(8,128)(2,1)S(1)}, u32[]{:S(2)}, u32[]{:S(2)}) collective-permute-start(bf16[2560,128]{1,0:T(8,128)(2,1)S(1)} %add_convert_fusion.3), channel_id=1, source_target_pairs={{0,16},{4,20},{8,24},{12,28},{16,0},{20,4},{24,8},{28,12},{32,48},... | collective-permute-start | bytes 1966088 | tf_op jit(solution)/shard_map/ppermute | solution.py:38
  159.2 29.3 %copy-start.2 = (bf16[2560,128]{1,0:T(8,128)(2,1)S(1)}, bf16[2560,128]{1,0:T(8,128)(2,1)}, u32[]{:S(2)}) copy-start(bf16[2560,128]{1,0:T(8,128)(2,1)} %get-tuple-element.54) | copy-start | bytes 1966084
  159.2 29.3 %collective-permute-start.25 = (bf16[2560,128]{1,0:T(8,128)(2,1)S(1)}, bf16[2560,128]{1,0:T(8,128)(2,1)S(1)}, u32[]{:S(2)}, u32[]{:S(2)}) collective-permute-start(bf16[2560,128]{1,0:T(8,128)(2,1)S(1)} %add_convert_fusion.2), channel_id=1, source_target_pairs={{0,24},{4,28},{8,0},{12,4},{16,8},{20,12},{24,16},{28,20},{32,56},... | collective-permute-start | bytes 1966088 | tf_op jit(solution)/shard_map/ppermute | solution.py:38
  162.0 26.4 %collective-permute-start.26 = (bf16[2560,128]{1,0:T(8,128)(2,1)S(1)}, bf16[2560,128]{1,0:T(8,128)(2,1)S(1)}, u32[]{:S(2)}, u32[]{:S(2)}) collective-permute-start(bf16[2560,128]{1,0:T(8,128)(2,1)S(1)} %copy-done.14), channel_id=1, source_target_pairs={{0,4},{4,0},{8,12},{12,8},{16,20},{20,16},{24,28},{28,24},{32,36},... | collective-permute-start | bytes 1966088 | tf_op jit(solution)/shard_map/ppermute | solution.py:38
  188.9 9.7 %collective-permute-start.27 = (bf16[640,128]{1,0:T(8,128)(2,1)S(1)}, bf16[640,128]{1,0:T(8,128)(2,1)S(1)}, u32[]{:S(2)}, u32[]{:S(2)}) collective-permute-start(bf16[640,128]{1,0:T(8,128)(2,1)S(1)} %get-tuple-element.59), channel_id=1, source_target_pairs={{0,32},{4,484},{8,40},{12,492},{16,48},{20,500},{24,56},{28,508},{... | collective-permute-start | bytes 491528 | tf_op jit(solution)/shard_map/ppermute | solution.py:38
  191.3 7.9 %collective-permute-start.29 = (bf16[640,128]{1,0:T(8,128)(2,1)S(1)}, bf16[640,128]{1,0:T(8,128)(2,1)S(1)}, u32[]{:S(2)}, u32[]{:S(2)}) collective-permute-start(bf16[640,128]{1,0:T(8,128)(2,1)S(1)} %get-tuple-element.60), channel_id=1, source_target_pairs={{0,480},{4,36},{8,488},{12,44},{16,496},{20,52},{24,504},{28,60},{... | collective-permute-start | bytes 491528 | tf_op jit(solution)/shard_map/ppermute | solution.py:38
  196.4 10.8 %collective-permute-start.28 = (bf16[640,128]{1,0:T(8,128)(2,1)S(1)}, bf16[640,128]{1,0:T(8,128)(2,1)S(1)}, u32[]{:S(2)}, u32[]{:S(2)}) collective-permute-start(bf16[640,128]{1,0:T(8,128)(2,1)S(1)} %get-tuple-element.61), channel_id=1, source_target_pairs={{0,64},{4,452},{8,72},{12,460},{16,80},{20,468},{24,88},{28,476},{... | collective-permute-start | bytes 491528 | tf_op jit(solution)/shard_map/ppermute | solution.py:38
  207.3 27.5 %copy-start.5 = (f32[4,3200]{1,0:T(4,128)S(1)}, f32[4,3200]{1,0:T(4,128)}, u32[]{:S(2)}) copy-start(f32[4,3200]{1,0:T(4,128)} %get-tuple-element.53) | copy-start | bytes 153604
  207.6 17.0 %collective-permute-start.30 = (bf16[150,128]{1,0:T(8,128)(2,1)S(1)}, bf16[150,128]{1,0:T(8,128)(2,1)S(1)}, u32[]{:S(2)}, u32[]{:S(2)}) collective-permute-start(bf16[150,128]{1,0:T(8,128)(2,1)S(1)} %pad_maximum_fusion.5), channel_id=1, source_target_pairs={{0,128},{4,388},{8,136},{12,396},{16,144},{20,404},{24,152},{28,41... | collective-permute-start | bytes 115208 | tf_op jit(solution)/shard_map/ppermute | solution.py:38
  212.3 14.9 %collective-permute-start.31 = (bf16[150,128]{1,0:T(8,128)(2,1)S(1)}, bf16[150,128]{1,0:T(8,128)(2,1)S(1)}, u32[]{:S(2)}, u32[]{:S(2)}) collective-permute-start(bf16[150,128]{1,0:T(8,128)(2,1)S(1)} %pad_maximum_fusion.6), channel_id=1, source_target_pairs={{0,256},{4,260},{8,264},{12,268},{16,272},{20,276},{24,280},{28,28... | collective-permute-start | bytes 115208 | tf_op jit(solution)/shard_map/ppermute | solution.py:38
  219.6 9.8 %collective-permute-start.32 = (bf16[150,128]{1,0:T(8,128)(2,1)S(1)}, bf16[150,128]{1,0:T(8,128)(2,1)S(1)}, u32[]{:S(2)}, u32[]{:S(2)}) collective-permute-start(bf16[150,128]{1,0:T(8,128)(2,1)S(1)} %pad_maximum_fusion.7), channel_id=1, source_target_pairs={{0,384},{4,132},{8,392},{12,140},{16,400},{20,148},{24,408},{28,15... | collective-permute-start | bytes 115208 | tf_op jit(solution)/shard_map/ppermute | solution.py:38
  230.2 10.8 %all-to-all-start = ((f32[4,10,640]{2,1,0:T(8,128)}), f32[4,10,640]{2,1,0:T(8,128)S(1)}, u32[]{:S(2)}, u32[]{:S(2)}) async-start(f32[4,10,640]{2,1,0:T(8,128)} %broadcast_in_dim.37), calls=%async_computation | async-start | bytes 327680 | tf_op jit(solution)/shard_map/all_to_all | solution.py:421

commit v4 on v3

--- a/solution.py
+++ b/solution.py
@@ -1,5 +1,6 @@
 import jax
 import jax.numpy as jnp
+import numpy as np
 from jax import lax
 from jax.experimental import pallas as pl
 from jax.experimental.pallas import tpu as pltpu
@@ -20,6 +21,7 @@
 UNITS = (5, 8, 6)
 WEIGHT_ROWS = 240 + 256 + 192
 TERM_ROWS = 400 + 240
+INVERSE_AT, POSITION_AT = (0, 1536, 2560), (3584, 4864, 5888)
 VMEM_LIMIT = 56 * 2**20
 F32, BF16 = jnp.float32, jnp.bfloat16
 
@@ -68,7 +70,7 @@
         return total
 
     a = [add(pieces[x], push(pieces[4 + x], dc=1)).astype(BF16) for x in range(4)]
-    arrived, beside = lax.optimization_barrier(([push(a[x], dx=x) for x in (1, 2, 3)], beside))
+    arrived, beside = lax.optimization_barrier(([push(a[x], dx=x) for x in (2, 1, 3)], beside))
     total = add(a[0], *arrived).astype(BF16)
     parts = [total[n * TERM_ROWS : (n + 1) * TERM_ROWS] for n in range(4)]
     total = add(parts[0], *(push(parts[n], dz=NEAR[n]) for n in (1, 2, 3))).astype(BF16)
@@ -93,6 +95,10 @@
 
 def mm_nt(a, b):
     return lax.dot_general(a, b, (((1,), (1,)), ((), ())), preferred_element_type=F32)
+
+
+def mm_tn(a, b, precision=None):
+    return lax.dot_general(a, b, (((0,), (0,)), ((), ())), precision=precision, preferred_element_type=F32)
 
 
 def frame_slot(row):
@@ -105,25 +111,25 @@
 
 def rotate_kernel(*refs):
     pieces = refs[:8]
-    rot, place, target, local, inv0, inv1, inv2 = refs[8:15]
-    m0, m1, m2, turned_grad = refs[15:19]
-    feats, srcf, dstf, gradf, n0, n1, n2 = refs[19:]
+    rot, edge_rows, local, maps = refs[8:12]
+    m0, m1, m2, turned_grad = refs[12:16]
+    feats, srcf, dstf, gradf, n0, n1, n2 = refs[16:]
     for k, piece in enumerate(pieces):
         for near in range(4):
             row = k * 64 + near * 16
             for u in range(LCOEF):
                 at = near * FAR_ROWS + u * 16
                 feats[row : row + 16, u * CH : (u + 1) * CH] = piece[at : at + 16, :]
-    source_hot = hot(place[...], (EDGES, 512), 1)
-    t = target[...]
-    lanes = lax.broadcasted_iota(jnp.int32, (EDGES, 16), 1)
-    feat_hot = jnp.where(lanes == t, F32(1), F32(0)).astype(BF16)
-    grad_hot = jnp.where((lanes == t + 4) | (lanes == t + 8), F32(1), F32(0)).astype(BF16)
+    source_hot = hot(edge_rows[0:1, :], (512, EDGES), 0)
+    t = edge_rows[1:2, :]
+    rows = lax.broadcasted_iota(jnp.int32, (16, EDGES), 0)
+    feat_hot = jnp.where(rows == t, F32(1), F32(0)).astype(BF16)
+    grad_hot = jnp.where((rows == t + 4) | (rows == t + 8), F32(1), F32(0)).astype(BF16)
     for first in range(0, FULL, 640):
         cut = slice(first, first + 640)
-        srcf[:, cut] = mm(source_hot, feats[:, cut]).astype(BF16)
-        dstf[:, cut] = mm(feat_hot, local[:, cut]).astype(BF16)
-        gradf[:, cut] = mm(grad_hot, local[:, cut])
+        srcf[:, cut] = mm_tn(source_hot, feats[:, cut]).astype(BF16)
+        dstf[:, cut] = mm_tn(feat_hot, local[:, cut]).astype(BF16)
+        gradf[:, cut] = mm_tn(grad_hot, local[:, cut])
 
     stacked = (n0, n1, n2)
 
@@ -150,19 +156,19 @@
         return carry
 
     lax.fori_loop(0, EDGES // BLOCK, turn, 0)
-    for natural, ordered, inverse in ((n0, m0, inv0), (n1, m1, inv1), (n2, m2, inv2)):
+    for natural, ordered, start in ((n0, m0, INVERSE_AT[0]), (n1, m1, INVERSE_AT[1]), (n2, m2, INVERSE_AT[2])):
         depth = natural.shape[1]
         for first in range(0, ordered.shape[1], 256):
-            cut = slice(first, first + 256)
-            ordered[:, cut] = mm(natural[...], hot(inverse[:, cut], (depth, 256), 0)).astype(BF16)
+            inverse = maps[:, start + first : start + first + 256]
+            ordered[:, first : first + 256] = mm(natural[...], hot(inverse, (depth, 256), 0)).astype(BF16)
 
 
 def layer_kernel(*refs):
     pieces = refs[:8]
-    m0, m1, m2, turned_grad, rot, bias, target, live_ref, alpha_ref, place, pos0, pos1, pos2 = refs[8:21]
-    terms_out = refs[21:29]
-    scaled_out, grad_dst = refs[29:31]
-    w0, w1, w2, values, d0, d1, d2, p0, p1, p2, g0, g1, g2, src_terms = refs[31:]
+    m0, m1, m2, turned_grad, rot, bias, alpha_ref, edge_rows, maps = refs[8:17]
+    terms_out = refs[17:25]
+    scaled_out, grad_dst = refs[25:27]
+    w0, w1, w2, values, d0, d1, d2, p0, p1, p2, g0, g1, g2, src_terms = refs[27:]
     for k, piece in enumerate(pieces):
         for near in range(4):
             at = near * WEIGHT_ROWS
@@ -184,15 +190,15 @@
     v = z0[:, :CH]
     sigma = 1.0 / (1.0 + jnp.exp(-v))
     alpha = alpha_ref[...]
-    logits = bias[...] + mm((v * sigma).astype(BF16), alpha)
-    live = live_ref[...] > 0
-    t = target[...]
+    logits = bias[...] + mm_nt(alpha, (v * sigma).astype(BF16))
+    t = edge_rows[1:2, :]
+    live = edge_rows[2:3, :] > 0
     members = [live & (t == n) for n in range(4)]
 
     def over_targets(array, empty, reduce):
-        result = jnp.zeros((EDGES, HEADS), F32)
+        result = jnp.zeros((HEADS, EDGES), F32)
         for member in members:
-            one = reduce(jnp.where(member, array, F32(empty)), axis=0, keepdims=True)
+            one = reduce(jnp.where(member, array, F32(empty)), axis=1, keepdims=True)
             result = jnp.where(member, one, result)
         return result
 
@@ -205,7 +211,7 @@
         == lax.broadcasted_iota(jnp.int32, (HEADS, CH), 0)
     )
     spread = jnp.where(head_of, F32(1), F32(0))
-    scale = jnp.dot(attn, spread, precision=lax.Precision.HIGHEST, preferred_element_type=F32)
+    scale = mm_tn(attn, spread, lax.Precision.HIGHEST)
     dscale = jnp.zeros((EDGES, CH), F32)
     for row in range(MCOEF):
         cut = slice(row * CH, (row + 1) * CH)
@@ -213,13 +219,10 @@
         dscale = dscale + turned_grad[:, cut] * value
         scaled_out[:, cut] = (scale * value).astype(BF16)
     dattn = lax.dot_general(
-        dscale, spread, (((1,), (1,)), ((), ())), precision=lax.Precision.HIGHEST, preferred_element_type=F32
+        spread, dscale, (((1,), (1,)), ((), ())), precision=lax.Precision.HIGHEST, preferred_element_type=F32
     )
     dlogits = attn * (dattn - over_targets(attn * dattn, 0.0, jnp.sum))
-    dscalars = lax.dot_general(
-        dlogits, alpha.astype(F32), (((1,), (1,)), ((), ())), precision=lax.Precision.HIGHEST,
-        preferred_element_type=F32,
-    ).astype(BF16).astype(F32)
+    dscalars = mm_tn(dlogits, alpha.astype(F32), lax.Precision.HIGHEST).astype(BF16).astype(F32)
     dv = dscalars * (sigma * (1.0 + v * (1.0 - sigma)))
     for row in range(MCOEF):
         cut = slice(row * CH, (row + 1) * CH)
@@ -244,11 +247,11 @@
             for u in range(5):
                 at = near * TERM_ROWS + 400 + u * 48
                 terms_out[k][at : at + 48, :] = dw[row : row + 48, u * CH : (u + 1) * CH].astype(BF16)
-    for d, w, p, g, pos in ((d0, w0, p0, g0, pos0), (d1, w1, p1, g1, pos1), (d2, w2, p2, g2, pos2)):
+    for d, w, p, g, start in zip((d0, d1, d2), (w0, w1, w2), (p0, p1, p2), (g0, g1, g2), POSITION_AT):
         p[...] = mm_nt(d[...], w[...]).astype(BF16)
         for first in range(0, g.shape[1], 256):
-            cut = slice(first, first + 256)
-            g[:, cut] = mm(p[...], hot(pos[:, cut], (w.shape[0], 256), 0)).astype(BF16)
+            position = maps[:, start + first : start + first + 256]
+            g[:, first : first + 256] = mm(p[...], hot(position, (w.shape[0], 256), 0)).astype(BF16)
     stacked = (g0, g1, g2)
     for row in range(MCOEF):
         array, base, column = frame_slot(row)
@@ -274,7 +277,7 @@
         return carry
 
     lax.fori_loop(0, EDGES // BLOCK, turn, 0)
-    chosen = hot(place[...], (512, EDGES), 0)
+    chosen = hot(edge_rows[0:1, :], (512, EDGES), 0)
     for first in range(0, FULL, 640):
         block = mm(chosen, src_terms[:, first : first + 640]).astype(BF16)
         for k in range(8):
@@ -285,7 +288,7 @@
                     terms_out[k][at : at + 16, :] = block[row : row + 16, n * CH : (n + 1) * CH]
 
 
-def nodes_kernel(rot, scaled, grad_dst, target, node_out, grad_local, back, terms):
+def nodes_kernel(rot, scaled, grad_dst, edge_rows, node_out, grad_local, back, terms):
     def turn(step, carry):
         e0 = pl.multiple_of(step * BLOCK, BLOCK)
         rows_here = pl.ds(e0, BLOCK)
@@ -307,7 +310,7 @@
         return carry
 
     lax.fori_loop(0, EDGES // BLOCK, turn, 0)
-    chosen = hot(target[...], (16, EDGES), 0)
+    chosen = hot(edge_rows[1:2, :], (16, EDGES), 0)
     for first in range(0, FULL, 640):
         cut = slice(first, first + 640)
         node_out[:, cut] = mm(chosen, back[:, cut])[:4].astype(BF16)
@@ -333,6 +336,21 @@
     return array.reshape(rows, width // CH, CH).transpose(1, 0, 2).reshape(-1, CH)
 
 
+def index_maps(me):
+    inverse, position = [], []
+    for rows, depth in zip((10, 8, 6), DEPTHS):
+        p = np.arange(32 * depth)
+        inside = p % depth
+        inverse.append((p // depth, np.minimum(inside // rows, 3), np.full_like(p, rows), inside % rows, inside < 4 * rows))
+        k = np.arange(128 * rows)
+        position.append((k // rows, np.full_like(k, depth), np.full_like(k, rows), k % rows))
+    place, far, rows, rest, inside = (jnp.asarray(np.concatenate(a), jnp.int32) for a in zip(*inverse))
+    natural = jnp.where(inside > 0, block_owner(place, far, me) * rows + rest, -1)
+    owner, depth, rows, rest = (jnp.asarray(np.concatenate(a), jnp.int32) for a in zip(*position))
+    block, far = block_place(owner, me)
+    return jnp.concatenate([natural, block * depth + far * rows + rest])[None]
+
+
 def local(
     node_feat, rotation, source_owner, source_row, target_row, live_count, edge_bias,
     w_m0, w_m1, w_m2, w_alpha, out_grad,
@@ -340,10 +358,9 @@
     me = lax.axis_index("edge")
     features = node_feat[0]
     rotor_rows = rotation[0]
-    targets = target_row[0]
     live = (jnp.arange(EDGES, dtype=jnp.int32) < live_count[0, 0]).astype(jnp.int32)
     block, far = block_place(source_owner[0, :, 0], me)
-    place = block * 16 + far * 4 + source_row[0]
+    edge_rows = jnp.stack([block * 16 + far * 4 + source_row[0], target_row[0], live], axis=0)
 
     w1 = jnp.concatenate([w_m1[0], w_m1[1]], axis=1)
     w2 = jnp.concatenate([w_m2[0], w_m2[1]], axis=1)
@@ -364,21 +381,7 @@
     weight_x = x_pieces(jnp.concatenate([b[FAR_ROWS:] for b in blocks], axis=0))
     feature_pieces = feature_x + tuple(pull(a, dc=1) for a in feature_x)
 
-    def inverse_of(rows, depth):
-        p = jnp.arange(32 * depth, dtype=jnp.int32)
-        inside = p % depth
-        owner = block_owner(p // depth, inside // rows, me)
-        return jnp.where(inside < 4 * rows, owner * rows + inside % rows, -1)[None]
-
-    def position_of(rows, depth):
-        k = jnp.arange(128 * rows, dtype=jnp.int32)
-        block, far = block_place(k // rows, me)
-        return (block * depth + far * rows + k % rows)[None]
-
-    sizes = tuple(zip((10, 8, 6), DEPTHS))
-    inverses = [inverse_of(*s) for s in sizes]
-    positions = [position_of(*s) for s in sizes]
-
+    maps = index_maps(me)
     cotangent = out_grad[0]
     high = lax.reduce_precision(cotangent, 8, 7)
     own_rows = jnp.concatenate(
@@ -387,20 +390,18 @@
 
     m0, m1, m2, turned_grad = call(
         rotate_kernel, "rotate",
-        (*feature_pieces, rotor_rows, place[:, None], targets[:, None], own_rows, *inverses),
+        (*feature_pieces, rotor_rows, edge_rows, own_rows, maps),
         [((160, 1536), BF16), ((320, 1024), BF16), ((320, 1024), BF16), ((160, MCOEF * CH), F32)],
         [((512, FULL), BF16), ((160, FULL), BF16), ((160, FULL), BF16), ((160, FULL), F32),
          ((160, 1280), BF16), ((320, 1024), BF16), ((320, 768), BF16)],
         3_000_000_000,
     )
-    turned, others = lax.optimization_barrier(((m0, m1, m2, turned_grad), weight_x[1:]))
-    m0, m1, m2, turned_grad = turned
-    weight_x = weight_x[:1] + tuple(others)
+    others = [lax.optimization_barrier((m0, weight_x[x]))[1] for x in (1, 2, 3)]
+    weight_x = (weight_x[0], *others)
     weight_pieces = weight_x + tuple(pull(a, dc=1) for a in weight_x)
     outs = call(
         layer_kernel, "layer",
-        (*weight_pieces, m0, m1, m2, turned_grad, rotor_rows, edge_bias[0], targets[:, None], live[:, None],
-         w_alpha, place[None], *positions),
+        (*weight_pieces, m0, m1, m2, turned_grad, rotor_rows, edge_bias[0].T, w_alpha.T, edge_rows, maps),
         [((4 * TERM_ROWS, CH), BF16)] * 8 + [((160, MCOEF * CH), BF16), ((160, MCOEF * CH), BF16)],
         [((1536, 640), BF16), ((1024, 1024), BF16), ((1024, 768), BF16), ((160, MCOEF * CH), BF16),
          ((160, 640), BF16), ((320, 1024), BF16), ((320, 768), BF16),
@@ -410,7 +411,7 @@
     )
     term_pieces, (scaled, grad_dst) = outs[:8], outs[8:]
     node_out, grad_local = call(
-        nodes_kernel, "nodes", (rotor_rows, scaled, grad_dst, targets[None]),
+        nodes_kernel, "nodes", (rotor_rows, scaled, grad_dst, edge_rows),
         [((4, FULL), BF16), ((4, FULL), F32)], [((160, FULL), BF16), ((160, FULL), BF16)],
         600_000_000,
     )

time: 244 us -> 234 us (0.959)
  waiting for transfers between devices: 64.7 us -> 59.1 us
  other arithmetic: 11.2 us -> 7.5 us
    add x5 -> x2, other arithmetic: 3.85 us -> 0.11 us  [the longest x1 0.05 us: index_maps(): return jnp.concatenate([natural, block * depth + far * rows + rest])[None]]
    ppermute x13, waiting for transfers between devices: 32.6 us -> 29.7 us  [push(): lax.ppermute(a, 'edge', [(i, where_to(i, dz, dx, dc)) for i in range(128)])]
    ppermute x20, waiting for transfers between devices: 26.6 us -> 23.9 us  [pull(): lax.ppermute(a, 'edge', [(where_to(i, dz, dx, dc), i) for i in range(128)])]
  transfers between devices with their start and end apart: 34 -> 34, of which waited for: 14 -> 15; matrix products, arithmetic and copies ran while one was open for 5% -> 3% of each run, Pallas kernels for 6% -> 6%
where the time goes in v4:
time: 234 us; the launch traced here: 232 us
  starting transfers between devices  122 us (52%)
  waiting for transfers between devices  59.1 us (25%)
  Pallas kernels  32.8 us (14%)
  local copies, waits for them, and re-layouts  7.74 us (3%)
  other arithmetic  7.5 us (3%)
  between operations  2.65 us (1%)
    ppermute x20, starting transfers between devices, pull(): lax.ppermute(a, 'edge', [(where_to(i, dz, dx, dc), i) for i in range(128)])  71.5 us
    ppermute x13, starting transfers between devices, push(): lax.ppermute(a, 'edge', [(i, where_to(i, dz, dx, dc)) for i in range(128)])  45.6 us
    pallas_call x3, Pallas kernels, call(): pl.pallas_call(kernel, out_shape=tuple((jax.ShapeDtypeStruct(s, t) for s,...  32.8 us
    ppermute x13, waiting for transfers between devices, push(): lax.ppermute(a, 'edge', [(i, where_to(i, dz, dx, dc)) for i in range(128)])  29.7 us
    ppermute x20, waiting for transfers between devices, pull(): lax.ppermute(a, 'edge', [(where_to(i, dz, dx, dc), i) for i in range(128)])  23.9 us
    all_to_all x1, waiting for transfers between devices, local(): lax.all_to_all(jnp.broadcast_to(shard, (n_rep, 10, 640)), 'rep', split_ax...  5.51 us
  transfers between devices with their start and end apart: 34, of which 15 were waited for; matrix products, arithmetic and copies ran while one was open for 3% of the time, Pallas kernels for 6%

profile of v4, /device:TPU:6, one launch (start us, length us, event | category | flops | bytes accessed | tf_op | source)
XLA Modules:
  0.0 231.5 jit_solution(1666280084265240266)
XLA Ops:
  0.6 0.7 slice_bitcast_fusion.4
  1.3 0.8 fusion.48
  2.2 0.8 reshape.530
  3.0 0.8 reshape_squeeze.3
  3.9 9.1 %collective-permute-start.2 = (bf16[250,128]{1,0:T(8,128)(2,1)S(1)}, bf16[250,128]{1,0:T(8,128)(2,1)S(1)}, u32[]{:S(2)}, u32[]{:S(2)}) collective-permute-start(bf16[250,128]{1,0:T(8,128)(2,1)S(1)} %pad_maximum_fusion.3), channel_id=1, source_target_pairs={{384,0},{132,4},{392,8},{140,12},{400,16},{148,20},{408,24},{156,2... | collective-permute-start | bytes 192008 | tf_op jit(solution)/shard_map/ppermute | solution.py:36
  13.0 10.9 %collective-permute-start.1 = (bf16[250,128]{1,0:T(8,128)(2,1)S(1)}, bf16[250,128]{1,0:T(8,128)(2,1)S(1)}, u32[]{:S(2)}, u32[]{:S(2)}) collective-permute-start(bf16[250,128]{1,0:T(8,128)(2,1)S(1)} %pad_maximum_fusion.3), channel_id=1, source_target_pairs={{256,0},{260,4},{264,8},{268,12},{272,16},{276,20},{280,24},{284,2... | collective-permute-start | bytes 192008 | tf_op jit(solution)/shard_map/ppermute | solution.py:36
  23.9 5.5 %collective-permute-start = (bf16[250,128]{1,0:T(8,128)(2,1)S(1)}, bf16[250,128]{1,0:T(8,128)(2,1)S(1)}, u32[]{:S(2)}, u32[]{:S(2)}) collective-permute-start(bf16[250,128]{1,0:T(8,128)(2,1)S(1)} %pad_maximum_fusion.3), channel_id=1, source_target_pairs={{128,0},{388,4},{136,8},{396,12},{144,16},{404,20},{152,24},{412,2... | collective-permute-start | bytes 192008 | tf_op jit(solution)/shard_map/ppermute | solution.py:36
  29.4 0.8 reduce-precision_convert_fusion
  30.4 1.5 maximum_maximum_fusion.refs_10_
  31.9 0.8 fusion.12
  33.0 2.2 collective-permute-done
  36.3 2.3 %collective-permute-start.5 = (bf16[1088,128]{1,0:T(8,128)(2,1)S(1)}, bf16[1088,128]{1,0:T(8,128)(2,1)S(1)}, u32[]{:S(2)}, u32[]{:S(2)}) collective-permute-start(bf16[1088,128]{1,0:T(8,128)(2,1)S(1)} %pad_maximum_fusion.1), channel_id=1, source_target_pairs={{480,0},{36,4},{488,8},{44,12},{496,16},{52,20},{504,24},{60,28},{... | collective-permute-start | bytes 835592 | tf_op jit(solution)/shard_map/ppermute | solution.py:36
  38.6 5.8 %collective-permute-start.4 = (bf16[1088,128]{1,0:T(8,128)(2,1)S(1)}, bf16[1088,128]{1,0:T(8,128)(2,1)S(1)}, u32[]{:S(2)}, u32[]{:S(2)}) collective-permute-start(bf16[1088,128]{1,0:T(8,128)(2,1)S(1)} %pad_maximum_fusion.1), channel_id=1, source_target_pairs={{64,0},{452,4},{72,8},{460,12},{80,16},{468,20},{88,24},{476,28},{... | collective-permute-start | bytes 835592 | tf_op jit(solution)/shard_map/ppermute | solution.py:36
  44.4 3.4 %collective-permute-start.3 = (bf16[1088,128]{1,0:T(8,128)(2,1)S(1)}, bf16[1088,128]{1,0:T(8,128)(2,1)S(1)}, u32[]{:S(2)}, u32[]{:S(2)}) collective-permute-start(bf16[1088,128]{1,0:T(8,128)(2,1)S(1)} %pad_maximum_fusion.1), channel_id=1, source_target_pairs={{32,0},{484,4},{40,8},{492,12},{48,16},{500,20},{56,24},{508,28},{... | collective-permute-start | bytes 835592 | tf_op jit(solution)/shard_map/ppermute | solution.py:36
  49.3 2.1 collective-permute-done.4
  51.4 3.0 %collective-permute-done.3 = bf16[1088,128]{1,0:T(8,128)(2,1)S(1)} collective-permute-done((bf16[1088,128]{1,0:T(8,128)(2,1)S(1)}, bf16[1088,128]{1,0:T(8,128)(2,1)S(1)}, u32[]{:S(2)}, u32[]{:S(2)}) %collective-permute-start.3) | collective-permute-done | bytes 278560 | tf_op jit(solution)/shard_map/ppermute | solution.py:36
  54.5 2.4 %collective-permute-start.8 = (bf16[1600,128]{1,0:T(8,128)(2,1)S(1)}, bf16[1600,128]{1,0:T(8,128)(2,1)S(1)}, u32[]{:S(2)}, u32[]{:S(2)}) collective-permute-start(bf16[1600,128]{1,0:T(8,128)(2,1)S(1)} %pad_maximum_fusion.refs_0_), channel_id=1, source_target_pairs={{24,0},{28,4},{0,8},{4,12},{8,16},{12,20},{16,24},{20,28},{56,32},... | collective-permute-start | bytes 1228808 | tf_op jit(solution)/shard_map/ppermute | solution.py:36
  56.9 2.0 collective-permute-start.9
  58.9 4.3 %collective-permute-start.7 = (bf16[1600,128]{1,0:T(8,128)(2,1)S(1)}, bf16[1600,128]{1,0:T(8,128)(2,1)S(1)}, u32[]{:S(2)}, u32[]{:S(2)}) collective-permute-start(bf16[1600,128]{1,0:T(8,128)(2,1)S(1)} %pad_maximum_fusion.refs_0_), channel_id=1, source_target_pairs={{16,0},{20,4},{24,8},{28,12},{0,16},{4,20},{8,24},{12,28},{48,32},... | collective-permute-start | bytes 1228808 | tf_op jit(solution)/shard_map/ppermute | solution.py:36
  63.2 1.9 collective-permute-start.6
  65.2 3.5 %collective-permute-done.8.refs_3_ = bf16[1600,128]{1,0:T(8,128)(2,1)S(1)} collective-permute-done((bf16[1600,128]{1,0:T(8,128)(2,1)S(1)}, bf16[1600,128]{1,0:T(8,128)(2,1)S(1)}, u32[]{:S(2)}, u32[]{:S(2)}) %collective-permute-start.8) | collective-permute-done | bytes 409632 | tf_op jit(solution)/shard_map/ppermute | solution.py:36
  68.7 1.9 collective-permute-start.12
  70.7 3.0 %collective-permute-start.15 = (bf16[2752,128]{1,0:T(8,128)(2,1)S(1)}, bf16[2752,128]{1,0:T(8,128)(2,1)S(1)}, u32[]{:S(2)}, u32[]{:S(2)}) collective-permute-start(bf16[2752,128]{1,0:T(8,128)(2,1)S(1)} %slice_dynamic-update-slice_fusion.refs_0_), channel_id=1, source_target_pairs={{24,0},{28,4},{0,8},{4,12},{8,16},{12,20},{16,24},{20,28},{56,32},... | collective-permute-start | bytes 2113544 | tf_op jit(solution)/shard_map/ppermute | solution.py:36
  73.7 3.7 %collective-permute-start.14 = (bf16[2752,128]{1,0:T(8,128)(2,1)S(1)}, bf16[2752,128]{1,0:T(8,128)(2,1)S(1)}, u32[]{:S(2)}, u32[]{:S(2)}) collective-permute-start(bf16[2752,128]{1,0:T(8,128)(2,1)S(1)} %slice_dynamic-update-slice_fusion.refs_0_), channel_id=1, source_target_pairs={{16,0},{20,4},{24,8},{28,12},{0,16},{4,20},{8,24},{12,28},{48,32},... | collective-permute-start | bytes 2113544 | tf_op jit(solution)/shard_map/ppermute | solution.py:36
  77.4 2.7 %collective-permute-start.13 = (bf16[2752,128]{1,0:T(8,128)(2,1)S(1)}, bf16[2752,128]{1,0:T(8,128)(2,1)S(1)}, u32[]{:S(2)}, u32[]{:S(2)}) collective-permute-start(bf16[2752,128]{1,0:T(8,128)(2,1)S(1)} %slice_dynamic-update-slice_fusion.refs_0_), channel_id=1, source_target_pairs={{8,0},{12,4},{16,8},{20,12},{24,16},{28,20},{0,24},{4,28},{40,32},... | collective-permute-start | bytes 2113544 | tf_op jit(solution)/shard_map/ppermute | solution.py:36
  80.1 3.2 %collective-permute-done.6.refs_1_ = bf16[1600,128]{1,0:T(8,128)(2,1)S(1)} collective-permute-done((bf16[1600,128]{1,0:T(8,128)(2,1)S(1)}, bf16[1600,128]{1,0:T(8,128)(2,1)S(1)}, u32[]{:S(2)}, u32[]{:S(2)}) %collective-permute-start.6) | collective-permute-done | bytes 409632 | tf_op jit(solution)/shard_map/ppermute | solution.py:36
  83.4 1.9 collective-permute-start.11
  85.3 2.4 %collective-permute-start.10 = (bf16[1600,128]{1,0:T(8,128)(2,1)S(1)}, bf16[1600,128]{1,0:T(8,128)(2,1)S(1)}, u32[]{:S(2)}, u32[]{:S(2)}) collective-permute-start(bf16[1600,128]{1,0:T(8,128)(2,1)S(1)} %collective-permute-done.6.refs_1_), channel_id=1, source_target_pairs={{4,0},{0,4},{12,8},{8,12},{20,16},{16,20},{28,24},{24,28},{36,32},... | collective-permute-start | bytes 1228808 | tf_op jit(solution)/shard_map/ppermute | solution.py:36
  88.4 1.9 collective-permute-start.16
  90.5 0.7 copy-done.30
  91.1 9.6 %rotate.1 = (bf16[160,1536]{1,0:T(8,128)(2,1)}, bf16[320,1024]{1,0:T(8,128)(2,1)}, bf16[320,1024]{1,0:T(8,128)(2,1)}, f32[160,2432]{1,0:T(8,128)}) custom-call(bf16[1600,128]{1,0:T(8,128)(2,1)} %copy-done.3, bf16[1600,128]{1,0:T(8,128)(2,1)} %copy-done.27, bf16[1600,128]{1,0:T(8,128)(2,1)} %copy-done.26, bf16[1600,128]{1,0:T(8,128)(2,1)} %copy-done.24, ...), custom_call_target="tpu_custom_call" | custom-call | flops 3000000000 | bytes 3559744 | tf_op jit(solution)/shard_map/rotate/pallas_call | solution.py:322
  100.8 2.4 %collective-permute-start.19 = (bf16[2752,128]{1,0:T(8,128)(2,1)S(1)}, bf16[2752,128]{1,0:T(8,128)(2,1)S(1)}, u32[]{:S(2)}, u32[]{:S(2)}) collective-permute-start(bf16[2752,128]{1,0:T(8,128)(2,1)S(1)} %collective-permute-done.15.refs_3_), channel_id=1, source_target_pairs={{4,0},{0,4},{12,8},{8,12},{20,16},{16,20},{28,24},{24,28},{36,32},... | collective-permute-start | bytes 2113544 | tf_op jit(solution)/shard_map/ppermute | solution.py:36
  103.2 1.9 collective-permute-start.18
  105.2 7.9 %collective-permute-done.13.refs_1_ = bf16[2752,128]{1,0:T(8,128)(2,1)S(1)} collective-permute-done((bf16[2752,128]{1,0:T(8,128)(2,1)S(1)}, bf16[2752,128]{1,0:T(8,128)(2,1)S(1)}, u32[]{:S(2)}, u32[]{:S(2)}) %collective-permute-start.13) | collective-permute-done | bytes 704544 | tf_op jit(solution)/shard_map/ppermute | solution.py:36
  113.1 2.1 collective-permute-start.17
  115.2 1.9 collective-permute-done.17.refs_5_
  117.2 0.9 copy-done.22
  118.0 17.9 %layer.1 = (bf16[2560,128]{1,0:T(8,128)(2,1)}, bf16[2560,128]{1,0:T(8,128)(2,1)}, bf16[2560,128]{1,0:T(8,128)(2,1)}, bf16[2560,128]{1,0:T(8,128)(2,1)}, bf16[256...) custom-call(bf16[2752,128]{1,0:T(8,128)(2,1)} %copy-done.12, ...), custom_call_target="tpu_custom_call" | custom-call | flops 5000000000 | bytes 9182528 | tf_op jit(solution)/shard_map/layer/pallas_call | solution.py:322
  136.0 2.2 collective-permute-start.20
  138.1 2.3 collective-permute-start.22
  140.4 2.0 collective-permute-start.24
  142.5 1.3 add_convert_fusion.4
  143.8 4.5 %collective-permute-start.21 = (bf16[2560,128]{1,0:T(8,128)(2,1)S(1)}, bf16[2560,128]{1,0:T(8,128)(2,1)S(1)}, u32[]{:S(2)}, u32[]{:S(2)}) collective-permute-start(bf16[2560,128]{1,0:T(8,128)(2,1)S(1)} %add_convert_fusion.4), channel_id=1, source_target_pairs={{0,16},{4,20},{8,24},{12,28},{16,0},{20,4},{24,8},{28,12},{32,48},... | collective-permute-start | bytes 1966088 | tf_op jit(solution)/shard_map/ppermute | solution.py:40
  148.5 3.3 %collective-permute-start.23 = (bf16[2560,128]{1,0:T(8,128)(2,1)S(1)}, bf16[2560,128]{1,0:T(8,128)(2,1)S(1)}, u32[]{:S(2)}, u32[]{:S(2)}) collective-permute-start(bf16[2560,128]{1,0:T(8,128)(2,1)S(1)} %add_convert_fusion.3), channel_id=1, source_target_pairs={{0,8},{4,12},{8,16},{12,20},{16,24},{20,28},{24,0},{28,4},{32,40},... | collective-permute-start | bytes 1966088 | tf_op jit(solution)/shard_map/ppermute | solution.py:40
  152.0 2.8 %collective-permute-start.25 = (bf16[2560,128]{1,0:T(8,128)(2,1)S(1)}, bf16[2560,128]{1,0:T(8,128)(2,1)S(1)}, u32[]{:S(2)}, u32[]{:S(2)}) collective-permute-start(bf16[2560,128]{1,0:T(8,128)(2,1)S(1)} %add_convert_fusion.2), channel_id=1, source_target_pairs={{0,24},{4,28},{8,0},{12,4},{16,8},{20,12},{24,16},{28,20},{32,56},... | collective-permute-start | bytes 1966088 | tf_op jit(solution)/shard_map/ppermute | solution.py:40
  154.8 1.9 collective-permute-start.26
  156.7 5.3 %nodes.1 = (bf16[4,3200]{1,0:T(4,128)(2,1)}, f32[4,3200]{1,0:T(4,128)}) custom-call(bf16[160,475]{1,0:T(8,128)(2,1)} %bitcast.91, bf16[160,2432]{1,0:T(8,128)(2,1)} %get-tuple-element.40.scaled, bf16[160,2432]{1,0:T(8,128)(2,1)} %get-tuple-element.41.grad_dst, s32[3,160]{1,0:T(4,128)} %pad_add_fusion.1.refs_9_.refs_15_.edge_rows), custom_call_target="tpu_custom_call" | custom-call | flops 600000000 | bytes 1710400 | tf_op jit(solution)/shard_map/nodes/pallas_call | solution.py:322
  162.0 2.9 %collective-permute-done.21 = bf16[2560,128]{1,0:T(8,128)(2,1)S(1)} collective-permute-done((bf16[2560,128]{1,0:T(8,128)(2,1)S(1)}, bf16[2560,128]{1,0:T(8,128)(2,1)S(1)}, u32[]{:S(2)}, u32[]{:S(2)}) %collective-permute-start.21) | collective-permute-done | bytes 655392 | tf_op jit(solution)/shard_map/ppermute | solution.py:40
  164.9 11.5 %collective-permute-done.23 = bf16[2560,128]{1,0:T(8,128)(2,1)S(1)} collective-permute-done((bf16[2560,128]{1,0:T(8,128)(2,1)S(1)}, bf16[2560,128]{1,0:T(8,128)(2,1)S(1)}, u32[]{:S(2)}, u32[]{:S(2)}) %collective-permute-start.23) | collective-permute-done | bytes 655392 | tf_op jit(solution)/shard_map/ppermute | solution.py:40
  176.4 2.0 collective-permute-done.25
  178.8 2.4 %collective-permute-start.27 = (bf16[640,128]{1,0:T(8,128)(2,1)S(1)}, bf16[640,128]{1,0:T(8,128)(2,1)S(1)}, u32[]{:S(2)}, u32[]{:S(2)}) collective-permute-start(bf16[640,128]{1,0:T(8,128)(2,1)S(1)} %get-tuple-element.51), channel_id=1, source_target_pairs={{0,32},{4,484},{8,40},{12,492},{16,48},{20,500},{24,56},{28,508},{... | collective-permute-start | bytes 491528 | tf_op jit(solution)/shard_map/ppermute | solution.py:40
  181.2 5.1 %collective-permute-start.29 = (bf16[640,128]{1,0:T(8,128)(2,1)S(1)}, bf16[640,128]{1,0:T(8,128)(2,1)S(1)}, u32[]{:S(2)}, u32[]{:S(2)}) collective-permute-start(bf16[640,128]{1,0:T(8,128)(2,1)S(1)} %get-tuple-element.52), channel_id=1, source_target_pairs={{0,480},{4,36},{8,488},{12,44},{16,496},{20,52},{24,504},{28,60},{... | collective-permute-start | bytes 491528 | tf_op jit(solution)/shard_map/ppermute | solution.py:40
  186.4 2.1 collective-permute-start.28
  188.5 0.6 collective-permute-done.29
  189.2 7.9 %collective-permute-done.28 = bf16[640,128]{1,0:T(8,128)(2,1)S(1)} collective-permute-done((bf16[640,128]{1,0:T(8,128)(2,1)S(1)}, bf16[640,128]{1,0:T(8,128)(2,1)S(1)}, u32[]{:S(2)}, u32[]{:S(2)}) %collective-permute-start.28) | collective-permute-done | bytes 163872 | tf_op jit(solution)/shard_map/ppermute | solution.py:40
  197.5 4.7 %collective-permute-start.30 = (bf16[150,128]{1,0:T(8,128)(2,1)S(1)}, bf16[150,128]{1,0:T(8,128)(2,1)S(1)}, u32[]{:S(2)}, u32[]{:S(2)}) collective-permute-start(bf16[150,128]{1,0:T(8,128)(2,1)S(1)} %pad_maximum_fusion.5), channel_id=1, source_target_pairs={{0,128},{4,388},{8,136},{12,396},{16,144},{20,404},{24,152},{28,41... | collective-permute-start | bytes 115208 | tf_op jit(solution)/shard_map/ppermute | solution.py:40
  202.2 7.2 %collective-permute-start.31 = (bf16[150,128]{1,0:T(8,128)(2,1)S(1)}, bf16[150,128]{1,0:T(8,128)(2,1)S(1)}, u32[]{:S(2)}, u32[]{:S(2)}) collective-permute-start(bf16[150,128]{1,0:T(8,128)(2,1)S(1)} %pad_maximum_fusion.6), channel_id=1, source_target_pairs={{0,256},{4,260},{8,264},{12,268},{16,272},{20,276},{24,280},{28,28... | collective-permute-start | bytes 115208 | tf_op jit(solution)/shard_map/ppermute | solution.py:40
  209.5 5.0 %collective-permute-start.32 = (bf16[150,128]{1,0:T(8,128)(2,1)S(1)}, bf16[150,128]{1,0:T(8,128)(2,1)S(1)}, u32[]{:S(2)}, u32[]{:S(2)}) collective-permute-start(bf16[150,128]{1,0:T(8,128)(2,1)S(1)} %pad_maximum_fusion.7), channel_id=1, source_target_pairs={{0,384},{4,132},{8,392},{12,140},{16,400},{20,148},{24,408},{28,15... | collective-permute-start | bytes 115208 | tf_op jit(solution)/shard_map/ppermute | solution.py:40
  214.6 2.6 %collective-permute-done.31 = bf16[150,128]{1,0:T(8,128)(2,1)S(1)} collective-permute-done((bf16[150,128]{1,0:T(8,128)(2,1)S(1)}, bf16[150,128]{1,0:T(8,128)(2,1)S(1)}, u32[]{:S(2)}, u32[]{:S(2)}) %collective-permute-start.31) | collective-permute-done | bytes 38432 | tf_op jit(solution)/shard_map/ppermute | solution.py:40
  217.1 2.2 collective-permute-done.32
  219.5 0.7 broadcast_in_dim.29
  220.1 4.6 %all-to-all-start = ((f32[4,10,640]{2,1,0:T(8,128)}), f32[4,10,640]{2,1,0:T(8,128)S(1)}, u32[]{:S(2)}, u32[]{:S(2)}) async-start(f32[4,10,640]{2,1,0:T(8,128)} %broadcast_in_dim.29), calls=%async_computation | async-start | bytes 327680 | tf_op jit(solution)/shard_map/all_to_all | solution.py:422
  224.8 0.6 fusion.1
  225.4 5.5 %all-to-all-done = f32[4,10,640]{2,1,0:T(8,128)S(1)} async-done(((f32[4,10,640]{2,1,0:T(8,128)}), f32[4,10,640]{2,1,0:T(8,128)S(1)}, u32[]{:S(2)}, u32[]{:S(2)}) %all-to-all-start) | async-done | bytes 102432 | tf_op jit(solution)/shard_map/all_to_all | solution.py:422
  (167 shorter events, 4.9 us)
Async XLA Ops:
  3.9 28.9 %collective-permute-start.2 = (bf16[250,128]{1,0:T(8,128)(2,1)S(1)}, bf16[250,128]{1,0:T(8,128)(2,1)S(1)}, u32[]{:S(2)}, u32[]{:S(2)}) collective-permute-start(bf16[250,128]{1,0:T(8,128)(2,1)S(1)} %pad_maximum_fusion.3), channel_id=1, source_target_pairs={{384,0},{132,4},{392,8},{140,12},{400,16},{148,20},{408,24},{156,2... | collective-permute-start | bytes 192008 | tf_op jit(solution)/shard_map/ppermute | solution.py:36
  13.0 19.9 %collective-permute-start.1 = (bf16[250,128]{1,0:T(8,128)(2,1)S(1)}, bf16[250,128]{1,0:T(8,128)(2,1)S(1)}, u32[]{:S(2)}, u32[]{:S(2)}) collective-permute-start(bf16[250,128]{1,0:T(8,128)(2,1)S(1)} %pad_maximum_fusion.3), channel_id=1, source_target_pairs={{256,0},{260,4},{264,8},{268,12},{272,16},{276,20},{280,24},{284,2... | collective-permute-start | bytes 192008 | tf_op jit(solution)/shard_map/ppermute | solution.py:36
  23.9 11.3 %collective-permute-start = (bf16[250,128]{1,0:T(8,128)(2,1)S(1)}, bf16[250,128]{1,0:T(8,128)(2,1)S(1)}, u32[]{:S(2)}, u32[]{:S(2)}) collective-permute-start(bf16[250,128]{1,0:T(8,128)(2,1)S(1)} %pad_maximum_fusion.3), channel_id=1, source_target_pairs={{128,0},{388,4},{136,8},{396,12},{144,16},{404,20},{152,24},{412,2... | collective-permute-start | bytes 192008 | tf_op jit(solution)/shard_map/ppermute | solution.py:36
  30.3 17.5 %copy-start.5 = (s32[3072]{0:T(1024)S(1)}, s32[3072]{0:T(1024)}, u32[]{:S(2)}) copy-start(s32[3072]{0:T(1024)} %constant.423) | copy-start | bytes 36868
  30.4 17.5 %copy-start.6 = (s32[3072]{0:T(1024)S(1)}, s32[3072]{0:T(1024)}, u32[]{:S(2)}) copy-start(s32[3072]{0:T(1024)} %constant.413) | copy-start | bytes 36868
  30.4 17.5 %copy-start.7 = (s32[3072]{0:T(1024)S(1)}, s32[3072]{0:T(1024)}, u32[]{:S(2)}) copy-start(s32[3072]{0:T(1024)} %constant.411) | copy-start | bytes 36868
  30.4 17.5 %copy-start.8 = (s32[3072]{0:T(1024)S(1)}, s32[3072]{0:T(1024)}, u32[]{:S(2)}) copy-start(s32[3072]{0:T(1024)} %constant.392) | copy-start | bytes 36868
  30.4 17.5 %copy-start.9 = (s32[3072]{0:T(1024)S(1)}, s32[3072]{0:T(1024)}, u32[]{:S(2)}) copy-start(s32[3072]{0:T(1024)} %constant.314.clone) | copy-start | bytes 36868
  30.4 17.5 %copy-start.10 = (s32[3072]{0:T(1024)S(1)}, s32[3072]{0:T(1024)}, u32[]{:S(2)}) copy-start(s32[3072]{0:T(1024)} %constant.313.clone) | copy-start | bytes 36868
  30.4 17.5 %copy-start.11 = (s32[3072]{0:T(1024)S(1)}, s32[3072]{0:T(1024)}, u32[]{:S(2)}) copy-start(s32[3072]{0:T(1024)} %constant.312.clone) | copy-start | bytes 36868
  36.3 13.0 %collective-permute-start.5 = (bf16[1088,128]{1,0:T(8,128)(2,1)S(1)}, bf16[1088,128]{1,0:T(8,128)(2,1)S(1)}, u32[]{:S(2)}, u32[]{:S(2)}) collective-permute-start(bf16[1088,128]{1,0:T(8,128)(2,1)S(1)} %pad_maximum_fusion.1), channel_id=1, source_target_pairs={{480,0},{36,4},{488,8},{44,12},{496,16},{52,20},{504,24},{60,28},{... | collective-permute-start | bytes 835592 | tf_op jit(solution)/shard_map/ppermute | solution.py:36
  38.6 12.8 %collective-permute-start.4 = (bf16[1088,128]{1,0:T(8,128)(2,1)S(1)}, bf16[1088,128]{1,0:T(8,128)(2,1)S(1)}, u32[]{:S(2)}, u32[]{:S(2)}) collective-permute-start(bf16[1088,128]{1,0:T(8,128)(2,1)S(1)} %pad_maximum_fusion.1), channel_id=1, source_target_pairs={{64,0},{452,4},{72,8},{460,12},{80,16},{468,20},{88,24},{476,28},{... | collective-permute-start | bytes 835592 | tf_op jit(solution)/shard_map/ppermute | solution.py:36
  44.4 10.0 %collective-permute-start.3 = (bf16[1088,128]{1,0:T(8,128)(2,1)S(1)}, bf16[1088,128]{1,0:T(8,128)(2,1)S(1)}, u32[]{:S(2)}, u32[]{:S(2)}) collective-permute-start(bf16[1088,128]{1,0:T(8,128)(2,1)S(1)} %pad_maximum_fusion.1), channel_id=1, source_target_pairs={{32,0},{484,4},{40,8},{492,12},{48,16},{500,20},{56,24},{508,28},{... | collective-permute-start | bytes 835592 | tf_op jit(solution)/shard_map/ppermute | solution.py:36
  49.2 38.5 %copy-start.14 = (s32[1,160]{1,0:T(1,128)S(1)}, s32[1,160]{1,0:T(1,128)}, u32[]{:S(2)}) copy-start(s32[1,160]{1,0:T(1,128)} %param.24) | copy-start | bytes 1924
  49.3 38.5 %copy-start.15 = (s32[1,160,1]{1,2,0:T(1,128)S(1)}, s32[1,160,1]{1,2,0:T(1,128)}, u32[]{:S(2)}) copy-start(s32[1,160,1]{1,2,0:T(1,128)} %param.23) | copy-start | bytes 1924
  49.3 38.5 %copy-start.13 = (s32[1,160]{1,0:T(1,128)S(1)}, s32[1,160]{1,0:T(1,128)}, u32[]{:S(2)}) copy-start(s32[1,160]{1,0:T(1,128)} %param.25) | copy-start | bytes 1924
  54.5 35.9 %copy-start.3 = (bf16[1600,128]{1,0:T(8,128)(2,1)}, bf16[1600,128]{1,0:T(8,128)(2,1)S(1)}, u32[]{:S(2)}) copy-start(bf16[1600,128]{1,0:T(8,128)(2,1)S(1)} %pad_maximum_fusion.refs_0_) | copy-start | bytes 1228804
  54.5 14.2 %collective-permute-start.8 = (bf16[1600,128]{1,0:T(8,128)(2,1)S(1)}, bf16[1600,128]{1,0:T(8,128)(2,1)S(1)}, u32[]{:S(2)}, u32[]{:S(2)}) collective-permute-start(bf16[1600,128]{1,0:T(8,128)(2,1)S(1)} %pad_maximum_fusion.refs_0_), channel_id=1, source_target_pairs={{24,0},{28,4},{0,8},{4,12},{8,16},{12,20},{16,24},{20,28},{56,32},... | collective-permute-start | bytes 1228808 | tf_op jit(solution)/shard_map/ppermute | solution.py:36
  56.9 16.8 %collective-permute-start.9 = (bf16[1600,128]{1,0:T(8,128)(2,1)S(1)}, bf16[1600,128]{1,0:T(8,128)(2,1)S(1)}, u32[]{:S(2)}, u32[]{:S(2)}) collective-permute-start(bf16[1600,128]{1,0:T(8,128)(2,1)S(1)} %pad_maximum_fusion.refs_0_), channel_id=1, source_target_pairs={{4,0},{0,4},{12,8},{8,12},{20,16},{16,20},{28,24},{24,28},{36,32},... | collective-permute-start | bytes 1228808 | tf_op jit(solution)/shard_map/ppermute | solution.py:36
  58.9 18.6 %collective-permute-start.7 = (bf16[1600,128]{1,0:T(8,128)(2,1)S(1)}, bf16[1600,128]{1,0:T(8,128)(2,1)S(1)}, u32[]{:S(2)}, u32[]{:S(2)}) collective-permute-start(bf16[1600,128]{1,0:T(8,128)(2,1)S(1)} %pad_maximum_fusion.refs_0_), channel_id=1, source_target_pairs={{16,0},{20,4},{24,8},{28,12},{0,16},{4,20},{8,24},{12,28},{48,32},... | collective-permute-start | bytes 1228808 | tf_op jit(solution)/shard_map/ppermute | solution.py:36
  63.2 20.2 %collective-permute-start.6 = (bf16[1600,128]{1,0:T(8,128)(2,1)S(1)}, bf16[1600,128]{1,0:T(8,128)(2,1)S(1)}, u32[]{:S(2)}, u32[]{:S(2)}) collective-permute-start(bf16[1600,128]{1,0:T(8,128)(2,1)S(1)} %pad_maximum_fusion.refs_0_), channel_id=1, source_target_pairs={{8,0},{12,4},{16,8},{20,12},{24,16},{28,20},{0,24},{4,28},{40,32},... | collective-permute-start | bytes 1228808 | tf_op jit(solution)/shard_map/ppermute | solution.py:36
  68.7 21.7 %copy-start.24 = (bf16[1600,128]{1,0:T(8,128)(2,1)}, bf16[1600,128]{1,0:T(8,128)(2,1)S(1)}, u32[]{:S(2)}) copy-start(bf16[1600,128]{1,0:T(8,128)(2,1)S(1)} %collective-permute-done.8.refs_3_) | copy-start | bytes 1228804
  68.7 16.6 %collective-permute-start.12 = (bf16[1600,128]{1,0:T(8,128)(2,1)S(1)}, bf16[1600,128]{1,0:T(8,128)(2,1)S(1)}, u32[]{:S(2)}, u32[]{:S(2)}) collective-permute-start(bf16[1600,128]{1,0:T(8,128)(2,1)S(1)} %collective-permute-done.8.refs_3_), channel_id=1, source_target_pairs={{4,0},{0,4},{12,8},{8,12},{20,16},{16,20},{28,24},{24,28},{36,32},... | collective-permute-start | bytes 1228808 | tf_op jit(solution)/shard_map/ppermute | solution.py:36
  70.6 30.1 %copy-start.12 = (bf16[2752,128]{1,0:T(8,128)(2,1)}, bf16[2752,128]{1,0:T(8,128)(2,1)S(1)}, u32[]{:S(2)}) copy-start(bf16[2752,128]{1,0:T(8,128)(2,1)S(1)} %slice_dynamic-update-slice_fusion.refs_0_) | copy-start | bytes 2113540
  70.7 30.1 %collective-permute-start.15 = (bf16[2752,128]{1,0:T(8,128)(2,1)S(1)}, bf16[2752,128]{1,0:T(8,128)(2,1)S(1)}, u32[]{:S(2)}, u32[]{:S(2)}) collective-permute-start(bf16[2752,128]{1,0:T(8,128)(2,1)S(1)} %slice_dynamic-update-slice_fusion.refs_0_), channel_id=1, source_target_pairs={{24,0},{28,4},{0,8},{4,12},{8,16},{12,20},{16,24},{20,28},{56,32},... | collective-permute-start | bytes 2113544 | tf_op jit(solution)/shard_map/ppermute | solution.py:36
  73.7 16.7 %copy-start.25 = (bf16[1600,128]{1,0:T(8,128)(2,1)}, bf16[1600,128]{1,0:T(8,128)(2,1)S(1)}, u32[]{:S(2)}) copy-start(bf16[1600,128]{1,0:T(8,128)(2,1)S(1)} %collective-permute-done.9.refs_4_) | copy-start | bytes 1228804
  73.7 29.5 %collective-permute-start.14 = (bf16[2752,128]{1,0:T(8,128)(2,1)S(1)}, bf16[2752,128]{1,0:T(8,128)(2,1)S(1)}, u32[]{:S(2)}, u32[]{:S(2)}) collective-permute-start(bf16[2752,128]{1,0:T(8,128)(2,1)S(1)} %slice_dynamic-update-slice_fusion.refs_0_), channel_id=1, source_target_pairs={{16,0},{20,4},{24,8},{28,12},{0,16},{4,20},{8,24},{12,28},{48,32},... | collective-permute-start | bytes 2113544 | tf_op jit(solution)/shard_map/ppermute | solution.py:36
  77.4 13.0 %copy-start.26 = (bf16[1600,128]{1,0:T(8,128)(2,1)}, bf16[1600,128]{1,0:T(8,128)(2,1)S(1)}, u32[]{:S(2)}) copy-start(bf16[1600,128]{1,0:T(8,128)(2,1)S(1)} %collective-permute-done.7.refs_2_) | copy-start | bytes 1228804
  77.4 35.6 %collective-permute-start.13 = (bf16[2752,128]{1,0:T(8,128)(2,1)S(1)}, bf16[2752,128]{1,0:T(8,128)(2,1)S(1)}, u32[]{:S(2)}, u32[]{:S(2)}) collective-permute-start(bf16[2752,128]{1,0:T(8,128)(2,1)S(1)} %slice_dynamic-update-slice_fusion.refs_0_), channel_id=1, source_target_pairs={{8,0},{12,4},{16,8},{20,12},{24,16},{28,20},{0,24},{4,28},{40,32},... | collective-permute-start | bytes 2113544 | tf_op jit(solution)/shard_map/ppermute | solution.py:36
  83.4 7.0 %copy-start.27 = (bf16[1600,128]{1,0:T(8,128)(2,1)}, bf16[1600,128]{1,0:T(8,128)(2,1)S(1)}, u32[]{:S(2)}) copy-start(bf16[1600,128]{1,0:T(8,128)(2,1)S(1)} %collective-permute-done.6.refs_1_) | copy-start | bytes 1228804
  83.4 5.1 %collective-permute-start.11 = (bf16[1600,128]{1,0:T(8,128)(2,1)S(1)}, bf16[1600,128]{1,0:T(8,128)(2,1)S(1)}, u32[]{:S(2)}, u32[]{:S(2)}) collective-permute-start(bf16[1600,128]{1,0:T(8,128)(2,1)S(1)} %collective-permute-done.7.refs_2_), channel_id=1, source_target_pairs={{4,0},{0,4},{12,8},{8,12},{20,16},{16,20},{28,24},{24,28},{36,32},... | collective-permute-start | bytes 1228808 | tf_op jit(solution)/shard_map/ppermute | solution.py:36
  85.3 5.1 %copy-start.28 = (bf16[1600,128]{1,0:T(8,128)(2,1)}, bf16[1600,128]{1,0:T(8,128)(2,1)S(1)}, u32[]{:S(2)}) copy-start(bf16[1600,128]{1,0:T(8,128)(2,1)S(1)} %collective-permute-done.12.refs_7_) | copy-start | bytes 1228804
  85.3 5.0 %collective-permute-start.10 = (bf16[1600,128]{1,0:T(8,128)(2,1)S(1)}, bf16[1600,128]{1,0:T(8,128)(2,1)S(1)}, u32[]{:S(2)}, u32[]{:S(2)}) collective-permute-start(bf16[1600,128]{1,0:T(8,128)(2,1)S(1)} %collective-permute-done.6.refs_1_), channel_id=1, source_target_pairs={{4,0},{0,4},{12,8},{8,12},{20,16},{16,20},{28,24},{24,28},{36,32},... | collective-permute-start | bytes 1228808 | tf_op jit(solution)/shard_map/ppermute | solution.py:36
  88.4 2.0 copy-start.29
  88.4 26.7 %collective-permute-start.16 = (bf16[2752,128]{1,0:T(8,128)(2,1)S(1)}, bf16[2752,128]{1,0:T(8,128)(2,1)S(1)}, u32[]{:S(2)}, u32[]{:S(2)}) collective-permute-start(bf16[2752,128]{1,0:T(8,128)(2,1)S(1)} %slice_dynamic-update-slice_fusion.refs_0_), channel_id=1, source_target_pairs={{4,0},{0,4},{12,8},{8,12},{20,16},{16,20},{28,24},{24,28},{36,32},... | collective-permute-start | bytes 2113544 | tf_op jit(solution)/shard_map/ppermute | solution.py:36
  100.8 16.3 %copy-start.16 = (bf16[2752,128]{1,0:T(8,128)(2,1)}, bf16[2752,128]{1,0:T(8,128)(2,1)S(1)}, u32[]{:S(2)}) copy-start(bf16[2752,128]{1,0:T(8,128)(2,1)S(1)} %collective-permute-done.15.refs_3_) | copy-start | bytes 2113540
  100.8 14.4 %collective-permute-start.19 = (bf16[2752,128]{1,0:T(8,128)(2,1)S(1)}, bf16[2752,128]{1,0:T(8,128)(2,1)S(1)}, u32[]{:S(2)}, u32[]{:S(2)}) collective-permute-start(bf16[2752,128]{1,0:T(8,128)(2,1)S(1)} %collective-permute-done.15.refs_3_), channel_id=1, source_target_pairs={{4,0},{0,4},{12,8},{8,12},{20,16},{16,20},{28,24},{24,28},{36,32},... | collective-permute-start | bytes 2113544 | tf_op jit(solution)/shard_map/ppermute | solution.py:36
  103.2 13.9 %copy-start.17 = (bf16[2752,128]{1,0:T(8,128)(2,1)}, bf16[2752,128]{1,0:T(8,128)(2,1)S(1)}, u32[]{:S(2)}) copy-start(bf16[2752,128]{1,0:T(8,128)(2,1)S(1)} %collective-permute-done.14.refs_2_) | copy-start | bytes 2113540
  103.2 12.0 %collective-permute-start.18 = (bf16[2752,128]{1,0:T(8,128)(2,1)S(1)}, bf16[2752,128]{1,0:T(8,128)(2,1)S(1)}, u32[]{:S(2)}, u32[]{:S(2)}) collective-permute-start(bf16[2752,128]{1,0:T(8,128)(2,1)S(1)} %collective-permute-done.14.refs_2_), channel_id=1, source_target_pairs={{4,0},{0,4},{12,8},{8,12},{20,16},{16,20},{28,24},{24,28},{36,32},... | collective-permute-start | bytes 2113544 | tf_op jit(solution)/shard_map/ppermute | solution.py:36
  113.1 4.1 %copy-start.18 = (bf16[2752,128]{1,0:T(8,128)(2,1)}, bf16[2752,128]{1,0:T(8,128)(2,1)S(1)}, u32[]{:S(2)}) copy-start(bf16[2752,128]{1,0:T(8,128)(2,1)S(1)} %collective-permute-done.13.refs_1_) | copy-start | bytes 2113540
  113.1 4.1 %collective-permute-start.17 = (bf16[2752,128]{1,0:T(8,128)(2,1)S(1)}, bf16[2752,128]{1,0:T(8,128)(2,1)S(1)}, u32[]{:S(2)}, u32[]{:S(2)}) collective-permute-start(bf16[2752,128]{1,0:T(8,128)(2,1)S(1)} %collective-permute-done.13.refs_1_), channel_id=1, source_target_pairs={{4,0},{0,4},{12,8},{8,12},{20,16},{16,20},{28,24},{24,28},{36,32},... | collective-permute-start | bytes 2113544 | tf_op jit(solution)/shard_map/ppermute | solution.py:36
  115.2 2.0 copy-start.19
  115.2 1.9 copy-start.20
  115.2 1.9 copy-start.21
  117.1 0.9 copy-start.22
  135.9 12.3 %copy-start.1 = (bf16[2560,128]{1,0:T(8,128)(2,1)S(1)}, bf16[2560,128]{1,0:T(8,128)(2,1)}, u32[]{:S(2)}) copy-start(bf16[2560,128]{1,0:T(8,128)(2,1)} %get-tuple-element.36) | copy-start | bytes 1966084
  136.0 6.5 %collective-permute-start.20 = (bf16[2560,128]{1,0:T(8,128)(2,1)}, bf16[2560,128]{1,0:T(8,128)(2,1)S(1)}, u32[]{:S(2)}, u32[]{:S(2)}) collective-permute-start(bf16[2560,128]{1,0:T(8,128)(2,1)} %get-tuple-element.35), channel_id=1, source_target_pairs={{0,4},{4,0},{8,12},{12,8},{16,20},{20,16},{24,28},{28,24},{32,36},... | collective-permute-start | bytes 1966088 | tf_op jit(solution)/shard_map/ppermute | solution.py:40
  138.1 10.1 %collective-permute-start.22 = (bf16[2560,128]{1,0:T(8,128)(2,1)}, bf16[2560,128]{1,0:T(8,128)(2,1)S(1)}, u32[]{:S(2)}, u32[]{:S(2)}) collective-permute-start(bf16[2560,128]{1,0:T(8,128)(2,1)} %get-tuple-element.37), channel_id=1, source_target_pairs={{0,4},{4,0},{8,12},{12,8},{16,20},{20,16},{24,28},{28,24},{32,36},... | collective-permute-start | bytes 1966088 | tf_op jit(solution)/shard_map/ppermute | solution.py:40
  140.4 11.3 %collective-permute-start.24 = (bf16[2560,128]{1,0:T(8,128)(2,1)}, bf16[2560,128]{1,0:T(8,128)(2,1)S(1)}, u32[]{:S(2)}, u32[]{:S(2)}) collective-permute-start(bf16[2560,128]{1,0:T(8,128)(2,1)} %get-tuple-element.39), channel_id=1, source_target_pairs={{0,4},{4,0},{8,12},{12,8},{16,20},{20,16},{24,28},{28,24},{32,36},... | collective-permute-start | bytes 1966088 | tf_op jit(solution)/shard_map/ppermute | solution.py:40
  143.8 8.0 %copy-start = (bf16[2560,128]{1,0:T(8,128)(2,1)S(1)}, bf16[2560,128]{1,0:T(8,128)(2,1)}, u32[]{:S(2)}) copy-start(bf16[2560,128]{1,0:T(8,128)(2,1)} %get-tuple-element.38) | copy-start | bytes 1966084
  143.8 21.1 %collective-permute-start.21 = (bf16[2560,128]{1,0:T(8,128)(2,1)S(1)}, bf16[2560,128]{1,0:T(8,128)(2,1)S(1)}, u32[]{:S(2)}, u32[]{:S(2)}) collective-permute-start(bf16[2560,128]{1,0:T(8,128)(2,1)S(1)} %add_convert_fusion.4), channel_id=1, source_target_pairs={{0,16},{4,20},{8,24},{12,28},{16,0},{20,4},{24,8},{28,12},{32,48},... | collective-permute-start | bytes 1966088 | tf_op jit(solution)/shard_map/ppermute | solution.py:40
  148.5 6.3 %copy-start.23 = (bf16[2560,128]{1,0:T(8,128)(2,1)S(1)}, bf16[2560,128]{1,0:T(8,128)(2,1)}, u32[]{:S(2)}) copy-start(bf16[2560,128]{1,0:T(8,128)(2,1)} %get-tuple-element.47) | copy-start | bytes 1966084
  148.5 27.9 %collective-permute-start.23 = (bf16[2560,128]{1,0:T(8,128)(2,1)S(1)}, bf16[2560,128]{1,0:T(8,128)(2,1)S(1)}, u32[]{:S(2)}, u32[]{:S(2)}) collective-permute-start(bf16[2560,128]{1,0:T(8,128)(2,1)S(1)} %add_convert_fusion.3), channel_id=1, source_target_pairs={{0,8},{4,12},{8,16},{12,20},{16,24},{20,28},{24,0},{28,4},{32,40},... | collective-permute-start | bytes 1966088 | tf_op jit(solution)/shard_map/ppermute | solution.py:40
  152.0 26.4 %copy-start.2 = (bf16[2560,128]{1,0:T(8,128)(2,1)S(1)}, bf16[2560,128]{1,0:T(8,128)(2,1)}, u32[]{:S(2)}) copy-start(bf16[2560,128]{1,0:T(8,128)(2,1)} %get-tuple-element.46) | copy-start | bytes 1966084
  152.0 26.4 %collective-permute-start.25 = (bf16[2560,128]{1,0:T(8,128)(2,1)S(1)}, bf16[2560,128]{1,0:T(8,128)(2,1)S(1)}, u32[]{:S(2)}, u32[]{:S(2)}) collective-permute-start(bf16[2560,128]{1,0:T(8,128)(2,1)S(1)} %add_convert_fusion.2), channel_id=1, source_target_pairs={{0,24},{4,28},{8,0},{12,4},{16,8},{20,12},{24,16},{28,20},{32,56},... | collective-permute-start | bytes 1966088 | tf_op jit(solution)/shard_map/ppermute | solution.py:40
  154.8 23.5 %collective-permute-start.26 = (bf16[2560,128]{1,0:T(8,128)(2,1)S(1)}, bf16[2560,128]{1,0:T(8,128)(2,1)S(1)}, u32[]{:S(2)}, u32[]{:S(2)}) collective-permute-start(bf16[2560,128]{1,0:T(8,128)(2,1)S(1)} %copy-done.23), channel_id=1, source_target_pairs={{0,4},{4,0},{8,12},{12,8},{16,20},{20,16},{24,28},{28,24},{32,36},... | collective-permute-start | bytes 1966088 | tf_op jit(solution)/shard_map/ppermute | solution.py:40
  178.8 9.7 %collective-permute-start.27 = (bf16[640,128]{1,0:T(8,128)(2,1)S(1)}, bf16[640,128]{1,0:T(8,128)(2,1)S(1)}, u32[]{:S(2)}, u32[]{:S(2)}) collective-permute-start(bf16[640,128]{1,0:T(8,128)(2,1)S(1)} %get-tuple-element.51), channel_id=1, source_target_pairs={{0,32},{4,484},{8,40},{12,492},{16,48},{20,500},{24,56},{28,508},{... | collective-permute-start | bytes 491528 | tf_op jit(solution)/shard_map/ppermute | solution.py:40
  181.2 8.0 %collective-permute-start.29 = (bf16[640,128]{1,0:T(8,128)(2,1)S(1)}, bf16[640,128]{1,0:T(8,128)(2,1)S(1)}, u32[]{:S(2)}, u32[]{:S(2)}) collective-permute-start(bf16[640,128]{1,0:T(8,128)(2,1)S(1)} %get-tuple-element.52), channel_id=1, source_target_pairs={{0,480},{4,36},{8,488},{12,44},{16,496},{20,52},{24,504},{28,60},{... | collective-permute-start | bytes 491528 | tf_op jit(solution)/shard_map/ppermute | solution.py:40
  186.4 10.7 %collective-permute-start.28 = (bf16[640,128]{1,0:T(8,128)(2,1)S(1)}, bf16[640,128]{1,0:T(8,128)(2,1)S(1)}, u32[]{:S(2)}, u32[]{:S(2)}) collective-permute-start(bf16[640,128]{1,0:T(8,128)(2,1)S(1)} %get-tuple-element.53), channel_id=1, source_target_pairs={{0,64},{4,452},{8,72},{12,460},{16,80},{20,468},{24,88},{28,476},{... | collective-permute-start | bytes 491528 | tf_op jit(solution)/shard_map/ppermute | solution.py:40
  197.2 27.5 %copy-start.4 = (f32[4,3200]{1,0:T(4,128)S(1)}, f32[4,3200]{1,0:T(4,128)}, u32[]{:S(2)}) copy-start(f32[4,3200]{1,0:T(4,128)} %get-tuple-element.45) | copy-start | bytes 153604
  197.5 17.0 %collective-permute-start.30 = (bf16[150,128]{1,0:T(8,128)(2,1)S(1)}, bf16[150,128]{1,0:T(8,128)(2,1)S(1)}, u32[]{:S(2)}, u32[]{:S(2)}) collective-permute-start(bf16[150,128]{1,0:T(8,128)(2,1)S(1)} %pad_maximum_fusion.5), channel_id=1, source_target_pairs={{0,128},{4,388},{8,136},{12,396},{16,144},{20,404},{24,152},{28,41... | collective-permute-start | bytes 115208 | tf_op jit(solution)/shard_map/ppermute | solution.py:40
  202.2 14.9 %collective-permute-start.31 = (bf16[150,128]{1,0:T(8,128)(2,1)S(1)}, bf16[150,128]{1,0:T(8,128)(2,1)S(1)}, u32[]{:S(2)}, u32[]{:S(2)}) collective-permute-start(bf16[150,128]{1,0:T(8,128)(2,1)S(1)} %pad_maximum_fusion.6), channel_id=1, source_target_pairs={{0,256},{4,260},{8,264},{12,268},{16,272},{20,276},{24,280},{28,28... | collective-permute-start | bytes 115208 | tf_op jit(solution)/shard_map/ppermute | solution.py:40
  209.5 9.8 %collective-permute-start.32 = (bf16[150,128]{1,0:T(8,128)(2,1)S(1)}, bf16[150,128]{1,0:T(8,128)(2,1)S(1)}, u32[]{:S(2)}, u32[]{:S(2)}) collective-permute-start(bf16[150,128]{1,0:T(8,128)(2,1)S(1)} %pad_maximum_fusion.7), channel_id=1, source_target_pairs={{0,384},{4,132},{8,392},{12,140},{16,400},{20,148},{24,408},{28,15... | collective-permute-start | bytes 115208 | tf_op jit(solution)/shard_map/ppermute | solution.py:40
  220.1 10.8 %all-to-all-start = ((f32[4,10,640]{2,1,0:T(8,128)}), f32[4,10,640]{2,1,0:T(8,128)S(1)}, u32[]{:S(2)}, u32[]{:S(2)}) async-start(f32[4,10,640]{2,1,0:T(8,128)} %broadcast_in_dim.29), calls=%async_computation | async-start | bytes 327680 | tf_op jit(solution)/shard_map/all_to_all | solution.py:422
  (1 other events, 0.8 us)

commit v5 on v4

--- a/solution.py
+++ b/solution.py
@@ -17,11 +17,10 @@
 ROWS_OF = {0: (0,), 1: (1, 5, 9), 2: (2, 6, 10, 13, 16), 3: (3, 7, 11, 14, 17), 4: (4, 8, 12, 15, 18)}
 NEAR = (0, 1, 2, -1)
 FAR_ROWS = 400
-DEPTHS = (48, 32, 32)
+DEPTHS = (40, 32, 24)
 UNITS = (5, 8, 6)
-WEIGHT_ROWS = 240 + 256 + 192
 TERM_ROWS = 400 + 240
-INVERSE_AT, POSITION_AT = (0, 1536, 2560), (3584, 4864, 5888)
+INVERSE_AT, POSITION_AT = (0, 1280, 2304), (3072, 4352, 5376)
 VMEM_LIMIT = 56 * 2**20
 F32, BF16 = jnp.float32, jnp.bfloat16
 
@@ -170,13 +169,12 @@
     scaled_out, grad_dst = refs[25:27]
     w0, w1, w2, values, d0, d1, d2, p0, p1, p2, g0, g1, g2, src_terms = refs[27:]
     for k, piece in enumerate(pieces):
-        for near in range(4):
-            at = near * WEIGHT_ROWS
-            for out, units, rows in zip((w0, w1, w2), UNITS, DEPTHS):
-                to = (k * 4 + near) * rows
-                for u in range(units):
-                    out[to : to + rows, u * CH : (u + 1) * CH] = piece[at : at + rows, :]
-                    at += rows
+        at = 0
+        for out, units, depth in zip((w0, w1, w2), UNITS, DEPTHS):
+            rows = 4 * depth
+            for u in range(units):
+                out[k * rows : (k + 1) * rows, u * CH : (u + 1) * CH] = piece[at : at + rows, :]
+                at += rows
     z0 = mm(m0[...], w0[...])
     for row in range(5):
         values[:, row * CH : (row + 1) * CH] = z0[:, row * CH : (row + 1) * CH].astype(BF16)
@@ -243,10 +241,11 @@
     dw = lax.dot_general(m0[...], d0[...], (((0,), (0,)), ((), ())), preferred_element_type=F32)
     for k in range(8):
         for near in range(4):
-            row = (k * 4 + near) * 48
+            row = (k * 4 + near) * 40
             for u in range(5):
                 at = near * TERM_ROWS + 400 + u * 48
-                terms_out[k][at : at + 48, :] = dw[row : row + 48, u * CH : (u + 1) * CH].astype(BF16)
+                rows = jnp.concatenate([dw[row : row + 40, u * CH : (u + 1) * CH], jnp.zeros((8, CH), F32)], axis=0)
+                terms_out[k][at : at + 48, :] = rows.astype(BF16)
     for d, w, p, g, start in zip((d0, d1, d2), (w0, w1, w2), (p0, p1, p2), (g0, g1, g2), POSITION_AT):
         p[...] = mm_nt(d[...], w[...]).astype(BF16)
         for first in range(0, g.shape[1], 256):
@@ -337,18 +336,15 @@
 
 
 def index_maps(me):
-    inverse, position = [], []
-    for rows, depth in zip((10, 8, 6), DEPTHS):
-        p = np.arange(32 * depth)
-        inside = p % depth
-        inverse.append((p // depth, np.minimum(inside // rows, 3), np.full_like(p, rows), inside % rows, inside < 4 * rows))
+    tables = []
+    for rows in (10, 8, 6):
         k = np.arange(128 * rows)
-        position.append((k // rows, np.full_like(k, depth), np.full_like(k, rows), k % rows))
-    place, far, rows, rest, inside = (jnp.asarray(np.concatenate(a), jnp.int32) for a in zip(*inverse))
-    natural = jnp.where(inside > 0, block_owner(place, far, me) * rows + rest, -1)
-    owner, depth, rows, rest = (jnp.asarray(np.concatenate(a), jnp.int32) for a in zip(*position))
-    block, far = block_place(owner, me)
-    return jnp.concatenate([natural, block * depth + far * rows + rest])[None]
+        tables.append((k // rows, np.full_like(k, rows), k % rows))
+    device, rows, rest = (jnp.asarray(np.concatenate(a), jnp.int32) for a in zip(*tables))
+    near, far = device // 4, device % 4
+    natural = block_owner(near, far, me) * rows + rest
+    block, far = block_place(device, me)
+    return jnp.concatenate([natural, (block * 4 + far) * rows + rest])[None]
 
 
 def local(
@@ -367,18 +363,24 @@
     shards = (features, w_m0, w1, w2)
     own = jnp.concatenate([units_of(a) for a in shards], axis=0)
     blocks = [own] + [pull(own, dz=4 * a) for a in (1, 2, 3)]
-    merged, at = [], 0
-    for shard, depth in zip(shards, (16,) + DEPTHS):
+
+    def merged(blocks, at, units, rows):
+        parts = [b[at : at + units * rows].reshape(units, rows, CH) for b in blocks]
+        return jnp.concatenate(parts, axis=1).reshape(-1, CH)
+
+    far_parts, at = [], 0
+    for shard in shards:
         rows, units = shard.shape[0], shard.shape[1] // CH
-        parts = [b[at : at + units * rows].reshape(units, rows, CH) for b in blocks]
-        if depth > 4 * rows:
-            parts.append(jnp.zeros((units, depth - 4 * rows, CH), BF16))
-        merged.append(jnp.concatenate(parts, axis=1).reshape(units * depth, CH))
+        far_parts.append(merged(blocks, at, units, rows))
         at += units * rows
-    far_block = jnp.concatenate(merged, axis=0)
+    far_block = jnp.concatenate(far_parts, axis=0)
     blocks = [far_block] + [pull(far_block, dz=NEAR[n]) for n in (1, 2, 3)]
     feature_x = x_pieces(jnp.concatenate([b[:FAR_ROWS] for b in blocks], axis=0))
-    weight_x = x_pieces(jnp.concatenate([b[FAR_ROWS:] for b in blocks], axis=0))
+    near_parts, at = [], FAR_ROWS
+    for units, depth in zip(UNITS, DEPTHS):
+        near_parts.append(merged(blocks, at, units, depth))
+        at += units * depth
+    weight_x = x_pieces(jnp.concatenate(near_parts, axis=0))
     feature_pieces = feature_x + tuple(pull(a, dc=1) for a in feature_x)
 
     maps = index_maps(me)
@@ -391,7 +393,7 @@
     m0, m1, m2, turned_grad = call(
         rotate_kernel, "rotate",
         (*feature_pieces, rotor_rows, edge_rows, own_rows, maps),
-        [((160, 1536), BF16), ((320, 1024), BF16), ((320, 1024), BF16), ((160, MCOEF * CH), F32)],
+        [((160, 1280), BF16), ((320, 1024), BF16), ((320, 768), BF16), ((160, MCOEF * CH), F32)],
         [((512, FULL), BF16), ((160, FULL), BF16), ((160, FULL), BF16), ((160, FULL), F32),
          ((160, 1280), BF16), ((320, 1024), BF16), ((320, 768), BF16)],
         3_000_000_000,
@@ -403,9 +405,9 @@
         layer_kernel, "layer",
         (*weight_pieces, m0, m1, m2, turned_grad, rotor_rows, edge_bias[0].T, w_alpha.T, edge_rows, maps),
         [((4 * TERM_ROWS, CH), BF16)] * 8 + [((160, MCOEF * CH), BF16), ((160, MCOEF * CH), BF16)],
-        [((1536, 640), BF16), ((1024, 1024), BF16), ((1024, 768), BF16), ((160, MCOEF * CH), BF16),
+        [((1280, 640), BF16), ((1024, 1024), BF16), ((768, 768), BF16), ((160, MCOEF * CH), BF16),
          ((160, 640), BF16), ((320, 1024), BF16), ((320, 768), BF16),
-         ((160, 1536), BF16), ((320, 1024), BF16), ((320, 1024), BF16),
+         ((160, 1280), BF16), ((320, 1024), BF16), ((320, 768), BF16),
          ((160, 1280), BF16), ((320, 1024), BF16), ((320, 768), BF16), ((160, FULL), BF16)],
         5_000_000_000, 160 * 136,
     )

time: 234 us -> 236 us (level)
  waiting for transfers between devices: 59.1 us -> 64.1 us
  starting transfers between devices: 122 us -> 119 us
    ppermute x20, waiting for transfers between devices: 23.9 us -> 26.7 us  [pull(): lax.ppermute(a, 'edge', [(where_to(i, dz, dx, dc), i) for i in range(128)])]
  transfers between devices with their start and end apart: 34 -> 34, of which waited for: 15 -> 17; matrix products, arithmetic and copies ran while one was open for 3% -> 4% of each run, Pallas kernels for 6% -> 6%
where the time goes in v5:
time: 236 us; the launch traced here: 233 us
  starting transfers between devices  119 us (50%)
  waiting for transfers between devices  64.1 us (27%)
  Pallas kernels  31.8 us (13%)
  other arithmetic  8.69 us (4%)
  local copies, waits for them, and re-layouts  7.11 us (3%)
  between operations  2.69 us (1%)
    ppermute x20, starting transfers between devices, pull(): lax.ppermute(a, 'edge', [(where_to(i, dz, dx, dc), i) for i in range(128)])  71.1 us
    ppermute x13, starting transfers between devices, push(): lax.ppermute(a, 'edge', [(i, where_to(i, dz, dx, dc)) for i in range(128)])  43.3 us
    ppermute x13, waiting for transfers between devices, push(): lax.ppermute(a, 'edge', [(i, where_to(i, dz, dx, dc)) for i in range(128)])  31.8 us
    pallas_call x3, Pallas kernels, call(): pl.pallas_call(kernel, out_shape=tuple((jax.ShapeDtypeStruct(s, t) for s,...  31.8 us
    ppermute x20, waiting for transfers between devices, pull(): lax.ppermute(a, 'edge', [(where_to(i, dz, dx, dc), i) for i in range(128)])  26.7 us
    all_to_all x1, waiting for transfers between devices, local(): lax.all_to_all(jnp.broadcast_to(shard, (n_rep, 10, 640)), 'rep', split_ax...  5.51 us
  transfers between devices with their start and end apart: 34, of which 17 were waited for; matrix products, arithmetic and copies ran while one was open for 4% of the time, Pallas kernels for 6%

profile of v5, /device:TPU:6, one launch (start us, length us, event | category | flops | bytes accessed | tf_op | source)
XLA Modules:
  0.0 233.3 jit_solution(6304138777755113352)
XLA Ops:
  0.6 0.7 slice_bitcast_fusion.4
  1.3 0.8 fusion.47
  2.2 0.8 reshape.566
  3.0 0.8 reshape_squeeze.3
  3.9 9.1 %collective-permute-start.2 = (bf16[250,128]{1,0:T(8,128)(2,1)S(1)}, bf16[250,128]{1,0:T(8,128)(2,1)S(1)}, u32[]{:S(2)}, u32[]{:S(2)}) collective-permute-start(bf16[250,128]{1,0:T(8,128)(2,1)S(1)} %pad_maximum_fusion.4), channel_id=1, source_target_pairs={{384,0},{132,4},{392,8},{140,12},{400,16},{148,20},{408,24},{156,2... | collective-permute-start | bytes 192008 | tf_op jit(solution)/shard_map/ppermute | solution.py:35
  13.0 10.9 %collective-permute-start.1 = (bf16[250,128]{1,0:T(8,128)(2,1)S(1)}, bf16[250,128]{1,0:T(8,128)(2,1)S(1)}, u32[]{:S(2)}, u32[]{:S(2)}) collective-permute-start(bf16[250,128]{1,0:T(8,128)(2,1)S(1)} %pad_maximum_fusion.4), channel_id=1, source_target_pairs={{256,0},{260,4},{264,8},{268,12},{272,16},{276,20},{280,24},{284,2... | collective-permute-start | bytes 192008 | tf_op jit(solution)/shard_map/ppermute | solution.py:35
  23.9 5.5 %collective-permute-start = (bf16[250,128]{1,0:T(8,128)(2,1)S(1)}, bf16[250,128]{1,0:T(8,128)(2,1)S(1)}, u32[]{:S(2)}, u32[]{:S(2)}) collective-permute-start(bf16[250,128]{1,0:T(8,128)(2,1)S(1)} %pad_maximum_fusion.4), channel_id=1, source_target_pairs={{128,0},{388,4},{136,8},{396,12},{144,16},{404,20},{152,24},{412,2... | collective-permute-start | bytes 192008 | tf_op jit(solution)/shard_map/ppermute | solution.py:35
  30.1 0.8 reduce-precision_convert_fusion
  31.0 1.5 maximum_maximum_fusion.refs_10_
  32.5 0.7 add_add_fusion
  33.2 1.3 pad_add_fusion.1.refs_9_.refs_15_.edge_rows
  35.6 2.5 %collective-permute-start.5 = (bf16[1000,128]{1,0:T(8,128)(2,1)S(1)}, bf16[1000,128]{1,0:T(8,128)(2,1)S(1)}, u32[]{:S(2)}, u32[]{:S(2)}) collective-permute-start(bf16[1000,128]{1,0:T(8,128)(2,1)S(1)} %pad_maximum_fusion.2), channel_id=1, source_target_pairs={{480,0},{36,4},{488,8},{44,12},{496,16},{52,20},{504,24},{60,28},{... | collective-permute-start | bytes 768008 | tf_op jit(solution)/shard_map/ppermute | solution.py:35
  38.1 5.6 %collective-permute-start.4 = (bf16[1000,128]{1,0:T(8,128)(2,1)S(1)}, bf16[1000,128]{1,0:T(8,128)(2,1)S(1)}, u32[]{:S(2)}, u32[]{:S(2)}) collective-permute-start(bf16[1000,128]{1,0:T(8,128)(2,1)S(1)} %pad_maximum_fusion.2), channel_id=1, source_target_pairs={{64,0},{452,4},{72,8},{460,12},{80,16},{468,20},{88,24},{476,28},{... | collective-permute-start | bytes 768008 | tf_op jit(solution)/shard_map/ppermute | solution.py:35
  43.7 3.4 %collective-permute-start.3 = (bf16[1000,128]{1,0:T(8,128)(2,1)S(1)}, bf16[1000,128]{1,0:T(8,128)(2,1)S(1)}, u32[]{:S(2)}, u32[]{:S(2)}) collective-permute-start(bf16[1000,128]{1,0:T(8,128)(2,1)S(1)} %pad_maximum_fusion.2), channel_id=1, source_target_pairs={{32,0},{484,4},{40,8},{492,12},{48,16},{500,20},{56,24},{508,28},{... | collective-permute-start | bytes 768008 | tf_op jit(solution)/shard_map/ppermute | solution.py:35
  47.8 2.4 %collective-permute-done.4 = bf16[1000,128]{1,0:T(8,128)(2,1)S(1)} collective-permute-done((bf16[1000,128]{1,0:T(8,128)(2,1)S(1)}, bf16[1000,128]{1,0:T(8,128)(2,1)S(1)}, u32[]{:S(2)}, u32[]{:S(2)}) %collective-permute-start.4) | collective-permute-done | bytes 256032 | tf_op jit(solution)/shard_map/ppermute | solution.py:35
  50.3 2.7 %collective-permute-done.3 = bf16[1000,128]{1,0:T(8,128)(2,1)S(1)} collective-permute-done((bf16[1000,128]{1,0:T(8,128)(2,1)S(1)}, bf16[1000,128]{1,0:T(8,128)(2,1)S(1)}, u32[]{:S(2)}, u32[]{:S(2)}) %collective-permute-start.3) | collective-permute-done | bytes 256032 | tf_op jit(solution)/shard_map/ppermute | solution.py:35
  53.0 2.4 %collective-permute-start.8 = (bf16[1600,128]{1,0:T(8,128)(2,1)S(1)}, bf16[1600,128]{1,0:T(8,128)(2,1)S(1)}, u32[]{:S(2)}, u32[]{:S(2)}) collective-permute-start(bf16[1600,128]{1,0:T(8,128)(2,1)S(1)} %pad_maximum_fusion.1.refs_0_), channel_id=1, source_target_pairs={{24,0},{28,4},{0,8},{4,12},{8,16},{12,20},{16,24},{20,28},{56,32},... | collective-permute-start | bytes 1228808 | tf_op jit(solution)/shard_map/ppermute | solution.py:35
  55.4 4.3 %collective-permute-start.7 = (bf16[1600,128]{1,0:T(8,128)(2,1)S(1)}, bf16[1600,128]{1,0:T(8,128)(2,1)S(1)}, u32[]{:S(2)}, u32[]{:S(2)}) collective-permute-start(bf16[1600,128]{1,0:T(8,128)(2,1)S(1)} %pad_maximum_fusion.1.refs_0_), channel_id=1, source_target_pairs={{16,0},{20,4},{24,8},{28,12},{0,16},{4,20},{8,24},{12,28},{48,32},... | collective-permute-start | bytes 1228808 | tf_op jit(solution)/shard_map/ppermute | solution.py:35
  59.8 1.9 collective-permute-start.6
  61.7 1.9 collective-permute-start.9
  63.7 3.5 %collective-permute-done.8.refs_3_ = bf16[1600,128]{1,0:T(8,128)(2,1)S(1)} collective-permute-done((bf16[1600,128]{1,0:T(8,128)(2,1)S(1)}, bf16[1600,128]{1,0:T(8,128)(2,1)S(1)}, u32[]{:S(2)}, u32[]{:S(2)}) %collective-permute-start.8) | collective-permute-done | bytes 409632 | tf_op jit(solution)/shard_map/ppermute | solution.py:35
  67.3 1.9 collective-permute-start.12
  70.2 1.0 collective-permute-done.7.refs_2_
  71.2 1.9 collective-permute-start.11
  73.1 5.6 %collective-permute-done.6.refs_1_ = bf16[1600,128]{1,0:T(8,128)(2,1)S(1)} collective-permute-done((bf16[1600,128]{1,0:T(8,128)(2,1)S(1)}, bf16[1600,128]{1,0:T(8,128)(2,1)S(1)}, u32[]{:S(2)}, u32[]{:S(2)}) %collective-permute-start.6) | collective-permute-done | bytes 409632 | tf_op jit(solution)/shard_map/ppermute | solution.py:35
  78.8 1.9 collective-permute-start.10
  80.8 3.4 %collective-permute-start.15 = (bf16[2400,128]{1,0:T(8,128)(2,1)S(1)}, bf16[2400,128]{1,0:T(8,128)(2,1)S(1)}, u32[]{:S(2)}, u32[]{:S(2)}) collective-permute-start(bf16[2400,128]{1,0:T(8,128)(2,1)S(1)} %pad_maximum_fusion.refs_0_), channel_id=1, source_target_pairs={{24,0},{28,4},{0,8},{4,12},{8,16},{12,20},{16,24},{20,28},{56,32},... | collective-permute-start | bytes 1843208 | tf_op jit(solution)/shard_map/ppermute | solution.py:35
  84.2 3.4 %collective-permute-start.14 = (bf16[2400,128]{1,0:T(8,128)(2,1)S(1)}, bf16[2400,128]{1,0:T(8,128)(2,1)S(1)}, u32[]{:S(2)}, u32[]{:S(2)}) collective-permute-start(bf16[2400,128]{1,0:T(8,128)(2,1)S(1)} %pad_maximum_fusion.refs_0_), channel_id=1, source_target_pairs={{16,0},{20,4},{24,8},{28,12},{0,16},{4,20},{8,24},{12,28},{48,32},... | collective-permute-start | bytes 1843208 | tf_op jit(solution)/shard_map/ppermute | solution.py:35
  87.7 2.7 %collective-permute-start.13 = (bf16[2400,128]{1,0:T(8,128)(2,1)S(1)}, bf16[2400,128]{1,0:T(8,128)(2,1)S(1)}, u32[]{:S(2)}, u32[]{:S(2)}) collective-permute-start(bf16[2400,128]{1,0:T(8,128)(2,1)S(1)} %pad_maximum_fusion.refs_0_), channel_id=1, source_target_pairs={{8,0},{12,4},{16,8},{20,12},{24,16},{28,20},{0,24},{4,28},{40,32},... | collective-permute-start | bytes 1843208 | tf_op jit(solution)/shard_map/ppermute | solution.py:35
  91.2 1.9 collective-permute-start.16
  93.2 0.7 copy-done.27
  93.9 9.5 %rotate.1 = (bf16[160,1280]{1,0:T(8,128)(2,1)}, bf16[320,1024]{1,0:T(8,128)(2,1)}, bf16[320,768]{1,0:T(8,128)(2,1)}, f32[160,2432]{1,0:T(8,128)}) custom-call(bf16[1600,128]{1,0:T(8,128)(2,1)} %copy-done.4, bf16[1600,128]{1,0:T(8,128)(2,1)} %copy-done.25, bf16[1600,128]{1,0:T(8,128)(2,1)} %copy-done.24, bf16[1600,128]{1,0:T(8,128)(2,1)} %copy-done.23, ...), custom_call_target="tpu_custom_call" | custom-call | flops 3000000000 | bytes 3557696 | tf_op jit(solution)/shard_map/rotate/pallas_call | solution.py:321
  103.4 2.4 %collective-permute-start.19 = (bf16[2400,128]{1,0:T(8,128)(2,1)S(1)}, bf16[2400,128]{1,0:T(8,128)(2,1)S(1)}, u32[]{:S(2)}, u32[]{:S(2)}) collective-permute-start(bf16[2400,128]{1,0:T(8,128)(2,1)S(1)} %collective-permute-done.15.refs_3_), channel_id=1, source_target_pairs={{4,0},{0,4},{12,8},{8,12},{20,16},{16,20},{28,24},{24,28},{36,32},... | collective-permute-start | bytes 1843208 | tf_op jit(solution)/shard_map/ppermute | solution.py:35
  105.8 1.9 collective-permute-start.18
  107.8 8.5 %collective-permute-done.13.refs_1_ = bf16[2400,128]{1,0:T(8,128)(2,1)S(1)} collective-permute-done((bf16[2400,128]{1,0:T(8,128)(2,1)S(1)}, bf16[2400,128]{1,0:T(8,128)(2,1)S(1)}, u32[]{:S(2)}, u32[]{:S(2)}) %collective-permute-start.13) | collective-permute-done | bytes 614432 | tf_op jit(solution)/shard_map/ppermute | solution.py:35
  116.3 2.1 collective-permute-start.17
  118.4 1.8 collective-permute-done.17.refs_5_
  120.2 0.8 copy-done.22
  121.0 17.1 %layer.1 = (bf16[2560,128]{1,0:T(8,128)(2,1)}, bf16[2560,128]{1,0:T(8,128)(2,1)}, bf16[2560,128]{1,0:T(8,128)(2,1)}, bf16[2560,128]{1,0:T(8,128)(2,1)}, bf16[256...) custom-call(bf16[2400,128]{1,0:T(8,128)(2,1)} %copy-done.3, ...), custom_call_target="tpu_custom_call" | custom-call | flops 5000000000 | bytes 8213824 | tf_op jit(solution)/shard_map/layer/pallas_call | solution.py:321
  138.1 2.2 collective-permute-start.20
  140.3 2.3 collective-permute-start.22
  142.5 2.0 collective-permute-start.24
  144.6 1.3 add_convert_fusion.4
  145.9 4.1 %collective-permute-start.21 = (bf16[2560,128]{1,0:T(8,128)(2,1)S(1)}, bf16[2560,128]{1,0:T(8,128)(2,1)S(1)}, u32[]{:S(2)}, u32[]{:S(2)}) collective-permute-start(bf16[2560,128]{1,0:T(8,128)(2,1)S(1)} %add_convert_fusion.4), channel_id=1, source_target_pairs={{0,16},{4,20},{8,24},{12,28},{16,0},{20,4},{24,8},{28,12},{32,48},... | collective-permute-start | bytes 1966088 | tf_op jit(solution)/shard_map/ppermute | solution.py:39
  150.2 3.3 %collective-permute-start.23 = (bf16[2560,128]{1,0:T(8,128)(2,1)S(1)}, bf16[2560,128]{1,0:T(8,128)(2,1)S(1)}, u32[]{:S(2)}, u32[]{:S(2)}) collective-permute-start(bf16[2560,128]{1,0:T(8,128)(2,1)S(1)} %add_convert_fusion.3), channel_id=1, source_target_pairs={{0,8},{4,12},{8,16},{12,20},{16,24},{20,28},{24,0},{28,4},{32,40},... | collective-permute-start | bytes 1966088 | tf_op jit(solution)/shard_map/ppermute | solution.py:39
  153.6 2.9 %collective-permute-start.25 = (bf16[2560,128]{1,0:T(8,128)(2,1)S(1)}, bf16[2560,128]{1,0:T(8,128)(2,1)S(1)}, u32[]{:S(2)}, u32[]{:S(2)}) collective-permute-start(bf16[2560,128]{1,0:T(8,128)(2,1)S(1)} %add_convert_fusion.2), channel_id=1, source_target_pairs={{0,24},{4,28},{8,0},{12,4},{16,8},{20,12},{24,16},{28,20},{32,56},... | collective-permute-start | bytes 1966088 | tf_op jit(solution)/shard_map/ppermute | solution.py:39
  156.5 1.9 collective-permute-start.26
  158.4 5.3 %nodes.1 = (bf16[4,3200]{1,0:T(4,128)(2,1)}, f32[4,3200]{1,0:T(4,128)}) custom-call(bf16[160,475]{1,0:T(8,128)(2,1)} %bitcast.124, bf16[160,2432]{1,0:T(8,128)(2,1)} %get-tuple-element.40.scaled, bf16[160,2432]{1,0:T(8,128)(2,1)} %get-tuple-element.41.grad_dst, s32[3,160]{1,0:T(4,128)} %pad_add_fusion.1.refs_9_.refs_15_.edge_rows), custom_call_target="tpu_custom_call" | custom-call | flops 600000000 | bytes 1710400 | tf_op jit(solution)/shard_map/nodes/pallas_call | solution.py:321
  163.7 3.3 %collective-permute-done.21 = bf16[2560,128]{1,0:T(8,128)(2,1)S(1)} collective-permute-done((bf16[2560,128]{1,0:T(8,128)(2,1)S(1)}, bf16[2560,128]{1,0:T(8,128)(2,1)S(1)}, u32[]{:S(2)}, u32[]{:S(2)}) %collective-permute-start.21) | collective-permute-done | bytes 655392 | tf_op jit(solution)/shard_map/ppermute | solution.py:39
  167.0 11.4 %collective-permute-done.23 = bf16[2560,128]{1,0:T(8,128)(2,1)S(1)} collective-permute-done((bf16[2560,128]{1,0:T(8,128)(2,1)S(1)}, bf16[2560,128]{1,0:T(8,128)(2,1)S(1)}, u32[]{:S(2)}, u32[]{:S(2)}) %collective-permute-start.23) | collective-permute-done | bytes 655392 | tf_op jit(solution)/shard_map/ppermute | solution.py:39
  178.4 2.0 collective-permute-done.25
  180.9 1.9 collective-permute-start.27
  182.9 5.1 %collective-permute-start.29 = (bf16[640,128]{1,0:T(8,128)(2,1)S(1)}, bf16[640,128]{1,0:T(8,128)(2,1)S(1)}, u32[]{:S(2)}, u32[]{:S(2)}) collective-permute-start(bf16[640,128]{1,0:T(8,128)(2,1)S(1)} %get-tuple-element.52), channel_id=1, source_target_pairs={{0,480},{4,36},{8,488},{12,44},{16,496},{20,52},{24,504},{28,60},{... | collective-permute-start | bytes 491528 | tf_op jit(solution)/shard_map/ppermute | solution.py:39
  188.0 1.9 collective-permute-start.28
  190.0 1.5 collective-permute-done.29
  191.5 7.3 %collective-permute-done.28 = bf16[640,128]{1,0:T(8,128)(2,1)S(1)} collective-permute-done((bf16[640,128]{1,0:T(8,128)(2,1)S(1)}, bf16[640,128]{1,0:T(8,128)(2,1)S(1)}, u32[]{:S(2)}, u32[]{:S(2)}) %collective-permute-start.28) | collective-permute-done | bytes 163872 | tf_op jit(solution)/shard_map/ppermute | solution.py:39
  199.2 4.9 %collective-permute-start.30 = (bf16[150,128]{1,0:T(8,128)(2,1)S(1)}, bf16[150,128]{1,0:T(8,128)(2,1)S(1)}, u32[]{:S(2)}, u32[]{:S(2)}) collective-permute-start(bf16[150,128]{1,0:T(8,128)(2,1)S(1)} %pad_maximum_fusion.7), channel_id=1, source_target_pairs={{0,128},{4,388},{8,136},{12,396},{16,144},{20,404},{24,152},{28,41... | collective-permute-start | bytes 115208 | tf_op jit(solution)/shard_map/ppermute | solution.py:39
  204.0 7.1 %collective-permute-start.31 = (bf16[150,128]{1,0:T(8,128)(2,1)S(1)}, bf16[150,128]{1,0:T(8,128)(2,1)S(1)}, u32[]{:S(2)}, u32[]{:S(2)}) collective-permute-start(bf16[150,128]{1,0:T(8,128)(2,1)S(1)} %pad_maximum_fusion.8), channel_id=1, source_target_pairs={{0,256},{4,260},{8,264},{12,268},{16,272},{20,276},{24,280},{28,28... | collective-permute-start | bytes 115208 | tf_op jit(solution)/shard_map/ppermute | solution.py:39
  211.2 3.7 %collective-permute-start.32 = (bf16[150,128]{1,0:T(8,128)(2,1)S(1)}, bf16[150,128]{1,0:T(8,128)(2,1)S(1)}, u32[]{:S(2)}, u32[]{:S(2)}) collective-permute-start(bf16[150,128]{1,0:T(8,128)(2,1)S(1)} %pad_maximum_fusion.9), channel_id=1, source_target_pairs={{0,384},{4,132},{8,392},{12,140},{16,400},{20,148},{24,408},{28,15... | collective-permute-start | bytes 115208 | tf_op jit(solution)/shard_map/ppermute | solution.py:39
  215.0 4.0 %collective-permute-done.31 = bf16[150,128]{1,0:T(8,128)(2,1)S(1)} collective-permute-done((bf16[150,128]{1,0:T(8,128)(2,1)S(1)}, bf16[150,128]{1,0:T(8,128)(2,1)S(1)}, u32[]{:S(2)}, u32[]{:S(2)}) %collective-permute-start.31) | collective-permute-done | bytes 38432 | tf_op jit(solution)/shard_map/ppermute | solution.py:39
  219.0 2.2 collective-permute-done.32
  221.4 0.7 broadcast_in_dim.19
  222.1 4.5 %all-to-all-start = ((f32[4,10,640]{2,1,0:T(8,128)}), f32[4,10,640]{2,1,0:T(8,128)S(1)}, u32[]{:S(2)}, u32[]{:S(2)}) async-start(f32[4,10,640]{2,1,0:T(8,128)} %broadcast_in_dim.19), calls=%async_computation | async-start | bytes 327680 | tf_op jit(solution)/shard_map/all_to_all | solution.py:424
  227.2 5.5 %all-to-all-done = f32[4,10,640]{2,1,0:T(8,128)S(1)} async-done(((f32[4,10,640]{2,1,0:T(8,128)}), f32[4,10,640]{2,1,0:T(8,128)S(1)}, u32[]{:S(2)}, u32[]{:S(2)}) %all-to-all-start) | async-done | bytes 102432 | tf_op jit(solution)/shard_map/all_to_all | solution.py:424
  (170 shorter events, 6.2 us)
Async XLA Ops:
  3.9 30.6 %collective-permute-start.2 = (bf16[250,128]{1,0:T(8,128)(2,1)S(1)}, bf16[250,128]{1,0:T(8,128)(2,1)S(1)}, u32[]{:S(2)}, u32[]{:S(2)}) collective-permute-start(bf16[250,128]{1,0:T(8,128)(2,1)S(1)} %pad_maximum_fusion.4), channel_id=1, source_target_pairs={{384,0},{132,4},{392,8},{140,12},{400,16},{148,20},{408,24},{156,2... | collective-permute-start | bytes 192008 | tf_op jit(solution)/shard_map/ppermute | solution.py:35
  13.0 21.7 %collective-permute-start.1 = (bf16[250,128]{1,0:T(8,128)(2,1)S(1)}, bf16[250,128]{1,0:T(8,128)(2,1)S(1)}, u32[]{:S(2)}, u32[]{:S(2)}) collective-permute-start(bf16[250,128]{1,0:T(8,128)(2,1)S(1)} %pad_maximum_fusion.4), channel_id=1, source_target_pairs={{256,0},{260,4},{264,8},{268,12},{272,16},{276,20},{280,24},{284,2... | collective-permute-start | bytes 192008 | tf_op jit(solution)/shard_map/ppermute | solution.py:35
  23.9 11.3 %collective-permute-start = (bf16[250,128]{1,0:T(8,128)(2,1)S(1)}, bf16[250,128]{1,0:T(8,128)(2,1)S(1)}, u32[]{:S(2)}, u32[]{:S(2)}) collective-permute-start(bf16[250,128]{1,0:T(8,128)(2,1)S(1)} %pad_maximum_fusion.4), channel_id=1, source_target_pairs={{128,0},{388,4},{136,8},{396,12},{144,16},{404,20},{152,24},{412,2... | collective-permute-start | bytes 192008 | tf_op jit(solution)/shard_map/ppermute | solution.py:35
  35.6 12.2 %collective-permute-start.5 = (bf16[1000,128]{1,0:T(8,128)(2,1)S(1)}, bf16[1000,128]{1,0:T(8,128)(2,1)S(1)}, u32[]{:S(2)}, u32[]{:S(2)}) collective-permute-start(bf16[1000,128]{1,0:T(8,128)(2,1)S(1)} %pad_maximum_fusion.2), channel_id=1, source_target_pairs={{480,0},{36,4},{488,8},{44,12},{496,16},{52,20},{504,24},{60,28},{... | collective-permute-start | bytes 768008 | tf_op jit(solution)/shard_map/ppermute | solution.py:35
  38.1 12.2 %collective-permute-start.4 = (bf16[1000,128]{1,0:T(8,128)(2,1)S(1)}, bf16[1000,128]{1,0:T(8,128)(2,1)S(1)}, u32[]{:S(2)}, u32[]{:S(2)}) collective-permute-start(bf16[1000,128]{1,0:T(8,128)(2,1)S(1)} %pad_maximum_fusion.2), channel_id=1, source_target_pairs={{64,0},{452,4},{72,8},{460,12},{80,16},{468,20},{88,24},{476,28},{... | collective-permute-start | bytes 768008 | tf_op jit(solution)/shard_map/ppermute | solution.py:35
  43.7 9.3 %collective-permute-start.3 = (bf16[1000,128]{1,0:T(8,128)(2,1)S(1)}, bf16[1000,128]{1,0:T(8,128)(2,1)S(1)}, u32[]{:S(2)}, u32[]{:S(2)}) collective-permute-start(bf16[1000,128]{1,0:T(8,128)(2,1)S(1)} %pad_maximum_fusion.2), channel_id=1, source_target_pairs={{32,0},{484,4},{40,8},{492,12},{48,16},{500,20},{56,24},{508,28},{... | collective-permute-start | bytes 768008 | tf_op jit(solution)/shard_map/ppermute | solution.py:35
  53.0 27.7 %copy-start.4 = (bf16[1600,128]{1,0:T(8,128)(2,1)}, bf16[1600,128]{1,0:T(8,128)(2,1)S(1)}, u32[]{:S(2)}) copy-start(bf16[1600,128]{1,0:T(8,128)(2,1)S(1)} %pad_maximum_fusion.1.refs_0_) | copy-start | bytes 1228804
  53.0 14.2 %collective-permute-start.8 = (bf16[1600,128]{1,0:T(8,128)(2,1)S(1)}, bf16[1600,128]{1,0:T(8,128)(2,1)S(1)}, u32[]{:S(2)}, u32[]{:S(2)}) collective-permute-start(bf16[1600,128]{1,0:T(8,128)(2,1)S(1)} %pad_maximum_fusion.1.refs_0_), channel_id=1, source_target_pairs={{24,0},{28,4},{0,8},{4,12},{8,16},{12,20},{16,24},{20,28},{56,32},... | collective-permute-start | bytes 1228808 | tf_op jit(solution)/shard_map/ppermute | solution.py:35
  55.4 15.8 %collective-permute-start.7 = (bf16[1600,128]{1,0:T(8,128)(2,1)S(1)}, bf16[1600,128]{1,0:T(8,128)(2,1)S(1)}, u32[]{:S(2)}, u32[]{:S(2)}) collective-permute-start(bf16[1600,128]{1,0:T(8,128)(2,1)S(1)} %pad_maximum_fusion.1.refs_0_), channel_id=1, source_target_pairs={{16,0},{20,4},{24,8},{28,12},{0,16},{4,20},{8,24},{12,28},{48,32},... | collective-permute-start | bytes 1228808 | tf_op jit(solution)/shard_map/ppermute | solution.py:35
  59.8 19.0 %collective-permute-start.6 = (bf16[1600,128]{1,0:T(8,128)(2,1)S(1)}, bf16[1600,128]{1,0:T(8,128)(2,1)S(1)}, u32[]{:S(2)}, u32[]{:S(2)}) collective-permute-start(bf16[1600,128]{1,0:T(8,128)(2,1)S(1)} %pad_maximum_fusion.1.refs_0_), channel_id=1, source_target_pairs={{8,0},{12,4},{16,8},{20,12},{24,16},{28,20},{0,24},{4,28},{40,32},... | collective-permute-start | bytes 1228808 | tf_op jit(solution)/shard_map/ppermute | solution.py:35
  61.7 22.5 %collective-permute-start.9 = (bf16[1600,128]{1,0:T(8,128)(2,1)S(1)}, bf16[1600,128]{1,0:T(8,128)(2,1)}, u32[]{:S(2)}, u32[]{:S(2)}) collective-permute-start(bf16[1600,128]{1,0:T(8,128)(2,1)S(1)} %pad_maximum_fusion.1.refs_0_), channel_id=1, source_target_pairs={{4,0},{0,4},{12,8},{8,12},{20,16},{16,20},{28,24},{24,28},{36,32},... | collective-permute-start | bytes 1228808 | tf_op jit(solution)/shard_map/ppermute | solution.py:35
  67.3 13.5 %copy-start.23 = (bf16[1600,128]{1,0:T(8,128)(2,1)}, bf16[1600,128]{1,0:T(8,128)(2,1)S(1)}, u32[]{:S(2)}) copy-start(bf16[1600,128]{1,0:T(8,128)(2,1)S(1)} %collective-permute-done.8.refs_3_) | copy-start | bytes 1228804
  67.3 20.4 %collective-permute-start.12 = (bf16[1600,128]{1,0:T(8,128)(2,1)S(1)}, bf16[1600,128]{1,0:T(8,128)(2,1)}, u32[]{:S(2)}, u32[]{:S(2)}) collective-permute-start(bf16[1600,128]{1,0:T(8,128)(2,1)S(1)} %collective-permute-done.8.refs_3_), channel_id=1, source_target_pairs={{4,0},{0,4},{12,8},{8,12},{20,16},{16,20},{28,24},{24,28},{36,32},... | collective-permute-start | bytes 1228808 | tf_op jit(solution)/shard_map/ppermute | solution.py:35
  69.2 21.2 %copy-start.6 = (s32[3072]{0:T(1024)S(1)}, s32[3072]{0:T(1024)}, u32[]{:S(2)}) copy-start(s32[3072]{0:T(1024)} %constant.415) | copy-start | bytes 36868
  69.2 21.2 %copy-start.7 = (s32[3072]{0:T(1024)S(1)}, s32[3072]{0:T(1024)}, u32[]{:S(2)}) copy-start(s32[3072]{0:T(1024)} %constant.405) | copy-start | bytes 36868
  69.2 21.2 %copy-start.8 = (s32[3072]{0:T(1024)S(1)}, s32[3072]{0:T(1024)}, u32[]{:S(2)}) copy-start(s32[3072]{0:T(1024)} %constant.403) | copy-start | bytes 36868
  69.2 21.2 %copy-start.9 = (s32[3072]{0:T(1024)S(1)}, s32[3072]{0:T(1024)}, u32[]{:S(2)}) copy-start(s32[3072]{0:T(1024)} %constant.386) | copy-start | bytes 36868
  69.2 21.2 %copy-start.10 = (s32[3072]{0:T(1024)S(1)}, s32[3072]{0:T(1024)}, u32[]{:S(2)}) copy-start(s32[3072]{0:T(1024)} %constant.378) | copy-start | bytes 36868
  69.2 21.2 %copy-start.11 = (s32[3072]{0:T(1024)S(1)}, s32[3072]{0:T(1024)}, u32[]{:S(2)}) copy-start(s32[3072]{0:T(1024)} %constant.361) | copy-start | bytes 36868
  69.2 21.2 %copy-start.12 = (s32[3072]{0:T(1024)S(1)}, s32[3072]{0:T(1024)}, u32[]{:S(2)}) copy-start(s32[3072]{0:T(1024)} %constant.334) | copy-start | bytes 36868
  69.3 21.2 %copy-start.13 = (s32[3072]{0:T(1024)S(1)}, s32[3072]{0:T(1024)}, u32[]{:S(2)}) copy-start(s32[3072]{0:T(1024)} %constant.293.clone) | copy-start | bytes 36868
  69.3 21.2 %copy-start.14 = (s32[3072]{0:T(1024)S(1)}, s32[3072]{0:T(1024)}, u32[]{:S(2)}) copy-start(s32[3072]{0:T(1024)} %constant.292.clone) | copy-start | bytes 36868
  71.2 21.9 %copy-start.24 = (bf16[1600,128]{1,0:T(8,128)(2,1)}, bf16[1600,128]{1,0:T(8,128)(2,1)S(1)}, u32[]{:S(2)}) copy-start(bf16[1600,128]{1,0:T(8,128)(2,1)S(1)} %collective-permute-done.7.refs_2_) | copy-start | bytes 1228804
  71.2 19.9 %collective-permute-start.11 = (bf16[1600,128]{1,0:T(8,128)(2,1)S(1)}, bf16[1600,128]{1,0:T(8,128)(2,1)S(1)}, u32[]{:S(2)}, u32[]{:S(2)}) collective-permute-start(bf16[1600,128]{1,0:T(8,128)(2,1)S(1)} %collective-permute-done.7.refs_2_), channel_id=1, source_target_pairs={{4,0},{0,4},{12,8},{8,12},{20,16},{16,20},{28,24},{24,28},{36,32},... | collective-permute-start | bytes 1228808 | tf_op jit(solution)/shard_map/ppermute | solution.py:35
  78.8 14.4 %copy-start.25 = (bf16[1600,128]{1,0:T(8,128)(2,1)}, bf16[1600,128]{1,0:T(8,128)(2,1)S(1)}, u32[]{:S(2)}) copy-start(bf16[1600,128]{1,0:T(8,128)(2,1)S(1)} %collective-permute-done.6.refs_1_) | copy-start | bytes 1228804
  78.8 14.3 %collective-permute-start.10 = (bf16[1600,128]{1,0:T(8,128)(2,1)S(1)}, bf16[1600,128]{1,0:T(8,128)(2,1)S(1)}, u32[]{:S(2)}, u32[]{:S(2)}) collective-permute-start(bf16[1600,128]{1,0:T(8,128)(2,1)S(1)} %collective-permute-done.6.refs_1_), channel_id=1, source_target_pairs={{4,0},{0,4},{12,8},{8,12},{20,16},{16,20},{28,24},{24,28},{36,32},... | collective-permute-start | bytes 1228808 | tf_op jit(solution)/shard_map/ppermute | solution.py:35
  80.8 22.6 %copy-start.3 = (bf16[2400,128]{1,0:T(8,128)(2,1)}, bf16[2400,128]{1,0:T(8,128)(2,1)S(1)}, u32[]{:S(2)}) copy-start(bf16[2400,128]{1,0:T(8,128)(2,1)S(1)} %pad_maximum_fusion.refs_0_) | copy-start | bytes 1843204
  80.8 22.6 %collective-permute-start.15 = (bf16[2400,128]{1,0:T(8,128)(2,1)S(1)}, bf16[2400,128]{1,0:T(8,128)(2,1)S(1)}, u32[]{:S(2)}, u32[]{:S(2)}) collective-permute-start(bf16[2400,128]{1,0:T(8,128)(2,1)S(1)} %pad_maximum_fusion.refs_0_), channel_id=1, source_target_pairs={{24,0},{28,4},{0,8},{4,12},{8,16},{12,20},{16,24},{20,28},{56,32},... | collective-permute-start | bytes 1843208 | tf_op jit(solution)/shard_map/ppermute | solution.py:35
  84.2 21.6 %collective-permute-start.14 = (bf16[2400,128]{1,0:T(8,128)(2,1)S(1)}, bf16[2400,128]{1,0:T(8,128)(2,1)S(1)}, u32[]{:S(2)}, u32[]{:S(2)}) collective-permute-start(bf16[2400,128]{1,0:T(8,128)(2,1)S(1)} %pad_maximum_fusion.refs_0_), channel_id=1, source_target_pairs={{16,0},{20,4},{24,8},{28,12},{0,16},{4,20},{8,24},{12,28},{48,32},... | collective-permute-start | bytes 1843208 | tf_op jit(solution)/shard_map/ppermute | solution.py:35
  87.7 28.6 %collective-permute-start.13 = (bf16[2400,128]{1,0:T(8,128)(2,1)S(1)}, bf16[2400,128]{1,0:T(8,128)(2,1)S(1)}, u32[]{:S(2)}, u32[]{:S(2)}) collective-permute-start(bf16[2400,128]{1,0:T(8,128)(2,1)S(1)} %pad_maximum_fusion.refs_0_), channel_id=1, source_target_pairs={{8,0},{12,4},{16,8},{20,12},{24,16},{28,20},{0,24},{4,28},{40,32},... | collective-permute-start | bytes 1843208 | tf_op jit(solution)/shard_map/ppermute | solution.py:35
  91.2 2.0 copy-start.26
  91.2 27.2 %collective-permute-start.16 = (bf16[2400,128]{1,0:T(8,128)(2,1)S(1)}, bf16[2400,128]{1,0:T(8,128)(2,1)S(1)}, u32[]{:S(2)}, u32[]{:S(2)}) collective-permute-start(bf16[2400,128]{1,0:T(8,128)(2,1)S(1)} %pad_maximum_fusion.refs_0_), channel_id=1, source_target_pairs={{4,0},{0,4},{12,8},{8,12},{20,16},{16,20},{28,24},{24,28},{36,32},... | collective-permute-start | bytes 1843208 | tf_op jit(solution)/shard_map/ppermute | solution.py:35
  93.1 0.8 copy-start.27
  103.4 16.8 %copy-start.16 = (bf16[2400,128]{1,0:T(8,128)(2,1)}, bf16[2400,128]{1,0:T(8,128)(2,1)S(1)}, u32[]{:S(2)}) copy-start(bf16[2400,128]{1,0:T(8,128)(2,1)S(1)} %collective-permute-done.15.refs_3_) | copy-start | bytes 1843204
  103.4 15.0 %collective-permute-start.19 = (bf16[2400,128]{1,0:T(8,128)(2,1)S(1)}, bf16[2400,128]{1,0:T(8,128)(2,1)S(1)}, u32[]{:S(2)}, u32[]{:S(2)}) collective-permute-start(bf16[2400,128]{1,0:T(8,128)(2,1)S(1)} %collective-permute-done.15.refs_3_), channel_id=1, source_target_pairs={{4,0},{0,4},{12,8},{8,12},{20,16},{16,20},{28,24},{24,28},{36,32},... | collective-permute-start | bytes 1843208 | tf_op jit(solution)/shard_map/ppermute | solution.py:35
  105.8 14.4 %copy-start.17 = (bf16[2400,128]{1,0:T(8,128)(2,1)}, bf16[2400,128]{1,0:T(8,128)(2,1)S(1)}, u32[]{:S(2)}) copy-start(bf16[2400,128]{1,0:T(8,128)(2,1)S(1)} %collective-permute-done.14.refs_2_) | copy-start | bytes 1843204
  105.8 12.6 %collective-permute-start.18 = (bf16[2400,128]{1,0:T(8,128)(2,1)S(1)}, bf16[2400,128]{1,0:T(8,128)(2,1)S(1)}, u32[]{:S(2)}, u32[]{:S(2)}) collective-permute-start(bf16[2400,128]{1,0:T(8,128)(2,1)S(1)} %collective-permute-done.14.refs_2_), channel_id=1, source_target_pairs={{4,0},{0,4},{12,8},{8,12},{20,16},{16,20},{28,24},{24,28},{36,32},... | collective-permute-start | bytes 1843208 | tf_op jit(solution)/shard_map/ppermute | solution.py:35
  116.3 3.9 %copy-start.18 = (bf16[2400,128]{1,0:T(8,128)(2,1)}, bf16[2400,128]{1,0:T(8,128)(2,1)S(1)}, u32[]{:S(2)}) copy-start(bf16[2400,128]{1,0:T(8,128)(2,1)S(1)} %collective-permute-done.13.refs_1_) | copy-start | bytes 1843204
  116.3 3.9 %collective-permute-start.17 = (bf16[2400,128]{1,0:T(8,128)(2,1)S(1)}, bf16[2400,128]{1,0:T(8,128)(2,1)S(1)}, u32[]{:S(2)}, u32[]{:S(2)}) collective-permute-start(bf16[2400,128]{1,0:T(8,128)(2,1)S(1)} %collective-permute-done.13.refs_1_), channel_id=1, source_target_pairs={{4,0},{0,4},{12,8},{8,12},{20,16},{16,20},{28,24},{24,28},{36,32},... | collective-permute-start | bytes 1843208 | tf_op jit(solution)/shard_map/ppermute | solution.py:35
  118.4 1.8 copy-start.19
  118.4 1.8 copy-start.20
  118.4 1.8 copy-start.21
  120.2 0.8 copy-start.22
  138.1 11.9 %copy-start.1 = (bf16[2560,128]{1,0:T(8,128)(2,1)S(1)}, bf16[2560,128]{1,0:T(8,128)(2,1)}, u32[]{:S(2)}) copy-start(bf16[2560,128]{1,0:T(8,128)(2,1)} %get-tuple-element.36) | copy-start | bytes 1966084
  138.1 6.5 %collective-permute-start.20 = (bf16[2560,128]{1,0:T(8,128)(2,1)}, bf16[2560,128]{1,0:T(8,128)(2,1)S(1)}, u32[]{:S(2)}, u32[]{:S(2)}) collective-permute-start(bf16[2560,128]{1,0:T(8,128)(2,1)} %get-tuple-element.35), channel_id=1, source_target_pairs={{0,4},{4,0},{8,12},{12,8},{16,20},{20,16},{24,28},{28,24},{32,36},... | collective-permute-start | bytes 1966088 | tf_op jit(solution)/shard_map/ppermute | solution.py:39
  140.3 9.7 %collective-permute-start.22 = (bf16[2560,128]{1,0:T(8,128)(2,1)}, bf16[2560,128]{1,0:T(8,128)(2,1)S(1)}, u32[]{:S(2)}, u32[]{:S(2)}) collective-permute-start(bf16[2560,128]{1,0:T(8,128)(2,1)} %get-tuple-element.37), channel_id=1, source_target_pairs={{0,4},{4,0},{8,12},{12,8},{16,20},{20,16},{24,28},{28,24},{32,36},... | collective-permute-start | bytes 1966088 | tf_op jit(solution)/shard_map/ppermute | solution.py:39
  142.5 10.9 %collective-permute-start.24 = (bf16[2560,128]{1,0:T(8,128)(2,1)}, bf16[2560,128]{1,0:T(8,128)(2,1)S(1)}, u32[]{:S(2)}, u32[]{:S(2)}) collective-permute-start(bf16[2560,128]{1,0:T(8,128)(2,1)} %get-tuple-element.39), channel_id=1, source_target_pairs={{0,4},{4,0},{8,12},{12,8},{16,20},{20,16},{24,28},{28,24},{32,36},... | collective-permute-start | bytes 1966088 | tf_op jit(solution)/shard_map/ppermute | solution.py:39
  145.9 7.6 %copy-start = (bf16[2560,128]{1,0:T(8,128)(2,1)S(1)}, bf16[2560,128]{1,0:T(8,128)(2,1)}, u32[]{:S(2)}) copy-start(bf16[2560,128]{1,0:T(8,128)(2,1)} %get-tuple-element.38) | copy-start | bytes 1966084
  145.9 21.1 %collective-permute-start.21 = (bf16[2560,128]{1,0:T(8,128)(2,1)S(1)}, bf16[2560,128]{1,0:T(8,128)(2,1)S(1)}, u32[]{:S(2)}, u32[]{:S(2)}) collective-permute-start(bf16[2560,128]{1,0:T(8,128)(2,1)S(1)} %add_convert_fusion.4), channel_id=1, source_target_pairs={{0,16},{4,20},{8,24},{12,28},{16,0},{20,4},{24,8},{28,12},{32,48},... | collective-permute-start | bytes 1966088 | tf_op jit(solution)/shard_map/ppermute | solution.py:39
  150.2 6.3 %copy-start.15 = (bf16[2560,128]{1,0:T(8,128)(2,1)S(1)}, bf16[2560,128]{1,0:T(8,128)(2,1)}, u32[]{:S(2)}) copy-start(bf16[2560,128]{1,0:T(8,128)(2,1)} %get-tuple-element.47) | copy-start | bytes 1966084
  150.2 28.3 %collective-permute-start.23 = (bf16[2560,128]{1,0:T(8,128)(2,1)S(1)}, bf16[2560,128]{1,0:T(8,128)(2,1)S(1)}, u32[]{:S(2)}, u32[]{:S(2)}) collective-permute-start(bf16[2560,128]{1,0:T(8,128)(2,1)S(1)} %add_convert_fusion.3), channel_id=1, source_target_pairs={{0,8},{4,12},{8,16},{12,20},{16,24},{20,28},{24,0},{28,4},{32,40},... | collective-permute-start | bytes 1966088 | tf_op jit(solution)/shard_map/ppermute | solution.py:39
  153.6 26.8 %copy-start.2 = (bf16[2560,128]{1,0:T(8,128)(2,1)S(1)}, bf16[2560,128]{1,0:T(8,128)(2,1)}, u32[]{:S(2)}) copy-start(bf16[2560,128]{1,0:T(8,128)(2,1)} %get-tuple-element.46) | copy-start | bytes 1966084
  153.6 26.8 %collective-permute-start.25 = (bf16[2560,128]{1,0:T(8,128)(2,1)S(1)}, bf16[2560,128]{1,0:T(8,128)(2,1)S(1)}, u32[]{:S(2)}, u32[]{:S(2)}) collective-permute-start(bf16[2560,128]{1,0:T(8,128)(2,1)S(1)} %add_convert_fusion.2), channel_id=1, source_target_pairs={{0,24},{4,28},{8,0},{12,4},{16,8},{20,12},{24,16},{28,20},{32,56},... | collective-permute-start | bytes 1966088 | tf_op jit(solution)/shard_map/ppermute | solution.py:39
  156.5 23.9 %collective-permute-start.26 = (bf16[2560,128]{1,0:T(8,128)(2,1)S(1)}, bf16[2560,128]{1,0:T(8,128)(2,1)S(1)}, u32[]{:S(2)}, u32[]{:S(2)}) collective-permute-start(bf16[2560,128]{1,0:T(8,128)(2,1)S(1)} %copy-done.15), channel_id=1, source_target_pairs={{0,4},{4,0},{8,12},{12,8},{16,20},{20,16},{24,28},{28,24},{32,36},... | collective-permute-start | bytes 1966088 | tf_op jit(solution)/shard_map/ppermute | solution.py:39
  180.9 9.0 %collective-permute-start.27 = (bf16[640,128]{1,0:T(8,128)(2,1)S(1)}, bf16[640,128]{1,0:T(8,128)(2,1)S(1)}, u32[]{:S(2)}, u32[]{:S(2)}) collective-permute-start(bf16[640,128]{1,0:T(8,128)(2,1)S(1)} %get-tuple-element.51), channel_id=1, source_target_pairs={{0,32},{4,484},{8,40},{12,492},{16,48},{20,500},{24,56},{28,508},{... | collective-permute-start | bytes 491528 | tf_op jit(solution)/shard_map/ppermute | solution.py:39
  182.9 8.6 %collective-permute-start.29 = (bf16[640,128]{1,0:T(8,128)(2,1)S(1)}, bf16[640,128]{1,0:T(8,128)(2,1)S(1)}, u32[]{:S(2)}, u32[]{:S(2)}) collective-permute-start(bf16[640,128]{1,0:T(8,128)(2,1)S(1)} %get-tuple-element.52), channel_id=1, source_target_pairs={{0,480},{4,36},{8,488},{12,44},{16,496},{20,52},{24,504},{28,60},{... | collective-permute-start | bytes 491528 | tf_op jit(solution)/shard_map/ppermute | solution.py:39
  188.0 10.8 %collective-permute-start.28 = (bf16[640,128]{1,0:T(8,128)(2,1)S(1)}, bf16[640,128]{1,0:T(8,128)(2,1)S(1)}, u32[]{:S(2)}, u32[]{:S(2)}) collective-permute-start(bf16[640,128]{1,0:T(8,128)(2,1)S(1)} %get-tuple-element.53), channel_id=1, source_target_pairs={{0,64},{4,452},{8,72},{12,460},{16,80},{20,468},{24,88},{28,476},{... | collective-permute-start | bytes 491528 | tf_op jit(solution)/shard_map/ppermute | solution.py:39
  198.9 27.6 %copy-start.5 = (f32[4,3200]{1,0:T(4,128)S(1)}, f32[4,3200]{1,0:T(4,128)}, u32[]{:S(2)}) copy-start(f32[4,3200]{1,0:T(4,128)} %get-tuple-element.45) | copy-start | bytes 153604
  199.2 15.8 %collective-permute-start.30 = (bf16[150,128]{1,0:T(8,128)(2,1)S(1)}, bf16[150,128]{1,0:T(8,128)(2,1)S(1)}, u32[]{:S(2)}, u32[]{:S(2)}) collective-permute-start(bf16[150,128]{1,0:T(8,128)(2,1)S(1)} %pad_maximum_fusion.7), channel_id=1, source_target_pairs={{0,128},{4,388},{8,136},{12,396},{16,144},{20,404},{24,152},{28,41... | collective-permute-start | bytes 115208 | tf_op jit(solution)/shard_map/ppermute | solution.py:39
  204.0 15.0 %collective-permute-start.31 = (bf16[150,128]{1,0:T(8,128)(2,1)S(1)}, bf16[150,128]{1,0:T(8,128)(2,1)S(1)}, u32[]{:S(2)}, u32[]{:S(2)}) collective-permute-start(bf16[150,128]{1,0:T(8,128)(2,1)S(1)} %pad_maximum_fusion.8), channel_id=1, source_target_pairs={{0,256},{4,260},{8,264},{12,268},{16,272},{20,276},{24,280},{28,28... | collective-permute-start | bytes 115208 | tf_op jit(solution)/shard_map/ppermute | solution.py:39
  211.2 10.0 %collective-permute-start.32 = (bf16[150,128]{1,0:T(8,128)(2,1)S(1)}, bf16[150,128]{1,0:T(8,128)(2,1)S(1)}, u32[]{:S(2)}, u32[]{:S(2)}) collective-permute-start(bf16[150,128]{1,0:T(8,128)(2,1)S(1)} %pad_maximum_fusion.9), channel_id=1, source_target_pairs={{0,384},{4,132},{8,392},{12,140},{16,400},{20,148},{24,408},{28,15... | collective-permute-start | bytes 115208 | tf_op jit(solution)/shard_map/ppermute | solution.py:39
  222.1 10.6 %all-to-all-start = ((f32[4,10,640]{2,1,0:T(8,128)}), f32[4,10,640]{2,1,0:T(8,128)S(1)}, u32[]{:S(2)}, u32[]{:S(2)}) async-start(f32[4,10,640]{2,1,0:T(8,128)} %broadcast_in_dim.19), calls=%async_computation | async-start | bytes 327680 | tf_op jit(solution)/shard_map/all_to_all | solution.py:424

commit v6 on v5

--- a/solution.py
+++ b/solution.py
@@ -20,7 +20,7 @@
 DEPTHS = (40, 32, 24)
 UNITS = (5, 8, 6)
 TERM_ROWS = 400 + 240
-INVERSE_AT, POSITION_AT = (0, 1280, 2304), (3072, 4352, 5376)
+SOURCE_AT, TARGET_AT, POSITION_AT = (0, 1280, 2304), (3072, 4352, 5376), (6144, 7424, 8448)
 VMEM_LIMIT = 56 * 2**20
 F32, BF16 = jnp.float32, jnp.bfloat16
 
@@ -108,30 +108,7 @@
     return 2, ((row - 13) // 3) * EDGES, (row - 13) % 3
 
 
-def rotate_kernel(*refs):
-    pieces = refs[:8]
-    rot, edge_rows, local, maps = refs[8:12]
-    m0, m1, m2, turned_grad = refs[12:16]
-    feats, srcf, dstf, gradf, n0, n1, n2 = refs[16:]
-    for k, piece in enumerate(pieces):
-        for near in range(4):
-            row = k * 64 + near * 16
-            for u in range(LCOEF):
-                at = near * FAR_ROWS + u * 16
-                feats[row : row + 16, u * CH : (u + 1) * CH] = piece[at : at + 16, :]
-    source_hot = hot(edge_rows[0:1, :], (512, EDGES), 0)
-    t = edge_rows[1:2, :]
-    rows = lax.broadcasted_iota(jnp.int32, (16, EDGES), 0)
-    feat_hot = jnp.where(rows == t, F32(1), F32(0)).astype(BF16)
-    grad_hot = jnp.where((rows == t + 4) | (rows == t + 8), F32(1), F32(0)).astype(BF16)
-    for first in range(0, FULL, 640):
-        cut = slice(first, first + 640)
-        srcf[:, cut] = mm_tn(source_hot, feats[:, cut]).astype(BF16)
-        dstf[:, cut] = mm_tn(feat_hot, local[:, cut]).astype(BF16)
-        gradf[:, cut] = mm_tn(grad_hot, local[:, cut])
-
-    stacked = (n0, n1, n2)
-
+def into_frames(rot, loads, stores):
     def turn(step, carry):
         e0 = pl.multiple_of(step * BLOCK, BLOCK)
         rows_here = pl.ds(e0, BLOCK)
@@ -139,23 +116,45 @@
         for degree, rows in ROWS_OF.items():
             sums = [None] * len(rows)
             for col in range(degree * degree, (degree + 1) ** 2):
-                cut = slice(col * CH, (col + 1) * CH)
-                s, d, g = srcf[rows_here, cut].astype(F32), dstf[rows_here, cut].astype(F32), gradf[rows_here, cut]
+                given = [load(rows_here, slice(col * CH, (col + 1) * CH)) for load in loads]
                 for n, row in enumerate(rows):
                     r = jnp.broadcast_to(rotors[:, row * LCOEF + col : row * LCOEF + col + 1], (BLOCK, CH))
-                    terms = (r * s, r * d, r * g)
-                    sums[n] = terms if sums[n] is None else tuple(a + b for a, b in zip(sums[n], terms))
+                    terms = [r * g for g in given]
+                    sums[n] = terms if sums[n] is None else [a + b for a, b in zip(sums[n], terms)]
             for n, row in enumerate(rows):
-                array, base, column = frame_slot(row)
-                out = stacked[array]
-                out_rows = pl.ds(pl.multiple_of(base + e0, BLOCK), BLOCK)
-                out[out_rows, column * 256 : column * 256 + CH] = sums[n][0].astype(BF16)
-                out[out_rows, column * 256 + CH : column * 256 + 256] = sums[n][1].astype(BF16)
-                turned_grad[rows_here, row * CH : (row + 1) * CH] = sums[n][2]
+                for store, total in zip(stores, sums[n]):
+                    store(e0, row, total)
         return carry
 
     lax.fori_loop(0, EDGES // BLOCK, turn, 0)
-    for natural, ordered, start in ((n0, m0, INVERSE_AT[0]), (n1, m1, INVERSE_AT[1]), (n2, m2, INVERSE_AT[2])):
+
+
+def store_stacked(stacked):
+    def store(e0, row, total):
+        array, base, column = frame_slot(row)
+        stacked[array][pl.ds(pl.multiple_of(base + e0, BLOCK), BLOCK), column * CH : (column + 1) * CH] = total.astype(BF16)
+
+    return store
+
+
+def local_kernel(rot, edge_rows, local, maps, m0, m1, m2, turned_grad, dstf, gradf, n0, n1, n2):
+    t = edge_rows[1:2, :]
+    rows = lax.broadcasted_iota(jnp.int32, (16, EDGES), 0)
+    feat_hot = jnp.where(rows == t, F32(1), F32(0)).astype(BF16)
+    grad_hot = jnp.where((rows == t + 4) | (rows == t + 8), F32(1), F32(0)).astype(BF16)
+    for first in range(0, FULL, 640):
+        cut = slice(first, first + 640)
+        dstf[:, cut] = mm_tn(feat_hot, local[:, cut]).astype(BF16)
+        gradf[:, cut] = mm_tn(grad_hot, local[:, cut])
+
+    def store_grad(e0, row, total):
+        turned_grad[pl.ds(e0, BLOCK), row * CH : (row + 1) * CH] = total
+
+    into_frames(
+        rot, [lambda rows, cut: dstf[rows, cut].astype(F32), lambda rows, cut: gradf[rows, cut]],
+        [store_stacked((n0, n1, n2)), store_grad],
+    )
+    for natural, ordered, start in zip((n0, n1, n2), (m0, m1, m2), TARGET_AT):
         depth = natural.shape[1]
         for first in range(0, ordered.shape[1], 256):
             inverse = maps[:, start + first : start + first + 256]
@@ -164,17 +163,34 @@
 
 def layer_kernel(*refs):
     pieces = refs[:8]
-    m0, m1, m2, turned_grad, rot, bias, alpha_ref, edge_rows, maps = refs[8:17]
+    t0, t1, t2, turned_grad, rot, bias, alpha_ref, edge_rows, maps = refs[8:17]
     terms_out = refs[17:25]
     scaled_out, grad_dst = refs[25:27]
-    w0, w1, w2, values, d0, d1, d2, p0, p1, p2, g0, g1, g2, src_terms = refs[27:]
+    w0, w1, w2, values, d0, d1, d2, p0, p1, p2, g0, g1, g2, src_terms, feats, n0, n1, n2, m0, m1, m2 = refs[27:]
     for k, piece in enumerate(pieces):
-        at = 0
+        for near in range(4):
+            row = k * 64 + near * 16
+            for u in range(LCOEF):
+                at = near * FAR_ROWS + u * 16
+                feats[row : row + 16, u * CH : (u + 1) * CH] = piece[at : at + 16, :]
+        at = 4 * FAR_ROWS
         for out, units, depth in zip((w0, w1, w2), UNITS, DEPTHS):
             rows = 4 * depth
             for u in range(units):
                 out[k * rows : (k + 1) * rows, u * CH : (u + 1) * CH] = piece[at : at + rows, :]
                 at += rows
+    source_hot = hot(edge_rows[0:1, :], (512, EDGES), 0)
+    for first in range(0, FULL, 640):
+        cut = slice(first, first + 640)
+        src_terms[:, cut] = mm_tn(source_hot, feats[:, cut]).astype(BF16)
+    into_frames(rot, [lambda rows, cut: src_terms[rows, cut].astype(F32)], [store_stacked((n0, n1, n2))])
+    for natural, targets, ordered, start in zip((n0, n1, n2), (t0, t1, t2), (m0, m1, m2), SOURCE_AT):
+        depth = natural.shape[1]
+        for first in range(0, ordered.shape[1], 256):
+            inverse = maps[:, start + first : start + first + 256]
+            turned = mm(natural[...], hot(inverse, (depth, 256), 0))
+            ordered[:, first : first + 256] = (turned + targets[:, first : first + 256].astype(F32)).astype(BF16)
+
     z0 = mm(m0[...], w0[...])
     for row in range(5):
         values[:, row * CH : (row + 1) * CH] = z0[:, row * CH : (row + 1) * CH].astype(BF16)
@@ -344,7 +360,10 @@
     near, far = device // 4, device % 4
     natural = block_owner(near, far, me) * rows + rest
     block, far = block_place(device, me)
-    return jnp.concatenate([natural, (block * 4 + far) * rows + rest])[None]
+    column, channel = natural // 256, natural % 256
+    source = jnp.where(channel < CH, column * CH + channel, -1)
+    target = jnp.where(channel < CH, -1, column * CH + channel - CH)
+    return jnp.concatenate([source, target, (block * 4 + far) * rows + rest])[None]
 
 
 def local(
@@ -375,13 +394,11 @@
         at += units * rows
     far_block = jnp.concatenate(far_parts, axis=0)
     blocks = [far_block] + [pull(far_block, dz=NEAR[n]) for n in (1, 2, 3)]
-    feature_x = x_pieces(jnp.concatenate([b[:FAR_ROWS] for b in blocks], axis=0))
     near_parts, at = [], FAR_ROWS
     for units, depth in zip(UNITS, DEPTHS):
         near_parts.append(merged(blocks, at, units, depth))
         at += units * depth
-    weight_x = x_pieces(jnp.concatenate(near_parts, axis=0))
-    feature_pieces = feature_x + tuple(pull(a, dc=1) for a in feature_x)
+    pieces = x_pieces(jnp.concatenate([b[:FAR_ROWS] for b in blocks] + near_parts, axis=0))
 
     maps = index_maps(me)
     cotangent = out_grad[0]
@@ -390,26 +407,25 @@
         [features, high.astype(BF16), (cotangent - high).astype(BF16), jnp.zeros((4, FULL), BF16)], axis=0
     )
 
-    m0, m1, m2, turned_grad = call(
-        rotate_kernel, "rotate",
-        (*feature_pieces, rotor_rows, edge_rows, own_rows, maps),
+    *targets, turned_grad = call(
+        local_kernel, "local", (rotor_rows, edge_rows, own_rows, maps),
         [((160, 1280), BF16), ((320, 1024), BF16), ((320, 768), BF16), ((160, MCOEF * CH), F32)],
-        [((512, FULL), BF16), ((160, FULL), BF16), ((160, FULL), BF16), ((160, FULL), F32),
-         ((160, 1280), BF16), ((320, 1024), BF16), ((320, 768), BF16)],
-        3_000_000_000,
-    )
-    others = [lax.optimization_barrier((m0, weight_x[x]))[1] for x in (1, 2, 3)]
-    weight_x = (weight_x[0], *others)
-    weight_pieces = weight_x + tuple(pull(a, dc=1) for a in weight_x)
+        [((160, FULL), BF16), ((160, FULL), F32), ((160, 640), BF16), ((320, 512), BF16), ((320, 384), BF16)],
+        1_500_000_000,
+    )
+    pieces = (pieces[0], *(lax.optimization_barrier((targets[0], pieces[x]))[1] for x in (1, 2, 3)))
+    pieces = pieces + tuple(pull(a, dc=1) for a in pieces)
     outs = call(
         layer_kernel, "layer",
-        (*weight_pieces, m0, m1, m2, turned_grad, rotor_rows, edge_bias[0].T, w_alpha.T, edge_rows, maps),
+        (*pieces, *targets, turned_grad, rotor_rows, edge_bias[0].T, w_alpha.T, edge_rows, maps),
         [((4 * TERM_ROWS, CH), BF16)] * 8 + [((160, MCOEF * CH), BF16), ((160, MCOEF * CH), BF16)],
         [((1280, 640), BF16), ((1024, 1024), BF16), ((768, 768), BF16), ((160, MCOEF * CH), BF16),
          ((160, 640), BF16), ((320, 1024), BF16), ((320, 768), BF16),
          ((160, 1280), BF16), ((320, 1024), BF16), ((320, 768), BF16),
-         ((160, 1280), BF16), ((320, 1024), BF16), ((320, 768), BF16), ((160, FULL), BF16)],
-        5_000_000_000, 160 * 136,
+         ((160, 1280), BF16), ((320, 1024), BF16), ((320, 768), BF16), ((160, FULL), BF16),
+         ((512, FULL), BF16), ((160, 640), BF16), ((320, 512), BF16), ((320, 384), BF16),
+         ((160, 1280), BF16), ((320, 1024), BF16), ((320, 768), BF16)],
+        6_000_000_000, 160 * 136,
     )
     term_pieces, (scaled, grad_dst) = outs[:8], outs[8:]
     node_out, grad_local = call(

time: 236 us -> 237 us (level)
  starting transfers between devices: 119 us -> 102 us
  waiting for transfers between devices: 64.1 us -> 79.4 us
  Pallas kernels: 31.8 us -> 35.8 us
    ppermute x20 -> x13, starting transfers between devices: 71.1 us -> 53.9 us  [pull(): lax.ppermute(a, 'edge', [(where_to(i, dz, dx, dc), i) for i in range(128)])]
    ppermute x20 -> x13, waiting for transfers between devices: 26.7 us -> 42.3 us  [pull(): lax.ppermute(a, 'edge', [(where_to(i, dz, dx, dc), i) for i in range(128)])]
    pallas_call x3, Pallas kernels: 31.8 us -> 35.8 us  [call(): pl.pallas_call(kernel, out_shape=tuple((jax.ShapeDtypeStruct(s, t) for s,...]
  transfers between devices with their start and end apart: 34 -> 27, of which waited for: 17 -> 16; matrix products, arithmetic and copies ran while one was open for 4% -> 3% of each run, Pallas kernels for 6% -> 5%
where the time goes in v6:
time: 237 us; the launch traced here: 235 us
  starting transfers between devices  102 us (43%)
  waiting for transfers between devices  79.4 us (34%)
  Pallas kernels  35.8 us (15%)
  other arithmetic  8.76 us (4%)
  local copies, waits for them, and re-layouts  6.6 us (3%)
  between operations  2.4 us (1%)
    ppermute x13, starting transfers between devices, pull(): lax.ppermute(a, 'edge', [(where_to(i, dz, dx, dc), i) for i in range(128)])  53.9 us
    ppermute x13, starting transfers between devices, push(): lax.ppermute(a, 'edge', [(i, where_to(i, dz, dx, dc)) for i in range(128)])  43.4 us
    ppermute x13, waiting for transfers between devices, pull(): lax.ppermute(a, 'edge', [(where_to(i, dz, dx, dc), i) for i in range(128)])  42.3 us
    pallas_call x3, Pallas kernels, call(): pl.pallas_call(kernel, out_shape=tuple((jax.ShapeDtypeStruct(s, t) for s,...  35.8 us
    ppermute x13, waiting for transfers between devices, push(): lax.ppermute(a, 'edge', [(i, where_to(i, dz, dx, dc)) for i in range(128)])  31.6 us
    all_to_all x1, waiting for transfers between devices, local(): lax.all_to_all(jnp.broadcast_to(shard, (n_rep, 10, 640)), 'rep', split_ax...  5.51 us
  transfers between devices with their start and end apart: 27, of which 16 were waited for; matrix products, arithmetic and copies ran while one was open for 3% of the time, Pallas kernels for 5%

profile of v6, /device:TPU:6, one launch (start us, length us, event | category | flops | bytes accessed | tf_op | source)
XLA Modules:
  0.0 234.8 jit_solution(1897897378967608411)
XLA Ops:
  0.6 0.7 slice_bitcast_fusion.4
  1.3 0.8 fusion.53
  2.2 0.8 reshape.567
  3.0 0.8 reshape_squeeze.3
  3.9 9.1 %collective-permute-start.2 = (bf16[250,128]{1,0:T(8,128)(2,1)S(1)}, bf16[250,128]{1,0:T(8,128)(2,1)S(1)}, u32[]{:S(2)}, u32[]{:S(2)}) collective-permute-start(bf16[250,128]{1,0:T(8,128)(2,1)S(1)} %pad_maximum_fusion.2), channel_id=1, source_target_pairs={{384,0},{132,4},{392,8},{140,12},{400,16},{148,20},{408,24},{156,2... | collective-permute-start | bytes 192008 | tf_op jit(solution)/shard_map/ppermute | solution.py:35
  13.0 10.9 %collective-permute-start.1 = (bf16[250,128]{1,0:T(8,128)(2,1)S(1)}, bf16[250,128]{1,0:T(8,128)(2,1)S(1)}, u32[]{:S(2)}, u32[]{:S(2)}) collective-permute-start(bf16[250,128]{1,0:T(8,128)(2,1)S(1)} %pad_maximum_fusion.2), channel_id=1, source_target_pairs={{256,0},{260,4},{264,8},{268,12},{272,16},{276,20},{280,24},{284,2... | collective-permute-start | bytes 192008 | tf_op jit(solution)/shard_map/ppermute | solution.py:35
  23.9 5.5 %collective-permute-start = (bf16[250,128]{1,0:T(8,128)(2,1)S(1)}, bf16[250,128]{1,0:T(8,128)(2,1)S(1)}, u32[]{:S(2)}, u32[]{:S(2)}) collective-permute-start(bf16[250,128]{1,0:T(8,128)(2,1)S(1)} %pad_maximum_fusion.2), channel_id=1, source_target_pairs={{128,0},{388,4},{136,8},{396,12},{144,16},{404,20},{152,24},{412,2... | collective-permute-start | bytes 192008 | tf_op jit(solution)/shard_map/ppermute | solution.py:35
  30.1 0.9 broadcast_select_fusion
  31.1 0.8 reduce-precision_convert_fusion
  32.0 0.7 add_add_fusion
  32.7 0.6 pad_add_fusion
  33.3 1.3 pad_add_fusion.1.edge_rows.refs_15_
  34.9 0.4 collective-permute-done
  35.6 2.6 %collective-permute-start.5 = (bf16[1000,128]{1,0:T(8,128)(2,1)S(1)}, bf16[1000,128]{1,0:T(8,128)(2,1)S(1)}, u32[]{:S(2)}, u32[]{:S(2)}) collective-permute-start(bf16[1000,128]{1,0:T(8,128)(2,1)S(1)} %pad_maximum_fusion), channel_id=1, source_target_pairs={{480,0},{36,4},{488,8},{44,12},{496,16},{52,20},{504,24},{60,28},{... | collective-permute-start | bytes 768008 | tf_op jit(solution)/shard_map/ppermute | solution.py:35
  38.2 5.5 %collective-permute-start.4 = (bf16[1000,128]{1,0:T(8,128)(2,1)S(1)}, bf16[1000,128]{1,0:T(8,128)(2,1)S(1)}, u32[]{:S(2)}, u32[]{:S(2)}) collective-permute-start(bf16[1000,128]{1,0:T(8,128)(2,1)S(1)} %pad_maximum_fusion), channel_id=1, source_target_pairs={{64,0},{452,4},{72,8},{460,12},{80,16},{468,20},{88,24},{476,28},{... | collective-permute-start | bytes 768008 | tf_op jit(solution)/shard_map/ppermute | solution.py:35
  43.7 3.4 %collective-permute-start.3 = (bf16[1000,128]{1,0:T(8,128)(2,1)S(1)}, bf16[1000,128]{1,0:T(8,128)(2,1)S(1)}, u32[]{:S(2)}, u32[]{:S(2)}) collective-permute-start(bf16[1000,128]{1,0:T(8,128)(2,1)S(1)} %pad_maximum_fusion), channel_id=1, source_target_pairs={{32,0},{484,4},{40,8},{492,12},{48,16},{500,20},{56,24},{508,28},{... | collective-permute-start | bytes 768008 | tf_op jit(solution)/shard_map/ppermute | solution.py:35
  47.2 3.1 %collective-permute-done.4 = bf16[1000,128]{1,0:T(8,128)(2,1)S(1)} collective-permute-done((bf16[1000,128]{1,0:T(8,128)(2,1)S(1)}, bf16[1000,128]{1,0:T(8,128)(2,1)S(1)}, u32[]{:S(2)}, u32[]{:S(2)}) %collective-permute-start.4) | collective-permute-done | bytes 256032 | tf_op jit(solution)/shard_map/ppermute | solution.py:35
  50.3 2.7 %collective-permute-done.3 = bf16[1000,128]{1,0:T(8,128)(2,1)S(1)} collective-permute-done((bf16[1000,128]{1,0:T(8,128)(2,1)S(1)}, bf16[1000,128]{1,0:T(8,128)(2,1)S(1)}, u32[]{:S(2)}, u32[]{:S(2)}) %collective-permute-start.3) | collective-permute-done | bytes 256032 | tf_op jit(solution)/shard_map/ppermute | solution.py:35
  53.1 0.5 concatenate.79
  53.8 0.3 concatenate.81
  54.2 2.4 %collective-permute-start.8 = (bf16[4000,128]{1,0:T(8,128)(2,1)S(1)}, bf16[4000,128]{1,0:T(8,128)(2,1)S(1)}, u32[]{:S(2)}, u32[]{:S(2)}) collective-permute-start(bf16[4000,128]{1,0:T(8,128)(2,1)S(1)} %constant_dynamic-update-slice_fusion.7.refs_0_), channel_id=1, source_target_pairs={{24,0},{28,4},{0,8},{4,12},{8,16},{12,20},{16,24},{20,28},{56,32},... | collective-permute-start | bytes 3072008 | tf_op jit(solution)/shard_map/ppermute | solution.py:35
  56.6 4.3 %collective-permute-start.7 = (bf16[4000,128]{1,0:T(8,128)(2,1)S(1)}, bf16[4000,128]{1,0:T(8,128)(2,1)S(1)}, u32[]{:S(2)}, u32[]{:S(2)}) collective-permute-start(bf16[4000,128]{1,0:T(8,128)(2,1)S(1)} %constant_dynamic-update-slice_fusion.7.refs_0_), channel_id=1, source_target_pairs={{16,0},{20,4},{24,8},{28,12},{0,16},{4,20},{8,24},{12,28},{48,32},... | collective-permute-start | bytes 3072008 | tf_op jit(solution)/shard_map/ppermute | solution.py:35
  60.9 1.9 collective-permute-start.6
  62.8 0.7 maximum_maximum_fusion.local
  63.6 7.0 %local.1 = (bf16[160,1280]{1,0:T(8,128)(2,1)}, bf16[320,1024]{1,0:T(8,128)(2,1)}, bf16[320,768]{1,0:T(8,128)(2,1)}, f32[160,2432]{1,0:T(8,128)}) custom-call(bf16[160,475]{1,0:T(8,128)(2,1)} %bitcast.122, s32[3,160]{1,0:T(4,128)} %pad_add_fusion.1.edge_rows.refs_15_, bf16[16,3200]{1,0:T(8,128)(2,1)} %maximum_maximum_fusion.local, s32[1,9216]{1,0:T(1,128)} %bitcast.120), custom_call_target="tpu_custom_call" | custom-call | flops 1500000000 | bytes 293184 | tf_op jit(solution)/shard_map/local/pallas_call | solution.py:337
  70.6 1.9 collective-permute-start.9
  72.5 9.1 %collective-permute-done.8.refs_3_ = bf16[4000,128]{1,0:T(8,128)(2,1)S(1)} collective-permute-done((bf16[4000,128]{1,0:T(8,128)(2,1)S(1)}, bf16[4000,128]{1,0:T(8,128)(2,1)S(1)}, u32[]{:S(2)}, u32[]{:S(2)}) %collective-permute-start.8) | collective-permute-done | bytes 1024032 | tf_op jit(solution)/shard_map/ppermute | solution.py:35
  81.5 4.0 %collective-permute-done.7.refs_2_ = bf16[4000,128]{1,0:T(8,128)(2,1)S(1)} collective-permute-done((bf16[4000,128]{1,0:T(8,128)(2,1)S(1)}, bf16[4000,128]{1,0:T(8,128)(2,1)S(1)}, u32[]{:S(2)}, u32[]{:S(2)}) %collective-permute-start.7) | collective-permute-done | bytes 1024032 | tf_op jit(solution)/shard_map/ppermute | solution.py:35
  85.5 20.7 %collective-permute-done.6.refs_1_ = bf16[4000,128]{1,0:T(8,128)(2,1)S(1)} collective-permute-done((bf16[4000,128]{1,0:T(8,128)(2,1)S(1)}, bf16[4000,128]{1,0:T(8,128)(2,1)S(1)}, u32[]{:S(2)}, u32[]{:S(2)}) %collective-permute-start.6) | collective-permute-done | bytes 1024032 | tf_op jit(solution)/shard_map/ppermute | solution.py:35
  106.2 1.9 collective-permute-start.10
  108.2 2.4 %collective-permute-start.11 = (bf16[4000,128]{1,0:T(8,128)(2,1)S(1)}, bf16[4000,128]{1,0:T(8,128)(2,1)S(1)}, u32[]{:S(2)}, u32[]{:S(2)}) collective-permute-start(bf16[4000,128]{1,0:T(8,128)(2,1)S(1)} %collective-permute-done.7.refs_2_), channel_id=1, source_target_pairs={{4,0},{0,4},{12,8},{8,12},{20,16},{16,20},{28,24},{24,28},{36,32},... | collective-permute-start | bytes 3072008 | tf_op jit(solution)/shard_map/ppermute | solution.py:35
  110.6 2.1 collective-permute-start.12
  112.8 2.3 collective-permute-done.12.refs_7_
  115.1 0.9 copy-done.12
  116.1 23.5 %layer.1 = (bf16[2560,128]{1,0:T(8,128)(2,1)}, bf16[2560,128]{1,0:T(8,128)(2,1)}, bf16[2560,128]{1,0:T(8,128)(2,1)}, bf16[2560,128]{1,0:T(8,128)(2,1)}, bf16[256...) custom-call(bf16[4000,128]{1,0:T(8,128)(2,1)} %copy-done.5, ...), custom_call_target="tpu_custom_call" | custom-call | flops 6000000000 | bytes 11502912 | tf_op jit(solution)/shard_map/layer/pallas_call | solution.py:337
  139.6 2.2 collective-permute-start.13
  141.8 2.3 collective-permute-start.15
  144.1 2.0 collective-permute-start.17
  146.1 1.3 add_convert_fusion.4
  147.4 4.5 %collective-permute-start.14 = (bf16[2560,128]{1,0:T(8,128)(2,1)S(1)}, bf16[2560,128]{1,0:T(8,128)(2,1)S(1)}, u32[]{:S(2)}, u32[]{:S(2)}) collective-permute-start(bf16[2560,128]{1,0:T(8,128)(2,1)S(1)} %add_convert_fusion.4), channel_id=1, source_target_pairs={{0,16},{4,20},{8,24},{12,28},{16,0},{20,4},{24,8},{28,12},{32,48},... | collective-permute-start | bytes 1966088 | tf_op jit(solution)/shard_map/ppermute | solution.py:39
  151.9 0.2 add_convert_fusion.3
  152.1 3.2 %collective-permute-start.16 = (bf16[2560,128]{1,0:T(8,128)(2,1)S(1)}, bf16[2560,128]{1,0:T(8,128)(2,1)S(1)}, u32[]{:S(2)}, u32[]{:S(2)}) collective-permute-start(bf16[2560,128]{1,0:T(8,128)(2,1)S(1)} %add_convert_fusion.3), channel_id=1, source_target_pairs={{0,8},{4,12},{8,16},{12,20},{16,24},{20,28},{24,0},{28,4},{32,40},... | collective-permute-start | bytes 1966088 | tf_op jit(solution)/shard_map/ppermute | solution.py:39
  155.6 2.9 %collective-permute-start.18 = (bf16[2560,128]{1,0:T(8,128)(2,1)S(1)}, bf16[2560,128]{1,0:T(8,128)(2,1)S(1)}, u32[]{:S(2)}, u32[]{:S(2)}) collective-permute-start(bf16[2560,128]{1,0:T(8,128)(2,1)S(1)} %add_convert_fusion.2), channel_id=1, source_target_pairs={{0,24},{4,28},{8,0},{12,4},{16,8},{20,12},{24,16},{28,20},{32,56},... | collective-permute-start | bytes 1966088 | tf_op jit(solution)/shard_map/ppermute | solution.py:39
  158.4 1.9 collective-permute-start.19
  160.4 5.3 %nodes.1 = (bf16[4,3200]{1,0:T(4,128)(2,1)}, f32[4,3200]{1,0:T(4,128)}) custom-call(bf16[160,475]{1,0:T(8,128)(2,1)} %bitcast.124, bf16[160,2432]{1,0:T(8,128)(2,1)} %get-tuple-element.40.scaled, bf16[160,2432]{1,0:T(8,128)(2,1)} %get-tuple-element.41.grad_dst, s32[3,160]{1,0:T(4,128)} %pad_add_fusion.1.edge_rows.refs_15_), custom_call_target="tpu_custom_call" | custom-call | flops 600000000 | bytes 1710400 | tf_op jit(solution)/shard_map/nodes/pallas_call | solution.py:337
  165.6 2.9 %collective-permute-done.14 = bf16[2560,128]{1,0:T(8,128)(2,1)S(1)} collective-permute-done((bf16[2560,128]{1,0:T(8,128)(2,1)S(1)}, bf16[2560,128]{1,0:T(8,128)(2,1)S(1)}, u32[]{:S(2)}, u32[]{:S(2)}) %collective-permute-start.14) | collective-permute-done | bytes 655392 | tf_op jit(solution)/shard_map/ppermute | solution.py:39
  168.5 11.4 %collective-permute-done.16 = bf16[2560,128]{1,0:T(8,128)(2,1)S(1)} collective-permute-done((bf16[2560,128]{1,0:T(8,128)(2,1)S(1)}, bf16[2560,128]{1,0:T(8,128)(2,1)S(1)}, u32[]{:S(2)}, u32[]{:S(2)}) %collective-permute-start.16) | collective-permute-done | bytes 655392 | tf_op jit(solution)/shard_map/ppermute | solution.py:39
  180.0 2.0 collective-permute-done.18
  182.0 0.4 add_convert_fusion
  182.5 1.9 collective-permute-start.20
  184.4 5.1 %collective-permute-start.22 = (bf16[640,128]{1,0:T(8,128)(2,1)S(1)}, bf16[640,128]{1,0:T(8,128)(2,1)S(1)}, u32[]{:S(2)}, u32[]{:S(2)}) collective-permute-start(bf16[640,128]{1,0:T(8,128)(2,1)S(1)} %get-tuple-element.54), channel_id=1, source_target_pairs={{0,480},{4,36},{8,488},{12,44},{16,496},{20,52},{24,504},{28,60},{... | collective-permute-start | bytes 491528 | tf_op jit(solution)/shard_map/ppermute | solution.py:39
  189.5 2.0 collective-permute-start.21
  191.5 1.5 collective-permute-done.22
  193.0 7.4 %collective-permute-done.21 = bf16[640,128]{1,0:T(8,128)(2,1)S(1)} collective-permute-done((bf16[640,128]{1,0:T(8,128)(2,1)S(1)}, bf16[640,128]{1,0:T(8,128)(2,1)S(1)}, u32[]{:S(2)}, u32[]{:S(2)}) %collective-permute-start.21) | collective-permute-done | bytes 163872 | tf_op jit(solution)/shard_map/ppermute | solution.py:39
  200.8 4.8 %collective-permute-start.23 = (bf16[150,128]{1,0:T(8,128)(2,1)S(1)}, bf16[150,128]{1,0:T(8,128)(2,1)S(1)}, u32[]{:S(2)}, u32[]{:S(2)}) collective-permute-start(bf16[150,128]{1,0:T(8,128)(2,1)S(1)} %pad_maximum_fusion.5), channel_id=1, source_target_pairs={{0,128},{4,388},{8,136},{12,396},{16,144},{20,404},{24,152},{28,41... | collective-permute-start | bytes 115208 | tf_op jit(solution)/shard_map/ppermute | solution.py:39
  205.6 7.0 %collective-permute-start.24 = (bf16[150,128]{1,0:T(8,128)(2,1)S(1)}, bf16[150,128]{1,0:T(8,128)(2,1)S(1)}, u32[]{:S(2)}, u32[]{:S(2)}) collective-permute-start(bf16[150,128]{1,0:T(8,128)(2,1)S(1)} %pad_maximum_fusion.6), channel_id=1, source_target_pairs={{0,256},{4,260},{8,264},{12,268},{16,272},{20,276},{24,280},{28,28... | collective-permute-start | bytes 115208 | tf_op jit(solution)/shard_map/ppermute | solution.py:39
  212.6 3.6 %collective-permute-start.25 = (bf16[150,128]{1,0:T(8,128)(2,1)S(1)}, bf16[150,128]{1,0:T(8,128)(2,1)S(1)}, u32[]{:S(2)}, u32[]{:S(2)}) collective-permute-start(bf16[150,128]{1,0:T(8,128)(2,1)S(1)} %pad_maximum_fusion.7), channel_id=1, source_target_pairs={{0,384},{4,132},{8,392},{12,140},{16,400},{20,148},{24,408},{28,15... | collective-permute-start | bytes 115208 | tf_op jit(solution)/shard_map/ppermute | solution.py:39
  216.3 4.6 %collective-permute-done.24 = bf16[150,128]{1,0:T(8,128)(2,1)S(1)} collective-permute-done((bf16[150,128]{1,0:T(8,128)(2,1)S(1)}, bf16[150,128]{1,0:T(8,128)(2,1)S(1)}, u32[]{:S(2)}, u32[]{:S(2)}) %collective-permute-start.24) | collective-permute-done | bytes 38432 | tf_op jit(solution)/shard_map/ppermute | solution.py:39
  220.9 1.7 collective-permute-done.25
  222.8 0.7 broadcast_in_dim.23
  223.4 4.6 %all-to-all-start = ((f32[4,10,640]{2,1,0:T(8,128)}), f32[4,10,640]{2,1,0:T(8,128)S(1)}, u32[]{:S(2)}, u32[]{:S(2)}) async-start(f32[4,10,640]{2,1,0:T(8,128)} %broadcast_in_dim.23), calls=%async_computation | async-start | bytes 327680 | tf_op jit(solution)/shard_map/all_to_all | solution.py:440
  228.0 0.6 fusion.1
  228.7 5.5 %all-to-all-done = f32[4,10,640]{2,1,0:T(8,128)S(1)} async-done(((f32[4,10,640]{2,1,0:T(8,128)}), f32[4,10,640]{2,1,0:T(8,128)S(1)}, u32[]{:S(2)}, u32[]{:S(2)}) %all-to-all-start) | async-done | bytes 102432 | tf_op jit(solution)/shard_map/all_to_all | solution.py:440
  234.2 0.6 reduce_sum.9
  (131 shorter events, 1.7 us)
Async XLA Ops:
  3.9 30.8 %collective-permute-start.2 = (bf16[250,128]{1,0:T(8,128)(2,1)S(1)}, bf16[250,128]{1,0:T(8,128)(2,1)S(1)}, u32[]{:S(2)}, u32[]{:S(2)}) collective-permute-start(bf16[250,128]{1,0:T(8,128)(2,1)S(1)} %pad_maximum_fusion.2), channel_id=1, source_target_pairs={{384,0},{132,4},{392,8},{140,12},{400,16},{148,20},{408,24},{156,2... | collective-permute-start | bytes 192008 | tf_op jit(solution)/shard_map/ppermute | solution.py:35
  13.0 21.8 %collective-permute-start.1 = (bf16[250,128]{1,0:T(8,128)(2,1)S(1)}, bf16[250,128]{1,0:T(8,128)(2,1)S(1)}, u32[]{:S(2)}, u32[]{:S(2)}) collective-permute-start(bf16[250,128]{1,0:T(8,128)(2,1)S(1)} %pad_maximum_fusion.2), channel_id=1, source_target_pairs={{256,0},{260,4},{264,8},{268,12},{272,16},{276,20},{280,24},{284,2... | collective-permute-start | bytes 192008 | tf_op jit(solution)/shard_map/ppermute | solution.py:35
  23.9 11.3 %collective-permute-start = (bf16[250,128]{1,0:T(8,128)(2,1)S(1)}, bf16[250,128]{1,0:T(8,128)(2,1)S(1)}, u32[]{:S(2)}, u32[]{:S(2)}) collective-permute-start(bf16[250,128]{1,0:T(8,128)(2,1)S(1)} %pad_maximum_fusion.2), channel_id=1, source_target_pairs={{128,0},{388,4},{136,8},{396,12},{144,16},{404,20},{152,24},{412,2... | collective-permute-start | bytes 192008 | tf_op jit(solution)/shard_map/ppermute | solution.py:35
  35.6 17.4 %collective-permute-start.5 = (bf16[1000,128]{1,0:T(8,128)(2,1)S(1)}, bf16[1000,128]{1,0:T(8,128)(2,1)S(1)}, u32[]{:S(2)}, u32[]{:S(2)}) collective-permute-start(bf16[1000,128]{1,0:T(8,128)(2,1)S(1)} %pad_maximum_fusion), channel_id=1, source_target_pairs={{480,0},{36,4},{488,8},{44,12},{496,16},{52,20},{504,24},{60,28},{... | collective-permute-start | bytes 768008 | tf_op jit(solution)/shard_map/ppermute | solution.py:35
  38.2 12.1 %collective-permute-start.4 = (bf16[1000,128]{1,0:T(8,128)(2,1)S(1)}, bf16[1000,128]{1,0:T(8,128)(2,1)S(1)}, u32[]{:S(2)}, u32[]{:S(2)}) collective-permute-start(bf16[1000,128]{1,0:T(8,128)(2,1)S(1)} %pad_maximum_fusion), channel_id=1, source_target_pairs={{64,0},{452,4},{72,8},{460,12},{80,16},{468,20},{88,24},{476,28},{... | collective-permute-start | bytes 768008 | tf_op jit(solution)/shard_map/ppermute | solution.py:35
  43.7 9.3 %collective-permute-start.3 = (bf16[1000,128]{1,0:T(8,128)(2,1)S(1)}, bf16[1000,128]{1,0:T(8,128)(2,1)S(1)}, u32[]{:S(2)}, u32[]{:S(2)}) collective-permute-start(bf16[1000,128]{1,0:T(8,128)(2,1)S(1)} %pad_maximum_fusion), channel_id=1, source_target_pairs={{32,0},{484,4},{40,8},{492,12},{48,16},{500,20},{56,24},{508,28},{... | collective-permute-start | bytes 768008 | tf_op jit(solution)/shard_map/ppermute | solution.py:35
  53.1 9.7 %copy-start.3 = (bf16[1,4,3200]{2,1,0:T(4,128)(2,1)S(1)}, bf16[1,4,3200]{2,1,0:T(4,128)(2,1)}, u32[]{:S(2)}) copy-start(bf16[1,4,3200]{2,1,0:T(4,128)(2,1)} %param.15) | copy-start | bytes 76804
  54.2 16.4 %copy-start.5 = (bf16[4000,128]{1,0:T(8,128)(2,1)}, bf16[4000,128]{1,0:T(8,128)(2,1)S(1)}, u32[]{:S(2)}) copy-start(bf16[4000,128]{1,0:T(8,128)(2,1)S(1)} %constant_dynamic-update-slice_fusion.7.refs_0_) | copy-start | bytes 3072004
  54.2 27.4 %collective-permute-start.8 = (bf16[4000,128]{1,0:T(8,128)(2,1)S(1)}, bf16[4000,128]{1,0:T(8,128)(2,1)S(1)}, u32[]{:S(2)}, u32[]{:S(2)}) collective-permute-start(bf16[4000,128]{1,0:T(8,128)(2,1)S(1)} %constant_dynamic-update-slice_fusion.7.refs_0_), channel_id=1, source_target_pairs={{24,0},{28,4},{0,8},{4,12},{8,16},{12,20},{16,24},{20,28},{56,32},... | collective-permute-start | bytes 3072008 | tf_op jit(solution)/shard_map/ppermute | solution.py:35
  56.6 29.0 %collective-permute-start.7 = (bf16[4000,128]{1,0:T(8,128)(2,1)S(1)}, bf16[4000,128]{1,0:T(8,128)(2,1)S(1)}, u32[]{:S(2)}, u32[]{:S(2)}) collective-permute-start(bf16[4000,128]{1,0:T(8,128)(2,1)S(1)} %constant_dynamic-update-slice_fusion.7.refs_0_), channel_id=1, source_target_pairs={{16,0},{20,4},{24,8},{28,12},{0,16},{4,20},{8,24},{12,28},{48,32},... | collective-permute-start | bytes 3072008 | tf_op jit(solution)/shard_map/ppermute | solution.py:35
  60.9 45.3 %collective-permute-start.6 = (bf16[4000,128]{1,0:T(8,128)(2,1)S(1)}, bf16[4000,128]{1,0:T(8,128)(2,1)S(1)}, u32[]{:S(2)}, u32[]{:S(2)}) collective-permute-start(bf16[4000,128]{1,0:T(8,128)(2,1)S(1)} %constant_dynamic-update-slice_fusion.7.refs_0_), channel_id=1, source_target_pairs={{8,0},{12,4},{16,8},{20,12},{24,16},{28,20},{0,24},{4,28},{40,32},... | collective-permute-start | bytes 3072008 | tf_op jit(solution)/shard_map/ppermute | solution.py:35
  70.6 42.1 %collective-permute-start.9 = (bf16[4000,128]{1,0:T(8,128)(2,1)S(1)}, bf16[4000,128]{1,0:T(8,128)(2,1)S(1)}, u32[]{:S(2)}, u32[]{:S(2)}) collective-permute-start(bf16[4000,128]{1,0:T(8,128)(2,1)S(1)} %constant_dynamic-update-slice_fusion.7.refs_0_), channel_id=1, source_target_pairs={{4,0},{0,4},{12,8},{8,12},{20,16},{16,20},{28,24},{24,28},{36,32},... | collective-permute-start | bytes 3072008 | tf_op jit(solution)/shard_map/ppermute | solution.py:35
  81.5 34.5 %copy-start.6 = (bf16[4000,128]{1,0:T(8,128)(2,1)}, bf16[4000,128]{1,0:T(8,128)(2,1)S(1)}, u32[]{:S(2)}) copy-start(bf16[4000,128]{1,0:T(8,128)(2,1)S(1)} %collective-permute-done.8.refs_3_) | copy-start | bytes 3072004
  85.5 30.5 %copy-start.7 = (bf16[4000,128]{1,0:T(8,128)(2,1)}, bf16[4000,128]{1,0:T(8,128)(2,1)S(1)}, u32[]{:S(2)}) copy-start(bf16[4000,128]{1,0:T(8,128)(2,1)S(1)} %collective-permute-done.7.refs_2_) | copy-start | bytes 3072004
  106.2 9.8 %copy-start.8 = (bf16[4000,128]{1,0:T(8,128)(2,1)}, bf16[4000,128]{1,0:T(8,128)(2,1)S(1)}, u32[]{:S(2)}) copy-start(bf16[4000,128]{1,0:T(8,128)(2,1)S(1)} %collective-permute-done.6.refs_1_) | copy-start | bytes 3072004
  106.2 6.5 %collective-permute-start.10 = (bf16[4000,128]{1,0:T(8,128)(2,1)S(1)}, bf16[4000,128]{1,0:T(8,128)(2,1)S(1)}, u32[]{:S(2)}, u32[]{:S(2)}) collective-permute-start(bf16[4000,128]{1,0:T(8,128)(2,1)S(1)} %collective-permute-done.6.refs_1_), channel_id=1, source_target_pairs={{4,0},{0,4},{12,8},{8,12},{20,16},{16,20},{28,24},{24,28},{36,32},... | collective-permute-start | bytes 3072008 | tf_op jit(solution)/shard_map/ppermute | solution.py:35
  108.2 4.6 %collective-permute-start.11 = (bf16[4000,128]{1,0:T(8,128)(2,1)S(1)}, bf16[4000,128]{1,0:T(8,128)(2,1)S(1)}, u32[]{:S(2)}, u32[]{:S(2)}) collective-permute-start(bf16[4000,128]{1,0:T(8,128)(2,1)S(1)} %collective-permute-done.7.refs_2_), channel_id=1, source_target_pairs={{4,0},{0,4},{12,8},{8,12},{20,16},{16,20},{28,24},{24,28},{36,32},... | collective-permute-start | bytes 3072008 | tf_op jit(solution)/shard_map/ppermute | solution.py:35
  110.6 4.5 %collective-permute-start.12 = (bf16[4000,128]{1,0:T(8,128)(2,1)S(1)}, bf16[4000,128]{1,0:T(8,128)(2,1)S(1)}, u32[]{:S(2)}, u32[]{:S(2)}) collective-permute-start(bf16[4000,128]{1,0:T(8,128)(2,1)S(1)} %collective-permute-done.8.refs_3_), channel_id=1, source_target_pairs={{4,0},{0,4},{12,8},{8,12},{20,16},{16,20},{28,24},{24,28},{36,32},... | collective-permute-start | bytes 3072008 | tf_op jit(solution)/shard_map/ppermute | solution.py:35
  112.7 3.4 %copy-start.9 = (bf16[4000,128]{1,0:T(8,128)(2,1)}, bf16[4000,128]{1,0:T(8,128)(2,1)S(1)}, u32[]{:S(2)}) copy-start(bf16[4000,128]{1,0:T(8,128)(2,1)S(1)} %collective-permute-done.9.refs_4_) | copy-start | bytes 3072004
  112.7 3.3 %copy-start.10 = (bf16[4000,128]{1,0:T(8,128)(2,1)}, bf16[4000,128]{1,0:T(8,128)(2,1)S(1)}, u32[]{:S(2)}) copy-start(bf16[4000,128]{1,0:T(8,128)(2,1)S(1)} %collective-permute-done.10.refs_5_) | copy-start | bytes 3072004
  112.8 3.3 %copy-start.11 = (bf16[4000,128]{1,0:T(8,128)(2,1)}, bf16[4000,128]{1,0:T(8,128)(2,1)S(1)}, u32[]{:S(2)}) copy-start(bf16[4000,128]{1,0:T(8,128)(2,1)S(1)} %collective-permute-done.11.refs_6_) | copy-start | bytes 3072004
  115.1 0.9 copy-start.12
  139.6 12.3 %copy-start.1 = (bf16[2560,128]{1,0:T(8,128)(2,1)S(1)}, bf16[2560,128]{1,0:T(8,128)(2,1)}, u32[]{:S(2)}) copy-start(bf16[2560,128]{1,0:T(8,128)(2,1)} %get-tuple-element.36) | copy-start | bytes 1966084
  139.6 6.5 %collective-permute-start.13 = (bf16[2560,128]{1,0:T(8,128)(2,1)}, bf16[2560,128]{1,0:T(8,128)(2,1)S(1)}, u32[]{:S(2)}, u32[]{:S(2)}) collective-permute-start(bf16[2560,128]{1,0:T(8,128)(2,1)} %get-tuple-element.35), channel_id=1, source_target_pairs={{0,4},{4,0},{8,12},{12,8},{16,20},{20,16},{24,28},{28,24},{32,36},... | collective-permute-start | bytes 1966088 | tf_op jit(solution)/shard_map/ppermute | solution.py:39
  141.8 10.1 %collective-permute-start.15 = (bf16[2560,128]{1,0:T(8,128)(2,1)}, bf16[2560,128]{1,0:T(8,128)(2,1)S(1)}, u32[]{:S(2)}, u32[]{:S(2)}) collective-permute-start(bf16[2560,128]{1,0:T(8,128)(2,1)} %get-tuple-element.37), channel_id=1, source_target_pairs={{0,4},{4,0},{8,12},{12,8},{16,20},{20,16},{24,28},{28,24},{32,36},... | collective-permute-start | bytes 1966088 | tf_op jit(solution)/shard_map/ppermute | solution.py:39
  144.1 11.3 %collective-permute-start.17 = (bf16[2560,128]{1,0:T(8,128)(2,1)}, bf16[2560,128]{1,0:T(8,128)(2,1)S(1)}, u32[]{:S(2)}, u32[]{:S(2)}) collective-permute-start(bf16[2560,128]{1,0:T(8,128)(2,1)} %get-tuple-element.39), channel_id=1, source_target_pairs={{0,4},{4,0},{8,12},{12,8},{16,20},{20,16},{24,28},{28,24},{32,36},... | collective-permute-start | bytes 1966088 | tf_op jit(solution)/shard_map/ppermute | solution.py:39
  147.4 8.0 %copy-start = (bf16[2560,128]{1,0:T(8,128)(2,1)S(1)}, bf16[2560,128]{1,0:T(8,128)(2,1)}, u32[]{:S(2)}) copy-start(bf16[2560,128]{1,0:T(8,128)(2,1)} %get-tuple-element.38) | copy-start | bytes 1966084
  147.4 21.1 %collective-permute-start.14 = (bf16[2560,128]{1,0:T(8,128)(2,1)S(1)}, bf16[2560,128]{1,0:T(8,128)(2,1)S(1)}, u32[]{:S(2)}, u32[]{:S(2)}) collective-permute-start(bf16[2560,128]{1,0:T(8,128)(2,1)S(1)} %add_convert_fusion.4), channel_id=1, source_target_pairs={{0,16},{4,20},{8,24},{12,28},{16,0},{20,4},{24,8},{28,12},{32,48},... | collective-permute-start | bytes 1966088 | tf_op jit(solution)/shard_map/ppermute | solution.py:39
  152.1 6.3 %copy-start.13 = (bf16[2560,128]{1,0:T(8,128)(2,1)S(1)}, bf16[2560,128]{1,0:T(8,128)(2,1)}, u32[]{:S(2)}) copy-start(bf16[2560,128]{1,0:T(8,128)(2,1)} %get-tuple-element.47) | copy-start | bytes 1966084
  152.1 27.9 %collective-permute-start.16 = (bf16[2560,128]{1,0:T(8,128)(2,1)S(1)}, bf16[2560,128]{1,0:T(8,128)(2,1)S(1)}, u32[]{:S(2)}, u32[]{:S(2)}) collective-permute-start(bf16[2560,128]{1,0:T(8,128)(2,1)S(1)} %add_convert_fusion.3), channel_id=1, source_target_pairs={{0,8},{4,12},{8,16},{12,20},{16,24},{20,28},{24,0},{28,4},{32,40},... | collective-permute-start | bytes 1966088 | tf_op jit(solution)/shard_map/ppermute | solution.py:39
  155.6 26.4 %copy-start.2 = (bf16[2560,128]{1,0:T(8,128)(2,1)S(1)}, bf16[2560,128]{1,0:T(8,128)(2,1)}, u32[]{:S(2)}) copy-start(bf16[2560,128]{1,0:T(8,128)(2,1)} %get-tuple-element.46) | copy-start | bytes 1966084
  155.6 26.4 %collective-permute-start.18 = (bf16[2560,128]{1,0:T(8,128)(2,1)S(1)}, bf16[2560,128]{1,0:T(8,128)(2,1)S(1)}, u32[]{:S(2)}, u32[]{:S(2)}) collective-permute-start(bf16[2560,128]{1,0:T(8,128)(2,1)S(1)} %add_convert_fusion.2), channel_id=1, source_target_pairs={{0,24},{4,28},{8,0},{12,4},{16,8},{20,12},{24,16},{28,20},{32,56},... | collective-permute-start | bytes 1966088 | tf_op jit(solution)/shard_map/ppermute | solution.py:39
  158.4 23.5 %collective-permute-start.19 = (bf16[2560,128]{1,0:T(8,128)(2,1)S(1)}, bf16[2560,128]{1,0:T(8,128)(2,1)S(1)}, u32[]{:S(2)}, u32[]{:S(2)}) collective-permute-start(bf16[2560,128]{1,0:T(8,128)(2,1)S(1)} %copy-done.13), channel_id=1, source_target_pairs={{0,4},{4,0},{8,12},{12,8},{16,20},{20,16},{24,28},{28,24},{32,36},... | collective-permute-start | bytes 1966088 | tf_op jit(solution)/shard_map/ppermute | solution.py:39
  182.5 9.1 %collective-permute-start.20 = (bf16[640,128]{1,0:T(8,128)(2,1)S(1)}, bf16[640,128]{1,0:T(8,128)(2,1)S(1)}, u32[]{:S(2)}, u32[]{:S(2)}) collective-permute-start(bf16[640,128]{1,0:T(8,128)(2,1)S(1)} %get-tuple-element.53), channel_id=1, source_target_pairs={{0,32},{4,484},{8,40},{12,492},{16,48},{20,500},{24,56},{28,508},{... | collective-permute-start | bytes 491528 | tf_op jit(solution)/shard_map/ppermute | solution.py:39
  184.4 8.6 %collective-permute-start.22 = (bf16[640,128]{1,0:T(8,128)(2,1)S(1)}, bf16[640,128]{1,0:T(8,128)(2,1)S(1)}, u32[]{:S(2)}, u32[]{:S(2)}) collective-permute-start(bf16[640,128]{1,0:T(8,128)(2,1)S(1)} %get-tuple-element.54), channel_id=1, source_target_pairs={{0,480},{4,36},{8,488},{12,44},{16,496},{20,52},{24,504},{28,60},{... | collective-permute-start | bytes 491528 | tf_op jit(solution)/shard_map/ppermute | solution.py:39
  189.5 10.9 %collective-permute-start.21 = (bf16[640,128]{1,0:T(8,128)(2,1)S(1)}, bf16[640,128]{1,0:T(8,128)(2,1)S(1)}, u32[]{:S(2)}, u32[]{:S(2)}) collective-permute-start(bf16[640,128]{1,0:T(8,128)(2,1)S(1)} %get-tuple-element.55), channel_id=1, source_target_pairs={{0,64},{4,452},{8,72},{12,460},{16,80},{20,468},{24,88},{28,476},{... | collective-permute-start | bytes 491528 | tf_op jit(solution)/shard_map/ppermute | solution.py:39
  200.5 27.6 %copy-start.4 = (f32[4,3200]{1,0:T(4,128)S(1)}, f32[4,3200]{1,0:T(4,128)}, u32[]{:S(2)}) copy-start(f32[4,3200]{1,0:T(4,128)} %get-tuple-element.45) | copy-start | bytes 153604
  200.8 15.5 %collective-permute-start.23 = (bf16[150,128]{1,0:T(8,128)(2,1)S(1)}, bf16[150,128]{1,0:T(8,128)(2,1)S(1)}, u32[]{:S(2)}, u32[]{:S(2)}) collective-permute-start(bf16[150,128]{1,0:T(8,128)(2,1)S(1)} %pad_maximum_fusion.5), channel_id=1, source_target_pairs={{0,128},{4,388},{8,136},{12,396},{16,144},{20,404},{24,152},{28,41... | collective-permute-start | bytes 115208 | tf_op jit(solution)/shard_map/ppermute | solution.py:39
  205.6 15.3 %collective-permute-start.24 = (bf16[150,128]{1,0:T(8,128)(2,1)S(1)}, bf16[150,128]{1,0:T(8,128)(2,1)S(1)}, u32[]{:S(2)}, u32[]{:S(2)}) collective-permute-start(bf16[150,128]{1,0:T(8,128)(2,1)S(1)} %pad_maximum_fusion.6), channel_id=1, source_target_pairs={{0,256},{4,260},{8,264},{12,268},{16,272},{20,276},{24,280},{28,28... | collective-permute-start | bytes 115208 | tf_op jit(solution)/shard_map/ppermute | solution.py:39
  212.6 10.0 %collective-permute-start.25 = (bf16[150,128]{1,0:T(8,128)(2,1)S(1)}, bf16[150,128]{1,0:T(8,128)(2,1)S(1)}, u32[]{:S(2)}, u32[]{:S(2)}) collective-permute-start(bf16[150,128]{1,0:T(8,128)(2,1)S(1)} %pad_maximum_fusion.7), channel_id=1, source_target_pairs={{0,384},{4,132},{8,392},{12,140},{16,400},{20,148},{24,408},{28,15... | collective-permute-start | bytes 115208 | tf_op jit(solution)/shard_map/ppermute | solution.py:39
  223.4 10.8 %all-to-all-start = ((f32[4,10,640]{2,1,0:T(8,128)}), f32[4,10,640]{2,1,0:T(8,128)S(1)}, u32[]{:S(2)}, u32[]{:S(2)}) async-start(f32[4,10,640]{2,1,0:T(8,128)} %broadcast_in_dim.23), calls=%async_computation | async-start | bytes 327680 | tf_op jit(solution)/shard_map/all_to_all | solution.py:440

commit v7 on v6

--- a/solution.py
+++ b/solution.py
@@ -20,6 +20,7 @@
 DEPTHS = (40, 32, 24)
 UNITS = (5, 8, 6)
 TERM_ROWS = 400 + 240
+X_SPLIT = 1600 + 3 * 160
 SOURCE_AT, TARGET_AT, POSITION_AT = (0, 1280, 2304), (3072, 4352, 5376), (6144, 7424, 8448)
 VMEM_LIMIT = 56 * 2**20
 F32, BF16 = jnp.float32, jnp.bfloat16
@@ -57,8 +58,10 @@
     return z * 8 + x * 2 + (me % 2 + cr) % 2
 
 
-def x_pieces(block):
-    return (block,) + tuple(pull(block, dx=x) for x in (1, 2, 3))
+def gather_x(block, first):
+    right, left = pull(block, dx=1), pull(block, dx=3)
+    right, left = (lax.optimization_barrier((first, a))[1] for a in (right, left))
+    return block, right, pull(right[:X_SPLIT], dx=1), pull(left[X_SPLIT:], dx=3), left
 
 
 def scatter_sum(pieces, beside):
@@ -69,8 +72,12 @@
         return total
 
     a = [add(pieces[x], push(pieces[4 + x], dc=1)).astype(BF16) for x in range(4)]
-    arrived, beside = lax.optimization_barrier(([push(a[x], dx=x) for x in (2, 1, 3)], beside))
-    total = add(a[0], *arrived).astype(BF16)
+    half = 2 * TERM_ROWS
+    up, down = push(a[2][:half], dx=1), push(a[2][half:], dx=3)
+    right = push(jnp.concatenate([add(a[1][:half], up).astype(BF16), a[1][half:]], axis=0), dx=1)
+    left = push(jnp.concatenate([a[3][:half], add(a[3][half:], down).astype(BF16)], axis=0), dx=3)
+    (right, left), beside = lax.optimization_barrier(((right, left), beside))
+    total = add(a[0], right, left).astype(BF16)
     parts = [total[n * TERM_ROWS : (n + 1) * TERM_ROWS] for n in range(4)]
     total = add(parts[0], *(push(parts[n], dz=NEAR[n]) for n in (1, 2, 3))).astype(BF16)
     terms, shard = total[:400].reshape(25, 16, CH), total[400:].reshape(5, 48, CH)
@@ -162,22 +169,27 @@
 
 
 def layer_kernel(*refs):
-    pieces = refs[:8]
-    t0, t1, t2, turned_grad, rot, bias, alpha_ref, edge_rows, maps = refs[8:17]
-    terms_out = refs[17:25]
-    scaled_out, grad_dst = refs[25:27]
-    w0, w1, w2, values, d0, d1, d2, p0, p1, p2, g0, g1, g2, src_terms, feats, n0, n1, n2, m0, m1, m2 = refs[27:]
-    for k, piece in enumerate(pieces):
+    t0, t1, t2, turned_grad, rot, bias, alpha_ref, edge_rows, maps = refs[10:19]
+    terms_out = refs[19:27]
+    scaled_out, grad_dst = refs[27:29]
+    w0, w1, w2, values, d0, d1, d2, p0, p1, p2, g0, g1, g2, src_terms, feats, n0, n1, n2, m0, m1, m2 = refs[29:]
+    for k in range(8):
+        own, right, upper, lower, left = refs[k // 4 * 5 : k // 4 * 5 + 5]
+
+        def rows_at(at, rows, whole=(own, right, None, left)[k % 4], upper=upper, lower=lower):
+            if whole is not None:
+                return whole[at : at + rows, :]
+            return upper[at : at + rows, :] if at < X_SPLIT else lower[at - X_SPLIT : at - X_SPLIT + rows, :]
+
         for near in range(4):
             row = k * 64 + near * 16
             for u in range(LCOEF):
-                at = near * FAR_ROWS + u * 16
-                feats[row : row + 16, u * CH : (u + 1) * CH] = piece[at : at + 16, :]
+                feats[row : row + 16, u * CH : (u + 1) * CH] = rows_at(near * FAR_ROWS + u * 16, 16)
         at = 4 * FAR_ROWS
         for out, units, depth in zip((w0, w1, w2), UNITS, DEPTHS):
             rows = 4 * depth
             for u in range(units):
-                out[k * rows : (k + 1) * rows, u * CH : (u + 1) * CH] = piece[at : at + rows, :]
+                out[k * rows : (k + 1) * rows, u * CH : (u + 1) * CH] = rows_at(at, rows)
                 at += rows
     source_hot = hot(edge_rows[0:1, :], (512, EDGES), 0)
     for first in range(0, FULL, 640):
@@ -398,7 +410,7 @@
     for units, depth in zip(UNITS, DEPTHS):
         near_parts.append(merged(blocks, at, units, depth))
         at += units * depth
-    pieces = x_pieces(jnp.concatenate([b[:FAR_ROWS] for b in blocks] + near_parts, axis=0))
+    near_block = jnp.concatenate([b[:FAR_ROWS] for b in blocks] + near_parts, axis=0)
 
     maps = index_maps(me)
     cotangent = out_grad[0]
@@ -413,7 +425,7 @@
         [((160, FULL), BF16), ((160, FULL), F32), ((160, 640), BF16), ((320, 512), BF16), ((320, 384), BF16)],
         1_500_000_000,
     )
-    pieces = (pieces[0], *(lax.optimization_barrier((targets[0], pieces[x]))[1] for x in (1, 2, 3)))
+    pieces = gather_x(near_block, targets[0])
     pieces = pieces + tuple(pull(a, dc=1) for a in pieces)
     outs = call(
         layer_kernel, "layer",

time: 237 us -> 241 us (1.017)
  starting transfers between devices: 102 us -> 113 us
  waiting for transfers between devices: 79.4 us -> 71.2 us
    ppermute x13 -> x15, waiting for transfers between devices: 42.3 us -> 33.3 us  [pull(): lax.ppermute(a, 'edge', [(where_to(i, dz, dx, dc), i) for i in range(128)])]
    ppermute x13 -> x15, starting transfers between devices: 53.9 us -> 60.1 us  [pull(): lax.ppermute(a, 'edge', [(where_to(i, dz, dx, dc), i) for i in range(128)])]
    ppermute x13 -> x14, starting transfers between devices: 43.4 us -> 48.5 us  [push(): lax.ppermute(a, 'edge', [(i, where_to(i, dz, dx, dc)) for i in range(128)])]
    ppermute x13 -> x14, waiting for transfers between devices: 31.6 us -> 32.3 us  [push(): lax.ppermute(a, 'edge', [(i, where_to(i, dz, dx, dc)) for i in range(128)])]
  transfers between devices with their start and end apart: 27 -> 30, of which waited for: 16 -> 16; matrix products, arithmetic and copies ran while one was open for 3% -> 3% of each run, Pallas kernels for 5% -> 5%
where the time goes in v7:
time: 241 us; the launch traced here: 239 us
  starting transfers between devices  113 us (47%)
  waiting for transfers between devices  71.2 us (30%)
  Pallas kernels  35.7 us (15%)
  other arithmetic  8.94 us (4%)
  local copies, waits for them, and re-layouts  7.4 us (3%)
  between operations  2.52 us (1%)
    ppermute x15, starting transfers between devices, pull(): lax.ppermute(a, 'edge', [(where_to(i, dz, dx, dc), i) for i in range(128)])  60.1 us
    ppermute x14, starting transfers between devices, push(): lax.ppermute(a, 'edge', [(i, where_to(i, dz, dx, dc)) for i in range(128)])  48.5 us
    pallas_call x3, Pallas kernels, call(): pl.pallas_call(kernel, out_shape=tuple((jax.ShapeDtypeStruct(s, t) for s,...  35.7 us
    ppermute x15, waiting for transfers between devices, pull(): lax.ppermute(a, 'edge', [(where_to(i, dz, dx, dc), i) for i in range(128)])  33.3 us
    ppermute x14, waiting for transfers between devices, push(): lax.ppermute(a, 'edge', [(i, where_to(i, dz, dx, dc)) for i in range(128)])  32.3 us
    all_to_all x1, waiting for transfers between devices, local(): lax.all_to_all(jnp.broadcast_to(shard, (n_rep, 10, 640)), 'rep', split_ax...  5.51 us
  transfers between devices with their start and end apart: 30, of which 16 were waited for; matrix products, arithmetic and copies ran while one was open for 3% of the time, Pallas kernels for 5%

profile of v7, /device:TPU:6, one launch (start us, length us, event | category | flops | bytes accessed | tf_op | source)
XLA Modules:
  0.0 239.0 jit_solution(14843396924189443979)
XLA Ops:
  0.6 0.7 slice_bitcast_fusion.4
  1.3 0.8 fusion.54
  2.2 0.8 reshape.567
  3.0 0.8 reshape_squeeze.3
  3.9 9.1 %collective-permute-start.2 = (bf16[250,128]{1,0:T(8,128)(2,1)S(1)}, bf16[250,128]{1,0:T(8,128)(2,1)S(1)}, u32[]{:S(2)}, u32[]{:S(2)}) collective-permute-start(bf16[250,128]{1,0:T(8,128)(2,1)S(1)} %pad_maximum_fusion.4), channel_id=1, source_target_pairs={{384,0},{132,4},{392,8},{140,12},{400,16},{148,20},{408,24},{156,2... | collective-permute-start | bytes 192008 | tf_op jit(solution)/shard_map/ppermute | solution.py:36
  13.0 10.9 %collective-permute-start.1 = (bf16[250,128]{1,0:T(8,128)(2,1)S(1)}, bf16[250,128]{1,0:T(8,128)(2,1)S(1)}, u32[]{:S(2)}, u32[]{:S(2)}) collective-permute-start(bf16[250,128]{1,0:T(8,128)(2,1)S(1)} %pad_maximum_fusion.4), channel_id=1, source_target_pairs={{256,0},{260,4},{264,8},{268,12},{272,16},{276,20},{280,24},{284,2... | collective-permute-start | bytes 192008 | tf_op jit(solution)/shard_map/ppermute | solution.py:36
  23.9 5.5 %collective-permute-start = (bf16[250,128]{1,0:T(8,128)(2,1)S(1)}, bf16[250,128]{1,0:T(8,128)(2,1)S(1)}, u32[]{:S(2)}, u32[]{:S(2)}) collective-permute-start(bf16[250,128]{1,0:T(8,128)(2,1)S(1)} %pad_maximum_fusion.4), channel_id=1, source_target_pairs={{128,0},{388,4},{136,8},{396,12},{144,16},{404,20},{152,24},{412,2... | collective-permute-start | bytes 192008 | tf_op jit(solution)/shard_map/ppermute | solution.py:36
  30.1 0.9 broadcast_select_fusion
  31.1 0.8 reduce-precision_convert_fusion
  32.0 0.7 add_add_fusion
  32.7 0.6 pad_add_fusion
  33.3 1.3 pad_add_fusion.1.edge_rows.refs_17_
  34.9 0.4 collective-permute-done
  35.6 2.6 %collective-permute-start.5 = (bf16[1000,128]{1,0:T(8,128)(2,1)S(1)}, bf16[1000,128]{1,0:T(8,128)(2,1)S(1)}, u32[]{:S(2)}, u32[]{:S(2)}) collective-permute-start(bf16[1000,128]{1,0:T(8,128)(2,1)S(1)} %pad_maximum_fusion.2), channel_id=1, source_target_pairs={{480,0},{36,4},{488,8},{44,12},{496,16},{52,20},{504,24},{60,28},{... | collective-permute-start | bytes 768008 | tf_op jit(solution)/shard_map/ppermute | solution.py:36
  38.2 5.5 %collective-permute-start.4 = (bf16[1000,128]{1,0:T(8,128)(2,1)S(1)}, bf16[1000,128]{1,0:T(8,128)(2,1)S(1)}, u32[]{:S(2)}, u32[]{:S(2)}) collective-permute-start(bf16[1000,128]{1,0:T(8,128)(2,1)S(1)} %pad_maximum_fusion.2), channel_id=1, source_target_pairs={{64,0},{452,4},{72,8},{460,12},{80,16},{468,20},{88,24},{476,28},{... | collective-permute-start | bytes 768008 | tf_op jit(solution)/shard_map/ppermute | solution.py:36
  43.7 3.4 %collective-permute-start.3 = (bf16[1000,128]{1,0:T(8,128)(2,1)S(1)}, bf16[1000,128]{1,0:T(8,128)(2,1)S(1)}, u32[]{:S(2)}, u32[]{:S(2)}) collective-permute-start(bf16[1000,128]{1,0:T(8,128)(2,1)S(1)} %pad_maximum_fusion.2), channel_id=1, source_target_pairs={{32,0},{484,4},{40,8},{492,12},{48,16},{500,20},{56,24},{508,28},{... | collective-permute-start | bytes 768008 | tf_op jit(solution)/shard_map/ppermute | solution.py:36
  47.2 3.1 %collective-permute-done.4 = bf16[1000,128]{1,0:T(8,128)(2,1)S(1)} collective-permute-done((bf16[1000,128]{1,0:T(8,128)(2,1)S(1)}, bf16[1000,128]{1,0:T(8,128)(2,1)S(1)}, u32[]{:S(2)}, u32[]{:S(2)}) %collective-permute-start.4) | collective-permute-done | bytes 256032 | tf_op jit(solution)/shard_map/ppermute | solution.py:36
  50.3 2.7 %collective-permute-done.3 = bf16[1000,128]{1,0:T(8,128)(2,1)S(1)} collective-permute-done((bf16[1000,128]{1,0:T(8,128)(2,1)S(1)}, bf16[1000,128]{1,0:T(8,128)(2,1)S(1)}, u32[]{:S(2)}, u32[]{:S(2)}) %collective-permute-start.3) | collective-permute-done | bytes 256032 | tf_op jit(solution)/shard_map/ppermute | solution.py:36
  53.1 0.5 concatenate.85
  54.2 2.4 collective-permute-start.8
  56.6 3.5 %collective-permute-start.6 = (bf16[4000,128]{1,0:T(8,128)(2,1)S(1)}, bf16[4000,128]{1,0:T(8,128)(2,1)S(1)}, u32[]{:S(2)}, u32[]{:S(2)}) collective-permute-start(bf16[4000,128]{1,0:T(8,128)(2,1)S(1)} %constant_dynamic-update-slice_fusion.7.refs_0_), channel_id=1, source_target_pairs={{8,0},{12,4},{16,8},{20,12},{24,16},{28,20},{0,24},{4,28},{40,32},... | collective-permute-start | bytes 3072008 | tf_op jit(solution)/shard_map/ppermute | solution.py:36
  60.0 0.7 maximum_maximum_fusion.local
  60.8 6.9 %local.1 = (bf16[160,1280]{1,0:T(8,128)(2,1)}, bf16[320,1024]{1,0:T(8,128)(2,1)}, bf16[320,768]{1,0:T(8,128)(2,1)}, f32[160,2432]{1,0:T(8,128)}) custom-call(bf16[160,475]{1,0:T(8,128)(2,1)} %bitcast.122, s32[3,160]{1,0:T(4,128)} %pad_add_fusion.1.edge_rows.refs_17_, bf16[16,3200]{1,0:T(8,128)(2,1)} %maximum_maximum_fusion.local, s32[1,9216]{1,0:T(1,128)} %bitcast.120), custom_call_target="tpu_custom_call" | custom-call | flops 1500000000 | bytes 293184 | tf_op jit(solution)/shard_map/local/pallas_call | solution.py:349
  67.7 16.3 %collective-permute-done.6.refs_1_ = bf16[4000,128]{1,0:T(8,128)(2,1)S(1)} collective-permute-done((bf16[4000,128]{1,0:T(8,128)(2,1)S(1)}, bf16[4000,128]{1,0:T(8,128)(2,1)S(1)}, u32[]{:S(2)}, u32[]{:S(2)}) %collective-permute-start.6) | collective-permute-done | bytes 1024032 | tf_op jit(solution)/shard_map/ppermute | solution.py:36
  84.0 2.3 collective-permute-start.7
  86.3 1.9 collective-permute-start.10
  88.2 2.4 %collective-permute-start.11 = (bf16[4000,128]{1,0:T(8,128)(2,1)S(1)}, bf16[4000,128]{1,0:T(8,128)(2,1)S(1)}, u32[]{:S(2)}, u32[]{:S(2)}) collective-permute-start(bf16[4000,128]{1,0:T(8,128)(2,1)S(1)} %collective-permute-done.6.refs_1_), channel_id=1, source_target_pairs={{4,0},{0,4},{12,8},{8,12},{20,16},{16,20},{28,24},{24,28},{36,32},... | collective-permute-start | bytes 3072008 | tf_op jit(solution)/shard_map/ppermute | solution.py:36
  90.7 1.9 collective-permute-start.14
  92.6 4.8 %collective-permute-start.9 = (bf16[1920,128]{1,0:T(8,128)(2,1)S(1)}, bf16[1920,128]{1,0:T(8,128)(2,1)S(1)}, u32[]{:S(2)}, u32[]{:S(2)}) collective-permute-start(bf16[1920,128]{1,0:T(8,128)(2,1)S(1)} %slice.185), channel_id=1, source_target_pairs={{24,0},{28,4},{0,8},{4,12},{8,16},{12,20},{16,24},{20,28},{56,32},... | collective-permute-start | bytes 1474568 | tf_op jit(solution)/shard_map/ppermute | solution.py:36
  97.4 2.6 %collective-permute-done.7.refs_2_ = bf16[2080,128]{1,0:T(8,128)(2,1)S(1)} collective-permute-done((bf16[2080,128]{1,0:T(8,128)(2,1)S(1)}, bf16[2080,128]{1,0:T(8,128)(2,1)S(1)}, u32[]{:S(2)}, u32[]{:S(2)}) %collective-permute-start.7) | collective-permute-done | bytes 532512 | tf_op jit(solution)/shard_map/ppermute | solution.py:36
  100.1 1.9 collective-permute-start.12
  102.0 6.6 %collective-permute-done.9.refs_3_ = bf16[1920,128]{1,0:T(8,128)(2,1)S(1)} collective-permute-done((bf16[1920,128]{1,0:T(8,128)(2,1)S(1)}, bf16[1920,128]{1,0:T(8,128)(2,1)S(1)}, u32[]{:S(2)}, u32[]{:S(2)}) %collective-permute-start.9) | collective-permute-done | bytes 491552 | tf_op jit(solution)/shard_map/ppermute | solution.py:36
  108.6 2.1 collective-permute-start.13
  110.7 1.6 collective-permute-done.13.refs_8_
  112.3 0.7 copy-done.15
  114.0 23.6 %layer.1 = (bf16[2560,128]{1,0:T(8,128)(2,1)}, bf16[2560,128]{1,0:T(8,128)(2,1)}, bf16[2560,128]{1,0:T(8,128)(2,1)}, bf16[2560,128]{1,0:T(8,128)(2,1)}, bf16[256...) custom-call(bf16[4000,128]{1,0:T(8,128)(2,1)} %copy-done.7, ...), custom_call_target="tpu_custom_call" | custom-call | flops 6000000000 | bytes 11502912 | tf_op jit(solution)/shard_map/layer/pallas_call | solution.py:349
  137.5 2.2 collective-permute-start.15
  139.7 2.3 collective-permute-start.16
  142.0 2.0 collective-permute-start.19
  144.1 1.3 add_convert_fusion.4
  145.6 2.5 %collective-permute-start.20 = (bf16[1280,128]{1,0:T(8,128)(2,1)S(1)}, bf16[1280,128]{1,0:T(8,128)(2,1)S(1)}, u32[]{:S(2)}, u32[]{:S(2)}) collective-permute-start(bf16[1280,128]{1,0:T(8,128)(2,1)S(1)} %get-tuple-element.52), channel_id=1, source_target_pairs={{0,24},{4,28},{8,0},{12,4},{16,8},{20,12},{24,16},{28,20},{32,56},... | collective-permute-start | bytes 983048 | tf_op jit(solution)/shard_map/ppermute | solution.py:40
  148.1 5.2 %collective-permute-start.17 = (bf16[1280,128]{1,0:T(8,128)(2,1)S(1)}, bf16[1280,128]{1,0:T(8,128)(2,1)S(1)}, u32[]{:S(2)}, u32[]{:S(2)}) collective-permute-start(bf16[1280,128]{1,0:T(8,128)(2,1)S(1)} %get-tuple-element.53), channel_id=1, source_target_pairs={{0,8},{4,12},{8,16},{12,20},{16,24},{20,28},{24,0},{28,4},{32,40},... | collective-permute-start | bytes 983048 | tf_op jit(solution)/shard_map/ppermute | solution.py:40
  153.6 7.2 %collective-permute-done.17 = bf16[1280,128]{1,0:T(8,128)(2,1)S(1)} collective-permute-done((bf16[1280,128]{1,0:T(8,128)(2,1)S(1)}, bf16[1280,128]{1,0:T(8,128)(2,1)S(1)}, u32[]{:S(2)}, u32[]{:S(2)}) %collective-permute-start.17) | collective-permute-done | bytes 327712 | tf_op jit(solution)/shard_map/ppermute | solution.py:40
  160.9 6.0 %collective-permute-start.18 = (bf16[2560,128]{1,0:T(8,128)(2,1)S(1)}, bf16[2560,128]{1,0:T(8,128)(2,1)S(1)}, u32[]{:S(2)}, u32[]{:S(2)}) collective-permute-start(bf16[2560,128]{1,0:T(8,128)(2,1)S(1)} %pad_maximum_fusion), channel_id=1, source_target_pairs={{0,8},{4,12},{8,16},{12,20},{16,24},{20,28},{24,0},{28,4},{32,40},... | collective-permute-start | bytes 1966088 | tf_op jit(solution)/shard_map/ppermute | solution.py:40
  167.1 2.1 collective-permute-start.21
  169.1 1.9 collective-permute-start.22
  171.1 5.3 %nodes.1 = (bf16[4,3200]{1,0:T(4,128)(2,1)}, f32[4,3200]{1,0:T(4,128)}) custom-call(bf16[160,475]{1,0:T(8,128)(2,1)} %bitcast.124, bf16[160,2432]{1,0:T(8,128)(2,1)} %get-tuple-element.37.scaled, bf16[160,2432]{1,0:T(8,128)(2,1)} %get-tuple-element.38.grad_dst, s32[3,160]{1,0:T(4,128)} %pad_add_fusion.1.edge_rows.refs_17_), custom_call_target="tpu_custom_call" | custom-call | flops 600000000 | bytes 1710400 | tf_op jit(solution)/shard_map/nodes/pallas_call | solution.py:349
  176.3 4.0 %collective-permute-done.18 = bf16[2560,128]{1,0:T(8,128)(2,1)S(1)} collective-permute-done((bf16[2560,128]{1,0:T(8,128)(2,1)S(1)}, bf16[2560,128]{1,0:T(8,128)(2,1)S(1)}, u32[]{:S(2)}, u32[]{:S(2)}) %collective-permute-start.18) | collective-permute-done | bytes 655392 | tf_op jit(solution)/shard_map/ppermute | solution.py:40
  180.4 5.8 %collective-permute-done.21 = bf16[2560,128]{1,0:T(8,128)(2,1)S(1)} collective-permute-done((bf16[2560,128]{1,0:T(8,128)(2,1)S(1)}, bf16[2560,128]{1,0:T(8,128)(2,1)S(1)}, u32[]{:S(2)}, u32[]{:S(2)}) %collective-permute-start.21) | collective-permute-done | bytes 655392 | tf_op jit(solution)/shard_map/ppermute | solution.py:40
  186.6 1.9 collective-permute-start.23
  188.5 5.1 %collective-permute-start.25 = (bf16[640,128]{1,0:T(8,128)(2,1)S(1)}, bf16[640,128]{1,0:T(8,128)(2,1)S(1)}, u32[]{:S(2)}, u32[]{:S(2)}) collective-permute-start(bf16[640,128]{1,0:T(8,128)(2,1)S(1)} %get-tuple-element.50), channel_id=1, source_target_pairs={{0,480},{4,36},{8,488},{12,44},{16,496},{20,52},{24,504},{28,60},{... | collective-permute-start | bytes 491528 | tf_op jit(solution)/shard_map/ppermute | solution.py:40
  193.7 2.0 collective-permute-start.24
  195.9 3.6 %collective-permute-done.25 = bf16[640,128]{1,0:T(8,128)(2,1)S(1)} collective-permute-done((bf16[640,128]{1,0:T(8,128)(2,1)S(1)}, bf16[640,128]{1,0:T(8,128)(2,1)S(1)}, u32[]{:S(2)}, u32[]{:S(2)}) %collective-permute-start.25) | collective-permute-done | bytes 163872 | tf_op jit(solution)/shard_map/ppermute | solution.py:40
  199.5 5.0 %collective-permute-done.24 = bf16[640,128]{1,0:T(8,128)(2,1)S(1)} collective-permute-done((bf16[640,128]{1,0:T(8,128)(2,1)S(1)}, bf16[640,128]{1,0:T(8,128)(2,1)S(1)}, u32[]{:S(2)}, u32[]{:S(2)}) %collective-permute-start.24) | collective-permute-done | bytes 163872 | tf_op jit(solution)/shard_map/ppermute | solution.py:40
  204.9 4.8 %collective-permute-start.26 = (bf16[150,128]{1,0:T(8,128)(2,1)S(1)}, bf16[150,128]{1,0:T(8,128)(2,1)S(1)}, u32[]{:S(2)}, u32[]{:S(2)}) collective-permute-start(bf16[150,128]{1,0:T(8,128)(2,1)S(1)} %pad_maximum_fusion.7), channel_id=1, source_target_pairs={{0,128},{4,388},{8,136},{12,396},{16,144},{20,404},{24,152},{28,41... | collective-permute-start | bytes 115208 | tf_op jit(solution)/shard_map/ppermute | solution.py:40
  209.7 7.0 %collective-permute-start.27 = (bf16[150,128]{1,0:T(8,128)(2,1)S(1)}, bf16[150,128]{1,0:T(8,128)(2,1)S(1)}, u32[]{:S(2)}, u32[]{:S(2)}) collective-permute-start(bf16[150,128]{1,0:T(8,128)(2,1)S(1)} %pad_maximum_fusion.8), channel_id=1, source_target_pairs={{0,256},{4,260},{8,264},{12,268},{16,272},{20,276},{24,280},{28,28... | collective-permute-start | bytes 115208 | tf_op jit(solution)/shard_map/ppermute | solution.py:40
  216.8 3.6 %collective-permute-start.28 = (bf16[150,128]{1,0:T(8,128)(2,1)S(1)}, bf16[150,128]{1,0:T(8,128)(2,1)S(1)}, u32[]{:S(2)}, u32[]{:S(2)}) collective-permute-start(bf16[150,128]{1,0:T(8,128)(2,1)S(1)} %pad_maximum_fusion.9), channel_id=1, source_target_pairs={{0,384},{4,132},{8,392},{12,140},{16,400},{20,148},{24,408},{28,15... | collective-permute-start | bytes 115208 | tf_op jit(solution)/shard_map/ppermute | solution.py:40
  220.4 4.4 %collective-permute-done.27 = bf16[150,128]{1,0:T(8,128)(2,1)S(1)} collective-permute-done((bf16[150,128]{1,0:T(8,128)(2,1)S(1)}, bf16[150,128]{1,0:T(8,128)(2,1)S(1)}, u32[]{:S(2)}, u32[]{:S(2)}) %collective-permute-start.27) | collective-permute-done | bytes 38432 | tf_op jit(solution)/shard_map/ppermute | solution.py:40
  224.8 2.0 collective-permute-done.28
  226.9 0.7 broadcast_in_dim.23
  227.6 4.6 %all-to-all-start = ((f32[4,10,640]{2,1,0:T(8,128)}), f32[4,10,640]{2,1,0:T(8,128)S(1)}, u32[]{:S(2)}, u32[]{:S(2)}) async-start(f32[4,10,640]{2,1,0:T(8,128)} %broadcast_in_dim.23), calls=%async_computation | async-start | bytes 327680 | tf_op jit(solution)/shard_map/all_to_all | solution.py:452
  232.2 0.6 fusion.1
  232.9 5.5 %all-to-all-done = f32[4,10,640]{2,1,0:T(8,128)S(1)} async-done(((f32[4,10,640]{2,1,0:T(8,128)}), f32[4,10,640]{2,1,0:T(8,128)S(1)}, u32[]{:S(2)}, u32[]{:S(2)}) %all-to-all-start) | async-done | bytes 102432 | tf_op jit(solution)/shard_map/all_to_all | solution.py:452
  238.4 0.6 reduce_sum.9
  (150 shorter events, 4.0 us)
Async XLA Ops:
  3.9 30.8 %collective-permute-start.2 = (bf16[250,128]{1,0:T(8,128)(2,1)S(1)}, bf16[250,128]{1,0:T(8,128)(2,1)S(1)}, u32[]{:S(2)}, u32[]{:S(2)}) collective-permute-start(bf16[250,128]{1,0:T(8,128)(2,1)S(1)} %pad_maximum_fusion.4), channel_id=1, source_target_pairs={{384,0},{132,4},{392,8},{140,12},{400,16},{148,20},{408,24},{156,2... | collective-permute-start | bytes 192008 | tf_op jit(solution)/shard_map/ppermute | solution.py:36
  13.0 21.8 %collective-permute-start.1 = (bf16[250,128]{1,0:T(8,128)(2,1)S(1)}, bf16[250,128]{1,0:T(8,128)(2,1)S(1)}, u32[]{:S(2)}, u32[]{:S(2)}) collective-permute-start(bf16[250,128]{1,0:T(8,128)(2,1)S(1)} %pad_maximum_fusion.4), channel_id=1, source_target_pairs={{256,0},{260,4},{264,8},{268,12},{272,16},{276,20},{280,24},{284,2... | collective-permute-start | bytes 192008 | tf_op jit(solution)/shard_map/ppermute | solution.py:36
  23.9 11.3 %collective-permute-start = (bf16[250,128]{1,0:T(8,128)(2,1)S(1)}, bf16[250,128]{1,0:T(8,128)(2,1)S(1)}, u32[]{:S(2)}, u32[]{:S(2)}) collective-permute-start(bf16[250,128]{1,0:T(8,128)(2,1)S(1)} %pad_maximum_fusion.4), channel_id=1, source_target_pairs={{128,0},{388,4},{136,8},{396,12},{144,16},{404,20},{152,24},{412,2... | collective-permute-start | bytes 192008 | tf_op jit(solution)/shard_map/ppermute | solution.py:36
  35.6 17.4 %collective-permute-start.5 = (bf16[1000,128]{1,0:T(8,128)(2,1)S(1)}, bf16[1000,128]{1,0:T(8,128)(2,1)S(1)}, u32[]{:S(2)}, u32[]{:S(2)}) collective-permute-start(bf16[1000,128]{1,0:T(8,128)(2,1)S(1)} %pad_maximum_fusion.2), channel_id=1, source_target_pairs={{480,0},{36,4},{488,8},{44,12},{496,16},{52,20},{504,24},{60,28},{... | collective-permute-start | bytes 768008 | tf_op jit(solution)/shard_map/ppermute | solution.py:36
  38.2 12.1 %collective-permute-start.4 = (bf16[1000,128]{1,0:T(8,128)(2,1)S(1)}, bf16[1000,128]{1,0:T(8,128)(2,1)S(1)}, u32[]{:S(2)}, u32[]{:S(2)}) collective-permute-start(bf16[1000,128]{1,0:T(8,128)(2,1)S(1)} %pad_maximum_fusion.2), channel_id=1, source_target_pairs={{64,0},{452,4},{72,8},{460,12},{80,16},{468,20},{88,24},{476,28},{... | collective-permute-start | bytes 768008 | tf_op jit(solution)/shard_map/ppermute | solution.py:36
  43.7 9.3 %collective-permute-start.3 = (bf16[1000,128]{1,0:T(8,128)(2,1)S(1)}, bf16[1000,128]{1,0:T(8,128)(2,1)S(1)}, u32[]{:S(2)}, u32[]{:S(2)}) collective-permute-start(bf16[1000,128]{1,0:T(8,128)(2,1)S(1)} %pad_maximum_fusion.2), channel_id=1, source_target_pairs={{32,0},{484,4},{40,8},{492,12},{48,16},{500,20},{56,24},{508,28},{... | collective-permute-start | bytes 768008 | tf_op jit(solution)/shard_map/ppermute | solution.py:36
  53.1 6.9 %copy-start.5 = (bf16[1,4,3200]{2,1,0:T(4,128)(2,1)S(1)}, bf16[1,4,3200]{2,1,0:T(4,128)(2,1)}, u32[]{:S(2)}) copy-start(bf16[1,4,3200]{2,1,0:T(4,128)(2,1)} %param.15) | copy-start | bytes 76804
  54.2 32.1 %copy-start.7 = (bf16[4000,128]{1,0:T(8,128)(2,1)}, bf16[4000,128]{1,0:T(8,128)(2,1)S(1)}, u32[]{:S(2)}) copy-start(bf16[4000,128]{1,0:T(8,128)(2,1)S(1)} %constant_dynamic-update-slice_fusion.7.refs_0_) | copy-start | bytes 3072004
  54.2 36.5 %collective-permute-start.8 = (bf16[4000,128]{1,0:T(8,128)(2,1)S(1)}, bf16[4000,128]{1,0:T(8,128)(2,1)S(1)}, u32[]{:S(2)}, u32[]{:S(2)}) collective-permute-start(bf16[4000,128]{1,0:T(8,128)(2,1)S(1)} %constant_dynamic-update-slice_fusion.7.refs_0_), channel_id=1, source_target_pairs={{24,0},{28,4},{0,8},{4,12},{8,16},{12,20},{16,24},{20,28},{56,32},... | collective-permute-start | bytes 3072008 | tf_op jit(solution)/shard_map/ppermute | solution.py:36
  56.6 27.4 %collective-permute-start.6 = (bf16[4000,128]{1,0:T(8,128)(2,1)S(1)}, bf16[4000,128]{1,0:T(8,128)(2,1)S(1)}, u32[]{:S(2)}, u32[]{:S(2)}) collective-permute-start(bf16[4000,128]{1,0:T(8,128)(2,1)S(1)} %constant_dynamic-update-slice_fusion.7.refs_0_), channel_id=1, source_target_pairs={{8,0},{12,4},{16,8},{20,12},{24,16},{28,20},{0,24},{4,28},{40,32},... | collective-permute-start | bytes 3072008 | tf_op jit(solution)/shard_map/ppermute | solution.py:36
  84.0 29.1 %copy-start.3 = (bf16[4000,128]{1,0:T(8,128)(2,1)}, bf16[4000,128]{1,0:T(8,128)(2,1)S(1)}, u32[]{:S(2)}) copy-start(bf16[4000,128]{1,0:T(8,128)(2,1)S(1)} %collective-permute-done.6.refs_1_) | copy-start | bytes 3072004
  84.0 16.0 %collective-permute-start.7 = (bf16[2080,128]{1,0:T(8,128)(2,1)S(1)}, bf16[2080,128]{1,0:T(8,128)(2,1)S(1)}, u32[]{:S(2)}, u32[]{:S(2)}) collective-permute-start(bf16[2080,128]{1,0:T(8,128)(2,1)S(1)} %slice.184), channel_id=1, source_target_pairs={{8,0},{12,4},{16,8},{20,12},{24,16},{28,20},{0,24},{4,28},{40,32},... | collective-permute-start | bytes 1597448 | tf_op jit(solution)/shard_map/ppermute | solution.py:36
  86.3 24.4 %collective-permute-start.10 = (bf16[4000,128]{1,0:T(8,128)(2,1)S(1)}, bf16[4000,128]{1,0:T(8,128)(2,1)S(1)}, u32[]{:S(2)}, u32[]{:S(2)}) collective-permute-start(bf16[4000,128]{1,0:T(8,128)(2,1)S(1)} %constant_dynamic-update-slice_fusion.7.refs_0_), channel_id=1, source_target_pairs={{4,0},{0,4},{12,8},{8,12},{20,16},{16,20},{28,24},{24,28},{36,32},... | collective-permute-start | bytes 3072008 | tf_op jit(solution)/shard_map/ppermute | solution.py:36
  88.2 24.1 %collective-permute-start.11 = (bf16[4000,128]{1,0:T(8,128)(2,1)S(1)}, bf16[4000,128]{1,0:T(8,128)(2,1)S(1)}, u32[]{:S(2)}, u32[]{:S(2)}) collective-permute-start(bf16[4000,128]{1,0:T(8,128)(2,1)S(1)} %collective-permute-done.6.refs_1_), channel_id=1, source_target_pairs={{4,0},{0,4},{12,8},{8,12},{20,16},{16,20},{28,24},{24,28},{36,32},... | collective-permute-start | bytes 3072008 | tf_op jit(solution)/shard_map/ppermute | solution.py:36
  90.7 22.4 %copy-start.4 = (bf16[4000,128]{1,0:T(8,128)(2,1)}, bf16[4000,128]{1,0:T(8,128)(2,1)S(1)}, u32[]{:S(2)}) copy-start(bf16[4000,128]{1,0:T(8,128)(2,1)S(1)} %collective-permute-done.8.refs_4_) | copy-start | bytes 3072004
  90.7 21.7 %collective-permute-start.14 = (bf16[4000,128]{1,0:T(8,128)(2,1)S(1)}, bf16[4000,128]{1,0:T(8,128)(2,1)S(1)}, u32[]{:S(2)}, u32[]{:S(2)}) collective-permute-start(bf16[4000,128]{1,0:T(8,128)(2,1)S(1)} %collective-permute-done.8.refs_4_), channel_id=1, source_target_pairs={{4,0},{0,4},{12,8},{8,12},{20,16},{16,20},{28,24},{24,28},{36,32},... | collective-permute-start | bytes 3072008 | tf_op jit(solution)/shard_map/ppermute | solution.py:36
  92.6 15.9 %collective-permute-start.9 = (bf16[1920,128]{1,0:T(8,128)(2,1)S(1)}, bf16[1920,128]{1,0:T(8,128)(2,1)S(1)}, u32[]{:S(2)}, u32[]{:S(2)}) collective-permute-start(bf16[1920,128]{1,0:T(8,128)(2,1)S(1)} %slice.185), channel_id=1, source_target_pairs={{24,0},{28,4},{0,8},{4,12},{8,16},{12,20},{16,24},{20,28},{56,32},... | collective-permute-start | bytes 1474568 | tf_op jit(solution)/shard_map/ppermute | solution.py:36
  100.1 13.0 %copy-start.12 = (bf16[2080,128]{1,0:T(8,128)(2,1)}, bf16[2080,128]{1,0:T(8,128)(2,1)S(1)}, u32[]{:S(2)}) copy-start(bf16[2080,128]{1,0:T(8,128)(2,1)S(1)} %collective-permute-done.7.refs_2_) | copy-start | bytes 1597444
  100.1 12.3 %collective-permute-start.12 = (bf16[2080,128]{1,0:T(8,128)(2,1)S(1)}, bf16[2080,128]{1,0:T(8,128)(2,1)S(1)}, u32[]{:S(2)}, u32[]{:S(2)}) collective-permute-start(bf16[2080,128]{1,0:T(8,128)(2,1)S(1)} %collective-permute-done.7.refs_2_), channel_id=1, source_target_pairs={{4,0},{0,4},{12,8},{8,12},{20,16},{16,20},{28,24},{24,28},{36,32},... | collective-permute-start | bytes 1597448 | tf_op jit(solution)/shard_map/ppermute | solution.py:36
  108.6 4.5 %copy-start.14 = (bf16[1920,128]{1,0:T(8,128)(2,1)}, bf16[1920,128]{1,0:T(8,128)(2,1)S(1)}, u32[]{:S(2)}) copy-start(bf16[1920,128]{1,0:T(8,128)(2,1)S(1)} %collective-permute-done.9.refs_3_) | copy-start | bytes 1474564
  108.6 3.7 %collective-permute-start.13 = (bf16[1920,128]{1,0:T(8,128)(2,1)S(1)}, bf16[1920,128]{1,0:T(8,128)(2,1)S(1)}, u32[]{:S(2)}, u32[]{:S(2)}) collective-permute-start(bf16[1920,128]{1,0:T(8,128)(2,1)S(1)} %collective-permute-done.9.refs_3_), channel_id=1, source_target_pairs={{4,0},{0,4},{12,8},{8,12},{20,16},{16,20},{28,24},{24,28},{36,32},... | collective-permute-start | bytes 1474568 | tf_op jit(solution)/shard_map/ppermute | solution.py:36
  110.7 2.4 %copy-start.8 = (bf16[4000,128]{1,0:T(8,128)(2,1)}, bf16[4000,128]{1,0:T(8,128)(2,1)S(1)}, u32[]{:S(2)}) copy-start(bf16[4000,128]{1,0:T(8,128)(2,1)S(1)} %collective-permute-done.10.refs_5_) | copy-start | bytes 3072004
  112.3 0.8 copy-start.15
  112.3 1.1 copy-start.9
  112.3 1.5 copy-start.10
  113.1 0.9 copy-start.13
  137.5 7.8 %copy-start.2 = (bf16[2560,128]{1,0:T(8,128)(2,1)S(1)}, bf16[2560,128]{1,0:T(8,128)(2,1)}, u32[]{:S(2)}) copy-start(bf16[2560,128]{1,0:T(8,128)(2,1)} %get-tuple-element.33) | copy-start | bytes 1966084
  137.5 6.5 %collective-permute-start.15 = (bf16[2560,128]{1,0:T(8,128)(2,1)}, bf16[2560,128]{1,0:T(8,128)(2,1)S(1)}, u32[]{:S(2)}, u32[]{:S(2)}) collective-permute-start(bf16[2560,128]{1,0:T(8,128)(2,1)} %get-tuple-element.32), channel_id=1, source_target_pairs={{0,4},{4,0},{8,12},{12,8},{16,20},{20,16},{24,28},{28,24},{32,36},... | collective-permute-start | bytes 1966088 | tf_op jit(solution)/shard_map/ppermute | solution.py:40
  139.7 5.6 %collective-permute-start.16 = (bf16[2560,128]{1,0:T(8,128)(2,1)}, bf16[2560,128]{1,0:T(8,128)(2,1)S(1)}, u32[]{:S(2)}, u32[]{:S(2)}) collective-permute-start(bf16[2560,128]{1,0:T(8,128)(2,1)} %get-tuple-element.34), channel_id=1, source_target_pairs={{0,4},{4,0},{8,12},{12,8},{16,20},{20,16},{24,28},{28,24},{32,36},... | collective-permute-start | bytes 1966088 | tf_op jit(solution)/shard_map/ppermute | solution.py:40
  142.0 11.3 %collective-permute-start.19 = (bf16[2560,128]{1,0:T(8,128)(2,1)}, bf16[2560,128]{1,0:T(8,128)(2,1)S(1)}, u32[]{:S(2)}, u32[]{:S(2)}) collective-permute-start(bf16[2560,128]{1,0:T(8,128)(2,1)} %get-tuple-element.36), channel_id=1, source_target_pairs={{0,4},{4,0},{8,12},{12,8},{16,20},{20,16},{24,28},{28,24},{32,36},... | collective-permute-start | bytes 1966088 | tf_op jit(solution)/shard_map/ppermute | solution.py:40
  145.5 7.8 %copy-start.1 = (bf16[2560,128]{1,0:T(8,128)(2,1)S(1)}, bf16[2560,128]{1,0:T(8,128)(2,1)}, u32[]{:S(2)}) copy-start(bf16[2560,128]{1,0:T(8,128)(2,1)} %get-tuple-element.35) | copy-start | bytes 1966084
  145.6 21.3 %collective-permute-start.20 = (bf16[1280,128]{1,0:T(8,128)(2,1)S(1)}, bf16[1280,128]{1,0:T(8,128)(2,1)S(1)}, u32[]{:S(2)}, u32[]{:S(2)}) collective-permute-start(bf16[1280,128]{1,0:T(8,128)(2,1)S(1)} %get-tuple-element.52), channel_id=1, source_target_pairs={{0,24},{4,28},{8,0},{12,4},{16,8},{20,12},{24,16},{28,20},{32,56},... | collective-permute-start | bytes 983048 | tf_op jit(solution)/shard_map/ppermute | solution.py:40
  148.1 12.7 %collective-permute-start.17 = (bf16[1280,128]{1,0:T(8,128)(2,1)S(1)}, bf16[1280,128]{1,0:T(8,128)(2,1)S(1)}, u32[]{:S(2)}, u32[]{:S(2)}) collective-permute-start(bf16[1280,128]{1,0:T(8,128)(2,1)S(1)} %get-tuple-element.53), channel_id=1, source_target_pairs={{0,8},{4,12},{8,16},{12,20},{16,24},{20,28},{24,0},{28,4},{32,40},... | collective-permute-start | bytes 983048 | tf_op jit(solution)/shard_map/ppermute | solution.py:40
  160.9 8.2 %copy-start.11 = (bf16[2560,128]{1,0:T(8,128)(2,1)S(1)}, bf16[2560,128]{1,0:T(8,128)(2,1)}, u32[]{:S(2)}) copy-start(bf16[2560,128]{1,0:T(8,128)(2,1)} %get-tuple-element.44) | copy-start | bytes 1966084
  160.9 19.4 %collective-permute-start.18 = (bf16[2560,128]{1,0:T(8,128)(2,1)S(1)}, bf16[2560,128]{1,0:T(8,128)(2,1)S(1)}, u32[]{:S(2)}, u32[]{:S(2)}) collective-permute-start(bf16[2560,128]{1,0:T(8,128)(2,1)S(1)} %pad_maximum_fusion), channel_id=1, source_target_pairs={{0,8},{4,12},{8,16},{12,20},{16,24},{20,28},{24,0},{28,4},{32,40},... | collective-permute-start | bytes 1966088 | tf_op jit(solution)/shard_map/ppermute | solution.py:40
  167.1 19.2 %copy-start = (bf16[2560,128]{1,0:T(8,128)(2,1)S(1)}, bf16[2560,128]{1,0:T(8,128)(2,1)}, u32[]{:S(2)}) copy-start(bf16[2560,128]{1,0:T(8,128)(2,1)} %get-tuple-element.43) | copy-start | bytes 1966084
  167.1 19.1 %collective-permute-start.21 = (bf16[2560,128]{1,0:T(8,128)(2,1)S(1)}, bf16[2560,128]{1,0:T(8,128)(2,1)S(1)}, u32[]{:S(2)}, u32[]{:S(2)}) collective-permute-start(bf16[2560,128]{1,0:T(8,128)(2,1)S(1)} %pad_maximum_fusion.1), channel_id=1, source_target_pairs={{0,24},{4,28},{8,0},{12,4},{16,8},{20,12},{24,16},{28,20},{32,56},... | collective-permute-start | bytes 1966088 | tf_op jit(solution)/shard_map/ppermute | solution.py:40
  169.1 17.1 %collective-permute-start.22 = (bf16[2560,128]{1,0:T(8,128)(2,1)S(1)}, bf16[2560,128]{1,0:T(8,128)(2,1)S(1)}, u32[]{:S(2)}, u32[]{:S(2)}) collective-permute-start(bf16[2560,128]{1,0:T(8,128)(2,1)S(1)} %copy-done.11), channel_id=1, source_target_pairs={{0,4},{4,0},{8,12},{12,8},{16,20},{20,16},{24,28},{28,24},{32,36},... | collective-permute-start | bytes 1966088 | tf_op jit(solution)/shard_map/ppermute | solution.py:40
  186.6 9.3 %collective-permute-start.23 = (bf16[640,128]{1,0:T(8,128)(2,1)S(1)}, bf16[640,128]{1,0:T(8,128)(2,1)S(1)}, u32[]{:S(2)}, u32[]{:S(2)}) collective-permute-start(bf16[640,128]{1,0:T(8,128)(2,1)S(1)} %get-tuple-element.49), channel_id=1, source_target_pairs={{0,32},{4,484},{8,40},{12,492},{16,48},{20,500},{24,56},{28,508},{... | collective-permute-start | bytes 491528 | tf_op jit(solution)/shard_map/ppermute | solution.py:40
  188.5 11.0 %collective-permute-start.25 = (bf16[640,128]{1,0:T(8,128)(2,1)S(1)}, bf16[640,128]{1,0:T(8,128)(2,1)S(1)}, u32[]{:S(2)}, u32[]{:S(2)}) collective-permute-start(bf16[640,128]{1,0:T(8,128)(2,1)S(1)} %get-tuple-element.50), channel_id=1, source_target_pairs={{0,480},{4,36},{8,488},{12,44},{16,496},{20,52},{24,504},{28,60},{... | collective-permute-start | bytes 491528 | tf_op jit(solution)/shard_map/ppermute | solution.py:40
  193.7 10.9 %collective-permute-start.24 = (bf16[640,128]{1,0:T(8,128)(2,1)S(1)}, bf16[640,128]{1,0:T(8,128)(2,1)S(1)}, u32[]{:S(2)}, u32[]{:S(2)}) collective-permute-start(bf16[640,128]{1,0:T(8,128)(2,1)S(1)} %get-tuple-element.51), channel_id=1, source_target_pairs={{0,64},{4,452},{8,72},{12,460},{16,80},{20,468},{24,88},{28,476},{... | collective-permute-start | bytes 491528 | tf_op jit(solution)/shard_map/ppermute | solution.py:40
  204.6 27.6 %copy-start.6 = (f32[4,3200]{1,0:T(4,128)S(1)}, f32[4,3200]{1,0:T(4,128)}, u32[]{:S(2)}) copy-start(f32[4,3200]{1,0:T(4,128)} %get-tuple-element.42) | copy-start | bytes 153604
  204.9 15.5 %collective-permute-start.26 = (bf16[150,128]{1,0:T(8,128)(2,1)S(1)}, bf16[150,128]{1,0:T(8,128)(2,1)S(1)}, u32[]{:S(2)}, u32[]{:S(2)}) collective-permute-start(bf16[150,128]{1,0:T(8,128)(2,1)S(1)} %pad_maximum_fusion.7), channel_id=1, source_target_pairs={{0,128},{4,388},{8,136},{12,396},{16,144},{20,404},{24,152},{28,41... | collective-permute-start | bytes 115208 | tf_op jit(solution)/shard_map/ppermute | solution.py:40
  209.7 15.1 %collective-permute-start.27 = (bf16[150,128]{1,0:T(8,128)(2,1)S(1)}, bf16[150,128]{1,0:T(8,128)(2,1)S(1)}, u32[]{:S(2)}, u32[]{:S(2)}) collective-permute-start(bf16[150,128]{1,0:T(8,128)(2,1)S(1)} %pad_maximum_fusion.8), channel_id=1, source_target_pairs={{0,256},{4,260},{8,264},{12,268},{16,272},{20,276},{24,280},{28,28... | collective-permute-start | bytes 115208 | tf_op jit(solution)/shard_map/ppermute | solution.py:40
  216.8 10.0 %collective-permute-start.28 = (bf16[150,128]{1,0:T(8,128)(2,1)S(1)}, bf16[150,128]{1,0:T(8,128)(2,1)S(1)}, u32[]{:S(2)}, u32[]{:S(2)}) collective-permute-start(bf16[150,128]{1,0:T(8,128)(2,1)S(1)} %pad_maximum_fusion.9), channel_id=1, source_target_pairs={{0,384},{4,132},{8,392},{12,140},{16,400},{20,148},{24,408},{28,15... | collective-permute-start | bytes 115208 | tf_op jit(solution)/shard_map/ppermute | solution.py:40
  227.6 10.8 %all-to-all-start = ((f32[4,10,640]{2,1,0:T(8,128)}), f32[4,10,640]{2,1,0:T(8,128)S(1)}, u32[]{:S(2)}, u32[]{:S(2)}) async-start(f32[4,10,640]{2,1,0:T(8,128)} %broadcast_in_dim.23), calls=%async_computation | async-start | bytes 327680 | tf_op jit(solution)/shard_map/all_to_all | solution.py:452
